TPU v7x, 128 devices: a whole 4x4x4 slice. The times are simulated.
128 devices in a mesh: vol: 32 (over x, z, core), mem: 4 (over y).
Axes of the slice: x: 4, y: 4, z: 4, core: 2. Of those that a mesh axis runs over, the one named last changes fastest.
Arguments:
- potential: float32 [128, 256, 1024], P('vol', 'mem'), may hold values from -6 to 6
- conductivity: float32 [128, 256, 1024], P('vol', 'mem'), may hold values from 0.1 to 4
- ion_states: float32 [40, 2097152], P(None, ('vol', 'mem')), may hold values from 0 to 1
- rate_scale: float32 [2, 40], replicated, may hold values from 0.05 to 2
- rate_slope: float32 [2, 40], replicated, may hold values from -1 to 1
- type_cond: float32 [3, 40], replicated, may hold values from 0.005 to 0.05
- reversal: float32 [40], replicated, may hold values from -2 to 2
- facet_counts: int32 [8192], P(('vol', 'mem')), may hold values from 0 to 256, as said below
- intra_voxel: int32 [2097152], P(('vol', 'mem')), may hold values from 0 to 262143, as said below
- extra_voxel: int32 [2097152], P(('vol', 'mem')), may hold values from 0 to 262143, as said below
- cell_type: int32 [8192], P(('vol', 'mem')), may hold values from 0 to 2
- gap_partner: int32 [8192, 8], P(('vol', 'mem')), may hold values from 0 to 8191, as said below
- gap_cond: float32 [8192, 8], P(('vol', 'mem')), may hold values from 0.2 to 2
Outputs:
- potential_next: float32 [128, 256, 1024], P('vol', 'mem')
- states_next: float32 [40, 2097152], P(None, ('vol', 'mem'))
- membrane_current: float32 [2097152], P(('vol', 'mem'))
Inputs may be any that keep to these rules, and one draw needn't show every extreme that they name: `facet_counts`: within each brick's 64 cell slots, the cells with a positive count come first; a used cell has 64 to 256 facets; some brick has all its cells used and some cell uses all 256 slots. `intra_voxel`: local index x * 64 * 1024 + y * 1024 + z within the brick that holds the facet; the facets of the cell in slot s of its brick lie in local indices s * R to s * R + R - 1, with R = 4096. `extra_voxel`: local index x * 64 * 1024 + y * 1024 + z within the brick that holds the facet; the facets of the cell in slot s of its brick lie in local indices s * R to s * R + R - 1, with R = 4096. `gap_partner`: each partner is a cell with a positive count, in a brick whose first brick index differs from its own cell's by at most one.
All inputs are finite; a program needn't handle non-finite values.
Results may differ from a plain program's by a relative error of at most 0.0003.
Values sent between devices are 32-bit elements; how exact they have to be, the bound alone decides.
No kernel may reach another device: no remote copies, remote signals or barrier semaphores. Data moves between devices by JAX's collectives and lax.ppermute only.
A program may use at most 64 MiB of HBM per device.

v0:
```python
import math

import jax
import jax.numpy as jnp
from jax import lax
from jax.sharding import PartitionSpec as P

ITERS = 4


mass_coef = 1.0
time_step = 0.5
low_eig = 0.2
high_eig = 1.8


def with_halo(x, sides, width):
    for axis, dim in sides:
        size, length = (lax.axis_size(axis), x.shape[dim])
        up = [(i, (i + 1) % size) for i in range(size - 1)]
        down = [(j, i) for i, j in up]
        last = lax.slice_in_dim(x, length - width, length, axis=dim)
        initial = lax.slice_in_dim(x, 0, width, axis=dim)
        before = lax.ppermute(last, axis, up)
        after = lax.ppermute(initial, axis, down)
        x = jnp.concatenate([before, x, after], axis=dim)
    return x


def neighbour_views(extended):
    padded = jnp.pad(extended, ((0, 0), (0, 0), (1, 1)))
    centre = padded[1:-1, 1:-1, 1:-1]
    views = (
        padded[:-2, 1:-1, 1:-1],
        padded[2:, 1:-1, 1:-1],
        padded[1:-1, :-2, 1:-1],
        padded[1:-1, 2:, 1:-1],
        padded[1:-1, 1:-1, :-2],
        padded[1:-1, 1:-1, 2:],
    )
    return (centre, views)


def face_coeffs(cond_ext):
    centre, views = neighbour_views(cond_ext)
    coeffs = tuple((0.5 * (centre + other) for other in views))
    diagonal = mass_coef + time_step * (
        coeffs[0] + coeffs[1] + coeffs[2] + coeffs[3] + coeffs[4] + coeffs[5]
    )
    return (coeffs, diagonal)


def operator_apply(field_ext, coeffs, diagonal):
    centre, views = neighbour_views(field_ext)
    total = coeffs[0] * views[0]
    for number in range(1, 6):
        total = total + coeffs[number] * views[number]
    return diagonal * centre - time_step * total


def chebyshev(apply_fn, rhs_field, start, diagonal, inside):
    theta = 0.5 * (high_eig + low_eig)
    delta = 0.5 * (high_eig - low_eig)
    sigma_one = theta / delta
    cheb_rho = 1.0 / sigma_one
    iterate = start
    resid = inside * (rhs_field - apply_fn(iterate)) / diagonal
    update = resid / theta
    for sweep in range(ITERS):
        iterate = iterate + update
        if sweep + 1 < ITERS:
            resid = inside * (rhs_field - apply_fn(iterate)) / diagonal
            rho_next = 1.0 / (2.0 * sigma_one - cheb_rho)
            update = rho_next * cheb_rho * update + 2.0 * rho_next / delta * resid
            cheb_rho = rho_next
    return iterate


def ionic_update(states, voltage, type_flat, rate_scale, rate_slope, type_cond, reversal):
    opening = rate_scale[0][:, None] * jnp.exp(rate_slope[0][:, None] * voltage[None, :])
    closing = rate_scale[1][:, None] * jnp.exp(-rate_slope[1][:, None] * voltage[None, :])
    total = opening + closing
    steady = opening / total
    fresh = steady + (states - steady) * jnp.exp(-time_step * total)
    weighted = jnp.dot(type_cond, fresh, precision=lax.Precision.HIGHEST)
    offsets = jnp.dot(type_cond * reversal[None, :], fresh, precision=lax.Precision.HIGHEST)
    kinds = jnp.arange(type_cond.shape[0], dtype=jnp.int32)
    onehot = (type_flat[None, :] == kinds[:, None]).astype(fresh.dtype)
    ion_current = jnp.sum(onehot * (weighted * voltage[None, :] - offsets), axis=0)
    return (fresh, ion_current)


def facet_tables(voxels, cells_here, slots_cell, region, lanes):
    rows_region = region // lanes
    base = jnp.arange(cells_here, dtype=jnp.int32) * region
    offset = voxels.reshape(cells_here, slots_cell) - base[:, None]
    row_table = (
        (offset // lanes)[:, :, None] == jnp.arange(rows_region, dtype=jnp.int32)[None, None, :]
    ).astype(jnp.float32)
    lane_table = (
        (offset % lanes)[:, :, None] == jnp.arange(lanes, dtype=jnp.int32)[None, None, :]
    ).astype(jnp.float32)
    return (row_table, lane_table)


def pick_values(blocks, row_table, lane_table):
    chosen = jnp.einsum("cfa,cal->cfl", row_table, blocks, precision=lax.Precision.HIGHEST)
    return jnp.sum(chosen * lane_table, axis=2)


def place_values(values, row_table, lane_table):
    return jnp.einsum(
        "cfa,cfl->cal", row_table, lane_table * values[:, :, None], precision=lax.Precision.HIGHEST
    )


def per_device(
    potential,
    conductivity,
    ion_states,
    rate_scale,
    rate_slope,
    type_cond,
    reversal,
    facet_counts,
    intra_voxel,
    extra_voxel,
    cell_type,
    gap_partner,
    gap_cond,
):
    cells_here = facet_counts.shape[0]
    slots_cell = ion_states.shape[1] // cells_here
    flat_field = potential.reshape(-1)
    region = flat_field.shape[0] // cells_here
    lanes = math.gcd(region, 128)
    blocks = flat_field.reshape(cells_here, region // lanes, lanes)
    rows_in, lanes_in = facet_tables(intra_voxel, cells_here, slots_cell, region, lanes)
    rows_ex, lanes_ex = facet_tables(extra_voxel, cells_here, slots_cell, region, lanes)
    voltage = (
        pick_values(blocks, rows_in, lanes_in) - pick_values(blocks, rows_ex, lanes_ex)
    ).reshape(-1)
    active = (jnp.arange(slots_cell, dtype=jnp.int32)[None, :] < facet_counts[:, None]).reshape(-1)
    divisor = jnp.maximum(facet_counts, 1).astype(jnp.float32)
    cell_volt = (
        jnp.sum(jnp.where(active, voltage, 0.0).reshape(cells_here, slots_cell), axis=1) / divisor
    )
    column_volt = lax.all_gather(cell_volt, "mem", axis=0, tiled=True)
    band_volt = with_halo(column_volt[None, :], (("vol", 0),), 1)
    column_span = lax.axis_size("mem") * cells_here
    partner_row = gap_partner // column_span
    partner_col = gap_partner % column_span
    position = (partner_row - lax.axis_index("vol") + 1) * column_span + partner_col
    partner_volt = jnp.take(band_volt.reshape(-1), position)
    gap_current = jnp.sum(gap_cond * (cell_volt[:, None] - partner_volt), axis=1)
    gap_facet = jnp.repeat(gap_current / divisor, slots_cell)
    type_flat = jnp.repeat(cell_type, slots_cell)
    fresh, ion_current = ionic_update(
        ion_states, voltage, type_flat, rate_scale, rate_slope, type_cond, reversal
    )
    membrane_current = jnp.where(active, ion_current + gap_facet, 0.0)
    states_next = jnp.where(active[None, :], fresh, ion_states)
    current_cells = membrane_current.reshape(cells_here, slots_cell)
    source = place_values(current_cells, rows_in, lanes_in) - place_values(
        current_cells, rows_ex, lanes_ex
    )
    rhs_field = mass_coef * potential - time_step * source.reshape(potential.shape)
    cond_ext = with_halo(conductivity, (("vol", 0), ("mem", 1)), 1)
    coeffs, diagonal = face_coeffs(cond_ext)

    def apply_operator(field):
        field_ext = with_halo(field, (("vol", 0), ("mem", 1)), 1)
        return operator_apply(field_ext, coeffs, diagonal)

    potential_next = chebyshev(apply_operator, rhs_field, potential, diagonal, 1.0)
    return (potential_next, states_next, membrane_current)


def solution(mesh):
    in_specs = (
        P("vol", "mem", None),
        P("vol", "mem", None),
        P(None, ("vol", "mem")),
        P(),
        P(),
        P(),
        P(),
        P(("vol", "mem")),
        P(("vol", "mem")),
        P(("vol", "mem")),
        P(("vol", "mem")),
        P(("vol", "mem"), None),
        P(("vol", "mem"), None),
    )
    out_specs = (P("vol", "mem", None), P(None, ("vol", "mem")), P(("vol", "mem")))
    return jax.shard_map(
        per_device, mesh=mesh, in_specs=in_specs, out_specs=out_specs, check_vma=False
    )
```

profile of v0, /device:TPU:6, one launch (start us, length us, event | category | flops | bytes accessed | tf_op | source)
XLA Modules:
  0.0 161.5 jit_solution(590196926236685201)
XLA Ops:
  5.3 4.5 %select_reduce_fusion = f32[64,256]{1,0:T(8,128)S(1)} fusion(s32[64,256]{1,0:T(8,128)S(1)} %get-tuple-element.41, f32[64,32,128]{2,1,0:T(8,128)S(1)} %reshape_reshape.3, s32[64,256]{1,0:T(8,128)S(1)} %get-tuple-element.40), kind=kOutput, calls=%fused_computation.9 | convolution fusion | flops 812105728 | bytes 1245184 | tf_op jit(solution)/shard_map/cfa,cal->cfl/dot_general | solution.py:107
  9.8 4.5 %select_reduce_fusion.1 = f32[64,256]{1,0:T(8,128)S(1)} fusion(s32[64,256]{1,0:T(8,128)S(1)} %get-tuple-element.50, f32[64,32,128]{2,1,0:T(8,128)S(1)} %reshape_reshape.3, s32[64,256]{1,0:T(8,128)S(1)} %get-tuple-element.51), kind=kOutput, calls=%fused_computation.11 | convolution fusion | flops 812105728 | bytes 1245184 | tf_op jit(solution)/shard_map/cfa,cal->cfl/dot_general | solution.py:107
  14.7 10.7 %all-reduce.5 = f32[256]{0:T(256)S(1)} all-reduce(f32[256]{0:T(256)S(1)} %get-tuple-element.16), channel_id=1, replica_groups=mesh['vol'=32,'mem'=4] {'mem'}, use_global_device_ids=true, to_apply=%add.5 | all-reduce | flops 256 | bytes 2048
  25.5 3.6 %collective-permute-start.1 = (f32[1,256]{1,0:T(1,128)S(1)}, f32[1,256]{1,0:T(1,128)S(1)}, u32[]{:S(2)}, u32[]{:S(2)}) collective-permute-start(f32[1,256]{1,0:T(1,128)S(1)} %bitcast.30), channel_id=1, source_target_pairs={{4,0},{8,4},{12,8},{16,12},{20,16},{24,20},{28,24},{32,28},{36,32}... | collective-permute-start | bytes 3080 | tf_op jit(solution)/shard_map/ppermute | solution.py:25
  31.9 5.7 %collective-permute-start.7 = (f32[1,64,1024]{2,1,0:T(8,128)}, f32[1,64,1024]{2,1,0:T(8,128)S(1)}, u32[]{:S(2)}, u32[]{:S(2)}) collective-permute-start(f32[1,64,1024]{2,1,0:T(8,128)} %get-tuple-element.36), channel_id=1, source_target_pairs={{4,0},{8,4},{12,8},{16,12},{20,16},{24,20},{28,24},{32,28},{36,32}... | collective-permute-start | bytes 786440 | tf_op jit(solution)/shard_map/ppermute | solution.py:25
  42.8 4.9 %broadcast_select_fusion = (f32[40,16384]{1,0:T(8,128)}, f32[40,16384]{1,0:T(8,128)S(1)}) fusion(f32[40,16384]{1,0:T(8,128)} %param.15, pred[16384]{0:T(1024)(128)(4,1)S(1)} %lt.55, f32[40]{0:T(128)S(1)} %get-tuple-element.47, f32[40]{0:T(128)S(1)} %get-tuple-element.52, f32[16384]{0:T(1024)S(1)} %bitcast.26, f32[40]{0:T(128)S(1)} %get-tuple-element.46, ...), kind=kLoop, calls=%fused_computation.43 | loop fusion | flops 7208960 | bytes 7946880 | tf_op jit(solution)/shard_map/jit(_where)/select_n | solution.py:162
  50.7 5.9 %collective-permute-start.3 = (f32[1,64,1024]{2,1,0:T(8,128)}, f32[1,64,1024]{2,1,0:T(8,128)S(1)}, u32[]{:S(2)}, u32[]{:S(2)}) collective-permute-start(f32[1,64,1024]{2,1,0:T(8,128)} %get-tuple-element.35), channel_id=1, source_target_pairs={{4,0},{8,4},{12,8},{16,12},{20,16},{24,20},{28,24},{32,28},{36,32}... | collective-permute-start | bytes 786440 | tf_op jit(solution)/shard_map/ppermute | solution.py:25
  56.7 2.3 %gather_fusion = f32[512]{0:T(512)S(1)} fusion(f32[768]{0:T(1024)S(1)} %reshape.239, s32[1024]{0:T(1024)S(1)} %pad_clamp_fusion), kind=kCustom, calls=%fused_computation | custom fusion | bytes 6144 | tf_op jit(solution)/shard_map/jit(_take)/gather | solution.py:154
  59.3 6.3 %fusion.2 = f32[64,32,128]{2,1,0:T(8,128)S(1)} fusion(f32[64,256]{1,0:T(8,128)S(1)} %get-tuple-element.49, s32[64,256]{1,0:T(8,128)} %copy-done.5, s32[64,256]{1,0:T(8,128)} %copy-done.4), kind=kOutput, calls=%fused_computation.5 | convolution fusion | flops 810024960 | bytes 1245184 | tf_op jit(solution)/shard_map/cfa,cfl->cal/dot_general | solution.py:112
  65.6 6.4 %fusion.16 = f32[64,32,128]{2,1,0:T(8,128)} fusion(f32[64,32,128]{2,1,0:T(8,128)S(1)} %fusion.2, f32[64,256]{1,0:T(8,128)S(1)} %get-tuple-element.49, s32[64,256]{1,0:T(8,128)S(1)} %get-tuple-element.50, s32[64,256]{1,0:T(8,128)S(1)} %get-tuple-element.51), kind=kOutput, calls=%fused_computation.42 | convolution fusion | flops 810549248 | bytes 2293760 | tf_op jit(solution)/shard_map/cfa,cfl->cal/dot_general | solution.py:112
  72.0 2.4 %mul.303 = f32[4,64,1024]{2,1,0:T(8,128)} reshape(f32[64,32,128]{2,1,0:T(8,128)} %fusion.16) | data formatting | bytes 2097152 | tf_op jit(solution)/shard_map/mul | solution.py:167
  78.8 5.4 %collective-permute-start.4 = (f32[6,1,1024]{2,1,0:T(1,128)S(1)}, f32[6,1,1024]{2,1,0:T(1,128)S(1)}, u32[]{:S(2)}, u32[]{:S(2)}) collective-permute-start(f32[6,1,1024]{2,1,0:T(1,128)S(1)} %get-tuple-element.25), channel_id=1, source_target_pairs={{0,1},{1,2},{2,3},{4,5},{5,6},{6,7},{8,9},{9,10},{10,11},{12,13},{... | collective-permute-start | bytes 73736 | tf_op jit(solution)/shard_map/ppermute | solution.py:24
  86.3 2.6 %fusion.113 = (f32[4,64,1024]{2,1,0:T(8,128)S(1)}, f32[4,64,1024]{2,1,0:T(8,128)S(1)}, f32[4,64,1024]{2,1,0:T(8,128)S(1)}, f32[4,64,1024]{2,1,0:T(8,128)S(1)}, f...) fusion(f32[4,64,1024]{2,1,0:T(8,128)S(1)} %copy-done.2, ...), kind=kLoop, calls=%fused_computation.233 | loop fusion | flops 11796480 | bytes 18972672 | tf_op jit(solution)/shard_map/add | solution.py:70
  90.9 5.8 %collective-permute-start.11 = (f32[1,64,1024]{2,1,0:T(8,128)S(1)}, f32[1,64,1024]{2,1,0:T(8,128)S(1)}, u32[]{:S(2)}, u32[]{:S(2)}) collective-permute-start(f32[1,64,1024]{2,1,0:T(8,128)S(1)} %get-tuple-element.33), channel_id=1, source_target_pairs={{4,0},{8,4},{12,8},{16,12},{20,16},{24,20},{28,24},{32,28},{36,32}... | collective-permute-start | bytes 786440 | tf_op jit(solution)/shard_map/ppermute | solution.py:25
  100.6 4.2 %collective-permute-start.12 = (f32[6,1,1024]{2,1,0:T(1,128)S(1)}, f32[6,1,1024]{2,1,0:T(1,128)S(1)}, u32[]{:S(2)}, u32[]{:S(2)}) collective-permute-start(f32[6,1,1024]{2,1,0:T(1,128)S(1)} %get-tuple-element.22), channel_id=1, source_target_pairs={{0,1},{1,2},{2,3},{4,5},{5,6},{6,7},{8,9},{9,10},{10,11},{12,13},{... | collective-permute-start | bytes 73736 | tf_op jit(solution)/shard_map/ppermute | solution.py:24
  106.3 4.2 %collective-permute-done.13 = f32[6,1,1024]{2,1,0:T(1,128)S(1)} collective-permute-done((f32[6,1,1024]{2,1,0:T(1,128)S(1)}, f32[6,1,1024]{2,1,0:T(1,128)S(1)}, u32[]{:S(2)}, u32[]{:S(2)}) %collective-permute-start.13) | collective-permute-done | bytes 24608 | tf_op jit(solution)/shard_map/ppermute | solution.py:25
  115.3 5.8 %collective-permute-start.15 = (f32[1,64,1024]{2,1,0:T(8,128)S(1)}, f32[1,64,1024]{2,1,0:T(8,128)S(1)}, u32[]{:S(2)}, u32[]{:S(2)}) collective-permute-start(f32[1,64,1024]{2,1,0:T(8,128)S(1)} %get-tuple-element.31), channel_id=1, source_target_pairs={{4,0},{8,4},{12,8},{16,12},{20,16},{24,20},{28,24},{32,28},{36,32}... | collective-permute-start | bytes 786440 | tf_op jit(solution)/shard_map/ppermute | solution.py:25
  121.0 2.1 %collective-permute-done.14 = f32[1,64,1024]{2,1,0:T(8,128)S(1)} collective-permute-done((f32[1,64,1024]{2,1,0:T(8,128)S(1)}, f32[1,64,1024]{2,1,0:T(8,128)S(1)}, u32[]{:S(2)}, u32[]{:S(2)}) %collective-permute-start.14) | collective-permute-done | bytes 262176 | tf_op jit(solution)/shard_map/ppermute | solution.py:24
  124.9 3.9 %collective-permute-start.16 = (f32[6,1,1024]{2,1,0:T(1,128)S(1)}, f32[6,1,1024]{2,1,0:T(1,128)S(1)}, u32[]{:S(2)}, u32[]{:S(2)}) collective-permute-start(f32[6,1,1024]{2,1,0:T(1,128)S(1)} %get-tuple-element.20), channel_id=1, source_target_pairs={{0,1},{1,2},{2,3},{4,5},{5,6},{6,7},{8,9},{9,10},{10,11},{12,13},{... | collective-permute-start | bytes 73736 | tf_op jit(solution)/shard_map/ppermute | solution.py:24
  130.4 4.2 %collective-permute-done.17 = f32[6,1,1024]{2,1,0:T(1,128)S(1)} collective-permute-done((f32[6,1,1024]{2,1,0:T(1,128)S(1)}, f32[6,1,1024]{2,1,0:T(1,128)S(1)}, u32[]{:S(2)}, u32[]{:S(2)}) %collective-permute-start.17) | collective-permute-done | bytes 24608 | tf_op jit(solution)/shard_map/ppermute | solution.py:25
  139.4 5.8 %collective-permute-start.19 = (f32[1,64,1024]{2,1,0:T(8,128)S(1)}, f32[1,64,1024]{2,1,0:T(8,128)S(1)}, u32[]{:S(2)}, u32[]{:S(2)}) collective-permute-start(f32[1,64,1024]{2,1,0:T(8,128)S(1)} %get-tuple-element.29), channel_id=1, source_target_pairs={{4,0},{8,4},{12,8},{16,12},{20,16},{24,20},{28,24},{32,28},{36,32}... | collective-permute-start | bytes 786440 | tf_op jit(solution)/shard_map/ppermute | solution.py:25
  149.0 3.2 %collective-permute-start.20 = (f32[6,1,1024]{2,1,0:T(1,128)S(1)}, f32[6,1,1024]{2,1,0:T(1,128)S(1)}, u32[]{:S(2)}, u32[]{:S(2)}) collective-permute-start(f32[6,1,1024]{2,1,0:T(1,128)S(1)} %get-tuple-element.18), channel_id=1, source_target_pairs={{0,1},{1,2},{2,3},{4,5},{5,6},{6,7},{8,9},{9,10},{10,11},{12,13},{... | collective-permute-start | bytes 73736 | tf_op jit(solution)/shard_map/ppermute | solution.py:24
  154.2 3.8 %collective-permute-done.21 = f32[6,1,1024]{2,1,0:T(1,128)S(1)} collective-permute-done((f32[6,1,1024]{2,1,0:T(1,128)S(1)}, f32[6,1,1024]{2,1,0:T(1,128)S(1)}, u32[]{:S(2)}, u32[]{:S(2)}) %collective-permute-start.21) | collective-permute-done | bytes 24608 | tf_op jit(solution)/shard_map/ppermute | solution.py:25
  158.7 2.8 %fusion.27 = f32[4,64,1024]{2,1,0:T(8,128)} fusion(f32[4,64,1024]{2,1,0:T(8,128)S(1)} %get-tuple-element.5, f32[4,64,1024]{2,1,0:T(8,128)S(1)} %get-tuple-element.15, f32[4,64,1024]{2,1,0:T(8,128)S(1)} %get-tuple-element.14, f32[6,66,1026]{2,1,0:T(8,128)S(1)} %select_maximum_fusion, f32[4,64,1024]{2,1,0:T(8,128)S(1)} %get-tuple-element.13, ...), kind=kLoop, calls=%fused_computation.53 | loop fusion | flops 10747904 | bytes 12632064 | tf_op jit(solution)/shard_map/add | solution.py:70
  (112 shorter events, 48.3 us)
Async XLA Ops:
  0.6 42.0 %copy-start = (s32[64]{0:T(128)S(1)}, s32[64]{0:T(128)}, u32[]{:S(2)}) copy-start(s32[64]{0:T(128)} %param.23) | copy-start | bytes 772
  9.8 29.7 %copy-start.1 = (f32[4,64,1024]{2,1,0:T(8,128)S(1)}, f32[4,64,1024]{2,1,0:T(8,128)}, u32[]{:S(2)}) copy-start(f32[4,64,1024]{2,1,0:T(8,128)} %param.14) | copy-start | bytes 3145732
  25.5 25.2 %collective-permute-start.1 = (f32[1,256]{1,0:T(1,128)S(1)}, f32[1,256]{1,0:T(1,128)S(1)}, u32[]{:S(2)}, u32[]{:S(2)}) collective-permute-start(f32[1,256]{1,0:T(1,128)S(1)} %bitcast.30), channel_id=1, source_target_pairs={{4,0},{8,4},{12,8},{16,12},{20,16},{24,20},{28,24},{32,28},{36,32}... | collective-permute-start | bytes 3080 | tf_op jit(solution)/shard_map/ppermute | solution.py:25
  29.1 27.6 %collective-permute-start = (f32[1,256]{1,0:T(1,128)S(1)}, f32[1,256]{1,0:T(1,128)S(1)}, u32[]{:S(2)}, u32[]{:S(2)}) collective-permute-start(f32[1,256]{1,0:T(1,128)S(1)} %bitcast.31), channel_id=1, source_target_pairs={{0,4},{4,8},{8,12},{12,16},{16,20},{20,24},{24,28},{28,32},{32,36}... | collective-permute-start | bytes 3080 | tf_op jit(solution)/shard_map/ppermute | solution.py:24
  31.9 42.7 %collective-permute-start.7 = (f32[1,64,1024]{2,1,0:T(8,128)}, f32[1,64,1024]{2,1,0:T(8,128)S(1)}, u32[]{:S(2)}, u32[]{:S(2)}) collective-permute-start(f32[1,64,1024]{2,1,0:T(8,128)} %get-tuple-element.36), channel_id=1, source_target_pairs={{4,0},{8,4},{12,8},{16,12},{20,16},{24,20},{28,24},{32,28},{36,32}... | collective-permute-start | bytes 786440 | tf_op jit(solution)/shard_map/ppermute | solution.py:25
  37.6 36.8 %collective-permute-start.6 = (f32[1,64,1024]{2,1,0:T(8,128)}, f32[1,64,1024]{2,1,0:T(8,128)S(1)}, u32[]{:S(2)}, u32[]{:S(2)}) collective-permute-start(f32[1,64,1024]{2,1,0:T(8,128)} %get-tuple-element.37), channel_id=1, source_target_pairs={{0,4},{4,8},{8,12},{12,16},{16,20},{20,24},{24,28},{28,32},{32,36}... | collective-permute-start | bytes 786440 | tf_op jit(solution)/shard_map/ppermute | solution.py:24
  40.4 37.0 %collective-permute-start.2 = (f32[1,64,1024]{2,1,0:T(8,128)}, f32[1,64,1024]{2,1,0:T(8,128)S(1)}, u32[]{:S(2)}, u32[]{:S(2)}) collective-permute-start(f32[1,64,1024]{2,1,0:T(8,128)} %get-tuple-element.34), channel_id=1, source_target_pairs={{0,4},{4,8},{8,12},{12,16},{16,20},{20,24},{24,28},{28,32},{32,36}... | collective-permute-start | bytes 786440 | tf_op jit(solution)/shard_map/ppermute | solution.py:24
  50.7 26.8 %collective-permute-start.3 = (f32[1,64,1024]{2,1,0:T(8,128)}, f32[1,64,1024]{2,1,0:T(8,128)S(1)}, u32[]{:S(2)}, u32[]{:S(2)}) collective-permute-start(f32[1,64,1024]{2,1,0:T(8,128)} %get-tuple-element.35), channel_id=1, source_target_pairs={{4,0},{8,4},{12,8},{16,12},{20,16},{24,20},{28,24},{32,28},{36,32}... | collective-permute-start | bytes 786440 | tf_op jit(solution)/shard_map/ppermute | solution.py:25
  74.6 9.7 %collective-permute-start.8 = (f32[6,1,1024]{2,1,0:T(1,128)S(1)}, f32[6,1,1024]{2,1,0:T(1,128)S(1)}, u32[]{:S(2)}, u32[]{:S(2)}) collective-permute-start(f32[6,1,1024]{2,1,0:T(1,128)S(1)} %get-tuple-element.26), channel_id=1, source_target_pairs={{0,1},{1,2},{2,3},{4,5},{5,6},{6,7},{8,9},{9,10},{10,11},{12,13},{... | collective-permute-start | bytes 73736 | tf_op jit(solution)/shard_map/ppermute | solution.py:24
  76.0 8.2 %collective-permute-start.9 = (f32[6,1,1024]{2,1,0:T(1,128)S(1)}, f32[6,1,1024]{2,1,0:T(1,128)S(1)}, u32[]{:S(2)}, u32[]{:S(2)}) collective-permute-start(f32[6,1,1024]{2,1,0:T(1,128)S(1)} %get-tuple-element.27), channel_id=1, source_target_pairs={{1,0},{2,1},{3,2},{5,4},{6,5},{7,6},{9,8},{10,9},{11,10},{13,12},{... | collective-permute-start | bytes 73736 | tf_op jit(solution)/shard_map/ppermute | solution.py:25
  77.5 7.5 %collective-permute-start.5 = (f32[6,1,1024]{2,1,0:T(1,128)S(1)}, f32[6,1,1024]{2,1,0:T(1,128)S(1)}, u32[]{:S(2)}, u32[]{:S(2)}) collective-permute-start(f32[6,1,1024]{2,1,0:T(1,128)S(1)} %get-tuple-element.24), channel_id=1, source_target_pairs={{1,0},{2,1},{3,2},{5,4},{6,5},{7,6},{9,8},{10,9},{11,10},{13,12},{... | collective-permute-start | bytes 73736 | tf_op jit(solution)/shard_map/ppermute | solution.py:25
  78.8 6.7 %collective-permute-start.4 = (f32[6,1,1024]{2,1,0:T(1,128)S(1)}, f32[6,1,1024]{2,1,0:T(1,128)S(1)}, u32[]{:S(2)}, u32[]{:S(2)}) collective-permute-start(f32[6,1,1024]{2,1,0:T(1,128)S(1)} %get-tuple-element.25), channel_id=1, source_target_pairs={{0,1},{1,2},{2,3},{4,5},{5,6},{6,7},{8,9},{9,10},{10,11},{12,13},{... | collective-permute-start | bytes 73736 | tf_op jit(solution)/shard_map/ppermute | solution.py:24
  89.0 9.8 %collective-permute-start.10 = (f32[1,64,1024]{2,1,0:T(8,128)S(1)}, f32[1,64,1024]{2,1,0:T(8,128)S(1)}, u32[]{:S(2)}, u32[]{:S(2)}) collective-permute-start(f32[1,64,1024]{2,1,0:T(8,128)S(1)} %get-tuple-element.32), channel_id=1, source_target_pairs={{0,4},{4,8},{8,12},{12,16},{16,20},{20,24},{24,28},{28,32},{32,36}... | collective-permute-start | bytes 786440 | tf_op jit(solution)/shard_map/ppermute | solution.py:24
  90.9 9.6 %collective-permute-start.11 = (f32[1,64,1024]{2,1,0:T(8,128)S(1)}, f32[1,64,1024]{2,1,0:T(8,128)S(1)}, u32[]{:S(2)}, u32[]{:S(2)}) collective-permute-start(f32[1,64,1024]{2,1,0:T(8,128)S(1)} %get-tuple-element.33), channel_id=1, source_target_pairs={{4,0},{8,4},{12,8},{16,12},{20,16},{24,20},{28,24},{32,28},{36,32}... | collective-permute-start | bytes 786440 | tf_op jit(solution)/shard_map/ppermute | solution.py:25
  100.6 5.7 %collective-permute-start.12 = (f32[6,1,1024]{2,1,0:T(1,128)S(1)}, f32[6,1,1024]{2,1,0:T(1,128)S(1)}, u32[]{:S(2)}, u32[]{:S(2)}) collective-permute-start(f32[6,1,1024]{2,1,0:T(1,128)S(1)} %get-tuple-element.22), channel_id=1, source_target_pairs={{0,1},{1,2},{2,3},{4,5},{5,6},{6,7},{8,9},{9,10},{10,11},{12,13},{... | collective-permute-start | bytes 73736 | tf_op jit(solution)/shard_map/ppermute | solution.py:24
  104.8 5.7 %collective-permute-start.13 = (f32[6,1,1024]{2,1,0:T(1,128)S(1)}, f32[6,1,1024]{2,1,0:T(1,128)S(1)}, u32[]{:S(2)}, u32[]{:S(2)}) collective-permute-start(f32[6,1,1024]{2,1,0:T(1,128)S(1)} %get-tuple-element.23), channel_id=1, source_target_pairs={{1,0},{2,1},{3,2},{5,4},{6,5},{7,6},{9,8},{10,9},{11,10},{13,12},{... | collective-permute-start | bytes 73736 | tf_op jit(solution)/shard_map/ppermute | solution.py:25
  113.3 9.8 %collective-permute-start.14 = (f32[1,64,1024]{2,1,0:T(8,128)S(1)}, f32[1,64,1024]{2,1,0:T(8,128)S(1)}, u32[]{:S(2)}, u32[]{:S(2)}) collective-permute-start(f32[1,64,1024]{2,1,0:T(8,128)S(1)} %get-tuple-element.30), channel_id=1, source_target_pairs={{0,4},{4,8},{8,12},{12,16},{16,20},{20,24},{24,28},{28,32},{32,36}... | collective-permute-start | bytes 786440 | tf_op jit(solution)/shard_map/ppermute | solution.py:24
  115.3 9.6 %collective-permute-start.15 = (f32[1,64,1024]{2,1,0:T(8,128)S(1)}, f32[1,64,1024]{2,1,0:T(8,128)S(1)}, u32[]{:S(2)}, u32[]{:S(2)}) collective-permute-start(f32[1,64,1024]{2,1,0:T(8,128)S(1)} %get-tuple-element.31), channel_id=1, source_target_pairs={{4,0},{8,4},{12,8},{16,12},{20,16},{24,20},{28,24},{32,28},{36,32}... | collective-permute-start | bytes 786440 | tf_op jit(solution)/shard_map/ppermute | solution.py:25
  124.9 5.4 %collective-permute-start.16 = (f32[6,1,1024]{2,1,0:T(1,128)S(1)}, f32[6,1,1024]{2,1,0:T(1,128)S(1)}, u32[]{:S(2)}, u32[]{:S(2)}) collective-permute-start(f32[6,1,1024]{2,1,0:T(1,128)S(1)} %get-tuple-element.20), channel_id=1, source_target_pairs={{0,1},{1,2},{2,3},{4,5},{5,6},{6,7},{8,9},{9,10},{10,11},{12,13},{... | collective-permute-start | bytes 73736 | tf_op jit(solution)/shard_map/ppermute | solution.py:24
  128.9 5.7 %collective-permute-start.17 = (f32[6,1,1024]{2,1,0:T(1,128)S(1)}, f32[6,1,1024]{2,1,0:T(1,128)S(1)}, u32[]{:S(2)}, u32[]{:S(2)}) collective-permute-start(f32[6,1,1024]{2,1,0:T(1,128)S(1)} %get-tuple-element.21), channel_id=1, source_target_pairs={{1,0},{2,1},{3,2},{5,4},{6,5},{7,6},{9,8},{10,9},{11,10},{13,12},{... | collective-permute-start | bytes 73736 | tf_op jit(solution)/shard_map/ppermute | solution.py:25
  137.4 9.8 %collective-permute-start.18 = (f32[1,64,1024]{2,1,0:T(8,128)S(1)}, f32[1,64,1024]{2,1,0:T(8,128)S(1)}, u32[]{:S(2)}, u32[]{:S(2)}) collective-permute-start(f32[1,64,1024]{2,1,0:T(8,128)S(1)} %get-tuple-element.28), channel_id=1, source_target_pairs={{0,4},{4,8},{8,12},{12,16},{16,20},{20,24},{24,28},{28,32},{32,36}... | collective-permute-start | bytes 786440 | tf_op jit(solution)/shard_map/ppermute | solution.py:24
  139.4 9.6 %collective-permute-start.19 = (f32[1,64,1024]{2,1,0:T(8,128)S(1)}, f32[1,64,1024]{2,1,0:T(8,128)S(1)}, u32[]{:S(2)}, u32[]{:S(2)}) collective-permute-start(f32[1,64,1024]{2,1,0:T(8,128)S(1)} %get-tuple-element.29), channel_id=1, source_target_pairs={{4,0},{8,4},{12,8},{16,12},{20,16},{24,20},{28,24},{32,28},{36,32}... | collective-permute-start | bytes 786440 | tf_op jit(solution)/shard_map/ppermute | solution.py:25
  149.0 5.1 %collective-permute-start.20 = (f32[6,1,1024]{2,1,0:T(1,128)S(1)}, f32[6,1,1024]{2,1,0:T(1,128)S(1)}, u32[]{:S(2)}, u32[]{:S(2)}) collective-permute-start(f32[6,1,1024]{2,1,0:T(1,128)S(1)} %get-tuple-element.18), channel_id=1, source_target_pairs={{0,1},{1,2},{2,3},{4,5},{5,6},{6,7},{8,9},{9,10},{10,11},{12,13},{... | collective-permute-start | bytes 73736 | tf_op jit(solution)/shard_map/ppermute | solution.py:24
  152.2 5.7 %collective-permute-start.21 = (f32[6,1,1024]{2,1,0:T(1,128)S(1)}, f32[6,1,1024]{2,1,0:T(1,128)S(1)}, u32[]{:S(2)}, u32[]{:S(2)}) collective-permute-start(f32[6,1,1024]{2,1,0:T(1,128)S(1)} %get-tuple-element.19), channel_id=1, source_target_pairs={{1,0},{2,1},{3,2},{5,4},{6,5},{7,6},{9,8},{10,9},{11,10},{13,12},{... | collective-permute-start | bytes 73736 | tf_op jit(solution)/shard_map/ppermute | solution.py:25
  (12 other events, 142.0 us)
where the time goes:
time: 163 us; the launch traced here: 162 us
  starting transfers between devices  68.7 us (42%)
  matrix products  24.7 us (15%)
  waiting for transfers between devices  24.7 us (15%)
  other arithmetic  19.6 us (12%)
  local copies, waits for them, and re-layouts  11 us (7%)
  blocking collectives  10.7 us (7%)
  between operations  2.08 us (1%)
    ppermute x11, starting transfers between devices, with_halo(): after = lax.ppermute(initial, axis, down)  39 us
    ppermute x11, starting transfers between devices, with_halo(): before = lax.ppermute(last, axis, up)  29.7 us
    ppermute x11, waiting for transfers between devices, with_halo(): after = lax.ppermute(initial, axis, down)  17.5 us
    dot_general x2, matrix products, place_values(): jnp.einsum('cfa,cfl->cal', row_table, lane_table * values[:, :, None], pr...  12.7 us
    unnamed x1, blocking collectives  10.7 us
    add x4, other arithmetic, chebyshev(): iterate = iterate + update  9.55 us
    dot_general x2, matrix products, pick_values(): jnp.einsum('cfa,cal->cfl', row_table, blocks, precision=lax.Precision.HIG...  9.06 us
    ppermute x11, waiting for transfers between devices, with_halo(): before = lax.ppermute(last, axis, up)  7.2 us
  transfers between devices with their start and end apart: 22, of which 12 were waited for; matrix products, arithmetic and copies ran while one was open for 18% of the time, Pallas kernels for 0%

commit v1 on v0

v1 whole, which is shorter than its diff:
```python
import functools
import math

import jax
import jax.numpy as jnp
from jax import lax
from jax.experimental import pallas as pl
from jax.experimental.pallas import tpu as pltpu
from jax.sharding import PartitionSpec as P

LOG2E = math.log2(math.e)
SWEEPS = 4
F32 = jnp.float32
BF16 = jnp.bfloat16
ANY = pl.BlockSpec(memory_space=pl.ANY)
VM = pl.BlockSpec(memory_space=pltpu.VMEM)
SM = pl.BlockSpec(memory_space=pltpu.SMEM)
BIG = pltpu.CompilerParams(vmem_limit_bytes=48 * 1024 * 1024)


def sweep_factors():
    theta, delta = 1.0, 0.8
    sigma = theta / delta
    rho = 1.0 / sigma
    factors = []
    for _ in range(SWEEPS - 1):
        rho_next = 1.0 / (2.0 * sigma - rho)
        factors.append((rho_next * rho, 2.0 * rho_next / delta))
        rho = rho_next
    return factors


def iota(shape, dim):
    return lax.broadcasted_iota(jnp.int32, shape, dim)


def plane_of(parity, j):
    return j + parity * (3 - 2 * j)


def gather_kernel(p_ref, in_ref, ex_ref, cnt_ref, volt_ref, cell_ref):
    sub = iota((8, 128), 0)
    low = sub < 4

    def body(kk, carry):
        x = kk // 4
        blocks = [r[pl.ds(pl.multiple_of(8 * kk, 8), 8), :] & 4095 for r in (in_ref, ex_ref)]
        for q in range(2):
            row = pl.multiple_of((2 * (kk % 4) + q) * 8, 8)
            tiles = [p_ref[x, pl.ds(row, 8), 128 * z : 128 * z + 128] for z in range(8)]
            for h in range(2):
                picked = []
                for block in blocks:
                    a = jnp.broadcast_to(block[4 * q + h : 4 * q + h + 1], (8, 128))
                    b = jnp.broadcast_to(block[4 * q + 2 + h : 4 * q + 3 + h], (8, 128))
                    o = jnp.where(low, a, b)
                    lane = o & 127
                    z_of = (o >> 7) & 7
                    got = jnp.take_along_axis(tiles[0], lane, axis=1, mode="promise_in_bounds")
                    for z in range(1, 8):
                        new = jnp.take_along_axis(tiles[z], lane, axis=1, mode="promise_in_bounds")
                        got = jnp.where(z_of == z, new, got)
                    picked.append(jnp.where((o >> 10) == (sub & 3), got, 0.0))
                d = picked[0] - picked[1]
                d = d + pltpu.roll(d, 7, 0)
                d = d + pltpu.roll(d, 6, 0)
                volt_ref[pl.ds(8 * kk + 4 * q + h, 1), :] = d[0:1]
                volt_ref[pl.ds(8 * kk + 4 * q + 2 + h, 1), :] = d[4:5]
        return carry

    lax.fori_loop(0, 16, body, 0)
    turned = jnp.transpose(volt_ref[...])
    cnt = cnt_ref[...]
    lanes = iota((128, 128), 1)
    used = iota((128, 128), 0) + 128 * (lanes & 1) < cnt
    total = jnp.sum(jnp.where(used, turned, 0.0), axis=0, keepdims=True)
    even = (iota((1, 128), 1) & 1) == 0
    other = jnp.where(even, pltpu.roll(total, 127, 1), pltpu.roll(total, 1, 1))
    cell_ref[...] = (total + other) / jnp.maximum(cnt, 1).astype(F32)


def pack_kernel(meta, p_ref, c_ref, a_ref, b_ref, up_ref, down_ref, sem):
    par = meta[0]
    copies = []
    for i in range(3):
        copies.append((c_ref.at[plane_of(par, 3 - i)], a_ref.at[i]))
        copies.append((c_ref.at[plane_of(par, i)], b_ref.at[i]))
    copies.append((p_ref.at[plane_of(par, 3)], a_ref.at[3]))
    copies.append((p_ref.at[plane_of(par, 0)], b_ref.at[3]))
    for k, ref in enumerate((c_ref, p_ref)):
        copies.append((ref.at[:, 56:64], up_ref.at[4 * k : 4 * k + 4]))
        copies.append((ref.at[:, 0:8], down_ref.at[4 * k : 4 * k + 4]))
    run_copies(copies, sem)


def run_copies(copies, sem, start=0):
    made = [pltpu.make_async_copy(s, d, sem.at[start + n]) for n, (s, d) in enumerate(copies)]
    for m in made:
        m.start()
    for m in made:
        m.wait()


def ionic_kernel(cnt, typ, volt_ref, st_ref, rate_ref, g_ref, gr_ref, out_ref, ion_ref, act_ref):
    step = pl.program_id(0)
    cells = volt_ref.shape[0] // 2
    lane = iota((8, 128), 1)

    def body(cc, carry):
        n = cnt[step * cells + cc]
        ty = typ[step * cells + cc]
        for h in range(2):
            r = cc * 2 + h
            cols = pl.ds(pl.multiple_of(r * 128, 128), 128)
            v = jnp.broadcast_to(volt_ref[pl.ds(r, 1), :], (8, 128))
            active = lane + h * 128 < n
            w1 = w2 = None
            for k in range(5):
                rows = slice(8 * k, 8 * k + 8)
                st = st_ref[rows, cols]
                opening = jnp.exp2(rate_ref[0, rows] * v + rate_ref[1, rows])
                closing = jnp.exp2(rate_ref[2, rows] * v + rate_ref[3, rows])
                total = opening + closing
                rec = pl.reciprocal(total, approx=True)
                rec = rec * (2.0 - total * rec)
                steady = opening * rec
                fresh = steady + (st - steady) * jnp.exp2(total * (-0.5 * LOG2E))
                out_ref[rows, cols] = jnp.where(active, fresh, st)
                a = g_ref[ty, rows] * fresh
                b = gr_ref[ty, rows] * fresh
                w1 = a if w1 is None else w1 + a
                w2 = b if w2 is None else w2 + b
            ion = jnp.sum(w1 * v - w2, axis=0, keepdims=True)
            ion_ref[pl.ds(r, 1), :] = jnp.where(active[0:1], ion, 0.0)
            act_ref[pl.ds(r, 1), :] = jnp.where(active[0:1], 1.0, 0.0)
        return carry

    lax.fori_loop(0, cells, body, 0)


def scatter_kernel(ion_ref, act_ref, in_ref, ex_ref, s_ref, n_ref):
    row_iota = iota((32, 512), 0)
    lane_iota = iota((128, 512), 0)
    low = iota((8, 128), 0) < 4
    odd_row = (iota((8, 128), 0) & 2) // 2

    def body(kk, carry):
        rows8 = pl.ds(pl.multiple_of(8 * kk, 8), 8)
        x = kk // 4
        val = ion_ref[rows8, :]
        act = act_ref[rows8, :]
        hi = val.astype(BF16).astype(F32)
        lo = val - hi
        mids, lanes = [], []
        for ref in (in_ref, ex_ref):
            o = ref[rows8, :] & 4095
            mids.append((((o >> 7) & 7) ^ odd_row) * 4 + (o >> 10))
            lanes.append(o & 127)

        def line(a, b, s):
            r = 2 * s
            return jnp.concatenate([a[r : r + 1], a[r + 1 : r + 2], b[r : r + 1], b[r + 1 : r + 2]], axis=1)

        for q in range(2):
            results = []
            for s in (2 * q, 2 * q + 1):
                hit = line(mids[0], mids[1], s) == row_iota
                left = jnp.concatenate(
                    [jnp.where(hit, line(piece, -piece, s), 0.0).astype(BF16) for piece in (hi, lo, act)], axis=0
                )
                right = jnp.where(line(lanes[0], lanes[1], s) == lane_iota, 1.0, 0.0).astype(BF16)
                out = lax.dot_general(left, right, (((1,), (1,)), ((), ())), preferred_element_type=F32)
                results.append((out[0:32] + out[32:64], out[64:96]))
            row = pl.ds(pl.multiple_of((2 * (kk % 4) + q) * 8, 8), 8)
            for dst, e, o in ((s_ref, results[0][0], results[1][0]), (n_ref, results[0][1], results[1][1])):
                for j in range(4):
                    ej, oj = e[8 * j : 8 * j + 8], o[8 * j : 8 * j + 8]
                    dst[x, row, 256 * j : 256 * j + 128] = jnp.where(low, ej, oj)
                    dst[x, row, 256 * j + 128 : 256 * j + 256] = pltpu.roll(jnp.where(low, oj, ej), 4, 0)
        return carry

    lax.fori_loop(0, 16, body, 0)


def tile(ref, e, t):
    return ref[e, 8 * t : 8 * t + 8, :]


class Around:
    def __init__(self, ref, e):
        self.ref, self.e = ref, e
        self.sub = iota((8, 1024), 0)

    def at(self, t):
        ref, e = self.ref, self.e
        c = tile(ref, e, t)
        before, after = tile(ref, e, (t + 8) % 9), tile(ref, e, (t + 1) % 9)
        ym = jnp.where(self.sub == 0, pltpu.roll(before, 1, 0), pltpu.roll(c, 1, 0))
        yp = jnp.where(self.sub == 7, pltpu.roll(after, 7, 0), pltpu.roll(c, 7, 0))
        zm, zp = pltpu.roll(c, 1, 1), pltpu.roll(c, 1023, 1)
        return c, tile(ref, e - 1, t), tile(ref, e + 1, t), ym, yp, zm, zp


def couplings(around, t):
    lane = iota((8, 1024), 1)
    c, xm, xp, ym, yp, zm, zp = around.at(t)
    first, last = lane == 0, lane == 1023
    zm = jnp.where(first, 0.0, zm)
    zp = jnp.where(last, 0.0, zp)
    fs = [0.25 * (c + other) for other in (xm, xp, ym, yp, zm, zp)]
    diagonal = 1.0 + (((fs[0] + fs[1]) + (fs[2] + fs[3])) + (fs[4] + fs[5]))
    fs[4] = jnp.where(first, 0.0, fs[4])
    fs[5] = jnp.where(last, 0.0, fs[5])
    return fs, diagonal


def weighted(fs, views):
    t = [f * v for f, v in zip(fs, views)]
    return ((t[0] + t[1]) + (t[2] + t[3])) + (t[4] + t[5])


def start_kernel(meta, p_hbm, c_hbm, a_hbm, b_hbm, y_hbm, s_ref, n_ref, w_ref, k_ref, pe, ce, sem):
    par = meta[0]
    copies = []
    for e, hbm, yk in ((ce, c_hbm, 0), (pe, p_hbm, 4)):
        for j in range(4):
            copies.append((hbm.at[plane_of(par, j)], e.at[1 + j, 0:64]))
            copies.append((y_hbm.at[yk + plane_of(par, j)], e.at[1 + j, 64:72]))
    copies.append((a_hbm.at[0], ce.at[5, 0:64]))
    copies.append((b_hbm.at[0], ce.at[0, 0:64]))
    copies.append((a_hbm.at[3], pe.at[5, 0:64]))
    copies.append((b_hbm.at[3], pe.at[0, 0:64]))
    run_copies(copies, sem)

    def body(j, carry):
        x = plane_of(par, j)
        ca, pa = Around(ce, 1 + j), Around(pe, 1 + j)
        for t in range(8):
            rows = slice(8 * t, 8 * t + 8)
            fs, diagonal = couplings(ca, t)
            inv = 1.0 / diagonal
            views = pa.at(t)
            p = views[0]
            w_ref[x, rows, :] = (p + weighted(fs, views[1:]) - 0.5 * s_ref[x, rows, :]) * inv - p
            k_ref[x, rows, :] = (-0.5 * inv) * n_ref[x, rows, :]
        return carry

    lax.fori_loop(0, 4, body, 0)


def gap_kernel(meta, table_ref, part_ref, cond_ref, cnt_ref, ion_ref, act_ref, w_ref, k_ref,
               u_ref, a_ref, b_ref, up_ref, down_ref, mem_ref, spread):
    par, mine, v = meta[0], meta[2], meta[3]
    part = part_ref[...]
    brick = part >> 6
    bx, by = brick >> 2, brick & 3
    side = jnp.where(bx == v, 0, jnp.where(bx == (v ^ 1), 1, 2))
    row = side * 4 + ((mine - by) & 3)
    lane = (part & 63) * 2
    other = jnp.zeros((8, 128), F32)
    for r in range(12):
        line = jnp.broadcast_to(table_ref[r : r + 1, :], (8, 128))
        other = jnp.where(row == r, jnp.take_along_axis(line, lane, axis=1, mode="promise_in_bounds"), other)
    own = table_ref[0:1, :]
    current = jnp.sum(cond_ref[...] * (own - other), axis=0, keepdims=True)
    g = current / jnp.maximum(cnt_ref[...], 1).astype(F32)
    g8 = jnp.broadcast_to(g, (8, 128))
    mem_ref[...] = ion_ref[...] + act_ref[...] * jnp.transpose(jnp.broadcast_to(g, (128, 128)))
    for half in range(2):
        at = 64 * half + 2 * (iota((8, 128), 1) // 4)
        wide = jnp.take_along_axis(g8, at, axis=1, mode="promise_in_bounds")[0:1]
        spread[128 * half : 128 * half + 128, :] = jnp.transpose(jnp.broadcast_to(wide, (128, 128)))

    def body(j, carry):
        x = plane_of(par, j)
        for t in range(8):
            rows = slice(8 * t, 8 * t + 8)
            gt = spread[pl.ds(pl.multiple_of(x * 64 + 8 * t, 8), 8), :]
            u = w_ref[x, rows, :] + k_ref[x, rows, :] * jnp.tile(gt, (1, 8))
            u_ref[x, rows, :] = u
            if t == 0:
                down_ref[x] = u
            if t == 7:
                up_ref[x] = u

            @pl.when(j < 3)
            def _():
                b_ref[j, rows, :] = u

            @pl.when(j > 0)
            def _():
                a_ref[3 - j, rows, :] = u

        return carry

    lax.fori_loop(0, 4, body, 0)


def sweep_kernel(meta, p_ref, c_hbm, ca_hbm, cb_hbm, cy_hbm, cca_hbm, ccb_hbm,
                 u_hbm, ua_hbm, ub_hbm, uy_hbm, uca_hbm, ucb_hbm, out_ref,
                 c, u0, u1, u2, r, fx, fym, fyp, fzm, fzp, inv, sem):
    par, has_b, mine = meta[0], meta[1], meta[2]

    def loads(dst, own, a, b, y, ca, cb, start):
        copies = []
        for j in range(4):
            copies.append((own.at[plane_of(par, j)], dst.at[3 + j, 0:64]))
            copies.append((y.at[plane_of(par, j)], dst.at[3 + j, 64:72]))
        for i in range(3):
            copies.append((a.at[i], dst.at[7 + i, 0:64]))
            copies.append((b.at[i], dst.at[2 - i, 0:64]))
        for i in range(2):
            copies.append((ca.at[i], dst.at[7 + i, 64:72]))
            copies.append((cb.at[i], dst.at[2 - i, 64:72]))
        made = [pltpu.make_async_copy(s, d, sem.at[start + n]) for n, (s, d) in enumerate(copies)]
        for m in made:
            m.start()
        return made

    c_copies = loads(c, c_hbm, ca_hbm, cb_hbm, cy_hbm, cca_hbm, ccb_hbm, 0)
    u_copies = loads(u0, u_hbm, ua_hbm, ub_hbm, uy_hbm, uca_hbm, ucb_hbm, len(c_copies))
    zero8 = jnp.zeros((8, 1024), F32)
    for dst in (c, u0):
        dst[0, 64:72, :] = zero8
        dst[9, 64:72, :] = zero8
    sub = iota((8, 1024), 0)
    bottom = (sub < 3) & (mine != 3)
    top = (sub >= 5) & (mine != 0)
    keep = jnp.where(bottom | top, 1.0, 0.0)
    for m in c_copies:
        m.wait()

    def build(e, carry):
        around = Around(c, e)
        inside = jnp.where((e >= 3) | (has_b == 1), 1.0, 0.0)
        for t in range(9):
            rows = slice(8 * t, 8 * t + 8)
            fs, diagonal = couplings(around, t)
            part = inside / diagonal
            inv[e, rows, :] = part * keep if t == 8 else part
            fx[e - 1, rows, :] = fs[0]
            fx[e, rows, :] = fs[1]
            fym[e, rows, :] = fs[2]
            fyp[e, rows, :] = fs[3]
            fzm[e, rows, :] = fs[4]
            fzp[e, rows, :] = fs[5]
        return carry

    lax.fori_loop(1, 9, build, 0)
    for m in u_copies:
        m.wait()
    (a1, b1), (a2, b2), (a3, b3) = sweep_factors()

    def coupled(around, e, t):
        fs = [tile(fx, e - 1, t), tile(fx, e, t)] + [tile(f, e, t) for f in (fym, fyp, fzm, fzp)]
        views = around.at(t)
        return views[0], tile(inv, e, t) * weighted(fs, views[1:])

    def first(e, carry):
        around = Around(u0, e)
        for t in range(9):
            rows = slice(8 * t, 8 * t + 8)
            u, res = coupled(around, e, t)
            r[e, rows, :] = res
            u1[e, rows, :] = a1 * u + b1 * res
        return carry

    lax.fori_loop(1, 9, first, 0)

    def second(e, carry):
        around = Around(u1, e)
        for t in range(9):
            rows = slice(8 * t, 8 * t + 8)
            u, more = coupled(around, e, t)
            res = (tile(r, e, t) - u) + more
            r[e, rows, :] = res
            u2[e, rows, :] = a2 * u + b2 * res
        return carry

    lax.fori_loop(2, 8, second, 0)

    def third(j, carry):
        e = 3 + j
        x = plane_of(par, j)
        around = Around(u2, e)
        for t in range(8):
            rows = slice(8 * t, 8 * t + 8)
            u, more = coupled(around, e, t)
            res = (tile(r, e, t) - u) + more
            before = (p_ref[x, rows, :] + tile(u0, e, t)) + (tile(u1, e, t) + u)
            out_ref[x, rows, :] = before + (a3 * u + b3 * res)
        return carry

    lax.fori_loop(0, 4, third, 0)


def shape(*dims, kind=F32):
    return jax.ShapeDtypeStruct(dims, kind)


def per_device(potential, conductivity, ion_states, rate_scale, rate_slope, type_cond, reversal,
               facet_counts, intra_voxel, extra_voxel, cell_type, gap_partner, gap_cond):
    v, m = lax.axis_index("vol"), lax.axis_index("mem")
    par = v & 1
    nv = lax.axis_size("vol")
    has_b = jnp.where((v == 0) | (v == nv - 1), 0, 1)
    meta = jnp.stack([par, has_b, m, v]).astype(jnp.int32)
    swap_a = [pair for i in range(0, nv, 2) for pair in ((i, i + 1), (i + 1, i))]
    swap_b = [pair for i in range(1, nv - 1, 2) for pair in ((i, i + 1), (i + 1, i))]
    up = [(i, i + 1) for i in range(3)]
    down = [(i + 1, i) for i in range(3)]
    to_a = functools.partial(lax.ppermute, axis_name="vol", perm=swap_a)
    to_b = functools.partial(lax.ppermute, axis_name="vol", perm=swap_b)
    to_up = functools.partial(lax.ppermute, axis_name="mem", perm=up)
    to_down = functools.partial(lax.ppermute, axis_name="mem", perm=down)

    intra = intra_voxel.reshape(128, 128)
    extra = extra_voxel.reshape(128, 128)
    cnt_lane = jnp.repeat(facet_counts, 2).reshape(1, 128)

    volt, cells = pl.pallas_call(
        gather_kernel,
        out_shape=(shape(128, 128), shape(1, 128)),
        in_specs=[VM] * 4,
        out_specs=(VM, VM),
        cost_estimate=pl.CostEstimate(flops=4000000, bytes_accessed=1300000, transcendentals=0),
        name="voltages",
    )(potential, intra, extra, cnt_lane)

    column = [cells] + [
        lax.ppermute(cells, "mem", [(i, (i + d) % 4) for i in range(4)]) for d in (1, 2, 3)
    ]
    own_table = jnp.concatenate(column, axis=0)

    send_a, send_b, send_up, send_down = pl.pallas_call(
        pack_kernel,
        out_shape=(shape(4, 64, 1024), shape(4, 64, 1024), shape(8, 8, 1024), shape(8, 8, 1024)),
        in_specs=[SM, ANY, ANY],
        out_specs=(ANY,) * 4,
        scratch_shapes=[pltpu.SemaphoreType.DMA((12,))],
        cost_estimate=pl.CostEstimate(flops=0, bytes_accessed=5000000, transcendentals=0),
        name="pack",
    )(meta, potential, conductivity)

    def edge_rows(from_below, from_above):
        sub = lax.broadcasted_iota(jnp.int32, from_below.shape, 1)
        return jnp.where(sub < 3, from_above, jnp.where(sub >= 5, from_below, 0.0))

    def corners(rows4):
        toward_b = jnp.where(par == 0, rows4[0:2], jnp.stack([rows4[3], rows4[2]]))
        toward_a = jnp.where(par == 0, jnp.stack([rows4[3], rows4[2]]), rows4[0:2])
        return to_a(toward_a), to_b(toward_b)

    early_a, early_b = to_a(send_a), to_b(send_b)
    y_early = edge_rows(to_up(send_up), to_down(send_down))
    corner_a, corner_b = corners(y_early[0:4])

    rates = jnp.stack([
        rate_slope[0] * LOG2E, jnp.log2(rate_scale[0]), rate_slope[1] * (-LOG2E), jnp.log2(rate_scale[1]),
    ])
    rates = jnp.broadcast_to(rates[:, :, None], (4, 40, 128))
    g_wide = jnp.broadcast_to(type_cond[:, :, None], (3, 40, 128))
    gr_wide = jnp.broadcast_to((type_cond * reversal[None, :])[:, :, None], (3, 40, 128))
    steps = 4
    width = 16384 // steps
    facet_rows = pl.BlockSpec((128 // steps, 128), lambda i, *_: (i, 0))
    state_block = pl.BlockSpec((40, width), lambda i, *_: (0, i))
    whole = lambda n: pl.BlockSpec((n, 40, 128), lambda i, *_: (0, 0, 0))
    states_next, ion, act = pl.pallas_call(
        ionic_kernel,
        out_shape=(shape(40, 16384), shape(128, 128), shape(128, 128)),
        grid_spec=pltpu.PrefetchScalarGridSpec(
            num_scalar_prefetch=2,
            grid=(steps,),
            in_specs=[facet_rows, state_block, whole(4), whole(3), whole(3)],
            out_specs=(state_block, facet_rows, facet_rows),
        ),
        cost_estimate=pl.CostEstimate(flops=16000000, bytes_accessed=5300000, transcendentals=2600000),
        name="ionic",
    )(facet_counts, cell_type, volt, ion_states, rates, g_wide, gr_wide)

    source, count = pl.pallas_call(
        scatter_kernel,
        out_shape=(shape(4, 64, 1024), shape(4, 64, 1024)),
        in_specs=[VM] * 4,
        out_specs=(VM, VM),
        cost_estimate=pl.CostEstimate(flops=800000000, bytes_accessed=2300000, transcendentals=0),
        name="scatter",
    )(ion, act, intra, extra)

    w, k = pl.pallas_call(
        start_kernel,
        out_shape=(shape(4, 64, 1024), shape(4, 64, 1024)),
        in_specs=[SM, ANY, ANY, ANY, ANY, ANY, VM, VM],
        out_specs=(VM, VM),
        scratch_shapes=[pltpu.VMEM((6, 72, 1024), F32), pltpu.VMEM((6, 72, 1024), F32),
                        pltpu.SemaphoreType.DMA((20,))],
        compiler_params=BIG,
        cost_estimate=pl.CostEstimate(flops=16000000, bytes_accessed=6000000, transcendentals=0),
        name="start",
    )(meta, potential, conductivity, early_a, early_b, y_early, source, count)

    table = jnp.concatenate([own_table, to_a(own_table), to_b(own_table)], axis=0)
    part_lane = jnp.repeat(gap_partner.T, 2, axis=1)
    cond_lane = jnp.repeat(gap_cond.T, 2, axis=1)
    u, u_a, u_b, u_up, u_down, membrane = pl.pallas_call(
        gap_kernel,
        out_shape=(shape(4, 64, 1024), shape(3, 64, 1024), shape(3, 64, 1024), shape(4, 8, 1024),
                   shape(4, 8, 1024), shape(128, 128)),
        in_specs=[SM] + [VM] * 8,
        out_specs=(VM,) * 6,
        scratch_shapes=[pltpu.VMEM((256, 128), F32)],
        cost_estimate=pl.CostEstimate(flops=1000000, bytes_accessed=5000000, transcendentals=0),
        compiler_params=BIG,
        name="gap",
    )(meta, table, part_lane, cond_lane, cnt_lane, ion, act, w, k)

    late_b, late_a = to_b(u_b), to_a(u_a)
    y_late = edge_rows(to_up(u_up), to_down(u_down))
    late_corner_a, late_corner_b = corners(y_late)

    big = lambda n: pltpu.VMEM((n, 72, 1024), F32)
    potential_next = pl.pallas_call(
        sweep_kernel,
        out_shape=shape(4, 64, 1024),
        in_specs=[SM, VM] + [ANY] * 12,
        out_specs=VM,
        scratch_shapes=[big(10), big(10), big(9), big(8), big(9), big(9), big(9), big(9), big(9), big(9), big(9),
                        pltpu.SemaphoreType.DMA((36,))],
        compiler_params=BIG,
        cost_estimate=pl.CostEstimate(flops=50000000, bytes_accessed=10000000, transcendentals=0),
        name="sweeps",
    )(meta, potential, conductivity, early_a, early_b, y_early[0:4], corner_a, corner_b,
      u, late_a, late_b, y_late, late_corner_a, late_corner_b)
    return potential_next, states_next, membrane.reshape(16384)


def solution(mesh):
    in_specs = (
        P("vol", "mem", None), P("vol", "mem", None), P(None, ("vol", "mem")),
        P(), P(), P(), P(),
        P(("vol", "mem")), P(("vol", "mem")), P(("vol", "mem")), P(("vol", "mem")),
        P(("vol", "mem"), None), P(("vol", "mem"), None),
    )
    out_specs = (P("vol", "mem", None), P(None, ("vol", "mem")), P(("vol", "mem")))
    return jax.shard_map(per_device, mesh=mesh, in_specs=in_specs, out_specs=out_specs, check_vma=False)
```

time: 163 us -> 170 us (1.043)
  Pallas kernels: 0 us -> 118 us
  starting transfers between devices: 68.7 us -> 39.3 us
  matrix products: 24.7 us -> 0 us
  waiting for transfers between devices: 24.7 us -> 3.67 us
  other arithmetic: 19.6 us -> 2.47 us
  blocking collectives: 10.7 us -> 0 us
  local copies, waits for them, and re-layouts: 11 us -> 3.98 us
    pallas_call x0 -> x7, Pallas kernels: none -> 118 us  [the longest x1 81.3 us: per_device(): pl.pallas_call(pack_kernel, out_shape=(shape(4, 64, 1024), shape(4, 64, 1...]
    ppermute x22 -> x17, starting transfers between devices: 68.7 us -> 39.3 us  [the longest x4 7.76 us: corners(): return (to_a(toward_a), to_b(toward_b))]
    dot_general x6 -> x0, matrix products: 24.7 us -> none  [the longest x2 12.7 us: place_values(): jnp.einsum('cfa,cfl->cal', row_table, lane_table * values[:, :, None], pr...]
    ppermute x22 -> x17, waiting for transfers between devices: 24.7 us -> 3.67 us  [the longest x4 3.63 us: corners(): return (to_a(toward_a), to_b(toward_b))]
    unnamed x1 -> x0, blocking collectives: 10.7 us -> none
    add x4 -> x0, other arithmetic: 9.55 us -> none  [chebyshev(): iterate = iterate + update]
    select_n x4, other arithmetic: 5.72 us -> 1.16 us  [the longest x2 1.13 us: edge_rows(): return jnp.where(sub < 3, from_above, jnp.where(sub >= 5, from_below, 0.0))]
    concatenate x6 -> x1, other arithmetic: 3.7 us -> 0.63 us  [per_device(): own_table = jnp.concatenate(column, axis=0)]
  transfers between devices with their start and end apart: 22 -> 17, of which waited for: 12 -> 3; matrix products, arithmetic and copies ran while one was open for 18% -> 3% of each run, Pallas kernels for 0% -> 57%
where the time goes in v1:
time: 170 us; the launch traced here: 169 us
  Pallas kernels  118 us (69%)
  starting transfers between devices  39.3 us (23%)
  local copies, waits for them, and re-layouts  3.98 us (2%)
  waiting for transfers between devices  3.67 us (2%)
  other arithmetic  2.47 us (1%)
    pallas_call x1, Pallas kernels, per_device(): pl.pallas_call(pack_kernel, out_shape=(shape(4, 64, 1024), shape(4, 64, 1...  81.3 us
    pallas_call x1, Pallas kernels, per_device(): pl.pallas_call(sweep_kernel, out_shape=shape(4, 64, 1024), in_specs=[SM,...  10.5 us
    ppermute x4, starting transfers between devices, corners(): return (to_a(toward_a), to_b(toward_b))  7.76 us
    pallas_call x1, Pallas kernels, per_device(): pl.pallas_call(scatter_kernel, out_shape=(shape(4, 64, 1024), shape(4, 64...  7.38 us
    pallas_call x1, Pallas kernels, per_device(): pl.pallas_call(ionic_kernel, out_shape=(shape(40, 16384), shape(128, 128)...  6.85 us
    ppermute x2, starting transfers between devices, per_device(): y_early = edge_rows(to_up(send_up), to_down(send_down))  6.57 us
    ppermute x2, starting transfers between devices, per_device(): early_a, early_b = (to_a(send_a), to_b(send_b))  6.39 us
    ppermute x2, starting transfers between devices, per_device(): late_b, late_a = (to_b(u_b), to_a(u_a))  6.16 us
  transfers between devices with their start and end apart: 17, of which 3 were waited for; matrix products, arithmetic and copies ran while one was open for 3% of the time, Pallas kernels for 57%

profile of v1, /device:TPU:6, one launch (start us, length us, event | category | flops | bytes accessed | tf_op | source)
XLA Modules:
  0.0 168.8 jit_solution(1937415859224471385)
XLA Ops:
  0.7 0.7 broadcast_in_dim.37
  2.1 5.0 %voltages.1 = (f32[128,128]{1,0:T(8,128)}, f32[1,128]{1,0:T(1,128)}) custom-call(f32[4,64,1024]{2,1,0:T(8,128)} %p_ref.5, s32[128,128]{1,0:T(8,128)} %bitcast.13, s32[128,128]{1,0:T(8,128)} %bitcast.15, s32[1,128]{1,0:T(1,128)} %reshape_reshape.3.cnt_ref), custom_call_target="tpu_custom_call" | custom-call | flops 4000000 | bytes 1300000 | tf_op jit(solution)/shard_map/voltages/pallas_call | solution.py:421
  7.0 3.0 %collective-permute-start.8 = (f32[1,128]{1,0:T(1,128)}, f32[1,128]{1,0:T(1,128)S(1)}, u32[]{:S(2)}, u32[]{:S(2)}) collective-permute-start(f32[1,128]{1,0:T(1,128)} %get-tuple-element.26), channel_id=1, source_target_pairs={{0,3},{1,0},{2,1},{3,2},{4,7},{5,4},{6,5},{7,6},{8,11},{9,8},{10,9... | collective-permute-start | bytes 1544 | tf_op jit(solution)/shard_map/ppermute | solution.py:431
  10.7 1.0 collective-permute-start.6
  12.3 81.3 %pack.1 = (f32[4,64,1024]{2,1,0:T(8,128)}, f32[4,64,1024]{2,1,0:T(8,128)}, f32[8,8,1024]{2,1,0:T(8,128)}, f32[8,8,1024]{2,1,0:T(8,128)}) custom-call(s32[4]{0:T(128)} %pad_add_fusion.meta, f32[4,64,1024]{2,1,0:T(8,128)} %p_ref.5, f32[4,64,1024]{2,1,0:T(8,128)} %c_hbm.3), custom_call_target="tpu_custom_call" | custom-call | bytes 5000000 | tf_op jit(solution)/shard_map/pack/pallas_call | solution.py:435
  93.7 6.3 %collective-permute-start.1 = (f32[4,64,1024]{2,1,0:T(8,128)}, f32[4,64,1024]{2,1,0:T(8,128)}, u32[]{:S(2)}, u32[]{:S(2)}) collective-permute-start(f32[4,64,1024]{2,1,0:T(8,128)} %get-tuple-element.23), channel_id=1, source_target_pairs={{4,8},{8,4},{12,16},{16,12},{20,24},{24,20},{28,32},{32,28},{36,40... | collective-permute-start | bytes 3145736 | tf_op jit(solution)/shard_map/ppermute | solution.py:454
  100.1 1.3 collective-permute-start.2
  101.4 5.3 %collective-permute-start.3 = (f32[8,8,1024]{2,1,0:T(8,128)}, f32[8,8,1024]{2,1,0:T(8,128)}, u32[]{:S(2)}, u32[]{:S(2)}) collective-permute-start(f32[8,8,1024]{2,1,0:T(8,128)} %get-tuple-element.25), channel_id=1, source_target_pairs={{0,1},{1,2},{2,3},{4,5},{5,6},{6,7},{8,9},{9,10},{10,11},{12,13},{... | collective-permute-start | bytes 786440 | tf_op jit(solution)/shard_map/ppermute | solution.py:455
  107.3 1.9 %collective-permute-start.10 = (f32[4,128]{1,0:T(4,128)S(1)}, f32[4,128]{1,0:T(4,128)S(1)}, u32[]{:S(2)}, u32[]{:S(2)}) collective-permute-start(f32[4,128]{1,0:T(4,128)S(1)} %pad_maximum_fusion.2), channel_id=1, source_target_pairs={{4,8},{8,4},{12,16},{16,12},{20,24},{24,20},{28,32},{32,28},{36,40... | collective-permute-start | bytes 6152 | tf_op jit(solution)/shard_map/ppermute | solution.py:503
  109.2 0.7 broadcast_in_dim.42.gr_ref
  109.9 0.7 broadcast_in_dim.41.g_ref
  110.6 0.7 broadcast_in_dim.40.rate_ref
  111.4 6.9 %ionic.1 = (f32[40,16384]{1,0:T(8,128)}, f32[128,128]{1,0:T(8,128)}, f32[128,128]{1,0:T(8,128)}) custom-call(s32[64]{0:T(128)} %cnt.1, s32[64]{0:T(128)} %typ.1, f32[128,128]{1,0:T(8,128)} %get-tuple-element.27.volt_ref, f32[40,16384]{1,0:T(8,128)} %st_ref.1, f32[4,40,128]{2,1,0:T(8,128)} %broadcast_in_dim.40.rate_ref, ...), custom_call_target="tpu_custom_call" | custom-call | flops 16000000 | bytes 5300000 | tf_op jit(solution)/shard_map/ionic/pallas_call | solution.py:469
  118.4 7.4 %scatter.1 = (f32[4,64,1024]{2,1,0:T(8,128)}, f32[4,64,1024]{2,1,0:T(8,128)}) custom-call(f32[128,128]{1,0:T(8,128)} %get-tuple-element.28.ion_ref, f32[128,128]{1,0:T(8,128)} %get-tuple-element.29.act_ref, s32[128,128]{1,0:T(8,128)} %bitcast.14, s32[128,128]{1,0:T(8,128)} %bitcast.16), custom_call_target="tpu_custom_call" | custom-call | flops 800000000 | bytes 2300000 | tf_op jit(solution)/shard_map/scatter/pallas_call | solution.py:482
  126.2 1.0 select_select_fusion.y_hbm
  127.3 5.4 %start.1 = (f32[4,64,1024]{2,1,0:T(8,128)S(1)}, f32[4,64,1024]{2,1,0:T(8,128)S(1)}) custom-call(s32[4]{0:T(128)S(1)} %copy-done.5, f32[4,64,1024]{2,1,0:T(8,128)S(1)} %copy-done, f32[4,64,1024]{2,1,0:T(8,128)S(1)} %copy-done.1, f32[4,64,1024]{2,1,0:T(8,128)S(1)} %collective-permute-done.a_hbm.ca_hbm, f32[4,64,1024]{2,1,0:T(8,128)} %collective-permute-done.1.b_hbm.cb_hbm, ...), custom_call_target="tpu_custom_call" | custom-call | flops 16000000 | bytes 6000000 | tf_op jit(solution)/shard_map/start/pallas_call | solution.py:491
  132.8 1.8 %gap.1 = (f32[4,64,1024]{2,1,0:T(8,128)S(1)}, f32[3,64,1024]{2,1,0:T(8,128)S(1)}, f32[3,64,1024]{2,1,0:T(8,128)S(1)}, f32[4,8,1024]{2,1,0:T(8,128)S(1)}, f32[4,8,1024]{2,1,0:T(8,128)S(1)}, /*index=5*/f32[128,128]{1,0:T(8,128)}) custom-call(s32[4]{0:T(128)S(1)} %copy-done.5, f32[12,128]{1,0:T(8,128)S(1)} %concatenate.8.table_ref, ...), custom_call_target="tpu_custom_call" | custom-call | flops 1000000 | bytes 5000000 | tf_op jit(solution)/shard_map/gap/pallas_call | solution.py:506
  134.6 1.3 collective-permute-start.13
  135.9 4.6 %collective-permute-start.14 = (f32[4,8,1024]{2,1,0:T(8,128)S(1)}, f32[4,8,1024]{2,1,0:T(8,128)S(1)}, u32[]{:S(2)}, u32[]{:S(2)}) collective-permute-start(f32[4,8,1024]{2,1,0:T(8,128)S(1)} %get-tuple-element.38), channel_id=1, source_target_pairs={{0,1},{1,2},{2,3},{4,5},{5,6},{6,7},{8,9},{9,10},{10,11},{12,13},{... | collective-permute-start | bytes 393224 | tf_op jit(solution)/shard_map/ppermute | solution.py:519
  140.6 6.1 %collective-permute-start.12 = (f32[3,64,1024]{2,1,0:T(8,128)S(1)}, f32[3,64,1024]{2,1,0:T(8,128)S(1)}, u32[]{:S(2)}, u32[]{:S(2)}) collective-permute-start(f32[3,64,1024]{2,1,0:T(8,128)S(1)} %get-tuple-element.36), channel_id=1, source_target_pairs={{4,8},{8,4},{12,16},{16,12},{20,24},{24,20},{28,32},{32,28},{36,40... | collective-permute-start | bytes 2359304 | tf_op jit(solution)/shard_map/ppermute | solution.py:518
  146.7 1.9 %collective-permute-start.5 = (f32[2,8,1024]{2,1,0:T(8,128)S(1)}, f32[2,8,1024]{2,1,0:T(8,128)S(1)}, u32[]{:S(2)}, u32[]{:S(2)}) collective-permute-start(f32[2,8,1024]{2,1,0:T(8,128)S(1)} %get-tuple-element.41), channel_id=1, source_target_pairs={{4,8},{8,4},{12,16},{16,12},{20,24},{24,20},{28,32},{32,28},{36,40... | collective-permute-start | bytes 196616 | tf_op jit(solution)/shard_map/ppermute | solution.py:452
  148.8 5.8 %collective-permute-start.16 = (f32[2,8,1024]{2,1,0:T(8,128)S(1)}, f32[2,8,1024]{2,1,0:T(8,128)S(1)}, u32[]{:S(2)}, u32[]{:S(2)}) collective-permute-start(f32[2,8,1024]{2,1,0:T(8,128)S(1)} %get-tuple-element.45), channel_id=1, source_target_pairs={{4,8},{8,4},{12,16},{16,12},{20,24},{24,20},{28,32},{32,28},{36,40... | collective-permute-start | bytes 196616 | tf_op jit(solution)/shard_map/ppermute | solution.py:452
  154.6 2.4 %collective-permute-done.5.ccb_hbm = f32[2,8,1024]{2,1,0:T(8,128)S(1)} collective-permute-done((f32[2,8,1024]{2,1,0:T(8,128)S(1)}, f32[2,8,1024]{2,1,0:T(8,128)S(1)}, u32[]{:S(2)}, u32[]{:S(2)}) %collective-permute-start.5) | collective-permute-done | bytes 65568 | tf_op jit(solution)/shard_map/ppermute | solution.py:452
  158.3 10.5 %sweeps.1 = f32[4,64,1024]{2,1,0:T(8,128)} custom-call(s32[4]{0:T(128)S(1)} %copy-done.5, f32[4,64,1024]{2,1,0:T(8,128)S(1)} %copy-done, f32[4,64,1024]{2,1,0:T(8,128)S(1)} %copy-done.1, f32[4,64,1024]{2,1,0:T(8,128)S(1)} %collective-permute-done.a_hbm.ca_hbm, f32[4,64,1024]{2,1,0:T(8,128)} %collective-permute-done.1.b_hbm.cb_hbm, ...), custom_call_target="tpu_custom_call" | custom-call | flops 50000000 | bytes 10000000 | tf_op jit(solution)/shard_map/sweeps/pallas_call | solution.py:523
  (70 shorter events, 4.8 us)
Async XLA Ops:
  0.6 99.4 %copy-start.7 = (f32[3,40]{1,0:T(4,128)S(1)}, f32[3,40]{1,0:T(4,128)}, u32[]{:S(2)}) copy-start(f32[3,40]{1,0:T(4,128)} %param.18) | copy-start | bytes 1444
  0.6 99.4 %copy-start.13 = (f32[40]{0:T(128)S(1)}, f32[40]{0:T(128)}, u32[]{:S(2)}) copy-start(f32[40]{0:T(128)} %param.19) | copy-start | bytes 484
  0.7 99.4 %copy-start.12 = (f32[2,40]{1,0:T(2,128)S(1)}, f32[2,40]{1,0:T(2,128)}, u32[]{:S(2)}) copy-start(f32[2,40]{1,0:T(2,128)} %param.17) | copy-start | bytes 964
  0.7 99.4 %copy-start.11 = (f32[2,40]{1,0:T(2,128)S(1)}, f32[2,40]{1,0:T(2,128)}, u32[]{:S(2)}) copy-start(f32[2,40]{1,0:T(2,128)} %param.16) | copy-start | bytes 964
  7.0 93.1 %collective-permute-start.8 = (f32[1,128]{1,0:T(1,128)}, f32[1,128]{1,0:T(1,128)S(1)}, u32[]{:S(2)}, u32[]{:S(2)}) collective-permute-start(f32[1,128]{1,0:T(1,128)} %get-tuple-element.26), channel_id=1, source_target_pairs={{0,3},{1,0},{2,1},{3,2},{4,7},{5,4},{6,5},{7,6},{8,11},{9,8},{10,9... | collective-permute-start | bytes 1544 | tf_op jit(solution)/shard_map/ppermute | solution.py:431
  10.1 91.3 %collective-permute-start.7 = (f32[1,128]{1,0:T(1,128)}, f32[1,128]{1,0:T(1,128)S(1)}, u32[]{:S(2)}, u32[]{:S(2)}) collective-permute-start(f32[1,128]{1,0:T(1,128)} %get-tuple-element.26), channel_id=1, source_target_pairs={{0,2},{1,3},{2,0},{3,1},{4,6},{5,7},{6,4},{7,5},{8,10},{9,11},{10,... | collective-permute-start | bytes 1544 | tf_op jit(solution)/shard_map/ppermute | solution.py:431
  10.7 96.0 %collective-permute-start.6 = (f32[1,128]{1,0:T(1,128)}, f32[1,128]{1,0:T(1,128)S(1)}, u32[]{:S(2)}, u32[]{:S(2)}) collective-permute-start(f32[1,128]{1,0:T(1,128)} %get-tuple-element.26), channel_id=1, source_target_pairs={{0,1},{1,2},{2,3},{3,0},{4,5},{5,6},{6,7},{7,4},{8,9},{9,10},{10,1... | collective-permute-start | bytes 1544 | tf_op jit(solution)/shard_map/ppermute | solution.py:431
  93.6 33.6 %collective-permute-start = (f32[4,64,1024]{2,1,0:T(8,128)}, f32[4,64,1024]{2,1,0:T(8,128)S(1)}, u32[]{:S(2)}, u32[]{:S(2)}) collective-permute-start(f32[4,64,1024]{2,1,0:T(8,128)} %get-tuple-element.22), channel_id=1, source_target_pairs={{0,4},{4,0},{8,12},{12,8},{16,20},{20,16},{24,28},{28,24},{32,36},... | collective-permute-start | bytes 3145736 | tf_op jit(solution)/shard_map/ppermute | solution.py:454
  93.7 33.6 %collective-permute-start.1 = (f32[4,64,1024]{2,1,0:T(8,128)}, f32[4,64,1024]{2,1,0:T(8,128)}, u32[]{:S(2)}, u32[]{:S(2)}) collective-permute-start(f32[4,64,1024]{2,1,0:T(8,128)} %get-tuple-element.23), channel_id=1, source_target_pairs={{4,8},{8,4},{12,16},{16,12},{20,24},{24,20},{28,32},{32,28},{36,40... | collective-permute-start | bytes 3145736 | tf_op jit(solution)/shard_map/ppermute | solution.py:454
  100.1 26.1 %collective-permute-start.2 = (f32[8,8,1024]{2,1,0:T(8,128)}, f32[8,8,1024]{2,1,0:T(8,128)S(1)}, u32[]{:S(2)}, u32[]{:S(2)}) collective-permute-start(f32[8,8,1024]{2,1,0:T(8,128)} %get-tuple-element.24), channel_id=1, source_target_pairs={{1,0},{2,1},{3,2},{5,4},{6,5},{7,6},{9,8},{10,9},{11,10},{13,12},{... | collective-permute-start | bytes 786440 | tf_op jit(solution)/shard_map/ppermute | solution.py:455
  101.4 24.8 %collective-permute-start.3 = (f32[8,8,1024]{2,1,0:T(8,128)}, f32[8,8,1024]{2,1,0:T(8,128)}, u32[]{:S(2)}, u32[]{:S(2)}) collective-permute-start(f32[8,8,1024]{2,1,0:T(8,128)} %get-tuple-element.25), channel_id=1, source_target_pairs={{0,1},{1,2},{2,3},{4,5},{5,6},{6,7},{8,9},{9,10},{10,11},{12,13},{... | collective-permute-start | bytes 786440 | tf_op jit(solution)/shard_map/ppermute | solution.py:455
  107.3 11.0 %collective-permute-start.10 = (f32[4,128]{1,0:T(4,128)S(1)}, f32[4,128]{1,0:T(4,128)S(1)}, u32[]{:S(2)}, u32[]{:S(2)}) collective-permute-start(f32[4,128]{1,0:T(4,128)S(1)} %pad_maximum_fusion.2), channel_id=1, source_target_pairs={{4,8},{8,4},{12,16},{16,12},{20,24},{24,20},{28,32},{32,28},{36,40... | collective-permute-start | bytes 6152 | tf_op jit(solution)/shard_map/ppermute | solution.py:503
  118.2 9.0 %copy-start = (f32[4,64,1024]{2,1,0:T(8,128)S(1)}, f32[4,64,1024]{2,1,0:T(8,128)}, u32[]{:S(2)}) copy-start(f32[4,64,1024]{2,1,0:T(8,128)} %p_ref.5) | copy-start | bytes 3145732
  118.3 9.0 %copy-start.1 = (f32[4,64,1024]{2,1,0:T(8,128)S(1)}, f32[4,64,1024]{2,1,0:T(8,128)}, u32[]{:S(2)}) copy-start(f32[4,64,1024]{2,1,0:T(8,128)} %c_hbm.3) | copy-start | bytes 3145732
  118.3 7.8 %collective-permute-start.9 = (f32[4,128]{1,0:T(4,128)S(1)}, f32[4,128]{1,0:T(4,128)S(1)}, u32[]{:S(2)}, u32[]{:S(2)}) collective-permute-start(f32[4,128]{1,0:T(4,128)S(1)} %pad_maximum_fusion.2), channel_id=1, source_target_pairs={{0,4},{4,0},{8,12},{12,8},{16,20},{20,16},{24,28},{28,24},{32,36},... | collective-permute-start | bytes 6152 | tf_op jit(solution)/shard_map/ppermute | solution.py:503
  134.6 22.4 %copy-start.2 = (f32[4,64,1024]{2,1,0:T(8,128)}, f32[4,64,1024]{2,1,0:T(8,128)S(1)}, u32[]{:S(2)}) copy-start(f32[4,64,1024]{2,1,0:T(8,128)S(1)} %get-tuple-element.34.u_hbm) | copy-start | bytes 3145732
  134.6 14.0 %collective-permute-start.13 = (f32[4,8,1024]{2,1,0:T(8,128)S(1)}, f32[4,8,1024]{2,1,0:T(8,128)S(1)}, u32[]{:S(2)}, u32[]{:S(2)}) collective-permute-start(f32[4,8,1024]{2,1,0:T(8,128)S(1)} %get-tuple-element.37), channel_id=1, source_target_pairs={{1,0},{2,1},{3,2},{5,4},{6,5},{7,6},{9,8},{10,9},{11,10},{13,12},{... | collective-permute-start | bytes 393224 | tf_op jit(solution)/shard_map/ppermute | solution.py:519
  135.9 12.8 %collective-permute-start.14 = (f32[4,8,1024]{2,1,0:T(8,128)S(1)}, f32[4,8,1024]{2,1,0:T(8,128)S(1)}, u32[]{:S(2)}, u32[]{:S(2)}) collective-permute-start(f32[4,8,1024]{2,1,0:T(8,128)S(1)} %get-tuple-element.38), channel_id=1, source_target_pairs={{0,1},{1,2},{2,3},{4,5},{5,6},{6,7},{8,9},{9,10},{10,11},{12,13},{... | collective-permute-start | bytes 393224 | tf_op jit(solution)/shard_map/ppermute | solution.py:519
  140.5 17.8 %collective-permute-start.11 = (f32[3,64,1024]{2,1,0:T(8,128)S(1)}, f32[3,64,1024]{2,1,0:T(8,128)S(1)}, u32[]{:S(2)}, u32[]{:S(2)}) collective-permute-start(f32[3,64,1024]{2,1,0:T(8,128)S(1)} %get-tuple-element.35), channel_id=1, source_target_pairs={{0,4},{4,0},{8,12},{12,8},{16,20},{20,16},{24,28},{28,24},{32,36},... | collective-permute-start | bytes 2359304 | tf_op jit(solution)/shard_map/ppermute | solution.py:518
  140.6 17.7 %collective-permute-start.12 = (f32[3,64,1024]{2,1,0:T(8,128)S(1)}, f32[3,64,1024]{2,1,0:T(8,128)S(1)}, u32[]{:S(2)}, u32[]{:S(2)}) collective-permute-start(f32[3,64,1024]{2,1,0:T(8,128)S(1)} %get-tuple-element.36), channel_id=1, source_target_pairs={{4,8},{8,4},{12,16},{16,12},{20,24},{24,20},{28,32},{32,28},{36,40... | collective-permute-start | bytes 2359304 | tf_op jit(solution)/shard_map/ppermute | solution.py:518
  146.7 10.3 %collective-permute-start.5 = (f32[2,8,1024]{2,1,0:T(8,128)S(1)}, f32[2,8,1024]{2,1,0:T(8,128)S(1)}, u32[]{:S(2)}, u32[]{:S(2)}) collective-permute-start(f32[2,8,1024]{2,1,0:T(8,128)S(1)} %get-tuple-element.41), channel_id=1, source_target_pairs={{4,8},{8,4},{12,16},{16,12},{20,24},{24,20},{28,32},{32,28},{36,40... | collective-permute-start | bytes 196616 | tf_op jit(solution)/shard_map/ppermute | solution.py:452
  148.6 8.4 %collective-permute-start.4 = (f32[2,8,1024]{2,1,0:T(8,128)S(1)}, f32[2,8,1024]{2,1,0:T(8,128)S(1)}, u32[]{:S(2)}, u32[]{:S(2)}) collective-permute-start(f32[2,8,1024]{2,1,0:T(8,128)S(1)} %get-tuple-element.42), channel_id=1, source_target_pairs={{0,4},{4,0},{8,12},{12,8},{16,20},{20,16},{24,28},{28,24},{32,36},... | collective-permute-start | bytes 196616 | tf_op jit(solution)/shard_map/ppermute | solution.py:452
  148.8 8.9 %collective-permute-start.16 = (f32[2,8,1024]{2,1,0:T(8,128)S(1)}, f32[2,8,1024]{2,1,0:T(8,128)S(1)}, u32[]{:S(2)}, u32[]{:S(2)}) collective-permute-start(f32[2,8,1024]{2,1,0:T(8,128)S(1)} %get-tuple-element.45), channel_id=1, source_target_pairs={{4,8},{8,4},{12,16},{16,12},{20,24},{24,20},{28,32},{32,28},{36,40... | collective-permute-start | bytes 196616 | tf_op jit(solution)/shard_map/ppermute | solution.py:452
  157.0 1.3 collective-permute-start.15
  (7 other events, 48.5 us)

commit v2 on v1

--- a/solution.py
+++ b/solution.py
@@ -15,7 +15,10 @@
 ANY = pl.BlockSpec(memory_space=pl.ANY)
 VM = pl.BlockSpec(memory_space=pltpu.VMEM)
 SM = pl.BlockSpec(memory_space=pltpu.SMEM)
-BIG = pltpu.CompilerParams(vmem_limit_bytes=48 * 1024 * 1024)
+
+
+def grant(mib):
+    return pltpu.CompilerParams(vmem_limit_bytes=mib * 1024 * 1024)
 
 
 def sweep_factors():
@@ -68,7 +71,7 @@
                 volt_ref[pl.ds(8 * kk + 4 * q + 2 + h, 1), :] = d[4:5]
         return carry
 
-    lax.fori_loop(0, 16, body, 0)
+    lax.fori_loop(0, 16, body, 0, unroll=4)
     turned = jnp.transpose(volt_ref[...])
     cnt = cnt_ref[...]
     lanes = iota((128, 128), 1)
@@ -79,26 +82,17 @@
     cell_ref[...] = (total + other) / jnp.maximum(cnt, 1).astype(F32)
 
 
-def pack_kernel(meta, p_ref, c_ref, a_ref, b_ref, up_ref, down_ref, sem):
+def pack_kernel(meta, p_ref, c_ref, a_ref, b_ref, up_ref, down_ref):
     par = meta[0]
-    copies = []
     for i in range(3):
-        copies.append((c_ref.at[plane_of(par, 3 - i)], a_ref.at[i]))
-        copies.append((c_ref.at[plane_of(par, i)], b_ref.at[i]))
-    copies.append((p_ref.at[plane_of(par, 3)], a_ref.at[3]))
-    copies.append((p_ref.at[plane_of(par, 0)], b_ref.at[3]))
+        a_ref[i] = c_ref[plane_of(par, 3 - i)]
+        b_ref[i] = c_ref[plane_of(par, i)]
+    a_ref[3] = p_ref[plane_of(par, 3)]
+    b_ref[3] = p_ref[plane_of(par, 0)]
     for k, ref in enumerate((c_ref, p_ref)):
-        copies.append((ref.at[:, 56:64], up_ref.at[4 * k : 4 * k + 4]))
-        copies.append((ref.at[:, 0:8], down_ref.at[4 * k : 4 * k + 4]))
-    run_copies(copies, sem)
-
-
-def run_copies(copies, sem, start=0):
-    made = [pltpu.make_async_copy(s, d, sem.at[start + n]) for n, (s, d) in enumerate(copies)]
-    for m in made:
-        m.start()
-    for m in made:
-        m.wait()
+        for x in range(4):
+            up_ref[4 * k + x] = ref[x, 56:64]
+            down_ref[4 * k + x] = ref[x, 0:8]
 
 
 def ionic_kernel(cnt, typ, volt_ref, st_ref, rate_ref, g_ref, gr_ref, out_ref, ion_ref, act_ref):
@@ -106,36 +100,42 @@
     cells = volt_ref.shape[0] // 2
     lane = iota((8, 128), 1)
 
-    def body(cc, carry):
-        n = cnt[step * cells + cc]
-        ty = typ[step * cells + cc]
-        for h in range(2):
-            r = cc * 2 + h
-            cols = pl.ds(pl.multiple_of(r * 128, 128), 128)
-            v = jnp.broadcast_to(volt_ref[pl.ds(r, 1), :], (8, 128))
-            active = lane + h * 128 < n
-            w1 = w2 = None
-            for k in range(5):
-                rows = slice(8 * k, 8 * k + 8)
-                st = st_ref[rows, cols]
-                opening = jnp.exp2(rate_ref[0, rows] * v + rate_ref[1, rows])
-                closing = jnp.exp2(rate_ref[2, rows] * v + rate_ref[3, rows])
-                total = opening + closing
-                rec = pl.reciprocal(total, approx=True)
-                rec = rec * (2.0 - total * rec)
-                steady = opening * rec
-                fresh = steady + (st - steady) * jnp.exp2(total * (-0.5 * LOG2E))
-                out_ref[rows, cols] = jnp.where(active, fresh, st)
-                a = g_ref[ty, rows] * fresh
-                b = gr_ref[ty, rows] * fresh
-                w1 = a if w1 is None else w1 + a
-                w2 = b if w2 is None else w2 + b
-            ion = jnp.sum(w1 * v - w2, axis=0, keepdims=True)
-            ion_ref[pl.ds(r, 1), :] = jnp.where(active[0:1], ion, 0.0)
-            act_ref[pl.ds(r, 1), :] = jnp.where(active[0:1], 1.0, 0.0)
-        return carry
-
-    lax.fori_loop(0, cells, body, 0)
+    def body(group, carry):
+        rows8 = pl.ds(pl.multiple_of(8 * group, 8), 8)
+        volts = volt_ref[rows8, :]
+        counts, types, v, active, cols = [], [], [], [], []
+        for q in range(4):
+            counts.append(cnt[step * cells + 4 * group + q])
+            types.append(typ[step * cells + 4 * group + q])
+        for r in range(8):
+            v.append(jnp.broadcast_to(volts[r : r + 1], (8, 128)))
+            active.append(lane + (r % 2) * 128 < counts[r // 2])
+            cols.append(pl.ds(pl.multiple_of(1024 * group + 128 * r, 128), 128))
+        w1, w2 = [None] * 8, [None] * 8
+        for k in range(5):
+            rows = slice(8 * k, 8 * k + 8)
+            rate = [rate_ref[i, rows] for i in range(4)]
+            for q in range(4):
+                g, gr = g_ref[types[q], rows], gr_ref[types[q], rows]
+                for r in (2 * q, 2 * q + 1):
+                    st = st_ref[rows, cols[r]]
+                    opening = jnp.exp2(rate[0] * v[r] + rate[1])
+                    closing = jnp.exp2(rate[2] * v[r] + rate[3])
+                    total = opening + closing
+                    rec = pl.reciprocal(total, approx=True)
+                    rec = rec * (2.0 - total * rec)
+                    steady = opening * rec
+                    fresh = steady + (st - steady) * jnp.exp2(total * (-0.5 * LOG2E))
+                    out_ref[rows, cols[r]] = jnp.where(active[r], fresh, st)
+                    w1[r] = g * fresh if k == 0 else w1[r] + g * fresh
+                    w2[r] = gr * fresh if k == 0 else w2[r] + gr * fresh
+        used = jnp.concatenate([jnp.where(a, 1.0, 0.0)[0:1] for a in active], axis=0)
+        ion = [jnp.sum(w1[r] * v[r] - w2[r], axis=0, keepdims=True) for r in range(8)]
+        ion_ref[rows8, :] = jnp.concatenate(ion, axis=0) * used
+        act_ref[rows8, :] = used
+        return carry
+
+    lax.fori_loop(0, cells // 4, body, 0)
 
 
 def scatter_kernel(ion_ref, act_ref, in_ref, ex_ref, s_ref, n_ref):
@@ -179,7 +179,7 @@
                     dst[x, row, 256 * j + 128 : 256 * j + 256] = pltpu.roll(jnp.where(low, oj, ej), 4, 0)
         return carry
 
-    lax.fori_loop(0, 16, body, 0)
+    lax.fori_loop(0, 16, body, 0, unroll=4)
 
 
 def tile(ref, e, t):
@@ -219,30 +219,75 @@
     return ((t[0] + t[1]) + (t[2] + t[3])) + (t[4] + t[5])
 
 
-def start_kernel(meta, p_hbm, c_hbm, a_hbm, b_hbm, y_hbm, s_ref, n_ref, w_ref, k_ref, pe, ce, sem):
-    par = meta[0]
+def halo_copies(par, dst, own, a, b, y, ca, cb, sem, start, own_y=0):
     copies = []
-    for e, hbm, yk in ((ce, c_hbm, 0), (pe, p_hbm, 4)):
-        for j in range(4):
-            copies.append((hbm.at[plane_of(par, j)], e.at[1 + j, 0:64]))
-            copies.append((y_hbm.at[yk + plane_of(par, j)], e.at[1 + j, 64:72]))
-    copies.append((a_hbm.at[0], ce.at[5, 0:64]))
-    copies.append((b_hbm.at[0], ce.at[0, 0:64]))
-    copies.append((a_hbm.at[3], pe.at[5, 0:64]))
-    copies.append((b_hbm.at[3], pe.at[0, 0:64]))
-    run_copies(copies, sem)
+    for j in range(4):
+        copies.append((own.at[plane_of(par, j)], dst.at[3 + j, 0:64]))
+        copies.append((y.at[own_y + plane_of(par, j)], dst.at[3 + j, 64:72]))
+    for i in range(3):
+        copies.append((a.at[i], dst.at[7 + i, 0:64]))
+        copies.append((b.at[i], dst.at[2 - i, 0:64]))
+    for i in range(2):
+        copies.append((ca.at[i], dst.at[7 + i, 64:72]))
+        copies.append((cb.at[i], dst.at[2 - i, 64:72]))
+    return begin(copies, sem, start)
+
+
+def begin(copies, sem, start):
+    made = [pltpu.make_async_copy(s, d, sem.at[start + n]) for n, (s, d) in enumerate(copies)]
+    for m in made:
+        m.start()
+    return made
+
+
+def operator_kernel(meta, p_hbm, c_hbm, a_hbm, b_hbm, y_hbm, ca_hbm, cb_hbm, s_ref, n_ref,
+                    fx, fym, fyp, fzm, fzp, inv, w_ref, k_ref, c, pe, sem):
+    par, has_b, mine = meta[0], meta[1], meta[2]
+    made = halo_copies(par, c, c_hbm, a_hbm, b_hbm, y_hbm, ca_hbm, cb_hbm, sem, 0)
+    copies = [(a_hbm.at[3], pe.at[5, 0:64]), (b_hbm.at[3], pe.at[0, 0:64])]
+    for j in range(4):
+        copies.append((p_hbm.at[plane_of(par, j)], pe.at[1 + j, 0:64]))
+        copies.append((y_hbm.at[4 + plane_of(par, j)], pe.at[1 + j, 64:72]))
+    made += begin(copies, sem, len(made))
+    zero8 = jnp.zeros((8, 1024), F32)
+    c[0, 64:72, :] = zero8
+    c[9, 64:72, :] = zero8
+    sub = iota((8, 1024), 0)
+    bottom = (sub < 3) & (mine != 3)
+    top = (sub >= 5) & (mine != 0)
+    keep = jnp.where(bottom | top, 1.0, 0.0)
+    for m in made:
+        m.wait()
+
+    def build(e, carry):
+        around = Around(c, e)
+        inside = jnp.where((e >= 3) | (has_b == 1), 1.0, 0.0)
+        for t in range(9):
+            rows = slice(8 * t, 8 * t + 8)
+            fs, diagonal = couplings(around, t)
+            part = inside / diagonal
+            inv[e - 1, rows, :] = part * keep if t == 8 else part
+            fx[e - 1, rows, :] = fs[0]
+            fx[e, rows, :] = fs[1]
+            fym[e - 1, rows, :] = fs[2]
+            fyp[e - 1, rows, :] = fs[3]
+            fzm[e - 1, rows, :] = fs[4]
+            fzp[e - 1, rows, :] = fs[5]
+        return carry
+
+    lax.fori_loop(1, 9, build, 0)
 
     def body(j, carry):
         x = plane_of(par, j)
-        ca, pa = Around(ce, 1 + j), Around(pe, 1 + j)
+        pa = Around(pe, 1 + j)
         for t in range(8):
             rows = slice(8 * t, 8 * t + 8)
-            fs, diagonal = couplings(ca, t)
-            inv = 1.0 / diagonal
+            fs = [tile(fx, j + 2, t), tile(fx, j + 3, t)] + [tile(f, j + 2, t) for f in (fym, fyp, fzm, fzp)]
+            part = tile(inv, j + 2, t)
             views = pa.at(t)
             p = views[0]
-            w_ref[x, rows, :] = (p + weighted(fs, views[1:]) - 0.5 * s_ref[x, rows, :]) * inv - p
-            k_ref[x, rows, :] = (-0.5 * inv) * n_ref[x, rows, :]
+            w_ref[x, rows, :] = (p + weighted(fs, views[1:]) - 0.5 * s_ref[x, rows, :]) * part - p
+            k_ref[x, rows, :] = (-0.5 * part) * n_ref[x, rows, :]
         return carry
 
     lax.fori_loop(0, 4, body, 0)
@@ -296,65 +341,21 @@
     lax.fori_loop(0, 4, body, 0)
 
 
-def sweep_kernel(meta, p_ref, c_hbm, ca_hbm, cb_hbm, cy_hbm, cca_hbm, ccb_hbm,
-                 u_hbm, ua_hbm, ub_hbm, uy_hbm, uca_hbm, ucb_hbm, out_ref,
-                 c, u0, u1, u2, r, fx, fym, fyp, fzm, fzp, inv, sem):
-    par, has_b, mine = meta[0], meta[1], meta[2]
-
-    def loads(dst, own, a, b, y, ca, cb, start):
-        copies = []
-        for j in range(4):
-            copies.append((own.at[plane_of(par, j)], dst.at[3 + j, 0:64]))
-            copies.append((y.at[plane_of(par, j)], dst.at[3 + j, 64:72]))
-        for i in range(3):
-            copies.append((a.at[i], dst.at[7 + i, 0:64]))
-            copies.append((b.at[i], dst.at[2 - i, 0:64]))
-        for i in range(2):
-            copies.append((ca.at[i], dst.at[7 + i, 64:72]))
-            copies.append((cb.at[i], dst.at[2 - i, 64:72]))
-        made = [pltpu.make_async_copy(s, d, sem.at[start + n]) for n, (s, d) in enumerate(copies)]
-        for m in made:
-            m.start()
-        return made
-
-    c_copies = loads(c, c_hbm, ca_hbm, cb_hbm, cy_hbm, cca_hbm, ccb_hbm, 0)
-    u_copies = loads(u0, u_hbm, ua_hbm, ub_hbm, uy_hbm, uca_hbm, ucb_hbm, len(c_copies))
+def sweep_kernel(meta, p_ref, fx, fym, fyp, fzm, fzp, inv, u_hbm, ua_hbm, ub_hbm, uy_hbm, uca_hbm, ucb_hbm,
+                 out_ref, u0, u1, u2, r, sem):
+    par = meta[0]
+    made = halo_copies(par, u0, u_hbm, ua_hbm, ub_hbm, uy_hbm, uca_hbm, ucb_hbm, sem, 0)
     zero8 = jnp.zeros((8, 1024), F32)
-    for dst in (c, u0):
-        dst[0, 64:72, :] = zero8
-        dst[9, 64:72, :] = zero8
-    sub = iota((8, 1024), 0)
-    bottom = (sub < 3) & (mine != 3)
-    top = (sub >= 5) & (mine != 0)
-    keep = jnp.where(bottom | top, 1.0, 0.0)
-    for m in c_copies:
-        m.wait()
-
-    def build(e, carry):
-        around = Around(c, e)
-        inside = jnp.where((e >= 3) | (has_b == 1), 1.0, 0.0)
-        for t in range(9):
-            rows = slice(8 * t, 8 * t + 8)
-            fs, diagonal = couplings(around, t)
-            part = inside / diagonal
-            inv[e, rows, :] = part * keep if t == 8 else part
-            fx[e - 1, rows, :] = fs[0]
-            fx[e, rows, :] = fs[1]
-            fym[e, rows, :] = fs[2]
-            fyp[e, rows, :] = fs[3]
-            fzm[e, rows, :] = fs[4]
-            fzp[e, rows, :] = fs[5]
-        return carry
-
-    lax.fori_loop(1, 9, build, 0)
-    for m in u_copies:
+    u0[0, 64:72, :] = zero8
+    u0[9, 64:72, :] = zero8
+    for m in made:
         m.wait()
     (a1, b1), (a2, b2), (a3, b3) = sweep_factors()
 
     def coupled(around, e, t):
-        fs = [tile(fx, e - 1, t), tile(fx, e, t)] + [tile(f, e, t) for f in (fym, fyp, fzm, fzp)]
+        fs = [tile(fx, e - 1, t), tile(fx, e, t)] + [tile(f, e - 1, t) for f in (fym, fyp, fzm, fzp)]
         views = around.at(t)
-        return views[0], tile(inv, e, t) * weighted(fs, views[1:])
+        return views[0], tile(inv, e - 1, t) * weighted(fs, views[1:])
 
     def first(e, carry):
         around = Around(u0, e)
@@ -423,6 +424,7 @@
         out_shape=(shape(128, 128), shape(1, 128)),
         in_specs=[VM] * 4,
         out_specs=(VM, VM),
+        compiler_params=grant(8),
         cost_estimate=pl.CostEstimate(flops=4000000, bytes_accessed=1300000, transcendentals=0),
         name="voltages",
     )(potential, intra, extra, cnt_lane)
@@ -435,9 +437,9 @@
     send_a, send_b, send_up, send_down = pl.pallas_call(
         pack_kernel,
         out_shape=(shape(4, 64, 1024), shape(4, 64, 1024), shape(8, 8, 1024), shape(8, 8, 1024)),
-        in_specs=[SM, ANY, ANY],
-        out_specs=(ANY,) * 4,
-        scratch_shapes=[pltpu.SemaphoreType.DMA((12,))],
+        in_specs=[SM, VM, VM],
+        out_specs=(VM,) * 4,
+        compiler_params=grant(12),
         cost_estimate=pl.CostEstimate(flops=0, bytes_accessed=5000000, transcendentals=0),
         name="pack",
     )(meta, potential, conductivity)
@@ -475,6 +477,7 @@
             in_specs=[facet_rows, state_block, whole(4), whole(3), whole(3)],
             out_specs=(state_block, facet_rows, facet_rows),
         ),
+        compiler_params=grant(16),
         cost_estimate=pl.CostEstimate(flops=16000000, bytes_accessed=5300000, transcendentals=2600000),
         name="ionic",
     )(facet_counts, cell_type, volt, ion_states, rates, g_wide, gr_wide)
@@ -484,21 +487,23 @@
         out_shape=(shape(4, 64, 1024), shape(4, 64, 1024)),
         in_specs=[VM] * 4,
         out_specs=(VM, VM),
+        compiler_params=grant(12),
         cost_estimate=pl.CostEstimate(flops=800000000, bytes_accessed=2300000, transcendentals=0),
         name="scatter",
     )(ion, act, intra, extra)
 
-    w, k = pl.pallas_call(
-        start_kernel,
-        out_shape=(shape(4, 64, 1024), shape(4, 64, 1024)),
-        in_specs=[SM, ANY, ANY, ANY, ANY, ANY, VM, VM],
-        out_specs=(VM, VM),
-        scratch_shapes=[pltpu.VMEM((6, 72, 1024), F32), pltpu.VMEM((6, 72, 1024), F32),
-                        pltpu.SemaphoreType.DMA((20,))],
-        compiler_params=BIG,
+    coefficients = (shape(9, 72, 1024),) + (shape(8, 72, 1024),) * 5
+    *operator, w, k = pl.pallas_call(
+        operator_kernel,
+        out_shape=coefficients + (shape(4, 64, 1024), shape(4, 64, 1024)),
+        in_specs=[SM] + [ANY] * 7 + [VM, VM],
+        out_specs=(VM,) * 8,
+        scratch_shapes=[pltpu.VMEM((10, 72, 1024), F32), pltpu.VMEM((6, 72, 1024), F32),
+                        pltpu.SemaphoreType.DMA((28,))],
+        compiler_params=grant(28),
         cost_estimate=pl.CostEstimate(flops=16000000, bytes_accessed=6000000, transcendentals=0),
-        name="start",
-    )(meta, potential, conductivity, early_a, early_b, y_early, source, count)
+        name="operator",
+    )(meta, potential, conductivity, early_a, early_b, y_early, corner_a, corner_b, source, count)
 
     table = jnp.concatenate([own_table, to_a(own_table), to_b(own_table)], axis=0)
     part_lane = jnp.repeat(gap_partner.T, 2, axis=1)
@@ -511,7 +516,7 @@
         out_specs=(VM,) * 6,
         scratch_shapes=[pltpu.VMEM((256, 128), F32)],
         cost_estimate=pl.CostEstimate(flops=1000000, bytes_accessed=5000000, transcendentals=0),
-        compiler_params=BIG,
+        compiler_params=grant(20),
         name="gap",
     )(meta, table, part_lane, cond_lane, cnt_lane, ion, act, w, k)
 
@@ -523,15 +528,13 @@
     potential_next = pl.pallas_call(
         sweep_kernel,
         out_shape=shape(4, 64, 1024),
-        in_specs=[SM, VM] + [ANY] * 12,
+        in_specs=[SM] + [VM] * 7 + [ANY] * 6,
         out_specs=VM,
-        scratch_shapes=[big(10), big(10), big(9), big(8), big(9), big(9), big(9), big(9), big(9), big(9), big(9),
-                        pltpu.SemaphoreType.DMA((36,))],
-        compiler_params=BIG,
+        scratch_shapes=[big(10), big(9), big(8), big(9), pltpu.SemaphoreType.DMA((18,))],
+        compiler_params=grant(30),
         cost_estimate=pl.CostEstimate(flops=50000000, bytes_accessed=10000000, transcendentals=0),
         name="sweeps",
-    )(meta, potential, conductivity, early_a, early_b, y_early[0:4], corner_a, corner_b,
-      u, late_a, late_b, y_late, late_corner_a, late_corner_b)
+    )(meta, potential, *operator, u, late_a, late_b, y_late, late_corner_a, late_corner_b)
     return potential_next, states_next, membrane.reshape(16384)
 
 

time: 170 us -> 109 us (0.64)
  Pallas kernels: 118 us -> 26.5 us
  local copies, waits for them, and re-layouts: 3.98 us -> 24.7 us
  waiting for transfers between devices: 3.67 us -> 17.5 us
  starting transfers between devices: 39.3 us -> 35.9 us
    pallas_call x1, Pallas kernels: 81.3 us -> 2.07 us  [per_device(): pl.pallas_call(pack_kernel, out_shape=(shape(4, 64, 1024), shape(4, 64, 1...]
    unnamed x28 -> x82, local copies, waits for them, and re-layouts: 0.06 us -> 16.2 us
    ppermute x3, waiting for transfers between devices: 0.01 us -> 6.68 us  [per_device(): lax.ppermute(cells, 'mem', [(i, (i + d) % 4) for i in range(4)])]
    ppermute x4, waiting for transfers between devices: 3.63 us -> 8.17 us  [corners(): return (to_a(toward_a), to_b(toward_b))]
    pallas_call x1, Pallas kernels: 7.38 us -> 3.27 us  [per_device(): pl.pallas_call(scatter_kernel, out_shape=(shape(4, 64, 1024), shape(4, 64...]
    pallas_call x1, Pallas kernels: 4.97 us -> 2.03 us  [per_device(): pl.pallas_call(gather_kernel, out_shape=(shape(128, 128), shape(1, 128)),...]
    pallas_call x2, Pallas kernels: 15.9 us -> 13 us  [the longest x1 7.13 us: per_device(): pl.pallas_call(sweep_kernel, out_shape=shape(4, 64, 1024), in_specs=[SM]...]
    ppermute x1, waiting for transfers between devices: 0.01 us -> 2.66 us  [per_device(): to_b(own_table)]
  transfers between devices with their start and end apart: 17 -> 17, of which waited for: 3 -> 4; matrix products, arithmetic and copies ran while one was open for 3% -> 10% of each run, Pallas kernels for 57% -> 9%
where the time goes in v2:
time: 109 us; the launch traced here: 108 us
  starting transfers between devices  35.9 us (33%)
  Pallas kernels  26.5 us (24%)
  local copies, waits for them, and re-layouts  24.7 us (23%)
  waiting for transfers between devices  17.5 us (16%)
  other arithmetic  2 us (2%)
  between operations  1.16 us (1%)
    unnamed x82, local copies, waits for them, and re-layouts  16.2 us
    ppermute x4, waiting for transfers between devices, corners(): return (to_a(toward_a), to_b(toward_b))  8.17 us
    ppermute x4, starting transfers between devices, corners(): return (to_a(toward_a), to_b(toward_b))  7.29 us
    pallas_call x1, Pallas kernels, per_device(): pl.pallas_call(sweep_kernel, out_shape=shape(4, 64, 1024), in_specs=[SM]...  7.13 us
    ppermute x3, waiting for transfers between devices, per_device(): lax.ppermute(cells, 'mem', [(i, (i + d) % 4) for i in range(4)])  6.68 us
    ppermute x2, starting transfers between devices, per_device(): y_early = edge_rows(to_up(send_up), to_down(send_down))  6.53 us
    ppermute x2, starting transfers between devices, per_device(): early_a, early_b = (to_a(send_a), to_b(send_b))  6.31 us
    ppermute x2, starting transfers between devices, per_device(): y_late = edge_rows(to_up(u_up), to_down(u_down))  5.83 us
  transfers between devices with their start and end apart: 17, of which 4 were waited for; matrix products, arithmetic and copies ran while one was open for 10% of the time, Pallas kernels for 9%

profile of v2, /device:TPU:6, one launch (start us, length us, event | category | flops | bytes accessed | tf_op | source)
XLA Modules:
  0.0 107.8 jit_solution(17086765787025166540)
XLA Ops:
  3.2 2.1 %pack.1 = (f32[4,64,1024]{2,1,0:T(8,128)}, f32[4,64,1024]{2,1,0:T(8,128)}, f32[8,8,1024]{2,1,0:T(8,128)S(1)}, f32[8,8,1024]{2,1,0:T(8,128)}) custom-call(s32[4]{0:T(128)S(1)} %pad_add_fusion.meta, f32[4,64,1024]{2,1,0:T(8,128)S(1)} %copy-done, f32[4,64,1024]{2,1,0:T(8,128)S(1)} %copy-done.2), custom_call_target="tpu_custom_call" | custom-call | bytes 5000000 | tf_op jit(solution)/shard_map/pack/pallas_call | solution.py:437
  5.3 1.3 %collective-permute-start.2 = (f32[8,8,1024]{2,1,0:T(8,128)}, f32[8,8,1024]{2,1,0:T(8,128)}, u32[]{:S(2)}, u32[]{:S(2)}) collective-permute-start(f32[8,8,1024]{2,1,0:T(8,128)} %get-tuple-element.30), channel_id=1, source_target_pairs={{1,0},{2,1},{3,2},{5,4},{6,5},{7,6},{9,8},{10,9},{11,10},{13,12},{... | collective-permute-start | bytes 786440 | tf_op jit(solution)/shard_map/ppermute | solution.py:457
  6.6 5.2 %collective-permute-start.3 = (f32[8,8,1024]{2,1,0:T(8,128)S(1)}, f32[8,8,1024]{2,1,0:T(8,128)}, u32[]{:S(2)}, u32[]{:S(2)}) collective-permute-start(f32[8,8,1024]{2,1,0:T(8,128)S(1)} %get-tuple-element.31), channel_id=1, source_target_pairs={{0,1},{1,2},{2,3},{4,5},{5,6},{6,7},{8,9},{9,10},{10,11},{12,13},{... | collective-permute-start | bytes 786440 | tf_op jit(solution)/shard_map/ppermute | solution.py:457
  11.8 6.3 %collective-permute-start.1 = (f32[4,64,1024]{2,1,0:T(8,128)}, f32[4,64,1024]{2,1,0:T(8,128)}, u32[]{:S(2)}, u32[]{:S(2)}) collective-permute-start(f32[4,64,1024]{2,1,0:T(8,128)} %get-tuple-element.29), channel_id=1, source_target_pairs={{4,8},{8,4},{12,16},{16,12},{20,24},{24,20},{28,32},{32,28},{36,40... | collective-permute-start | bytes 3145736 | tf_op jit(solution)/shard_map/ppermute | solution.py:456
  20.7 2.0 %voltages.1 = (f32[128,128]{1,0:T(8,128)S(1)}, f32[1,128]{1,0:T(1,128)S(1)}) custom-call(f32[4,64,1024]{2,1,0:T(8,128)S(1)} %copy-done.1, s32[128,128]{1,0:T(8,128)S(1)} %bitcast.11, s32[128,128]{1,0:T(8,128)S(1)} %bitcast.13, s32[1,128]{1,0:T(1,128)S(1)} %reshape_reshape.3.cnt_ref), custom_call_target="tpu_custom_call" | custom-call | flops 4000000 | bytes 1300000 | tf_op jit(solution)/shard_map/voltages/pallas_call | solution.py:422
  23.8 3.7 %collective-permute-done.6 = f32[1,128]{1,0:T(1,128)S(1)} collective-permute-done((f32[1,128]{1,0:T(1,128)S(1)}, f32[1,128]{1,0:T(1,128)S(1)}, u32[]{:S(2)}, u32[]{:S(2)}) %collective-permute-start.6) | collective-permute-done | bytes 544 | tf_op jit(solution)/shard_map/ppermute | solution.py:433
  27.5 2.1 %collective-permute-start.7 = (f32[1,128]{1,0:T(1,128)S(1)}, f32[1,128]{1,0:T(1,128)S(1)}, u32[]{:S(2)}, u32[]{:S(2)}) collective-permute-start(f32[1,128]{1,0:T(1,128)S(1)} %get-tuple-element.43), channel_id=1, source_target_pairs={{0,2},{1,3},{2,0},{3,1},{4,6},{5,7},{6,4},{7,5},{8,10},{9,11},{10,... | collective-permute-start | bytes 1544 | tf_op jit(solution)/shard_map/ppermute | solution.py:433
  29.6 3.0 %collective-permute-done.7 = f32[1,128]{1,0:T(1,128)S(1)} collective-permute-done((f32[1,128]{1,0:T(1,128)S(1)}, f32[1,128]{1,0:T(1,128)S(1)}, u32[]{:S(2)}, u32[]{:S(2)}) %collective-permute-start.7) | collective-permute-done | bytes 544 | tf_op jit(solution)/shard_map/ppermute | solution.py:433
  33.5 1.7 %copy-done.25 = f32[40,16384]{1,0:T(8,128)S(1)} copy-done((f32[40,16384]{1,0:T(8,128)S(1)}, f32[40,16384]{1,0:T(8,128)}, u32[]{:S(2)}) %copy-start.25) | copy-done | bytes 2621464
  35.2 4.3 %ionic.1 = (f32[40,16384]{1,0:T(8,128)}, f32[128,128]{1,0:T(8,128)S(1)}, f32[128,128]{1,0:T(8,128)S(1)}) custom-call(s32[64]{0:T(128)S(1)} %copy-done.24, s32[64]{0:T(128)S(1)} %copy-done.26, f32[128,128]{1,0:T(8,128)S(1)} %get-tuple-element.32.volt_ref, f32[40,16384]{1,0:T(8,128)S(1)} %copy-done.25, f32[4,40,128]{2,1,0:T(8,128)S(1)} %broadcast_in_dim.38.rate_ref, ...), custom_call_target="tpu_custom_call" | custom-call | flops 16000000 | bytes 5300000 | tf_op jit(solution)/shard_map/ionic/pallas_call | solution.py:471
  40.8 2.1 %collective-permute-start.10 = (f32[4,128]{1,0:T(4,128)S(1)}, f32[4,128]{1,0:T(4,128)S(1)}, u32[]{:S(2)}, u32[]{:S(2)}) collective-permute-start(f32[4,128]{1,0:T(4,128)S(1)} %pad_maximum_fusion.3), channel_id=1, source_target_pairs={{4,8},{8,4},{12,16},{16,12},{20,24},{24,20},{28,32},{32,28},{36,40... | collective-permute-start | bytes 6152 | tf_op jit(solution)/shard_map/ppermute | solution.py:508
  45.3 2.7 %collective-permute-done.10 = f32[4,128]{1,0:T(4,128)S(1)} collective-permute-done((f32[4,128]{1,0:T(4,128)S(1)}, f32[4,128]{1,0:T(4,128)S(1)}, u32[]{:S(2)}, u32[]{:S(2)}) %collective-permute-start.10) | collective-permute-done | bytes 2080 | tf_op jit(solution)/shard_map/ppermute | solution.py:508
  48.5 3.1 %collective-permute-start.5 = (f32[2,8,1024]{2,1,0:T(8,128)}, f32[2,8,1024]{2,1,0:T(8,128)S(1)}, u32[]{:S(2)}, u32[]{:S(2)}) collective-permute-start(f32[2,8,1024]{2,1,0:T(8,128)} %get-tuple-element.53), channel_id=1, source_target_pairs={{4,8},{8,4},{12,16},{16,12},{20,24},{24,20},{28,32},{32,28},{36,40... | collective-permute-start | bytes 196616 | tf_op jit(solution)/shard_map/ppermute | solution.py:454
  55.0 3.3 %scatter.1 = (f32[4,64,1024]{2,1,0:T(8,128)S(1)}, f32[4,64,1024]{2,1,0:T(8,128)S(1)}) custom-call(f32[128,128]{1,0:T(8,128)S(1)} %copy-done.13, f32[128,128]{1,0:T(8,128)S(1)} %copy-done.16, s32[128,128]{1,0:T(8,128)S(1)} %bitcast.12, s32[128,128]{1,0:T(8,128)S(1)} %bitcast.14), custom_call_target="tpu_custom_call" | custom-call | flops 800000000 | bytes 2300000 | tf_op jit(solution)/shard_map/scatter/pallas_call | solution.py:485
  60.9 1.4 %broadcast_in_dim.41 = s32[8,64,2]{0,2,1:T(2,128)} broadcast(s32[8,64]{0,1:T(8,128)} %copy.16), dimensions={0,1} | broadcast | bytes 6144 | tf_op jit(solution)/shard_map/broadcast_in_dim | solution.py:509
  63.9 1.4 %broadcast_in_dim.42 = f32[8,64,2]{0,2,1:T(2,128)} broadcast(f32[8,64]{0,1:T(8,128)} %copy.17), dimensions={0,1} | broadcast | bytes 6144 | tf_op jit(solution)/shard_map/broadcast_in_dim | solution.py:510
  66.2 1.4 %concatenate.8.table_ref = f32[12,128]{1,0:T(8,128)S(1)} concatenate(f32[1,128]{1,0:T(1,128)} %copy-done.23, f32[1,128]{1,0:T(1,128)} %copy-done.35, f32[1,128]{1,0:T(1,128)} %copy-done.36, f32[1,128]{1,0:T(1,128)} %copy-done.37, f32[4,128]{1,0:T(4,128)} %collective-permute-done.9, f32[4,128]{1,0:T(4,128)} %copy-done.34), dimensions={0} | concatenate | bytes 12288 | tf_op jit(solution)/shard_map/concatenate | solution.py:508
  70.8 5.8 %operator.1 = (f32[9,72,1024]{2,1,0:T(8,128)S(1)}, f32[8,72,1024]{2,1,0:T(8,128)S(1)}, f32[8,72,1024]{2,1,0:T(8,128)S(1)}, f32[8,72,1024]{2,1,0:T(8,128)S(1)}, f...) custom-call(s32[4]{0:T(128)S(1)} %copy-done.19, ...), custom_call_target="tpu_custom_call" | custom-call | flops 16000000 | bytes 6000000 | tf_op jit(solution)/shard_map/operator/pallas_call | solution.py:496
  76.7 1.8 %gap.1 = (f32[4,64,1024]{2,1,0:T(8,128)S(1)}, f32[3,64,1024]{2,1,0:T(8,128)S(1)}, f32[3,64,1024]{2,1,0:T(8,128)S(1)}, f32[4,8,1024]{2,1,0:T(8,128)S(1)}, f32[4,8,1024]{2,1,0:T(8,128)S(1)}, /*index=5*/f32[128,128]{1,0:T(8,128)}) custom-call(s32[4]{0:T(128)S(1)} %copy-done.19, f32[12,128]{1,0:T(8,128)S(1)} %concatenate.8.table_ref, ...), custom_call_target="tpu_custom_call" | custom-call | flops 1000000 | bytes 5000000 | tf_op jit(solution)/shard_map/gap/pallas_call | solution.py:511
  79.8 4.6 %collective-permute-start.14 = (f32[4,8,1024]{2,1,0:T(8,128)S(1)}, f32[4,8,1024]{2,1,0:T(8,128)S(1)}, u32[]{:S(2)}, u32[]{:S(2)}) collective-permute-start(f32[4,8,1024]{2,1,0:T(8,128)S(1)} %get-tuple-element.50), channel_id=1, source_target_pairs={{0,1},{1,2},{2,3},{4,5},{5,6},{6,7},{8,9},{9,10},{10,11},{12,13},{... | collective-permute-start | bytes 393224 | tf_op jit(solution)/shard_map/ppermute | solution.py:524
  84.5 4.0 %collective-permute-start.12 = (f32[3,64,1024]{2,1,0:T(8,128)S(1)}, f32[3,64,1024]{2,1,0:T(8,128)S(1)}, u32[]{:S(2)}, u32[]{:S(2)}) collective-permute-start(f32[3,64,1024]{2,1,0:T(8,128)S(1)} %get-tuple-element.48), channel_id=1, source_target_pairs={{4,8},{8,4},{12,16},{16,12},{20,24},{24,20},{28,32},{32,28},{36,40... | collective-permute-start | bytes 2359304 | tf_op jit(solution)/shard_map/ppermute | solution.py:523
  88.8 3.7 %collective-permute-start.16 = (f32[2,8,1024]{2,1,0:T(8,128)S(1)}, f32[2,8,1024]{2,1,0:T(8,128)S(1)}, u32[]{:S(2)}, u32[]{:S(2)}) collective-permute-start(f32[2,8,1024]{2,1,0:T(8,128)S(1)} %get-tuple-element.57), channel_id=1, source_target_pairs={{4,8},{8,4},{12,16},{16,12},{20,24},{24,20},{28,32},{32,28},{36,40... | collective-permute-start | bytes 196616 | tf_op jit(solution)/shard_map/ppermute | solution.py:454
  92.5 8.2 %collective-permute-done.16.ucb_hbm = f32[2,8,1024]{2,1,0:T(8,128)S(1)} collective-permute-done((f32[2,8,1024]{2,1,0:T(8,128)S(1)}, f32[2,8,1024]{2,1,0:T(8,128)S(1)}, u32[]{:S(2)}, u32[]{:S(2)}) %collective-permute-start.16) | collective-permute-done | bytes 65568 | tf_op jit(solution)/shard_map/ppermute | solution.py:454
  100.6 7.1 %sweeps.1 = f32[4,64,1024]{2,1,0:T(8,128)} custom-call(s32[4]{0:T(128)S(1)} %copy-done.20, f32[4,64,1024]{2,1,0:T(8,128)S(1)} %copy-done.1, f32[9,72,1024]{2,1,0:T(8,128)S(1)} %get-tuple-element.37.fx, f32[8,72,1024]{2,1,0:T(8,128)S(1)} %get-tuple-element.38.fym, f32[8,72,1024]{2,1,0:T(8,128)S(1)} %get-tuple-element.39.fyp, ...), custom_call_target="tpu_custom_call" | custom-call | flops 50000000 | bytes 10000000 | tf_op jit(solution)/shard_map/sweeps/pallas_call | solution.py:528
  (123 shorter events, 24.4 us)
Async XLA Ops:
  0.6 32.8 %copy-start.24 = (s32[64]{0:T(128)S(1)}, s32[64]{0:T(128)}, u32[]{:S(2)}) copy-start(s32[64]{0:T(128)} %cnt.1) | copy-start | bytes 772
  0.6 23.1 %copy-start.38 = (f32[2,40]{1,0:T(2,128)S(1)}, f32[2,40]{1,0:T(2,128)}, u32[]{:S(2)}) copy-start(f32[2,40]{1,0:T(2,128)} %param.16) | copy-start | bytes 964
  0.7 23.1 %copy-start.27 = (f32[3,40]{1,0:T(4,128)S(1)}, f32[3,40]{1,0:T(4,128)}, u32[]{:S(2)}) copy-start(f32[3,40]{1,0:T(4,128)} %param.18) | copy-start | bytes 1444
  0.7 23.1 %copy-start.40 = (f32[40]{0:T(128)S(1)}, f32[40]{0:T(128)}, u32[]{:S(2)}) copy-start(f32[40]{0:T(128)} %param.19) | copy-start | bytes 484
  0.7 32.8 %copy-start.26 = (s32[64]{0:T(128)S(1)}, s32[64]{0:T(128)}, u32[]{:S(2)}) copy-start(s32[64]{0:T(128)} %typ.1) | copy-start | bytes 772
  5.3 37.6 %collective-permute-start.2 = (f32[8,8,1024]{2,1,0:T(8,128)}, f32[8,8,1024]{2,1,0:T(8,128)}, u32[]{:S(2)}, u32[]{:S(2)}) collective-permute-start(f32[8,8,1024]{2,1,0:T(8,128)} %get-tuple-element.30), channel_id=1, source_target_pairs={{1,0},{2,1},{3,2},{5,4},{6,5},{7,6},{9,8},{10,9},{11,10},{13,12},{... | collective-permute-start | bytes 786440 | tf_op jit(solution)/shard_map/ppermute | solution.py:457
  6.6 36.4 %collective-permute-start.3 = (f32[8,8,1024]{2,1,0:T(8,128)S(1)}, f32[8,8,1024]{2,1,0:T(8,128)}, u32[]{:S(2)}, u32[]{:S(2)}) collective-permute-start(f32[8,8,1024]{2,1,0:T(8,128)S(1)} %get-tuple-element.31), channel_id=1, source_target_pairs={{0,1},{1,2},{2,3},{4,5},{5,6},{6,7},{8,9},{9,10},{10,11},{12,13},{... | collective-permute-start | bytes 786440 | tf_op jit(solution)/shard_map/ppermute | solution.py:457
  11.8 55.8 %collective-permute-start = (f32[4,64,1024]{2,1,0:T(8,128)}, f32[4,64,1024]{2,1,0:T(8,128)S(1)}, u32[]{:S(2)}, u32[]{:S(2)}) collective-permute-start(f32[4,64,1024]{2,1,0:T(8,128)} %get-tuple-element.28), channel_id=1, source_target_pairs={{0,4},{4,0},{8,12},{12,8},{16,20},{20,16},{24,28},{28,24},{32,36},... | collective-permute-start | bytes 3145736 | tf_op jit(solution)/shard_map/ppermute | solution.py:456
  11.8 55.8 %collective-permute-start.1 = (f32[4,64,1024]{2,1,0:T(8,128)}, f32[4,64,1024]{2,1,0:T(8,128)}, u32[]{:S(2)}, u32[]{:S(2)}) collective-permute-start(f32[4,64,1024]{2,1,0:T(8,128)} %get-tuple-element.29), channel_id=1, source_target_pairs={{4,8},{8,4},{12,16},{16,12},{20,24},{24,20},{28,32},{32,28},{36,40... | collective-permute-start | bytes 3145736 | tf_op jit(solution)/shard_map/ppermute | solution.py:456
  22.8 4.8 %collective-permute-start.6 = (f32[1,128]{1,0:T(1,128)S(1)}, f32[1,128]{1,0:T(1,128)S(1)}, u32[]{:S(2)}, u32[]{:S(2)}) collective-permute-start(f32[1,128]{1,0:T(1,128)S(1)} %get-tuple-element.43), channel_id=1, source_target_pairs={{0,1},{1,2},{2,3},{3,0},{4,5},{5,6},{6,7},{7,4},{8,9},{9,10},{10,1... | collective-permute-start | bytes 1544 | tf_op jit(solution)/shard_map/ppermute | solution.py:433
  27.5 5.0 %collective-permute-start.7 = (f32[1,128]{1,0:T(1,128)S(1)}, f32[1,128]{1,0:T(1,128)S(1)}, u32[]{:S(2)}, u32[]{:S(2)}) collective-permute-start(f32[1,128]{1,0:T(1,128)S(1)} %get-tuple-element.43), channel_id=1, source_target_pairs={{0,2},{1,3},{2,0},{3,1},{4,6},{5,7},{6,4},{7,5},{8,10},{9,11},{10,... | collective-permute-start | bytes 1544 | tf_op jit(solution)/shard_map/ppermute | solution.py:433
  32.6 8.2 %collective-permute-start.8 = (f32[1,128]{1,0:T(1,128)S(1)}, f32[1,128]{1,0:T(1,128)S(1)}, u32[]{:S(2)}, u32[]{:S(2)}) collective-permute-start(f32[1,128]{1,0:T(1,128)S(1)} %get-tuple-element.43), channel_id=1, source_target_pairs={{0,3},{1,0},{2,1},{3,2},{4,7},{5,4},{6,5},{7,6},{8,11},{9,8},{10,9... | collective-permute-start | bytes 1544 | tf_op jit(solution)/shard_map/ppermute | solution.py:433
  40.7 27.0 %copy-start.3 = (f32[4,64,1024]{2,1,0:T(8,128)S(1)}, f32[4,64,1024]{2,1,0:T(8,128)}, u32[]{:S(2)}) copy-start(f32[4,64,1024]{2,1,0:T(8,128)} %c_hbm.1) | copy-start | bytes 3145732
  40.8 7.1 %collective-permute-start.10 = (f32[4,128]{1,0:T(4,128)S(1)}, f32[4,128]{1,0:T(4,128)S(1)}, u32[]{:S(2)}, u32[]{:S(2)}) collective-permute-start(f32[4,128]{1,0:T(4,128)S(1)} %pad_maximum_fusion.3), channel_id=1, source_target_pairs={{4,8},{8,4},{12,16},{16,12},{20,24},{24,20},{28,32},{32,28},{36,40... | collective-permute-start | bytes 6152 | tf_op jit(solution)/shard_map/ppermute | solution.py:508
  42.9 23.4 %collective-permute-start.9 = (f32[4,128]{1,0:T(4,128)S(1)}, f32[4,128]{1,0:T(4,128)}, u32[]{:S(2)}, u32[]{:S(2)}) collective-permute-start(f32[4,128]{1,0:T(4,128)S(1)} %pad_maximum_fusion.3), channel_id=1, source_target_pairs={{0,4},{4,0},{8,12},{12,8},{16,20},{20,16},{24,28},{28,24},{32,36},... | collective-permute-start | bytes 6152 | tf_op jit(solution)/shard_map/ppermute | solution.py:508
  44.8 22.9 %collective-permute-start.4 = (f32[2,8,1024]{2,1,0:T(8,128)}, f32[2,8,1024]{2,1,0:T(8,128)S(1)}, u32[]{:S(2)}, u32[]{:S(2)}) collective-permute-start(f32[2,8,1024]{2,1,0:T(8,128)} %get-tuple-element.54), channel_id=1, source_target_pairs={{0,4},{4,0},{8,12},{12,8},{16,20},{20,16},{24,28},{28,24},{32,36},... | collective-permute-start | bytes 196616 | tf_op jit(solution)/shard_map/ppermute | solution.py:454
  48.5 19.1 %collective-permute-start.5 = (f32[2,8,1024]{2,1,0:T(8,128)}, f32[2,8,1024]{2,1,0:T(8,128)S(1)}, u32[]{:S(2)}, u32[]{:S(2)}) collective-permute-start(f32[2,8,1024]{2,1,0:T(8,128)} %get-tuple-element.53), channel_id=1, source_target_pairs={{4,8},{8,4},{12,16},{16,12},{20,24},{24,20},{28,32},{32,28},{36,40... | collective-permute-start | bytes 196616 | tf_op jit(solution)/shard_map/ppermute | solution.py:454
  76.7 24.0 %copy-start.20 = (s32[4]{0:T(128)S(1)}, s32[4]{0:T(128)}, u32[]{:S(2)}) copy-start(s32[4]{0:T(128)} %copy-done.18) | copy-start | bytes 52
  78.6 10.0 %collective-permute-start.13 = (f32[4,8,1024]{2,1,0:T(8,128)S(1)}, f32[4,8,1024]{2,1,0:T(8,128)S(1)}, u32[]{:S(2)}, u32[]{:S(2)}) collective-permute-start(f32[4,8,1024]{2,1,0:T(8,128)S(1)} %get-tuple-element.49), channel_id=1, source_target_pairs={{1,0},{2,1},{3,2},{5,4},{6,5},{7,6},{9,8},{10,9},{11,10},{13,12},{... | collective-permute-start | bytes 393224 | tf_op jit(solution)/shard_map/ppermute | solution.py:524
  79.8 8.7 %collective-permute-start.14 = (f32[4,8,1024]{2,1,0:T(8,128)S(1)}, f32[4,8,1024]{2,1,0:T(8,128)S(1)}, u32[]{:S(2)}, u32[]{:S(2)}) collective-permute-start(f32[4,8,1024]{2,1,0:T(8,128)S(1)} %get-tuple-element.50), channel_id=1, source_target_pairs={{0,1},{1,2},{2,3},{4,5},{5,6},{6,7},{8,9},{9,10},{10,11},{12,13},{... | collective-permute-start | bytes 393224 | tf_op jit(solution)/shard_map/ppermute | solution.py:524
  84.4 16.2 %collective-permute-start.11 = (f32[3,64,1024]{2,1,0:T(8,128)S(1)}, f32[3,64,1024]{2,1,0:T(8,128)S(1)}, u32[]{:S(2)}, u32[]{:S(2)}) collective-permute-start(f32[3,64,1024]{2,1,0:T(8,128)S(1)} %get-tuple-element.47), channel_id=1, source_target_pairs={{0,4},{4,0},{8,12},{12,8},{16,20},{20,16},{24,28},{28,24},{32,36},... | collective-permute-start | bytes 2359304 | tf_op jit(solution)/shard_map/ppermute | solution.py:523
  84.5 16.1 %collective-permute-start.12 = (f32[3,64,1024]{2,1,0:T(8,128)S(1)}, f32[3,64,1024]{2,1,0:T(8,128)S(1)}, u32[]{:S(2)}, u32[]{:S(2)}) collective-permute-start(f32[3,64,1024]{2,1,0:T(8,128)S(1)} %get-tuple-element.48), channel_id=1, source_target_pairs={{4,8},{8,4},{12,16},{16,12},{20,24},{24,20},{28,32},{32,28},{36,40... | collective-permute-start | bytes 2359304 | tf_op jit(solution)/shard_map/ppermute | solution.py:523
  88.7 3.8 %collective-permute-start.15 = (f32[2,8,1024]{2,1,0:T(8,128)S(1)}, f32[2,8,1024]{2,1,0:T(8,128)S(1)}, u32[]{:S(2)}, u32[]{:S(2)}) collective-permute-start(f32[2,8,1024]{2,1,0:T(8,128)S(1)} %get-tuple-element.58), channel_id=1, source_target_pairs={{0,4},{4,0},{8,12},{12,8},{16,20},{20,16},{24,28},{28,24},{32,36},... | collective-permute-start | bytes 196616 | tf_op jit(solution)/shard_map/ppermute | solution.py:454
  88.8 11.8 %collective-permute-start.16 = (f32[2,8,1024]{2,1,0:T(8,128)S(1)}, f32[2,8,1024]{2,1,0:T(8,128)S(1)}, u32[]{:S(2)}, u32[]{:S(2)}) collective-permute-start(f32[2,8,1024]{2,1,0:T(8,128)S(1)} %get-tuple-element.57), channel_id=1, source_target_pairs={{4,8},{8,4},{12,16},{16,12},{20,24},{24,20},{28,32},{32,28},{36,40... | collective-permute-start | bytes 196616 | tf_op jit(solution)/shard_map/ppermute | solution.py:454
  (34 other events, 243.2 us)

commit v3 on v2

v3 whole, which is shorter than its diff:
```python
import functools
import math

import jax
import jax.numpy as jnp
from jax import lax
from jax.experimental import pallas as pl
from jax.experimental.pallas import tpu as pltpu
from jax.sharding import PartitionSpec as P

LOG2E = math.log2(math.e)
SWEEPS = 4
F32 = jnp.float32
BF16 = jnp.bfloat16
ANY = pl.BlockSpec(memory_space=pl.ANY)
HBM = pl.BlockSpec(memory_space=pltpu.HBM)
VM = pl.BlockSpec(memory_space=pltpu.VMEM)
SM = pl.BlockSpec(memory_space=pltpu.SMEM)


def grant(mib):
    return pltpu.CompilerParams(vmem_limit_bytes=mib * 1024 * 1024)


def sweep_factors():
    theta, delta = 1.0, 0.8
    sigma = theta / delta
    rho = 1.0 / sigma
    factors = []
    for _ in range(SWEEPS - 1):
        rho_next = 1.0 / (2.0 * sigma - rho)
        factors.append((rho_next * rho, 2.0 * rho_next / delta))
        rho = rho_next
    return factors


def iota(shape, dim):
    return lax.broadcasted_iota(jnp.int32, shape, dim)


def plane_of(parity, j):
    return j + parity * (3 - 2 * j)


def pair_sum(row):
    even = (iota((1, 128), 1) & 1) == 0
    return row + jnp.where(even, pltpu.roll(row, 127, 1), pltpu.roll(row, 1, 1))


def gather_kernel(meta, cnt, p_hbm, c_hbm, in_ref, ex_ref, part_ref, cond_ref,
                  volt_ref, cell_ref, act_ref, part_out, cond_out, a_hbm, b_hbm, up_hbm, down_hbm,
                  p_ref, c_ref, note, sem):
    par = meta[0]
    loads = begin([(p_hbm.at[x], p_ref.at[x]) for x in range(4)] + [(c_hbm.at[x], c_ref.at[x]) for x in range(4)], sem, 0)
    twice = iota((8, 128), 1) // 2
    for src, dst in ((part_ref, part_out), (cond_ref, cond_out)):
        wide = jnp.concatenate([src[...].astype(F32), jnp.zeros((64, 120), F32)], axis=1)
        turned = jnp.transpose(jnp.concatenate([wide, wide], axis=0))[0:8]
        dst[...] = jnp.take_along_axis(turned, twice, axis=1, mode="promise_in_bounds").astype(dst.dtype)
    for load in loads:
        load.wait()
    copies = []
    for i in range(3):
        copies.append((c_ref.at[plane_of(par, i)], b_hbm.at[i]))
        copies.append((c_ref.at[plane_of(par, 3 - i)], a_hbm.at[i]))
    copies.append((p_ref.at[plane_of(par, 0)], b_hbm.at[3]))
    copies.append((p_ref.at[plane_of(par, 3)], a_hbm.at[3]))
    for k, src in enumerate((c_ref, p_ref)):
        copies.append((src.at[:, 56:64], up_hbm.at[4 * k : 4 * k + 4]))
        copies.append((src.at[:, 0:8], down_hbm.at[4 * k : 4 * k + 4]))
    sends = begin(copies, sem, 8)
    sub = iota((8, 128), 0)
    low = sub < 4
    lane_row = iota((1, 128), 1)

    def body(kk, carry):
        x = kk // 4
        blocks = [r[pl.ds(pl.multiple_of(8 * kk, 8), 8), :] & 4095 for r in (in_ref, ex_ref)]
        for q in range(2):
            row = pl.multiple_of((2 * (kk % 4) + q) * 8, 8)
            tiles = [p_ref[x, pl.ds(row, 8), 128 * z : 128 * z + 128] for z in range(8)]
            for h in range(2):
                picked = []
                for block in blocks:
                    a = jnp.broadcast_to(block[4 * q + h : 4 * q + h + 1], (8, 128))
                    b = jnp.broadcast_to(block[4 * q + 2 + h : 4 * q + 3 + h], (8, 128))
                    o = jnp.where(low, a, b)
                    lane = o & 127
                    z_of = (o >> 7) & 7
                    got = jnp.take_along_axis(tiles[0], lane, axis=1, mode="promise_in_bounds")
                    for z in range(1, 8):
                        new = jnp.take_along_axis(tiles[z], lane, axis=1, mode="promise_in_bounds")
                        got = jnp.where(z_of == z, new, got)
                    picked.append(jnp.where((o >> 10) == (sub & 3), got, 0.0))
                d = picked[0] - picked[1]
                d = d + pltpu.roll(d, 7, 0)
                d = d + pltpu.roll(d, 6, 0)
                for i in range(2):
                    at = pl.ds(8 * kk + 4 * q + 2 * i + h, 1)
                    volt_ref[at, :] = d[4 * i : 4 * i + 1]
                    used = lane_row + 128 * h < cnt[4 * kk + 2 * q + i]
                    act_ref[at, :] = jnp.where(used, 1.0, 0.0)
        return carry

    lax.fori_loop(0, 16, body, 0, unroll=4)
    act = act_ref[...]
    total = jnp.sum(jnp.transpose(volt_ref[...] * act), axis=0, keepdims=True)
    count = jnp.sum(jnp.transpose(act), axis=0, keepdims=True)
    cells = pair_sum(total) / jnp.maximum(pair_sum(count), 1.0)
    cell_ref[...] = cells
    note[...] = jnp.zeros((8, 1024), F32)
    note[0:1, 0:128] = cells
    sends += begin([(note, up_hbm.at[8]), (note, down_hbm.at[8])], sem, 20)
    for send in sends:
        send.wait()


def begin(copies, sem, start):
    made = [pltpu.make_async_copy(s, d, sem.at[start + n]) for n, (s, d) in enumerate(copies)]
    for m in made:
        m.start()
    return made


def ionic_kernel(cnt, typ, volt_ref, st_ref, rate_ref, out_ref, ion_ref):
    step = pl.program_id(0)
    cells = volt_ref.shape[0] // 2
    lane = iota((8, 128), 1)

    def body(group, carry):
        rows8 = pl.ds(pl.multiple_of(8 * group, 8), 8)
        volts = volt_ref[rows8, :]
        counts, types, v, active, cols = [], [], [], [], []
        for q in range(4):
            counts.append(cnt[step * cells + 4 * group + q])
            types.append(typ[step * cells + 4 * group + q])
        for r in range(8):
            v.append(jnp.broadcast_to(volts[r : r + 1], (8, 128)))
            active.append(lane + (r % 2) * 128 < counts[r // 2])
            cols.append(pl.ds(pl.multiple_of(1024 * group + 128 * r, 128), 128))
        w1, w2 = [None] * 8, [None] * 8
        for k in range(5):
            rows = slice(8 * k, 8 * k + 8)
            rate = [rate_ref[i, rows] for i in range(4)]
            for q in range(4):
                g, gr = rate_ref[4 + types[q], rows], rate_ref[7 + types[q], rows]
                for r in (2 * q, 2 * q + 1):
                    st = st_ref[rows, cols[r]]
                    opening = jnp.exp2(rate[0] * v[r] + rate[1])
                    closing = jnp.exp2(rate[2] * v[r] + rate[3])
                    total = opening + closing
                    rec = pl.reciprocal(total, approx=True)
                    rec = rec * (2.0 - total * rec)
                    steady = opening * rec
                    fresh = steady + (st - steady) * jnp.exp2(total * (-0.5 * LOG2E))
                    out_ref[rows, cols[r]] = jnp.where(active[r], fresh, st)
                    w1[r] = g * fresh if k == 0 else w1[r] + g * fresh
                    w2[r] = gr * fresh if k == 0 else w2[r] + gr * fresh
        act = jnp.concatenate([jnp.where(a, 1.0, 0.0)[0:1] for a in active], axis=0)
        ion = [jnp.sum(w1[r] * v[r] - w2[r], axis=0, keepdims=True) for r in range(8)]
        val = jnp.concatenate(ion, axis=0) * act
        ion_ref[rows8, :] = val

        return carry

    lax.fori_loop(0, cells // 4, body, 0)


def scatter_kernel(ion_ref, act_ref, in_ref, ex_ref, after, s_ref, n_ref):
    row_iota = iota((32, 512), 0)
    lane_iota = iota((128, 512), 0)
    low = iota((8, 128), 0) < 4
    odd_row = (iota((8, 128), 0) & 2) // 2

    def body(kk, carry):
        rows8 = pl.ds(pl.multiple_of(8 * kk, 8), 8)
        x = kk // 4
        val = ion_ref[rows8, :]
        act = act_ref[rows8, :]
        hi = val.astype(BF16).astype(F32)
        lo = val - hi
        mids, lanes = [], []
        for ref in (in_ref, ex_ref):
            o = ref[rows8, :] & 4095
            mids.append((((o >> 7) & 7) ^ odd_row) * 4 + (o >> 10))
            lanes.append(o & 127)

        def line(a, b, s):
            r = 2 * s
            return jnp.concatenate([a[r : r + 1], a[r + 1 : r + 2], b[r : r + 1], b[r + 1 : r + 2]], axis=1)

        for q in range(2):
            results = []
            for s in (2 * q, 2 * q + 1):
                hit = line(mids[0], mids[1], s) == row_iota
                left = jnp.concatenate(
                    [jnp.where(hit, line(piece, -piece, s), 0.0).astype(BF16) for piece in (hi, lo, act)], axis=0
                )
                right = jnp.where(line(lanes[0], lanes[1], s) == lane_iota, 1.0, 0.0).astype(BF16)
                out = lax.dot_general(left, right, (((1,), (1,)), ((), ())), preferred_element_type=F32)
                results.append((out[0:32] + out[32:64], out[64:96]))
            row = pl.ds(pl.multiple_of((2 * (kk % 4) + q) * 8, 8), 8)
            for dst, e, o in ((s_ref, results[0][0], results[1][0]), (n_ref, results[0][1], results[1][1])):
                for j in range(4):
                    ej, oj = e[8 * j : 8 * j + 8], o[8 * j : 8 * j + 8]
                    dst[x, row, 256 * j : 256 * j + 128] = jnp.where(low, ej, oj)
                    dst[x, row, 256 * j + 128 : 256 * j + 256] = pltpu.roll(jnp.where(low, oj, ej), 4, 0)
        return carry

    lax.fori_loop(0, 16, body, 0, unroll=4)


def edge_rows(meta, below, above):
    sub = iota((8, 1024), 0)
    bottom = (sub < 3) & (meta[2] != 3)
    top = (sub >= 5) & (meta[2] != 0)
    return jnp.where(bottom, above, jnp.where(top, below, 0.0))


def early_edge_kernel(meta, below_ref, above_ref, far_ref, cell_ref, after, y_ref, table_ref, a_ref, b_ref):
    par = meta[0]
    for x in range(8):
        y_ref[x] = edge_rows(meta, below_ref[x], above_ref[x])
    table = jnp.concatenate(
        [cell_ref[...], below_ref[8, 0:1, 0:128], far_ref[...], above_ref[8, 0:1, 0:128],
         jnp.zeros((4, 128), F32)], axis=0)
    table_ref[...] = table
    for i in range(2):
        a_ref[i] = y_ref[plane_of(par, 3 - i)]
        b_ref[i] = y_ref[plane_of(par, i)]
    for ref in (a_ref, b_ref):
        ref[2] = jnp.zeros((8, 1024), F32)
        ref[2, :, 0:128] = table


def late_edge_kernel(meta, below_ref, above_ref, ua_in, ub_in, y_ref, ua_ref, ub_ref, sem):
    par = meta[0]
    for x in range(4):
        y_ref[x] = edge_rows(meta, below_ref[x], above_ref[x])
    copies = []
    for i in range(3):
        copies.append((y_ref.at[plane_of(par, 3 - i)], ua_ref.at[i, 64:72]))
        copies.append((y_ref.at[plane_of(par, i)], ub_ref.at[i, 64:72]))
    for m in begin(copies, sem, 0):
        m.wait()


def tile(ref, e, t):
    return ref[e, 8 * t : 8 * t + 8, :]


class Around:
    def __init__(self, ref, e):
        self.ref, self.e = ref, e
        self.sub = iota((8, 1024), 0)

    def at(self, t):
        ref, e = self.ref, self.e
        c = tile(ref, e, t)
        before, after = tile(ref, e, (t + 8) % 9), tile(ref, e, (t + 1) % 9)
        ym = jnp.where(self.sub == 0, pltpu.roll(before, 1, 0), pltpu.roll(c, 1, 0))
        yp = jnp.where(self.sub == 7, pltpu.roll(after, 7, 0), pltpu.roll(c, 7, 0))
        zm, zp = pltpu.roll(c, 1, 1), pltpu.roll(c, 1023, 1)
        return c, tile(ref, e - 1, t), tile(ref, e + 1, t), ym, yp, zm, zp


def couplings(around, t):
    lane = iota((8, 1024), 1)
    c, xm, xp, ym, yp, zm, zp = around.at(t)
    first, last = lane == 0, lane == 1023
    zm = jnp.where(first, 0.0, zm)
    zp = jnp.where(last, 0.0, zp)
    fs = [0.25 * (c + other) for other in (xm, xp, ym, yp, zm, zp)]
    diagonal = 1.0 + (((fs[0] + fs[1]) + (fs[2] + fs[3])) + (fs[4] + fs[5]))
    fs[4] = jnp.where(first, 0.0, fs[4])
    fs[5] = jnp.where(last, 0.0, fs[5])
    return fs, diagonal


def weighted(fs, views):
    t = [f * v for f, v in zip(fs, views)]
    return ((t[0] + t[1]) + (t[2] + t[3])) + (t[4] + t[5])


def first_kernel(meta, p_hbm, c_hbm, a_hbm, b_hbm, y_hbm, table_ref, ta_ref, tb_ref, part_ref, cond_ref,
                 ion_ref, act_ref, s_ref, n_ref, u_ref, a_ref, b_ref, up_ref, down_ref, mem_ref,
                 ce, pe, spread, sem):
    par, mine, v = meta[0], meta[2], meta[3]
    copies = []
    for e, hbm, yk in ((ce, c_hbm, 0), (pe, p_hbm, 4)):
        for j in range(4):
            copies.append((hbm.at[plane_of(par, j)], e.at[1 + j, 0:64]))
            copies.append((y_hbm.at[yk + plane_of(par, j)], e.at[1 + j, 64:72]))
    copies.append((a_hbm.at[0], ce.at[5, 0:64]))
    copies.append((b_hbm.at[0], ce.at[0, 0:64]))
    copies.append((a_hbm.at[3], pe.at[5, 0:64]))
    copies.append((b_hbm.at[3], pe.at[0, 0:64]))
    made = begin(copies, sem, 0)

    part = part_ref[...]
    brick = part >> 6
    bx, by = brick >> 2, brick & 3
    side = jnp.where(bx == v, 0, jnp.where(bx == (v ^ 1), 1, 2))
    row = side * 4 + ((mine - by) & 3)
    lane = (part & 63) * 2
    tables = (table_ref[...], ta_ref[2, :, 0:128], tb_ref[2, :, 0:128])
    other = jnp.zeros((8, 128), F32)
    for r in range(12):
        line = jnp.broadcast_to(tables[r // 4][r % 4 : r % 4 + 1], (8, 128))
        other = jnp.where(row == r, jnp.take_along_axis(line, lane, axis=1, mode="promise_in_bounds"), other)
    own = tables[0][0:1]
    current = jnp.sum(cond_ref[...] * (own - other), axis=0, keepdims=True)
    act = act_ref[...]
    count = pair_sum(jnp.sum(jnp.transpose(act), axis=0, keepdims=True))
    g = current / jnp.maximum(count, 1.0)
    g8 = jnp.broadcast_to(g, (8, 128))
    mem_ref[...] = ion_ref[...] + act * jnp.transpose(jnp.broadcast_to(g, (128, 128)))
    for half in range(2):
        at = 64 * half + 2 * (iota((8, 128), 1) // 4)
        wide = jnp.take_along_axis(g8, at, axis=1, mode="promise_in_bounds")[0:1]
        spread[128 * half : 128 * half + 128, :] = jnp.transpose(jnp.broadcast_to(wide, (128, 128)))
    for m in made:
        m.wait()

    def body(j, carry):
        x = plane_of(par, j)
        ca, pa = Around(ce, 1 + j), Around(pe, 1 + j)
        ja, jb = jnp.clip(3 - j, 0, 2), jnp.clip(j, 0, 2)
        for t in range(8):
            rows = slice(8 * t, 8 * t + 8)
            fs, diagonal = couplings(ca, t)
            inv = 1.0 / diagonal
            views = pa.at(t)
            p = views[0]
            gt = jnp.tile(spread[pl.ds(pl.multiple_of(x * 64 + 8 * t, 8), 8), :], (1, 8))
            source = s_ref[x, rows, :] + gt * n_ref[x, rows, :]
            u = (p + weighted(fs, views[1:]) - 0.5 * source) * inv - p
            u_ref[x, rows, :] = u
            if t == 0:
                down_ref[x] = u
            if t == 7:
                up_ref[x] = u

            @pl.when(j < 3)
            def _():
                b_ref[jb, rows, :] = u

            @pl.when(j > 0)
            def _():
                a_ref[ja, rows, :] = u

        return carry

    lax.fori_loop(0, 4, body, 0)


def operator_kernel(meta, c_hbm, a_hbm, b_hbm, y_hbm, ca_hbm, cb_hbm, after,
                    fx, fym, fyp, fzm, fzp, inv, c, sem):
    par, has_b, mine = meta[0], meta[1], meta[2]
    copies = []
    for j in range(4):
        copies.append((c_hbm.at[plane_of(par, j)], c.at[3 + j, 0:64]))
        copies.append((y_hbm.at[plane_of(par, j)], c.at[3 + j, 64:72]))
    for i in range(3):
        copies.append((a_hbm.at[i], c.at[7 + i, 0:64]))
        copies.append((b_hbm.at[i], c.at[2 - i, 0:64]))
    for i in range(2):
        copies.append((ca_hbm.at[i], c.at[7 + i, 64:72]))
        copies.append((cb_hbm.at[i], c.at[2 - i, 64:72]))
    made = begin(copies, sem, 0)
    zero8 = jnp.zeros((8, 1024), F32)
    c[0, 64:72, :] = zero8
    c[9, 64:72, :] = zero8
    sub = iota((8, 1024), 0)
    bottom = (sub < 3) & (mine != 3)
    top = (sub >= 5) & (mine != 0)
    keep = jnp.where(bottom | top, 1.0, 0.0)
    for m in made:
        m.wait()

    def build(e, carry):
        around = Around(c, e)
        inside = jnp.where((e >= 3) | (has_b == 1), 1.0, 0.0)
        for t in range(9):
            rows = slice(8 * t, 8 * t + 8)
            fs, diagonal = couplings(around, t)
            part = inside / diagonal
            inv[e - 1, rows, :] = part * keep if t == 8 else part
            fx[e - 1, rows, :] = fs[0]
            fx[e, rows, :] = fs[1]
            fym[e - 1, rows, :] = fs[2]
            fyp[e - 1, rows, :] = fs[3]
            fzm[e - 1, rows, :] = fs[4]
            fzp[e - 1, rows, :] = fs[5]
        return carry

    lax.fori_loop(1, 9, build, 0)


def sweep_kernel(meta, p_hbm, fx, fym, fyp, fzm, fzp, inv, u_hbm, ua_hbm, ub_hbm, uy_hbm,
                 out_ref, u0, u1, u2, r, p_ref, sem):
    par = meta[0]
    p_copies = begin([(p_hbm.at[x], p_ref.at[x]) for x in range(4)], sem, 14)
    copies = []
    for j in range(4):
        copies.append((u_hbm.at[plane_of(par, j)], u0.at[3 + j, 0:64]))
        copies.append((uy_hbm.at[plane_of(par, j)], u0.at[3 + j, 64:72]))
    for i in range(3):
        copies.append((ua_hbm.at[i], u0.at[7 + i]))
        copies.append((ub_hbm.at[i], u0.at[2 - i]))
    for m in begin(copies, sem, 0):
        m.wait()
    (a1, b1), (a2, b2), (a3, b3) = sweep_factors()

    def coupled(around, e, t):
        fs = [tile(fx, e - 1, t), tile(fx, e, t)] + [tile(f, e - 1, t) for f in (fym, fyp, fzm, fzp)]
        views = around.at(t)
        return views[0], tile(inv, e - 1, t) * weighted(fs, views[1:])

    def first(e, carry):
        around = Around(u0, e)
        for t in range(9):
            rows = slice(8 * t, 8 * t + 8)
            u, res = coupled(around, e, t)
            r[e, rows, :] = res
            u1[e, rows, :] = a1 * u + b1 * res
        return carry

    lax.fori_loop(1, 9, first, 0)

    def second(e, carry):
        around = Around(u1, e)
        for t in range(9):
            rows = slice(8 * t, 8 * t + 8)
            u, more = coupled(around, e, t)
            res = (tile(r, e, t) - u) + more
            r[e, rows, :] = res
            u2[e, rows, :] = a2 * u + b2 * res
        return carry

    lax.fori_loop(2, 8, second, 0)

    def third(j, carry):
        e = 3 + j
        x = plane_of(par, j)
        around = Around(u2, e)
        for t in range(8):
            rows = slice(8 * t, 8 * t + 8)
            u, more = coupled(around, e, t)
            res = (tile(r, e, t) - u) + more
            before = (p_ref[x, rows, :] + tile(u0, e, t)) + (tile(u1, e, t) + u)
            out_ref[x, rows, :] = before + (a3 * u + b3 * res)
        return carry

    for m in p_copies:
        m.wait()
    lax.fori_loop(0, 4, third, 0)


def shape(*dims, kind=F32):
    return jax.ShapeDtypeStruct(dims, kind)


def per_device(potential, conductivity, ion_states, rate_scale, rate_slope, type_cond, reversal,
               facet_counts, intra_voxel, extra_voxel, cell_type, gap_partner, gap_cond):
    v, m = lax.axis_index("vol"), lax.axis_index("mem")
    par = v & 1
    nv = lax.axis_size("vol")
    has_b = jnp.where((v == 0) | (v == nv - 1), 0, 1)
    meta = jnp.stack([par, has_b, m, v]).astype(jnp.int32)
    swap_a = [pair for i in range(0, nv, 2) for pair in ((i, i + 1), (i + 1, i))]
    swap_b = [pair for i in range(1, nv - 1, 2) for pair in ((i, i + 1), (i + 1, i))]
    on_mem = lambda x, pairs: lax.ppermute(x, "mem", pairs)
    ring = lambda d: [(i, (i + d) % 4) for i in range(4)]
    to_a = functools.partial(lax.ppermute, axis_name="vol", perm=swap_a)
    to_b = functools.partial(lax.ppermute, axis_name="vol", perm=swap_b)

    intra = intra_voxel.reshape(128, 128)
    extra = extra_voxel.reshape(128, 128)

    volt, cells, act, part_lane, cond_lane, send_a, send_b, send_up, send_down = pl.pallas_call(
        gather_kernel,
        out_shape=(shape(128, 128), shape(1, 128), shape(128, 128), shape(8, 128, kind=jnp.int32), shape(8, 128),
                   shape(4, 64, 1024), shape(4, 64, 1024), shape(9, 8, 1024), shape(9, 8, 1024)),
        in_specs=[SM, SM, HBM, HBM] + [VM] * 4,
        out_specs=(VM,) * 5 + (ANY,) * 4,
        scratch_shapes=[pltpu.VMEM((4, 64, 1024), F32), pltpu.VMEM((4, 64, 1024), F32), pltpu.VMEM((8, 1024), F32),
                        pltpu.SemaphoreType.DMA((22,))],
        compiler_params=grant(8),
        cost_estimate=pl.CostEstimate(flops=4000000, bytes_accessed=5000000, transcendentals=0),
        name="voltages",
    )(meta, facet_counts, potential, conductivity, intra, extra, gap_partner, gap_cond)

    below, above, far = on_mem(send_up, ring(1)), on_mem(send_down, ring(3)), on_mem(cells, ring(2))
    early_b, early_a = to_b(send_b), to_a(send_a)

    rates = jnp.concatenate([
        jnp.stack([rate_slope[0] * LOG2E, jnp.log2(rate_scale[0]), rate_slope[1] * (-LOG2E), jnp.log2(rate_scale[1])]),
        type_cond, type_cond * reversal[None, :]], axis=0)
    rates = jnp.broadcast_to(rates[:, :, None], (10, 40, 128))
    steps = 4
    width = 16384 // steps
    facet_rows = pl.BlockSpec((128 // steps, 128), lambda i, *_: (i, 0))
    state_block = pl.BlockSpec((40, width), lambda i, *_: (0, i))
    states_next, ion = pl.pallas_call(
        ionic_kernel,
        out_shape=(shape(40, 16384), shape(128, 128)),
        grid_spec=pltpu.PrefetchScalarGridSpec(
            num_scalar_prefetch=2,
            grid=(steps,),
            in_specs=[facet_rows, state_block, pl.BlockSpec((10, 40, 128), lambda i, *_: (0, 0, 0))],
            out_specs=(state_block, facet_rows),
        ),
        compiler_params=grant(12),
        cost_estimate=pl.CostEstimate(flops=16000000, bytes_accessed=7300000, transcendentals=2600000),
        name="ionic",
    )(facet_counts, cell_type, volt, ion_states, rates)

    y_early, table, more_a, more_b = pl.pallas_call(
        early_edge_kernel,
        out_shape=(shape(8, 8, 1024), shape(8, 128), shape(3, 8, 1024), shape(3, 8, 1024)),
        in_specs=[SM] + [VM] * 4 + [ANY],
        out_specs=(VM,) * 4,
        compiler_params=grant(6),
        cost_estimate=pl.CostEstimate(flops=300000, bytes_accessed=1000000, transcendentals=0),
        name="early_edges",
    )(meta, below, above, far, cells, ion)
    more_b, more_a = to_b(more_b), to_a(more_a)

    source, count = pl.pallas_call(
        scatter_kernel,
        out_shape=(shape(4, 64, 1024), shape(4, 64, 1024)),
        in_specs=[VM] * 4 + [ANY],
        out_specs=(VM, VM),
        compiler_params=grant(8),
        cost_estimate=pl.CostEstimate(flops=800000000, bytes_accessed=2300000, transcendentals=0),
        name="scatter",
    )(ion, act, intra, extra, table)

    u, u_a, u_b, u_up, u_down, membrane = pl.pallas_call(
        first_kernel,
        out_shape=(shape(4, 64, 1024), shape(3, 72, 1024), shape(3, 72, 1024), shape(4, 8, 1024),
                   shape(4, 8, 1024), shape(128, 128)),
        in_specs=[SM, HBM, HBM] + [ANY] * 3 + [VM] * 9,
        out_specs=(VM,) * 6,
        scratch_shapes=[pltpu.VMEM((6, 72, 1024), F32), pltpu.VMEM((6, 72, 1024), F32),
                        pltpu.VMEM((256, 128), F32), pltpu.SemaphoreType.DMA((20,))],
        compiler_params=grant(16),
        cost_estimate=pl.CostEstimate(flops=16000000, bytes_accessed=8000000, transcendentals=0),
        name="first",
    )(meta, potential, conductivity, early_a, early_b, y_early, table, more_a, more_b, part_lane, cond_lane,
      ion, act, source, count)

    low_rows = on_mem(u_up, [(i, i + 1) for i in range(3)])
    high_rows = on_mem(u_down, [(i + 1, i) for i in range(3)])

    big = lambda n: pltpu.VMEM((n, 72, 1024), F32)
    operator = pl.pallas_call(
        operator_kernel,
        out_shape=(shape(9, 72, 1024),) + (shape(8, 72, 1024),) * 5,
        in_specs=[SM, HBM] + [ANY] * 6,
        out_specs=(VM,) * 6,
        scratch_shapes=[big(10), pltpu.SemaphoreType.DMA((18,))],
        compiler_params=grant(20),
        cost_estimate=pl.CostEstimate(flops=16000000, bytes_accessed=17000000, transcendentals=0),
        name="operator",
    )(meta, conductivity, early_a, early_b, y_early, more_a, more_b, u_up)

    y_late, u_a, u_b = pl.pallas_call(
        late_edge_kernel,
        out_shape=(shape(4, 8, 1024), shape(3, 72, 1024), shape(3, 72, 1024)),
        in_specs=[SM, VM, VM, ANY, ANY],
        out_specs=(VM, ANY, ANY),
        input_output_aliases={3: 1, 4: 2},
        scratch_shapes=[pltpu.SemaphoreType.DMA((6,))],
        compiler_params=grant(4),
        cost_estimate=pl.CostEstimate(flops=100000, bytes_accessed=500000, transcendentals=0),
        name="late_edges",
    )(meta, low_rows, high_rows, u_a, u_b)
    late_b, late_a = to_b(u_b), to_a(u_a)

    potential_next = pl.pallas_call(
        sweep_kernel,
        out_shape=shape(4, 64, 1024),
        in_specs=[SM, HBM] + [VM] * 6 + [ANY] * 4,
        out_specs=VM,
        scratch_shapes=[big(10), big(9), big(8), big(9), pltpu.VMEM((4, 64, 1024), F32), pltpu.SemaphoreType.DMA((18,))],
        compiler_params=grant(30),
        cost_estimate=pl.CostEstimate(flops=50000000, bytes_accessed=10000000, transcendentals=0),
        name="sweeps",
    )(meta, potential, *operator, u, late_a, late_b, y_late)
    return potential_next, states_next, membrane.reshape(16384)


def solution(mesh):
    in_specs = (
        P("vol", "mem", None), P("vol", "mem", None), P(None, ("vol", "mem")),
        P(), P(), P(), P(),
        P(("vol", "mem")), P(("vol", "mem")), P(("vol", "mem")), P(("vol", "mem")),
        P(("vol", "mem"), None), P(("vol", "mem"), None),
    )
    out_specs = (P("vol", "mem", None), P(None, ("vol", "mem")), P(("vol", "mem")))
    return jax.shard_map(per_device, mesh=mesh, in_specs=in_specs, out_specs=out_specs, check_vma=False)
```

time: 109 us -> 80 us (0.73)
  local copies, waits for them, and re-layouts: 24.7 us -> 8.32 us
  starting transfers between devices: 35.9 us -> 23.6 us
  Pallas kernels: 26.5 us -> 30.3 us
  waiting for transfers between devices: 17.5 us -> 15.3 us
  other arithmetic: 2 us -> 0.09 us
    ppermute x15 -> x9, waiting for transfers between devices: 17.5 us -> 4.57 us  [the longest x5 2.5 us: per_device(): on_mem = lambda x, pairs: lax.ppermute(x, 'mem', pairs)]
    ppermute x2, waiting for transfers between devices: 0.01 us -> 10.7 us  [per_device(): late_b, late_a = (to_b(u_b), to_a(u_a))]
    ppermute x15 -> x9, starting transfers between devices: 31.8 us -> 21.5 us  [the longest x5 12.4 us: per_device(): on_mem = lambda x, pairs: lax.ppermute(x, 'mem', pairs)]
    unnamed x82 -> x34, local copies, waits for them, and re-layouts: 16.2 us -> 8.11 us
    pallas_call x5 -> x6, Pallas kernels: 18.9 us -> 22.8 us  [the longest x1 8.34 us: per_device(): pl.pallas_call(sweep_kernel, out_shape=shape(4, 64, 1024), in_specs=[SM,...]
    broadcast_in_dim x6 -> x1, local copies, waits for them, and re-layouts: 3.78 us -> 0.11 us  [per_device(): rates = jnp.broadcast_to(rates[:, :, None], (10, 40, 128))]
    ppermute x2, starting transfers between devices: 4.11 us -> 2.12 us  [per_device(): late_b, late_a = (to_b(u_b), to_a(u_a))]
    select_n x4 -> x0, other arithmetic: 1.88 us -> none  [the longest x2 1.21 us: edge_rows(): return jnp.where(sub < 3, from_above, jnp.where(sub >= 5, from_below, 0.0))]
  transfers between devices with their start and end apart: 17 -> 11, of which waited for: 4 -> 4; matrix products, arithmetic and copies ran while one was open for 10% -> 0% of each run, Pallas kernels for 9% -> 15%
where the time goes in v3:
time: 80 us; the launch traced here: 78.6 us
  Pallas kernels  30.3 us (38%)
  starting transfers between devices  23.6 us (30%)
  waiting for transfers between devices  15.3 us (19%)
  local copies, waits for them, and re-layouts  8.32 us (10%)
  between operations  0.94 us (1%)
    ppermute x5, starting transfers between devices, per_device(): on_mem = lambda x, pairs: lax.ppermute(x, 'mem', pairs)  12.4 us
    ppermute x2, waiting for transfers between devices, per_device(): late_b, late_a = (to_b(u_b), to_a(u_a))  10.7 us
    pallas_call x1, Pallas kernels, per_device(): pl.pallas_call(sweep_kernel, out_shape=shape(4, 64, 1024), in_specs=[SM,...  8.34 us
    unnamed x34, local copies, waits for them, and re-layouts  8.11 us
    ppermute x2, starting transfers between devices, per_device(): early_b, early_a = (to_b(send_b), to_a(send_a))  6.39 us
    pallas_call x1, Pallas kernels, per_device(): pl.pallas_call(first_kernel, out_shape=(shape(4, 64, 1024), shape(3, 72,...  5.94 us
    pallas_call x1, Pallas kernels, per_device(): pl.pallas_call(ionic_kernel, out_shape=(shape(40, 16384), shape(128, 128)...  4.28 us
    pallas_call x1, Pallas kernels, per_device(): pl.pallas_call(operator_kernel, out_shape=(shape(9, 72, 1024),) + (shape(...  3.67 us
  transfers between devices with their start and end apart: 11, of which 4 were waited for; matrix products, arithmetic and copies ran while one was open for 0% of the time, Pallas kernels for 15%

profile of v3, /device:TPU:6, one launch (start us, length us, event | category | flops | bytes accessed | tf_op | source)
XLA Modules:
  0.0 78.6 jit_solution(5478593771975060741)
XLA Ops:
  0.7 0.8 copy.18.part_ref
  2.3 1.2 %copy-done = f32[4,64,1024]{2,1,0:T(8,128)S(1)} copy-done((f32[4,64,1024]{2,1,0:T(8,128)S(1)}, f32[4,64,1024]{2,1,0:T(8,128)}, u32[]{:S(2)}) %copy-start) | copy-done | bytes 1048600
  3.6 1.2 %copy-done.2 = f32[4,64,1024]{2,1,0:T(8,128)S(1)} copy-done((f32[4,64,1024]{2,1,0:T(8,128)S(1)}, f32[4,64,1024]{2,1,0:T(8,128)}, u32[]{:S(2)}) %copy-start.2) | copy-done | bytes 1048600
  4.8 0.8 %copy-done.4 = s32[16384]{0:T(1024)S(1)} copy-done((s32[16384]{0:T(1024)S(1)}, s32[16384]{0:T(1024)}, u32[]{:S(2)}) %copy-start.4) | copy-done | bytes 65560
  5.6 0.8 %copy-done.6 = s32[16384]{0:T(1024)S(1)} copy-done((s32[16384]{0:T(1024)S(1)}, s32[16384]{0:T(1024)}, u32[]{:S(2)}) %copy-start.6) | copy-done | bytes 65560
  7.1 3.4 %voltages.1 = (f32[128,128]{1,0:T(8,128)S(1)}, f32[1,128]{1,0:T(1,128)S(1)}, f32[128,128]{1,0:T(8,128)S(1)}, s32[8,128]{1,0:T(8,128)S(1)}, f32[8,128]{1,0:T(8,12...) custom-call(s32[4]{0:T(128)S(1)} %pad_add_fusion.meta, ...), custom_call_target="tpu_custom_call" | custom-call | flops 4000000 | bytes 5000000 | tf_op jit(solution)/shard_map/voltages/pallas_call | solution.py:481
  10.6 6.3 %collective-permute-start.1 = (f32[4,64,1024]{2,1,0:T(8,128)}, f32[4,64,1024]{2,1,0:T(8,128)S(1)}, u32[]{:S(2)}, u32[]{:S(2)}) collective-permute-start(f32[4,64,1024]{2,1,0:T(8,128)} %get-tuple-element.36), channel_id=1, source_target_pairs={{4,8},{8,4},{12,16},{16,12},{20,24},{24,20},{28,32},{32,28},{36,40... | collective-permute-start | bytes 3145736 | tf_op jit(solution)/shard_map/ppermute | solution.py:495
  16.9 3.3 %collective-permute-start.4 = (f32[1,128]{1,0:T(1,128)S(1)}, f32[1,128]{1,0:T(1,128)S(1)}, u32[]{:S(2)}, u32[]{:S(2)}) collective-permute-start(f32[1,128]{1,0:T(1,128)S(1)} %get-tuple-element.39.cell_ref), channel_id=1, source_target_pairs={{0,2},{1,3},{2,0},{3,1},{4,6},{5,7},{6,4},{7,5},{8,10},{9,11},{10,... | collective-permute-start | bytes 1544 | tf_op jit(solution)/shard_map/ppermute | solution.py:473
  20.9 2.6 %collective-permute-start.3 = (f32[9,8,1024]{2,1,0:T(8,128)S(1)}, f32[9,8,1024]{2,1,0:T(8,128)S(1)}, u32[]{:S(2)}, u32[]{:S(2)}) collective-permute-start(f32[9,8,1024]{2,1,0:T(8,128)S(1)} %get-tuple-element.38), channel_id=1, source_target_pairs={{0,3},{1,0},{2,1},{3,2},{4,7},{5,4},{6,5},{7,6},{8,11},{9,8},{10,9... | collective-permute-start | bytes 884744 | tf_op jit(solution)/shard_map/ppermute | solution.py:473
  23.7 1.7 %copy-done.10 = f32[40,16384]{1,0:T(8,128)S(1)} copy-done((f32[40,16384]{1,0:T(8,128)S(1)}, f32[40,16384]{1,0:T(8,128)}, u32[]{:S(2)}) %copy-start.10) | copy-done | bytes 2621464
  25.5 4.3 %ionic.1 = (f32[40,16384]{1,0:T(8,128)}, f32[128,128]{1,0:T(8,128)S(1)}) custom-call(s32[64]{0:T(128)S(1)} %copy-done.9, s32[64]{0:T(128)S(1)} %copy-done.11, f32[128,128]{1,0:T(8,128)S(1)} %get-tuple-element.40.volt_ref, f32[40,16384]{1,0:T(8,128)S(1)} %copy-done.10, f32[10,40,128]{2,1,0:T(8,128)S(1)} %broadcast_in_dim.2.rate_ref), custom_call_target="tpu_custom_call" | custom-call | flops 16000000 | bytes 7300000 | tf_op jit(solution)/shard_map/ionic/pallas_call | solution.py:505
  30.5 2.7 %collective-permute-start.6 = (f32[3,8,1024]{2,1,0:T(8,128)S(1)}, f32[3,8,1024]{2,1,0:T(8,128)S(1)}, u32[]{:S(2)}, u32[]{:S(2)}) collective-permute-start(f32[3,8,1024]{2,1,0:T(8,128)S(1)} %get-tuple-element.44), channel_id=1, source_target_pairs={{4,8},{8,4},{12,16},{16,12},{20,24},{24,20},{28,32},{32,28},{36,40... | collective-permute-start | bytes 294920 | tf_op jit(solution)/shard_map/ppermute | solution.py:528
  33.1 3.3 %scatter.1 = (f32[4,64,1024]{2,1,0:T(8,128)S(1)}, f32[4,64,1024]{2,1,0:T(8,128)S(1)}) custom-call(f32[128,128]{1,0:T(8,128)S(1)} %get-tuple-element.41.after.ion_ref, f32[128,128]{1,0:T(8,128)S(1)} %get-tuple-element.48.act_ref, s32[128,128]{1,0:T(8,128)S(1)} %bitcast.8, s32[128,128]{1,0:T(8,128)S(1)} %bitcast.10, f32[8,128]{1,0:T(8,128)S(1)} %get-tuple-element.45.after.table_ref), custom_call_target="tpu_custom_call" | custom-call | flops 800000000 | bytes 2300000 | tf_op jit(solution)/shard_map/scatter/pallas_call | solution.py:530
  36.4 2.1 %collective-permute-done.6.tb_ref.cb_hbm = f32[3,8,1024]{2,1,0:T(8,128)S(1)} collective-permute-done((f32[3,8,1024]{2,1,0:T(8,128)S(1)}, f32[3,8,1024]{2,1,0:T(8,128)S(1)}, u32[]{:S(2)}, u32[]{:S(2)}) %collective-permute-start.6) | collective-permute-done | bytes 98336 | tf_op jit(solution)/shard_map/ppermute | solution.py:528
  38.5 5.9 %first.1 = (f32[4,64,1024]{2,1,0:T(8,128)S(1)}, f32[3,72,1024]{2,1,0:T(8,128)S(1)}, f32[3,72,1024]{2,1,0:T(8,128)S(1)}, f32[4,8,1024]{2,1,0:T(8,128)S(1)}, f32[4...) custom-call(s32[4]{0:T(128)S(1)} %pad_add_fusion.meta, f32[4,64,1024]{2,1,0:T(8,128)S(1)} %copy-done.1, ...), custom_call_target="tpu_custom_call" | custom-call | flops 16000000 | bytes 8000000 | tf_op jit(solution)/shard_map/first/pallas_call | solution.py:540
  44.5 1.3 %collective-permute-start.8 = (f32[4,8,1024]{2,1,0:T(8,128)S(1)}, f32[4,8,1024]{2,1,0:T(8,128)S(1)}, u32[]{:S(2)}, u32[]{:S(2)}) collective-permute-start(f32[4,8,1024]{2,1,0:T(8,128)S(1)} %get-tuple-element.59), channel_id=1, source_target_pairs={{1,0},{2,1},{3,2},{5,4},{6,5},{7,6},{9,8},{10,9},{11,10},{13,12},{... | collective-permute-start | bytes 393224 | tf_op jit(solution)/shard_map/ppermute | solution.py:473
  45.8 4.6 %collective-permute-start.7 = (f32[4,8,1024]{2,1,0:T(8,128)S(1)}, f32[4,8,1024]{2,1,0:T(8,128)S(1)}, u32[]{:S(2)}, u32[]{:S(2)}) collective-permute-start(f32[4,8,1024]{2,1,0:T(8,128)S(1)} %get-tuple-element.51.after), channel_id=1, source_target_pairs={{0,1},{1,2},{2,3},{4,5},{5,6},{6,7},{8,9},{9,10},{10,11},{12,13},{... | collective-permute-start | bytes 393224 | tf_op jit(solution)/shard_map/ppermute | solution.py:473
  50.3 1.0 %collective-permute-done.8.above_ref = f32[4,8,1024]{2,1,0:T(8,128)S(1)} collective-permute-done((f32[4,8,1024]{2,1,0:T(8,128)S(1)}, f32[4,8,1024]{2,1,0:T(8,128)S(1)}, u32[]{:S(2)}, u32[]{:S(2)}) %collective-permute-start.8) | collective-permute-done | bytes 131104 | tf_op jit(solution)/shard_map/ppermute | solution.py:473
  51.3 1.5 %collective-permute-done.7.below_ref = f32[4,8,1024]{2,1,0:T(8,128)S(1)} collective-permute-done((f32[4,8,1024]{2,1,0:T(8,128)S(1)}, f32[4,8,1024]{2,1,0:T(8,128)S(1)}, u32[]{:S(2)}, u32[]{:S(2)}) %collective-permute-start.7) | collective-permute-done | bytes 131104 | tf_op jit(solution)/shard_map/ppermute | solution.py:473
  52.8 0.9 %late_edges.1 = (f32[4,8,1024]{2,1,0:T(8,128)S(1)}, f32[3,72,1024]{2,1,0:T(8,128)S(1)}, f32[3,72,1024]{2,1,0:T(8,128)S(1)}) custom-call(s32[4]{0:T(128)S(1)} %pad_add_fusion.meta, f32[4,8,1024]{2,1,0:T(8,128)S(1)} %collective-permute-done.7.below_ref, ...), custom_call_target="tpu_custom_call", output_to_operand_aliasing={{1}: (3, {}), {2}: (4, {})} | custom-call | flops 100000 | bytes 500000 | tf_op jit(solution)/shard_map/late_edges/pallas_call | solution.py:569
  53.8 2.0 %collective-permute-start.10 = (f32[3,72,1024]{2,1,0:T(8,128)S(1)}, f32[3,72,1024]{2,1,0:T(8,128)S(1)}, u32[]{:S(2)}, u32[]{:S(2)}) collective-permute-start(f32[3,72,1024]{2,1,0:T(8,128)S(1)} %get-tuple-element.63), channel_id=1, source_target_pairs={{4,8},{8,4},{12,16},{16,12},{20,24},{24,20},{28,32},{32,28},{36,40... | collective-permute-start | bytes 2654216 | tf_op jit(solution)/shard_map/ppermute | solution.py:580
  55.8 3.7 %operator.1 = (f32[9,72,1024]{2,1,0:T(8,128)S(1)}, f32[8,72,1024]{2,1,0:T(8,128)S(1)}, f32[8,72,1024]{2,1,0:T(8,128)S(1)}, f32[8,72,1024]{2,1,0:T(8,128)S(1)}, f...) custom-call(s32[4]{0:T(128)S(1)} %pad_add_fusion.meta, f32[4,64,1024]{2,1,0:T(8,128)S(1)} %copy-done.3, ...), custom_call_target="tpu_custom_call" | custom-call | flops 16000000 | bytes 17000000 | tf_op jit(solution)/shard_map/operator/pallas_call | solution.py:558
  59.5 10.7 %collective-permute-done.10.ub_hbm = f32[3,72,1024]{2,1,0:T(8,128)S(1)} collective-permute-done((f32[3,72,1024]{2,1,0:T(8,128)S(1)}, f32[3,72,1024]{2,1,0:T(8,128)S(1)}, u32[]{:S(2)}, u32[]{:S(2)}) %collective-permute-start.10) | collective-permute-done | bytes 884768 | tf_op jit(solution)/shard_map/ppermute | solution.py:580
  70.3 8.3 %sweeps.1 = f32[4,64,1024]{2,1,0:T(8,128)} custom-call(s32[4]{0:T(128)S(1)} %pad_add_fusion.meta, f32[4,64,1024]{2,1,0:T(8,128)S(1)} %copy-done.1, f32[9,72,1024]{2,1,0:T(8,128)S(1)} %get-tuple-element.52.fx, f32[8,72,1024]{2,1,0:T(8,128)S(1)} %get-tuple-element.53.fym, f32[8,72,1024]{2,1,0:T(8,128)S(1)} %get-tuple-element.54.fyp, ...), custom_call_target="tpu_custom_call" | custom-call | flops 50000000 | bytes 10000000 | tf_op jit(solution)/shard_map/sweeps/pallas_call | solution.py:582
  (45 shorter events, 3.3 us)
Async XLA Ops:
  0.6 23.1 %copy-start.9 = (s32[64]{0:T(128)S(1)}, s32[64]{0:T(128)}, u32[]{:S(2)}) copy-start(s32[64]{0:T(128)} %cnt.3) | copy-start | bytes 772
  0.6 22.8 %copy-start.14 = (f32[2,40]{1,0:T(2,128)S(1)}, f32[2,40]{1,0:T(2,128)}, u32[]{:S(2)}) copy-start(f32[2,40]{1,0:T(2,128)} %param.17) | copy-start | bytes 964
  0.7 22.8 %copy-start.13 = (f32[2,40]{1,0:T(2,128)S(1)}, f32[2,40]{1,0:T(2,128)}, u32[]{:S(2)}) copy-start(f32[2,40]{1,0:T(2,128)} %param.16) | copy-start | bytes 964
  0.7 22.8 %copy-start.12 = (f32[3,40]{1,0:T(4,128)S(1)}, f32[3,40]{1,0:T(4,128)}, u32[]{:S(2)}) copy-start(f32[3,40]{1,0:T(4,128)} %param.18) | copy-start | bytes 1444
  0.7 22.8 %copy-start.15 = (f32[40]{0:T(128)S(1)}, f32[40]{0:T(128)}, u32[]{:S(2)}) copy-start(f32[40]{0:T(128)} %param.19) | copy-start | bytes 484
  0.7 23.0 %copy-start.11 = (s32[64]{0:T(128)S(1)}, s32[64]{0:T(128)}, u32[]{:S(2)}) copy-start(s32[64]{0:T(128)} %typ.1) | copy-start | bytes 772
  2.3 1.2 %copy-start = (f32[4,64,1024]{2,1,0:T(8,128)S(1)}, f32[4,64,1024]{2,1,0:T(8,128)}, u32[]{:S(2)}) copy-start(f32[4,64,1024]{2,1,0:T(8,128)} %p_hbm.5) | copy-start | bytes 3145732
  3.6 1.2 %copy-start.2 = (f32[4,64,1024]{2,1,0:T(8,128)S(1)}, f32[4,64,1024]{2,1,0:T(8,128)}, u32[]{:S(2)}) copy-start(f32[4,64,1024]{2,1,0:T(8,128)} %c_hbm.5) | copy-start | bytes 3145732
  10.5 28.0 %collective-permute-start = (f32[4,64,1024]{2,1,0:T(8,128)}, f32[4,64,1024]{2,1,0:T(8,128)S(1)}, u32[]{:S(2)}, u32[]{:S(2)}) collective-permute-start(f32[4,64,1024]{2,1,0:T(8,128)} %get-tuple-element.35), channel_id=1, source_target_pairs={{0,4},{4,0},{8,12},{12,8},{16,20},{20,16},{24,28},{28,24},{32,36},... | collective-permute-start | bytes 3145736 | tf_op jit(solution)/shard_map/ppermute | solution.py:495
  10.6 27.9 %collective-permute-start.1 = (f32[4,64,1024]{2,1,0:T(8,128)}, f32[4,64,1024]{2,1,0:T(8,128)S(1)}, u32[]{:S(2)}, u32[]{:S(2)}) collective-permute-start(f32[4,64,1024]{2,1,0:T(8,128)} %get-tuple-element.36), channel_id=1, source_target_pairs={{4,8},{8,4},{12,16},{16,12},{20,24},{24,20},{28,32},{32,28},{36,40... | collective-permute-start | bytes 3145736 | tf_op jit(solution)/shard_map/ppermute | solution.py:495
  16.9 12.8 %collective-permute-start.4 = (f32[1,128]{1,0:T(1,128)S(1)}, f32[1,128]{1,0:T(1,128)S(1)}, u32[]{:S(2)}, u32[]{:S(2)}) collective-permute-start(f32[1,128]{1,0:T(1,128)S(1)} %get-tuple-element.39.cell_ref), channel_id=1, source_target_pairs={{0,2},{1,3},{2,0},{3,1},{4,6},{5,7},{6,4},{7,5},{8,10},{9,11},{10,... | collective-permute-start | bytes 1544 | tf_op jit(solution)/shard_map/ppermute | solution.py:473
  20.2 9.6 %collective-permute-start.2 = (f32[9,8,1024]{2,1,0:T(8,128)S(1)}, f32[9,8,1024]{2,1,0:T(8,128)S(1)}, u32[]{:S(2)}, u32[]{:S(2)}) collective-permute-start(f32[9,8,1024]{2,1,0:T(8,128)S(1)} %get-tuple-element.37), channel_id=1, source_target_pairs={{0,1},{1,2},{2,3},{3,0},{4,5},{5,6},{6,7},{7,4},{8,9},{9,10},{10,1... | collective-permute-start | bytes 884744 | tf_op jit(solution)/shard_map/ppermute | solution.py:473
  20.9 8.9 %collective-permute-start.3 = (f32[9,8,1024]{2,1,0:T(8,128)S(1)}, f32[9,8,1024]{2,1,0:T(8,128)S(1)}, u32[]{:S(2)}, u32[]{:S(2)}) collective-permute-start(f32[9,8,1024]{2,1,0:T(8,128)S(1)} %get-tuple-element.38), channel_id=1, source_target_pairs={{0,3},{1,0},{2,1},{3,2},{4,7},{5,4},{6,5},{7,6},{8,11},{9,8},{10,9... | collective-permute-start | bytes 884744 | tf_op jit(solution)/shard_map/ppermute | solution.py:473
  23.7 1.7 %copy-start.10 = (f32[40,16384]{1,0:T(8,128)S(1)}, f32[40,16384]{1,0:T(8,128)}, u32[]{:S(2)}) copy-start(f32[40,16384]{1,0:T(8,128)} %st_ref.1) | copy-start | bytes 7864324
  25.5 7.7 %copy-start.5 = (s32[16384]{0:T(1024)S(1)}, s32[16384]{0:T(1024)}, u32[]{:S(2)}) copy-start(s32[16384]{0:T(1024)} %param.21) | copy-start | bytes 196612
  25.5 7.7 %copy-start.7 = (s32[16384]{0:T(1024)S(1)}, s32[16384]{0:T(1024)}, u32[]{:S(2)}) copy-start(s32[16384]{0:T(1024)} %param.22) | copy-start | bytes 196612
  29.7 8.8 %copy-start.1 = (f32[4,64,1024]{2,1,0:T(8,128)S(1)}, f32[4,64,1024]{2,1,0:T(8,128)}, u32[]{:S(2)}) copy-start(f32[4,64,1024]{2,1,0:T(8,128)} %p_hbm.5) | copy-start | bytes 3145732
  29.7 8.8 %copy-start.3 = (f32[4,64,1024]{2,1,0:T(8,128)S(1)}, f32[4,64,1024]{2,1,0:T(8,128)}, u32[]{:S(2)}) copy-start(f32[4,64,1024]{2,1,0:T(8,128)} %c_hbm.5) | copy-start | bytes 3145732
  30.4 6.1 %collective-permute-start.5 = (f32[3,8,1024]{2,1,0:T(8,128)S(1)}, f32[3,8,1024]{2,1,0:T(8,128)S(1)}, u32[]{:S(2)}, u32[]{:S(2)}) collective-permute-start(f32[3,8,1024]{2,1,0:T(8,128)S(1)} %get-tuple-element.43), channel_id=1, source_target_pairs={{0,4},{4,0},{8,12},{12,8},{16,20},{20,16},{24,28},{28,24},{32,36},... | collective-permute-start | bytes 294920 | tf_op jit(solution)/shard_map/ppermute | solution.py:528
  30.5 8.0 %collective-permute-start.6 = (f32[3,8,1024]{2,1,0:T(8,128)S(1)}, f32[3,8,1024]{2,1,0:T(8,128)S(1)}, u32[]{:S(2)}, u32[]{:S(2)}) collective-permute-start(f32[3,8,1024]{2,1,0:T(8,128)S(1)} %get-tuple-element.44), channel_id=1, source_target_pairs={{4,8},{8,4},{12,16},{16,12},{20,24},{24,20},{28,32},{32,28},{36,40... | collective-permute-start | bytes 294920 | tf_op jit(solution)/shard_map/ppermute | solution.py:528
  44.5 6.9 %collective-permute-start.8 = (f32[4,8,1024]{2,1,0:T(8,128)S(1)}, f32[4,8,1024]{2,1,0:T(8,128)S(1)}, u32[]{:S(2)}, u32[]{:S(2)}) collective-permute-start(f32[4,8,1024]{2,1,0:T(8,128)S(1)} %get-tuple-element.59), channel_id=1, source_target_pairs={{1,0},{2,1},{3,2},{5,4},{6,5},{7,6},{9,8},{10,9},{11,10},{13,12},{... | collective-permute-start | bytes 393224 | tf_op jit(solution)/shard_map/ppermute | solution.py:473
  45.8 7.1 %collective-permute-start.7 = (f32[4,8,1024]{2,1,0:T(8,128)S(1)}, f32[4,8,1024]{2,1,0:T(8,128)S(1)}, u32[]{:S(2)}, u32[]{:S(2)}) collective-permute-start(f32[4,8,1024]{2,1,0:T(8,128)S(1)} %get-tuple-element.51.after), channel_id=1, source_target_pairs={{0,1},{1,2},{2,3},{4,5},{5,6},{6,7},{8,9},{9,10},{10,11},{12,13},{... | collective-permute-start | bytes 393224 | tf_op jit(solution)/shard_map/ppermute | solution.py:473
  53.7 5.8 %collective-permute-start.9 = (f32[3,72,1024]{2,1,0:T(8,128)S(1)}, f32[3,72,1024]{2,1,0:T(8,128)S(1)}, u32[]{:S(2)}, u32[]{:S(2)}) collective-permute-start(f32[3,72,1024]{2,1,0:T(8,128)S(1)} %get-tuple-element.62), channel_id=1, source_target_pairs={{0,4},{4,0},{8,12},{12,8},{16,20},{20,16},{24,28},{28,24},{32,36},... | collective-permute-start | bytes 2654216 | tf_op jit(solution)/shard_map/ppermute | solution.py:580
  53.8 16.5 %collective-permute-start.10 = (f32[3,72,1024]{2,1,0:T(8,128)S(1)}, f32[3,72,1024]{2,1,0:T(8,128)S(1)}, u32[]{:S(2)}, u32[]{:S(2)}) collective-permute-start(f32[3,72,1024]{2,1,0:T(8,128)S(1)} %get-tuple-element.63), channel_id=1, source_target_pairs={{4,8},{8,4},{12,16},{16,12},{20,24},{24,20},{28,32},{32,28},{36,40... | collective-permute-start | bytes 2654216 | tf_op jit(solution)/shard_map/ppermute | solution.py:580
  (3 other events, 2.3 us)

commit v4 on v3

--- a/solution.py
+++ b/solution.py
@@ -54,21 +54,8 @@
     loads = begin([(p_hbm.at[x], p_ref.at[x]) for x in range(4)] + [(c_hbm.at[x], c_ref.at[x]) for x in range(4)], sem, 0)
     twice = iota((8, 128), 1) // 2
     for src, dst in ((part_ref, part_out), (cond_ref, cond_out)):
-        wide = jnp.concatenate([src[...].astype(F32), jnp.zeros((64, 120), F32)], axis=1)
-        turned = jnp.transpose(jnp.concatenate([wide, wide], axis=0))[0:8]
-        dst[...] = jnp.take_along_axis(turned, twice, axis=1, mode="promise_in_bounds").astype(dst.dtype)
-    for load in loads:
-        load.wait()
-    copies = []
-    for i in range(3):
-        copies.append((c_ref.at[plane_of(par, i)], b_hbm.at[i]))
-        copies.append((c_ref.at[plane_of(par, 3 - i)], a_hbm.at[i]))
-    copies.append((p_ref.at[plane_of(par, 0)], b_hbm.at[3]))
-    copies.append((p_ref.at[plane_of(par, 3)], a_hbm.at[3]))
-    for k, src in enumerate((c_ref, p_ref)):
-        copies.append((src.at[:, 56:64], up_hbm.at[4 * k : 4 * k + 4]))
-        copies.append((src.at[:, 0:8], down_hbm.at[4 * k : 4 * k + 4]))
-    sends = begin(copies, sem, 8)
+        wide = jnp.concatenate([src[...], src[...]], axis=1)
+        dst[...] = jnp.take_along_axis(wide, twice, axis=1, mode="promise_in_bounds")
     sub = iota((8, 128), 0)
     low = sub < 4
     lane_row = iota((1, 128), 1)
@@ -102,7 +89,23 @@
                     act_ref[at, :] = jnp.where(used, 1.0, 0.0)
         return carry
 
-    lax.fori_loop(0, 16, body, 0, unroll=4)
+    for x in range(4):
+        if x < 2:
+            loads[x].wait()
+        lax.fori_loop(4 * x, 4 * x + 4, body, 0, unroll=4)
+        if x == 1:
+            for load in loads[2:]:
+                load.wait()
+            copies = []
+            for i in range(3):
+                copies.append((c_ref.at[plane_of(par, i)], b_hbm.at[i]))
+                copies.append((c_ref.at[plane_of(par, 3 - i)], a_hbm.at[i]))
+            copies.append((p_ref.at[plane_of(par, 0)], b_hbm.at[3]))
+            copies.append((p_ref.at[plane_of(par, 3)], a_hbm.at[3]))
+            for k, src in enumerate((c_ref, p_ref)):
+                copies.append((src.at[:, 56:64], up_hbm.at[4 * k : 4 * k + 4]))
+                copies.append((src.at[:, 0:8], down_hbm.at[4 * k : 4 * k + 4]))
+            sends = begin(copies, sem, 8)
     act = act_ref[...]
     total = jnp.sum(jnp.transpose(volt_ref[...] * act), axis=0, keepdims=True)
     count = jnp.sum(jnp.transpose(act), axis=0, keepdims=True)
@@ -166,7 +169,7 @@
     lax.fori_loop(0, cells // 4, body, 0)
 
 
-def scatter_kernel(ion_ref, act_ref, in_ref, ex_ref, after, s_ref, n_ref):
+def scatter_kernel(ion_ref, act_ref, in_ref, ex_ref, s_ref, n_ref):
     row_iota = iota((32, 512), 0)
     lane_iota = iota((128, 512), 0)
     low = iota((8, 128), 0) < 4
@@ -233,48 +236,73 @@
         ref[2, :, 0:128] = table
 
 
-def late_edge_kernel(meta, below_ref, above_ref, ua_in, ub_in, y_ref, ua_ref, ub_ref, sem):
+def late_edge_kernel(meta, below_ref, above_ref, after, y_ref, a_ref, b_ref):
     par = meta[0]
     for x in range(4):
         y_ref[x] = edge_rows(meta, below_ref[x], above_ref[x])
-    copies = []
-    for i in range(3):
-        copies.append((y_ref.at[plane_of(par, 3 - i)], ua_ref.at[i, 64:72]))
-        copies.append((y_ref.at[plane_of(par, i)], ub_ref.at[i, 64:72]))
-    for m in begin(copies, sem, 0):
-        m.wait()
-
-
-def tile(ref, e, t):
-    return ref[e, 8 * t : 8 * t + 8, :]
-
-
-class Around:
-    def __init__(self, ref, e):
-        self.ref, self.e = ref, e
+    for i in range(2):
+        a_ref[i] = y_ref[plane_of(par, 3 - i)]
+        b_ref[i] = y_ref[plane_of(par, i)]
+
+
+def reader(par, own, a, b, y, ca=None, cb=None, own_y=0):
+    def get(e, t):
+        rows = slice(8 * t, 8 * t + 8)
+        if 3 <= e <= 6:
+            x = plane_of(par, e - 3)
+            return own[x, rows, :] if t < 8 else y[own_y + x]
+        halo, corner, i = (a, ca, e - 7) if e > 6 else (b, cb, 2 - e)
+        return halo[i, rows, :] if t < 8 else corner[i]
+
+    return get
+
+
+def stored(*held):
+    def get(e, t):
+        for ref, start, stop in held:
+            if start <= e < stop:
+                return ref[e - start, 8 * t : 8 * t + 8, :]
+
+    return get
+
+
+class Plane:
+    def __init__(self, get, e):
+        self.get, self.e = get, e
         self.sub = iota((8, 1024), 0)
-
-    def at(self, t):
-        ref, e = self.ref, self.e
-        c = tile(ref, e, t)
-        before, after = tile(ref, e, (t + 8) % 9), tile(ref, e, (t + 1) % 9)
-        ym = jnp.where(self.sub == 0, pltpu.roll(before, 1, 0), pltpu.roll(c, 1, 0))
-        yp = jnp.where(self.sub == 7, pltpu.roll(after, 7, 0), pltpu.roll(c, 7, 0))
-        zm, zp = pltpu.roll(c, 1, 1), pltpu.roll(c, 1023, 1)
-        return c, tile(ref, e - 1, t), tile(ref, e + 1, t), ym, yp, zm, zp
-
-
-def couplings(around, t):
+        self.kept = {}
+
+    def turned(self, t, by, keep):
+        found = self.kept.pop((t, by), None)
+        if found is None:
+            found = pltpu.roll(self.get(self.e, t), by, 0)
+            if keep:
+                self.kept[t, by] = found
+        return found
+
+    def views(self, t):
+        get, e = self.get, self.e
+        c = get(e, t)
+        ym = jnp.where(self.sub == 0, self.turned((t + 8) % 9, 1, False), self.turned(t, 1, True))
+        yp = jnp.where(self.sub == 7, self.turned((t + 1) % 9, 7, t < 8), self.turned(t, 7, False))
+        return c, get(e - 1, t), get(e + 1, t), ym, yp, pltpu.roll(c, 1, 1), pltpu.roll(c, 1023, 1)
+
+
+def inverse(x):
+    rec = pl.reciprocal(x, approx=True)
+    return rec * (2.0 - x * rec)
+
+
+def couplings(plane, t):
     lane = iota((8, 1024), 1)
-    c, xm, xp, ym, yp, zm, zp = around.at(t)
+    c, xm, xp, ym, yp, zm, zp = plane.views(t)
     first, last = lane == 0, lane == 1023
-    zm = jnp.where(first, 0.0, zm)
-    zp = jnp.where(last, 0.0, zp)
-    fs = [0.25 * (c + other) for other in (xm, xp, ym, yp, zm, zp)]
-    diagonal = 1.0 + (((fs[0] + fs[1]) + (fs[2] + fs[3])) + (fs[4] + fs[5]))
-    fs[4] = jnp.where(first, 0.0, fs[4])
-    fs[5] = jnp.where(last, 0.0, fs[5])
-    return fs, diagonal
+    c = 0.25 * c
+    xm, xp, ym, yp = (c + 0.25 * other for other in (xm, xp, ym, yp))
+    zm = c + 0.25 * jnp.where(first, 0.0, zm)
+    zp = c + 0.25 * jnp.where(last, 0.0, zp)
+    inv = inverse(1.0 + (((xm + xp) + (ym + yp)) + (zm + zp)))
+    return (xm, xp, ym, yp, jnp.where(first, 0.0, zm), jnp.where(last, 0.0, zp)), inv
 
 
 def weighted(fs, views):
@@ -282,21 +310,24 @@
     return ((t[0] + t[1]) + (t[2] + t[3])) + (t[4] + t[5])
 
 
-def first_kernel(meta, p_hbm, c_hbm, a_hbm, b_hbm, y_hbm, table_ref, ta_ref, tb_ref, part_ref, cond_ref,
-                 ion_ref, act_ref, s_ref, n_ref, u_ref, a_ref, b_ref, up_ref, down_ref, mem_ref,
-                 ce, pe, spread, sem):
+def prepare_kernel(meta, p_ref, c_ref, a_ref, b_ref, y_ref, s_ref, n_ref, w_ref, k_ref):
+    par = meta[0]
+    conduct = reader(par, c_ref, a_ref, b_ref, y_ref)
+    own = reader(par, p_ref, a_ref.at[3:4], b_ref.at[3:4], y_ref, own_y=4)
+    for e in range(3, 7):
+        x = plane_of(par, e - 3)
+        pc, pp = Plane(conduct, e), Plane(own, e)
+        for t in range(8):
+            rows = slice(8 * t, 8 * t + 8)
+            fs, inv = couplings(pc, t)
+            p, *views = pp.views(t)
+            w_ref[x, rows, :] = (p + weighted(fs, views) - 0.5 * s_ref[x, rows, :]) * inv - p
+            k_ref[x, rows, :] = (-0.5 * inv) * n_ref[x, rows, :]
+
+
+def gap_kernel(meta, table_ref, ta_ref, tb_ref, part_ref, cond_ref, ion_ref, act_ref, w_ref, k_ref,
+               u_ref, a_ref, b_ref, up_ref, down_ref, mem_ref, spread):
     par, mine, v = meta[0], meta[2], meta[3]
-    copies = []
-    for e, hbm, yk in ((ce, c_hbm, 0), (pe, p_hbm, 4)):
-        for j in range(4):
-            copies.append((hbm.at[plane_of(par, j)], e.at[1 + j, 0:64]))
-            copies.append((y_hbm.at[yk + plane_of(par, j)], e.at[1 + j, 64:72]))
-    copies.append((a_hbm.at[0], ce.at[5, 0:64]))
-    copies.append((b_hbm.at[0], ce.at[0, 0:64]))
-    copies.append((a_hbm.at[3], pe.at[5, 0:64]))
-    copies.append((b_hbm.at[3], pe.at[0, 0:64]))
-    made = begin(copies, sem, 0)
-
     part = part_ref[...]
     brick = part >> 6
     bx, by = brick >> 2, brick & 3
@@ -319,142 +350,128 @@
         at = 64 * half + 2 * (iota((8, 128), 1) // 4)
         wide = jnp.take_along_axis(g8, at, axis=1, mode="promise_in_bounds")[0:1]
         spread[128 * half : 128 * half + 128, :] = jnp.transpose(jnp.broadcast_to(wide, (128, 128)))
-    for m in made:
-        m.wait()
-
-    def body(j, carry):
+    for j in range(4):
         x = plane_of(par, j)
-        ca, pa = Around(ce, 1 + j), Around(pe, 1 + j)
-        ja, jb = jnp.clip(3 - j, 0, 2), jnp.clip(j, 0, 2)
         for t in range(8):
             rows = slice(8 * t, 8 * t + 8)
-            fs, diagonal = couplings(ca, t)
-            inv = 1.0 / diagonal
-            views = pa.at(t)
-            p = views[0]
             gt = jnp.tile(spread[pl.ds(pl.multiple_of(x * 64 + 8 * t, 8), 8), :], (1, 8))
-            source = s_ref[x, rows, :] + gt * n_ref[x, rows, :]
-            u = (p + weighted(fs, views[1:]) - 0.5 * source) * inv - p
+            u = w_ref[x, rows, :] + k_ref[x, rows, :] * gt
             u_ref[x, rows, :] = u
             if t == 0:
                 down_ref[x] = u
             if t == 7:
                 up_ref[x] = u
-
-            @pl.when(j < 3)
-            def _():
-                b_ref[jb, rows, :] = u
-
-            @pl.when(j > 0)
-            def _():
-                a_ref[ja, rows, :] = u
-
-        return carry
-
-    lax.fori_loop(0, 4, body, 0)
-
-
-def operator_kernel(meta, c_hbm, a_hbm, b_hbm, y_hbm, ca_hbm, cb_hbm, after,
-                    fx, fym, fyp, fzm, fzp, inv, c, sem):
+            if j < 3:
+                b_ref[j, rows, :] = u
+            if j > 0:
+                a_ref[3 - j, rows, :] = u
+
+
+def operator_kernel(meta, c_ref, a_ref, b_ref, y_ref, ca_ref, cb_ref, after, fx, fym, fyp, fzm, fzp, inv_ref):
     par, has_b, mine = meta[0], meta[1], meta[2]
-    copies = []
-    for j in range(4):
-        copies.append((c_hbm.at[plane_of(par, j)], c.at[3 + j, 0:64]))
-        copies.append((y_hbm.at[plane_of(par, j)], c.at[3 + j, 64:72]))
-    for i in range(3):
-        copies.append((a_hbm.at[i], c.at[7 + i, 0:64]))
-        copies.append((b_hbm.at[i], c.at[2 - i, 0:64]))
-    for i in range(2):
-        copies.append((ca_hbm.at[i], c.at[7 + i, 64:72]))
-        copies.append((cb_hbm.at[i], c.at[2 - i, 64:72]))
-    made = begin(copies, sem, 0)
-    zero8 = jnp.zeros((8, 1024), F32)
-    c[0, 64:72, :] = zero8
-    c[9, 64:72, :] = zero8
+    conduct = reader(par, c_ref, a_ref, b_ref, y_ref, ca_ref, cb_ref)
     sub = iota((8, 1024), 0)
     bottom = (sub < 3) & (mine != 3)
     top = (sub >= 5) & (mine != 0)
     keep = jnp.where(bottom | top, 1.0, 0.0)
-    for m in made:
-        m.wait()
-
-    def build(e, carry):
-        around = Around(c, e)
-        inside = jnp.where((e >= 3) | (has_b == 1), 1.0, 0.0)
-        for t in range(9):
+    inside = jnp.where(has_b == 1, 1.0, 0.0)
+    for e in range(1, 9):
+        plane = Plane(conduct, e)
+        for t in range(8 if e in (1, 8) else 9):
             rows = slice(8 * t, 8 * t + 8)
-            fs, diagonal = couplings(around, t)
-            part = inside / diagonal
-            inv[e - 1, rows, :] = part * keep if t == 8 else part
-            fx[e - 1, rows, :] = fs[0]
+            fs, inv = couplings(plane, t)
+            if e < 3:
+                inv = inv * inside
+            inv_ref[e - 1, rows, :] = inv * keep if t == 8 else inv
+            if e == 1 or (e == 2 and t == 8):
+                fx[e - 1, rows, :] = fs[0]
             fx[e, rows, :] = fs[1]
-            fym[e - 1, rows, :] = fs[2]
-            fyp[e - 1, rows, :] = fs[3]
-            fzm[e - 1, rows, :] = fs[4]
-            fzp[e - 1, rows, :] = fs[5]
-        return carry
-
-    lax.fori_loop(1, 9, build, 0)
-
-
-def sweep_kernel(meta, p_hbm, fx, fym, fyp, fzm, fzp, inv, u_hbm, ua_hbm, ub_hbm, uy_hbm,
-                 out_ref, u0, u1, u2, r, p_ref, sem):
+            for ref, f in zip((fym, fyp, fzm, fzp), fs[2:]):
+                ref[e - 1, rows, :] = f
+
+
+def coupled(coef, get, plane, t):
+    fx, fym, fyp, fzm, fzp, inv = coef
+    e = plane.e
+    rows = slice(8 * t, 8 * t + 8)
+    fs = [fx[e - 1, rows, :], fx[e, rows, :]] + [f[e - 1, rows, :] for f in (fym, fyp, fzm, fzp)]
+    u, *views = plane.views(t)
+    return u, inv[e - 1, rows, :] * weighted(fs, views)
+
+
+def put(held, e, t, value):
+    for ref, start, stop in held:
+        if start <= e < stop:
+            ref[e - start, 8 * t : 8 * t + 8, :] = value
+
+
+def step_one(coef, u0, e, r_held, u1_held):
+    a, b = sweep_factors()[0]
+    plane = Plane(u0, e)
+    for t in range(8 if e in (1, 8) else 9):
+        u, res = coupled(coef, u0, plane, t)
+        put(r_held, e, t, res)
+        put(u1_held, e, t, a * u + b * res)
+
+
+def step_two(coef, u1, r, e, r_held, u2_held):
+    a, b = sweep_factors()[1]
+    plane = Plane(u1, e)
+    for t in range(8 if e in (2, 7) else 9):
+        u, more = coupled(coef, u1, plane, t)
+        res = (r(e, t) - u) + more
+        put(r_held, e, t, res)
+        put(u2_held, e, t, a * u + b * res)
+
+
+def step_three(coef, p_ref, u0, u1, u2, r, e, x, out_ref, at):
+    a, b = sweep_factors()[2]
+    plane = Plane(u2, e)
+    for t in range(8):
+        rows = slice(8 * t, 8 * t + 8)
+        u, more = coupled(coef, u2, plane, t)
+        res = (r(e, t) - u) + more
+        before = (p_ref[x, rows, :] + u0(e, t)) + (u1(e, t) + u)
+        out_ref[at, rows, :] = before + (a * u + b * res)
+
+
+def near_kernel(meta, p_ref, fx, fym, fyp, fzm, fzp, inv, u_ref, a_ref, y_ref, ca_ref,
+                u1_out, r_out, u2_out, done_ref, u1_far, r_far, u2_far):
     par = meta[0]
-    p_copies = begin([(p_hbm.at[x], p_ref.at[x]) for x in range(4)], sem, 14)
-    copies = []
-    for j in range(4):
-        copies.append((u_hbm.at[plane_of(par, j)], u0.at[3 + j, 0:64]))
-        copies.append((uy_hbm.at[plane_of(par, j)], u0.at[3 + j, 64:72]))
-    for i in range(3):
-        copies.append((ua_hbm.at[i], u0.at[7 + i]))
-        copies.append((ub_hbm.at[i], u0.at[2 - i]))
-    for m in begin(copies, sem, 0):
-        m.wait()
-    (a1, b1), (a2, b2), (a3, b3) = sweep_factors()
-
-    def coupled(around, e, t):
-        fs = [tile(fx, e - 1, t), tile(fx, e, t)] + [tile(f, e - 1, t) for f in (fym, fyp, fzm, fzp)]
-        views = around.at(t)
-        return views[0], tile(inv, e - 1, t) * weighted(fs, views[1:])
-
-    def first(e, carry):
-        around = Around(u0, e)
-        for t in range(9):
-            rows = slice(8 * t, 8 * t + 8)
-            u, res = coupled(around, e, t)
-            r[e, rows, :] = res
-            u1[e, rows, :] = a1 * u + b1 * res
-        return carry
-
-    lax.fori_loop(1, 9, first, 0)
-
-    def second(e, carry):
-        around = Around(u1, e)
-        for t in range(9):
-            rows = slice(8 * t, 8 * t + 8)
-            u, more = coupled(around, e, t)
-            res = (tile(r, e, t) - u) + more
-            r[e, rows, :] = res
-            u2[e, rows, :] = a2 * u + b2 * res
-        return carry
-
-    lax.fori_loop(2, 8, second, 0)
-
-    def third(j, carry):
-        e = 3 + j
-        x = plane_of(par, j)
-        around = Around(u2, e)
-        for t in range(8):
-            rows = slice(8 * t, 8 * t + 8)
-            u, more = coupled(around, e, t)
-            res = (tile(r, e, t) - u) + more
-            before = (p_ref[x, rows, :] + tile(u0, e, t)) + (tile(u1, e, t) + u)
-            out_ref[x, rows, :] = before + (a3 * u + b3 * res)
-        return carry
-
-    for m in p_copies:
-        m.wait()
-    lax.fori_loop(0, 4, third, 0)
+    coef = (fx, fym, fyp, fzm, fzp, inv)
+    u0 = reader(par, u_ref, a_ref, None, y_ref, ca_ref)
+    u1_held = ((u1_out, 4, 6), (u1_far, 6, 9))
+    r1_held = ((r_out, 4, 5), (r_far, 5, 8))
+    r2_held = ((r_out.at[1:2], 5, 6), (r_far.at[1:2], 6, 7))
+    u2_held = ((u2_out, 5, 7), (u2_far, 7, 8))
+    for e in (8, 7, 6, 5, 4):
+        step_one(coef, u0, e, r1_held, u1_held)
+    for e in (7, 6, 5):
+        step_two(coef, stored(*u1_held), stored(*r1_held), e, r2_held, u2_held)
+    step_three(coef, p_ref, u0, stored(*u1_held), stored(*u2_held), stored(*r2_held), 6, plane_of(par, 3), done_ref, 0)
+
+
+def far_kernel(meta, p_ref, fx, fym, fyp, fzm, fzp, inv, u_ref, b_ref, y_ref, cb_ref, u1_in, r_in, u2_in, done_ref,
+               out_ref, u1_far, r_far, u2_far):
+    par = meta[0]
+    coef = (fx, fym, fyp, fzm, fzp, inv)
+    u0 = reader(par, u_ref, None, b_ref, y_ref, None, cb_ref)
+    u1_new = ((u1_far, 1, 4),)
+    u1 = stored(*u1_new, (u1_in, 4, 6))
+    r1_new = ((r_far, 2, 4),)
+    r1 = stored(*r1_new, (r_in, 4, 5))
+    r2_new = ((r_far.at[2:4], 3, 5),)
+    r2 = stored(*r2_new, (r_in.at[1:2], 5, 6))
+    u2_new = ((u2_far, 2, 5),)
+    u2 = stored(*u2_new, (u2_in, 5, 7))
+    for e in (1, 2, 3):
+        step_one(coef, u0, e, r1_new, u1_new)
+    for e in (2, 3, 4):
+        step_two(coef, u1, r1, e, r2_new, u2_new)
+    for e in (3, 4, 5):
+        x = plane_of(par, e - 3)
+        step_three(coef, p_ref, u0, u1, u2, r2, e, x, out_ref, x)
+    out_ref[plane_of(par, 3)] = done_ref[0]
 
 
 def shape(*dims, kind=F32):
@@ -486,10 +503,10 @@
         out_specs=(VM,) * 5 + (ANY,) * 4,
         scratch_shapes=[pltpu.VMEM((4, 64, 1024), F32), pltpu.VMEM((4, 64, 1024), F32), pltpu.VMEM((8, 1024), F32),
                         pltpu.SemaphoreType.DMA((22,))],
-        compiler_params=grant(8),
+        compiler_params=grant(60),
         cost_estimate=pl.CostEstimate(flops=4000000, bytes_accessed=5000000, transcendentals=0),
         name="voltages",
-    )(meta, facet_counts, potential, conductivity, intra, extra, gap_partner, gap_cond)
+    )(meta, facet_counts, potential, conductivity, intra, extra, gap_partner.T, gap_cond.T)
 
     below, above, far = on_mem(send_up, ring(1)), on_mem(send_down, ring(3)), on_mem(cells, ring(2))
     early_b, early_a = to_b(send_b), to_a(send_a)
@@ -511,10 +528,20 @@
             in_specs=[facet_rows, state_block, pl.BlockSpec((10, 40, 128), lambda i, *_: (0, 0, 0))],
             out_specs=(state_block, facet_rows),
         ),
-        compiler_params=grant(12),
+        compiler_params=grant(60),
         cost_estimate=pl.CostEstimate(flops=16000000, bytes_accessed=7300000, transcendentals=2600000),
         name="ionic",
     )(facet_counts, cell_type, volt, ion_states, rates)
+
+    source, count = pl.pallas_call(
+        scatter_kernel,
+        out_shape=(shape(4, 64, 1024), shape(4, 64, 1024)),
+        in_specs=[VM] * 4,
+        out_specs=(VM, VM),
+        compiler_params=grant(8),
+        cost_estimate=pl.CostEstimate(flops=800000000, bytes_accessed=2300000, transcendentals=0),
+        name="scatter",
+    )(ion, act, intra, extra)
 
     y_early, table, more_a, more_b = pl.pallas_call(
         early_edge_kernel,
@@ -524,71 +551,79 @@
         compiler_params=grant(6),
         cost_estimate=pl.CostEstimate(flops=300000, bytes_accessed=1000000, transcendentals=0),
         name="early_edges",
-    )(meta, below, above, far, cells, ion)
+    )(meta, below, above, far, cells, source)
     more_b, more_a = to_b(more_b), to_a(more_a)
 
-    source, count = pl.pallas_call(
-        scatter_kernel,
+    w, k = pl.pallas_call(
+        prepare_kernel,
         out_shape=(shape(4, 64, 1024), shape(4, 64, 1024)),
-        in_specs=[VM] * 4 + [ANY],
+        in_specs=[SM] + [VM] * 7,
         out_specs=(VM, VM),
-        compiler_params=grant(8),
-        cost_estimate=pl.CostEstimate(flops=800000000, bytes_accessed=2300000, transcendentals=0),
-        name="scatter",
-    )(ion, act, intra, extra, table)
+        compiler_params=grant(20),
+        cost_estimate=pl.CostEstimate(flops=16000000, bytes_accessed=8000000, transcendentals=0),
+        name="prepare",
+    )(meta, potential, conductivity, early_a, early_b, y_early, source, count)
 
     u, u_a, u_b, u_up, u_down, membrane = pl.pallas_call(
-        first_kernel,
-        out_shape=(shape(4, 64, 1024), shape(3, 72, 1024), shape(3, 72, 1024), shape(4, 8, 1024),
+        gap_kernel,
+        out_shape=(shape(4, 64, 1024), shape(3, 64, 1024), shape(3, 64, 1024), shape(4, 8, 1024),
                    shape(4, 8, 1024), shape(128, 128)),
-        in_specs=[SM, HBM, HBM] + [ANY] * 3 + [VM] * 9,
+        in_specs=[SM] + [VM] * 9,
         out_specs=(VM,) * 6,
-        scratch_shapes=[pltpu.VMEM((6, 72, 1024), F32), pltpu.VMEM((6, 72, 1024), F32),
-                        pltpu.VMEM((256, 128), F32), pltpu.SemaphoreType.DMA((20,))],
-        compiler_params=grant(16),
-        cost_estimate=pl.CostEstimate(flops=16000000, bytes_accessed=8000000, transcendentals=0),
-        name="first",
-    )(meta, potential, conductivity, early_a, early_b, y_early, table, more_a, more_b, part_lane, cond_lane,
-      ion, act, source, count)
-
+        scratch_shapes=[pltpu.VMEM((256, 128), F32)],
+        compiler_params=grant(12),
+        cost_estimate=pl.CostEstimate(flops=1000000, bytes_accessed=5000000, transcendentals=0),
+        name="gap",
+    )(meta, table, more_a, more_b, part_lane, cond_lane, ion, act, w, k)
+
+    late_b = to_b(u_b)
     low_rows = on_mem(u_up, [(i, i + 1) for i in range(3)])
     high_rows = on_mem(u_down, [(i + 1, i) for i in range(3)])
+    late_a = to_a(u_a)
 
     big = lambda n: pltpu.VMEM((n, 72, 1024), F32)
     operator = pl.pallas_call(
         operator_kernel,
         out_shape=(shape(9, 72, 1024),) + (shape(8, 72, 1024),) * 5,
-        in_specs=[SM, HBM] + [ANY] * 6,
+        in_specs=[SM] + [VM] * 6 + [ANY],
         out_specs=(VM,) * 6,
-        scratch_shapes=[big(10), pltpu.SemaphoreType.DMA((18,))],
-        compiler_params=grant(20),
+        compiler_params=grant(22),
         cost_estimate=pl.CostEstimate(flops=16000000, bytes_accessed=17000000, transcendentals=0),
         name="operator",
     )(meta, conductivity, early_a, early_b, y_early, more_a, more_b, u_up)
 
-    y_late, u_a, u_b = pl.pallas_call(
+    y_late, corner_a, corner_b = pl.pallas_call(
         late_edge_kernel,
-        out_shape=(shape(4, 8, 1024), shape(3, 72, 1024), shape(3, 72, 1024)),
-        in_specs=[SM, VM, VM, ANY, ANY],
-        out_specs=(VM, ANY, ANY),
-        input_output_aliases={3: 1, 4: 2},
-        scratch_shapes=[pltpu.SemaphoreType.DMA((6,))],
+        out_shape=(shape(4, 8, 1024), shape(2, 8, 1024), shape(2, 8, 1024)),
+        in_specs=[SM, VM, VM, ANY],
+        out_specs=(VM,) * 3,
         compiler_params=grant(4),
         cost_estimate=pl.CostEstimate(flops=100000, bytes_accessed=500000, transcendentals=0),
         name="late_edges",
-    )(meta, low_rows, high_rows, u_a, u_b)
-    late_b, late_a = to_b(u_b), to_a(u_a)
+    )(meta, low_rows, high_rows, operator[-1])
+    corner_b, corner_a = to_b(corner_b), to_a(corner_a)
+
+    u1, r, u2, done = pl.pallas_call(
+        near_kernel,
+        out_shape=(shape(2, 72, 1024), shape(2, 72, 1024), shape(2, 72, 1024), shape(1, 64, 1024)),
+        in_specs=[SM] + [VM] * 11,
+        out_specs=(VM,) * 4,
+        scratch_shapes=[big(3), big(3), big(1)],
+        compiler_params=grant(30),
+        cost_estimate=pl.CostEstimate(flops=25000000, bytes_accessed=10000000, transcendentals=0),
+        name="near",
+    )(meta, potential, *operator, u, late_a, y_late, corner_a)
 
     potential_next = pl.pallas_call(
-        sweep_kernel,
+        far_kernel,
         out_shape=shape(4, 64, 1024),
-        in_specs=[SM, HBM] + [VM] * 6 + [ANY] * 4,
+        in_specs=[SM] + [VM] * 15,
         out_specs=VM,
-        scratch_shapes=[big(10), big(9), big(8), big(9), pltpu.VMEM((4, 64, 1024), F32), pltpu.SemaphoreType.DMA((18,))],
+        scratch_shapes=[big(3), big(4), big(3)],
         compiler_params=grant(30),
-        cost_estimate=pl.CostEstimate(flops=50000000, bytes_accessed=10000000, transcendentals=0),
-        name="sweeps",
-    )(meta, potential, *operator, u, late_a, late_b, y_late)
+        cost_estimate=pl.CostEstimate(flops=25000000, bytes_accessed=10000000, transcendentals=0),
+        name="far",
+    )(meta, potential, *operator, u, late_b, y_late, corner_b, u1, r, u2, done)
     return potential_next, states_next, membrane.reshape(16384)
 
 

time: 80 us -> 68.1 us (0.85); the launches traced: 78.6 us -> 67.6 us
  waiting for transfers between devices: 15.3 us -> 4.91 us
  local copies, waits for them, and re-layouts: 8.32 us -> 2.6 us
  other arithmetic: 0.09 us -> 2.07 us
  Pallas kernels: 30.3 us -> 32 us
  starting transfers between devices: 23.6 us -> 25 us
    ppermute x2 -> x4, waiting for transfers between devices: 10.7 us -> 0.16 us  [the longest x2 0.16 us: per_device(): corner_b, corner_a = (to_b(corner_b), to_a(corner_a))]
    unnamed x34 -> x20, local copies, waits for them, and re-layouts: 8.11 us -> 1.01 us
    ppermute x2 -> x4, starting transfers between devices: 2.12 us -> 6.95 us  [the longest x2 4.22 us: per_device(): corner_b, corner_a = (to_b(corner_b), to_a(corner_a))]
    ppermute x5, starting transfers between devices: 12.4 us -> 9.18 us  [per_device(): on_mem = lambda x, pairs: lax.ppermute(x, 'mem', pairs)]
    pallas_call x1, Pallas kernels: 3.38 us -> 5.78 us  [per_device(): pl.pallas_call(gather_kernel, out_shape=(shape(128, 128), shape(1, 128),...]
    pallas_call x3 -> x5, Pallas kernels: 15.2 us -> 12.9 us  [the longest x1 4.32 us: per_device(): pl.pallas_call(far_kernel, out_shape=shape(4, 64, 1024), in_specs=[SM] +...]
    pallas_call x1, Pallas kernels: 4.28 us -> 6.11 us  [per_device(): pl.pallas_call(ionic_kernel, out_shape=(shape(40, 16384), shape(128, 128)...]
  transfers between devices with their start and end apart: 11 -> 13, of which waited for: 4 -> 3; matrix products, arithmetic and copies ran while one was open for 0% -> 4% of each run, Pallas kernels for 15% -> 30%
where the time goes in v4:
time: 68.1 us; the launch traced here: 67.6 us
  Pallas kernels  32 us (47%)
  starting transfers between devices  25 us (37%)
  waiting for transfers between devices  4.91 us (7%)
  local copies, waits for them, and re-layouts  2.6 us (4%)
  other arithmetic  2.07 us (3%)
  between operations  0.94 us (1%)
    ppermute x5, starting transfers between devices, per_device(): on_mem = lambda x, pairs: lax.ppermute(x, 'mem', pairs)  9.18 us
    ppermute x2, starting transfers between devices, per_device(): early_b, early_a = (to_b(send_b), to_a(send_a))  6.39 us
    pallas_call x1, Pallas kernels, per_device(): pl.pallas_call(ionic_kernel, out_shape=(shape(40, 16384), shape(128, 128)...  6.11 us
    pallas_call x1, Pallas kernels, per_device(): pl.pallas_call(gather_kernel, out_shape=(shape(128, 128), shape(1, 128),...  5.78 us
    pallas_call x1, Pallas kernels, per_device(): pl.pallas_call(far_kernel, out_shape=shape(4, 64, 1024), in_specs=[SM] +...  4.32 us
    ppermute x2, starting transfers between devices, per_device(): corner_b, corner_a = (to_b(corner_b), to_a(corner_a))  4.22 us
    pallas_call x1, Pallas kernels, per_device(): pl.pallas_call(operator_kernel, out_shape=(shape(9, 72, 1024),) + (shape(...  3.41 us
    pallas_call x1, Pallas kernels, per_device(): pl.pallas_call(near_kernel, out_shape=(shape(2, 72, 1024), shape(2, 72, 1...  3.37 us
  transfers between devices with their start and end apart: 13, of which 3 were waited for; matrix products, arithmetic and copies ran while one was open for 4% of the time, Pallas kernels for 30%

profile of v4, /device:TPU:6, one launch (start us, length us, event | category | flops | bytes accessed | tf_op | source)
XLA Modules:
  0.0 67.6 jit_solution(5990796119557642462)
XLA Ops:
  1.3 5.8 %voltages.1 = (f32[128,128]{1,0:T(8,128)}, f32[1,128]{1,0:T(1,128)}, f32[128,128]{1,0:T(8,128)}, s32[8,128]{1,0:T(8,128)}, f32[8,128]{1,0:T(8,128)}, /*index=5*/...) custom-call(s32[4]{0:T(128)} %pad_add_fusion.meta, s32[64]{0:T(128)} %cnt.3, ...), custom_call_target="tpu_custom_call" | custom-call | flops 4000000 | bytes 5000000 | tf_op jit(solution)/shard_map/voltages/pallas_call | solution.py:498
  7.1 6.3 %collective-permute-start.1 = (f32[4,64,1024]{2,1,0:T(8,128)}, f32[4,64,1024]{2,1,0:T(8,128)S(1)}, u32[]{:S(2)}, u32[]{:S(2)}) collective-permute-start(f32[4,64,1024]{2,1,0:T(8,128)} %get-tuple-element.42), channel_id=1, source_target_pairs={{4,8},{8,4},{12,16},{16,12},{20,24},{24,20},{28,32},{32,28},{36,40... | collective-permute-start | bytes 3145736 | tf_op jit(solution)/shard_map/ppermute | solution.py:512
  13.5 3.3 %collective-permute-start.4 = (f32[1,128]{1,0:T(1,128)}, f32[1,128]{1,0:T(1,128)S(1)}, u32[]{:S(2)}, u32[]{:S(2)}) collective-permute-start(f32[1,128]{1,0:T(1,128)} %get-tuple-element.45.cell_ref), channel_id=1, source_target_pairs={{0,2},{1,3},{2,0},{3,1},{4,6},{5,7},{6,4},{7,5},{8,10},{9,11},{10,... | collective-permute-start | bytes 1544 | tf_op jit(solution)/shard_map/ppermute | solution.py:490
  16.7 0.7 %collective-permute-start.2 = (f32[9,8,1024]{2,1,0:T(8,128)}, f32[9,8,1024]{2,1,0:T(8,128)S(1)}, u32[]{:S(2)}, u32[]{:S(2)}) collective-permute-start(f32[9,8,1024]{2,1,0:T(8,128)} %get-tuple-element.43), channel_id=1, source_target_pairs={{0,1},{1,2},{2,3},{3,0},{4,5},{5,6},{6,7},{7,4},{8,9},{9,10},{10,1... | collective-permute-start | bytes 884744 | tf_op jit(solution)/shard_map/ppermute | solution.py:490
  17.4 2.6 %collective-permute-start.3 = (f32[9,8,1024]{2,1,0:T(8,128)}, f32[9,8,1024]{2,1,0:T(8,128)S(1)}, u32[]{:S(2)}, u32[]{:S(2)}) collective-permute-start(f32[9,8,1024]{2,1,0:T(8,128)} %get-tuple-element.44), channel_id=1, source_target_pairs={{0,3},{1,0},{2,1},{3,2},{4,7},{5,4},{6,5},{7,6},{8,11},{9,8},{10,9... | collective-permute-start | bytes 884744 | tf_op jit(solution)/shard_map/ppermute | solution.py:490
  20.0 0.7 %broadcast_multiply_fusion = f32[3,40]{1,0:T(4,128)S(1)} fusion(f32[3,40]{1,0:T(4,128)} %param.18, f32[40]{0:T(128)} %param.19), kind=kLoop, calls=%fused_computation | loop fusion | flops 120 | bytes 1120 | tf_op jit(solution)/shard_map/mul | solution.py:516
  20.7 0.8 %log_multiply_fusion = (f32[1,40]{1,0:T(1,128)S(1)}, f32[1,40]{1,0:T(1,128)S(1)}, f32[1,40]{1,0:T(1,128)S(1)}, f32[1,40]{1,0:T(1,128)S(1)}) fusion(f32[2,40]{1,0:T(2,128)} %param.16, f32[2,40]{1,0:T(2,128)} %param.17), kind=kLoop, calls=%fused_computation.2 | loop fusion | flops 160 | bytes 1280 | tf_op jit(solution)/shard_map/log2 | solution.py:515
  21.4 0.8 %concatenate.3 = f32[10,40]{1,0:T(8,128)S(1)} concatenate(f32[1,40]{1,0:T(1,128)S(1)} %get-tuple-element.83, f32[1,40]{1,0:T(1,128)S(1)} %get-tuple-element.80, f32[1,40]{1,0:T(1,128)S(1)} %get-tuple-element.84, f32[1,40]{1,0:T(1,128)S(1)} %get-tuple-element.79, f32[3,40]{1,0:T(4,128)} %param.18, f32[3,40]{1,0:T(4,128)S(1)} %broadcast_multiply_fusion), dimensions={0} | concatenate | bytes 3200 | tf_op jit(solution)/shard_map/concatenate | solution.py:514
  22.2 0.8 %broadcast_in_dim.2.rate_ref = f32[10,40,128]{2,1,0:T(8,128)} broadcast(f32[10,40]{1,0:T(8,128)S(1)} %concatenate.3), dimensions={0,1} | broadcast | bytes 206400 | tf_op jit(solution)/shard_map/broadcast_in_dim | solution.py:517
  23.0 6.1 %ionic.1 = (f32[40,16384]{1,0:T(8,128)}, f32[128,128]{1,0:T(8,128)}) custom-call(s32[64]{0:T(128)} %cnt.3, s32[64]{0:T(128)} %typ.1, f32[128,128]{1,0:T(8,128)} %get-tuple-element.46.volt_ref, f32[40,16384]{1,0:T(8,128)} %st_ref.1, f32[10,40,128]{2,1,0:T(8,128)} %broadcast_in_dim.2.rate_ref), custom_call_target="tpu_custom_call" | custom-call | flops 16000000 | bytes 7300000 | tf_op jit(solution)/shard_map/ionic/pallas_call | solution.py:522
  29.2 1.0 %copy-done.5 = f32[128,128]{1,0:T(8,128)S(1)} copy-done((f32[128,128]{1,0:T(8,128)S(1)}, f32[128,128]{1,0:T(8,128)}, u32[]{:S(2)}) %copy-start.5) | copy-done | bytes 65560
  30.2 3.3 %scatter.1 = (f32[4,64,1024]{2,1,0:T(8,128)S(1)}, f32[4,64,1024]{2,1,0:T(8,128)S(1)}) custom-call(f32[128,128]{1,0:T(8,128)S(1)} %copy-done.5, f32[128,128]{1,0:T(8,128)S(1)} %copy-done.4, s32[128,128]{1,0:T(8,128)S(1)} %bitcast.10, s32[128,128]{1,0:T(8,128)S(1)} %bitcast.12), custom_call_target="tpu_custom_call" | custom-call | flops 800000000 | bytes 2300000 | tf_op jit(solution)/shard_map/scatter/pallas_call | solution.py:536
  34.2 2.4 %collective-permute-start.6 = (f32[3,8,1024]{2,1,0:T(8,128)S(1)}, f32[3,8,1024]{2,1,0:T(8,128)S(1)}, u32[]{:S(2)}, u32[]{:S(2)}) collective-permute-start(f32[3,8,1024]{2,1,0:T(8,128)S(1)} %get-tuple-element.52), channel_id=1, source_target_pairs={{4,8},{8,4},{12,16},{16,12},{20,24},{24,20},{28,32},{32,28},{36,40... | collective-permute-start | bytes 294920 | tf_op jit(solution)/shard_map/ppermute | solution.py:555
  36.7 3.0 %prepare.1 = (f32[4,64,1024]{2,1,0:T(8,128)S(1)}, f32[4,64,1024]{2,1,0:T(8,128)S(1)}) custom-call(s32[4]{0:T(128)S(1)} %copy-done.6, f32[4,64,1024]{2,1,0:T(8,128)S(1)} %copy-done, f32[4,64,1024]{2,1,0:T(8,128)S(1)} %copy-done.1, f32[4,64,1024]{2,1,0:T(8,128)S(1)} %collective-permute-done.a_ref, f32[4,64,1024]{2,1,0:T(8,128)S(1)} %collective-permute-done.1.b_ref, ...), custom_call_target="tpu_custom_call" | custom-call | flops 16000000 | bytes 8000000 | tf_op jit(solution)/shard_map/prepare/pallas_call | solution.py:557
  39.7 2.6 %collective-permute-done.6.tb_ref.cb_ref = f32[3,8,1024]{2,1,0:T(8,128)S(1)} collective-permute-done((f32[3,8,1024]{2,1,0:T(8,128)S(1)}, f32[3,8,1024]{2,1,0:T(8,128)S(1)}, u32[]{:S(2)}, u32[]{:S(2)}) %collective-permute-start.6) | collective-permute-done | bytes 98336 | tf_op jit(solution)/shard_map/ppermute | solution.py:555
  42.2 1.6 %gap.1 = (f32[4,64,1024]{2,1,0:T(8,128)S(1)}, f32[3,64,1024]{2,1,0:T(8,128)S(1)}, f32[3,64,1024]{2,1,0:T(8,128)S(1)}, f32[4,8,1024]{2,1,0:T(8,128)S(1)}, f32[4,8,1024]{2,1,0:T(8,128)S(1)}, /*index=5*/f32[128,128]{1,0:T(8,128)}) custom-call(s32[4]{0:T(128)S(1)} %copy-done.6, f32[8,128]{1,0:T(8,128)S(1)} %get-tuple-element.53.table_ref, ...), custom_call_target="tpu_custom_call" | custom-call | flops 1000000 | bytes 5000000 | tf_op jit(solution)/shard_map/gap/pallas_call | solution.py:567
  43.9 2.7 %collective-permute-start.7 = (f32[3,64,1024]{2,1,0:T(8,128)S(1)}, f32[3,64,1024]{2,1,0:T(8,128)S(1)}, u32[]{:S(2)}, u32[]{:S(2)}) collective-permute-start(f32[3,64,1024]{2,1,0:T(8,128)S(1)} %get-tuple-element.67), channel_id=1, source_target_pairs={{4,8},{8,4},{12,16},{16,12},{20,24},{24,20},{28,32},{32,28},{36,40... | collective-permute-start | bytes 2359304 | tf_op jit(solution)/shard_map/ppermute | solution.py:579
  46.6 1.4 %collective-permute-start.8 = (f32[4,8,1024]{2,1,0:T(8,128)S(1)}, f32[4,8,1024]{2,1,0:T(8,128)S(1)}, u32[]{:S(2)}, u32[]{:S(2)}) collective-permute-start(f32[4,8,1024]{2,1,0:T(8,128)S(1)} %get-tuple-element.59.after), channel_id=1, source_target_pairs={{0,1},{1,2},{2,3},{4,5},{5,6},{6,7},{8,9},{9,10},{10,11},{12,13},{... | collective-permute-start | bytes 393224 | tf_op jit(solution)/shard_map/ppermute | solution.py:490
  48.0 1.3 %collective-permute-start.9 = (f32[4,8,1024]{2,1,0:T(8,128)S(1)}, f32[4,8,1024]{2,1,0:T(8,128)S(1)}, u32[]{:S(2)}, u32[]{:S(2)}) collective-permute-start(f32[4,8,1024]{2,1,0:T(8,128)S(1)} %get-tuple-element.68), channel_id=1, source_target_pairs={{1,0},{2,1},{3,2},{5,4},{6,5},{7,6},{9,8},{10,9},{11,10},{13,12},{... | collective-permute-start | bytes 393224 | tf_op jit(solution)/shard_map/ppermute | solution.py:490
  49.3 3.4 %operator.1 = (f32[9,72,1024]{2,1,0:T(8,128)S(1)}, f32[8,72,1024]{2,1,0:T(8,128)S(1)}, f32[8,72,1024]{2,1,0:T(8,128)S(1)}, f32[8,72,1024]{2,1,0:T(8,128)S(1)}, f...) custom-call(s32[4]{0:T(128)S(1)} %copy-done.6, f32[4,64,1024]{2,1,0:T(8,128)S(1)} %copy-done.1, ...), custom_call_target="tpu_custom_call" | custom-call | flops 16000000 | bytes 17000000 | tf_op jit(solution)/shard_map/operator/pallas_call | solution.py:585
  52.7 2.2 %collective-permute-done.9.above_ref = f32[4,8,1024]{2,1,0:T(8,128)S(1)} collective-permute-done((f32[4,8,1024]{2,1,0:T(8,128)S(1)}, f32[4,8,1024]{2,1,0:T(8,128)S(1)}, u32[]{:S(2)}, u32[]{:S(2)}) %collective-permute-start.9) | collective-permute-done | bytes 131104 | tf_op jit(solution)/shard_map/ppermute | solution.py:490
  55.6 4.1 %collective-permute-start.10 = (f32[2,8,1024]{2,1,0:T(8,128)S(1)}, f32[2,8,1024]{2,1,0:T(8,128)S(1)}, u32[]{:S(2)}, u32[]{:S(2)}) collective-permute-start(f32[2,8,1024]{2,1,0:T(8,128)S(1)} %get-tuple-element.70), channel_id=1, source_target_pairs={{4,8},{8,4},{12,16},{16,12},{20,24},{24,20},{28,32},{32,28},{36,40... | collective-permute-start | bytes 196616 | tf_op jit(solution)/shard_map/ppermute | solution.py:604
  59.7 3.4 %near.1 = (f32[2,72,1024]{2,1,0:T(8,128)S(1)}, f32[2,72,1024]{2,1,0:T(8,128)S(1)}, f32[2,72,1024]{2,1,0:T(8,128)S(1)}, f32[1,64,1024]{2,1,0:T(8,128)S(1)}) custom-call(s32[4]{0:T(128)S(1)} %copy-done.6, f32[4,64,1024]{2,1,0:T(8,128)S(1)} %copy-done, f32[9,72,1024]{2,1,0:T(8,128)S(1)} %get-tuple-element.60.fx, f32[8,72,1024]{2,1,0:T(8,128)S(1)} %get-tuple-element.61.fym, ...), custom_call_target="tpu_custom_call" | custom-call | flops 25000000 | bytes 10000000 | tf_op jit(solution)/shard_map/near/pallas_call | solution.py:606
  63.2 4.3 %far.1 = f32[4,64,1024]{2,1,0:T(8,128)} custom-call(s32[4]{0:T(128)S(1)} %copy-done.6, f32[4,64,1024]{2,1,0:T(8,128)S(1)} %copy-done, f32[9,72,1024]{2,1,0:T(8,128)S(1)} %get-tuple-element.60.fx, f32[8,72,1024]{2,1,0:T(8,128)S(1)} %get-tuple-element.61.fym, f32[8,72,1024]{2,1,0:T(8,128)S(1)} %get-tuple-element.62.fyp, ...), custom_call_target="tpu_custom_call" | custom-call | flops 25000000 | bytes 10000000 | tf_op jit(solution)/shard_map/far/pallas_call | solution.py:617
  (37 shorter events, 2.3 us)
Async XLA Ops:
  7.1 29.6 %collective-permute-start = (f32[4,64,1024]{2,1,0:T(8,128)}, f32[4,64,1024]{2,1,0:T(8,128)S(1)}, u32[]{:S(2)}, u32[]{:S(2)}) collective-permute-start(f32[4,64,1024]{2,1,0:T(8,128)} %get-tuple-element.41), channel_id=1, source_target_pairs={{0,4},{4,0},{8,12},{12,8},{16,20},{20,16},{24,28},{28,24},{32,36},... | collective-permute-start | bytes 3145736 | tf_op jit(solution)/shard_map/ppermute | solution.py:512
  7.1 29.5 %collective-permute-start.1 = (f32[4,64,1024]{2,1,0:T(8,128)}, f32[4,64,1024]{2,1,0:T(8,128)S(1)}, u32[]{:S(2)}, u32[]{:S(2)}) collective-permute-start(f32[4,64,1024]{2,1,0:T(8,128)} %get-tuple-element.42), channel_id=1, source_target_pairs={{4,8},{8,4},{12,16},{16,12},{20,24},{24,20},{28,32},{32,28},{36,40... | collective-permute-start | bytes 3145736 | tf_op jit(solution)/shard_map/ppermute | solution.py:512
  13.5 20.0 %collective-permute-start.4 = (f32[1,128]{1,0:T(1,128)}, f32[1,128]{1,0:T(1,128)S(1)}, u32[]{:S(2)}, u32[]{:S(2)}) collective-permute-start(f32[1,128]{1,0:T(1,128)} %get-tuple-element.45.cell_ref), channel_id=1, source_target_pairs={{0,2},{1,3},{2,0},{3,1},{4,6},{5,7},{6,4},{7,5},{8,10},{9,11},{10,... | collective-permute-start | bytes 1544 | tf_op jit(solution)/shard_map/ppermute | solution.py:490
  16.7 16.7 %collective-permute-start.2 = (f32[9,8,1024]{2,1,0:T(8,128)}, f32[9,8,1024]{2,1,0:T(8,128)S(1)}, u32[]{:S(2)}, u32[]{:S(2)}) collective-permute-start(f32[9,8,1024]{2,1,0:T(8,128)} %get-tuple-element.43), channel_id=1, source_target_pairs={{0,1},{1,2},{2,3},{3,0},{4,5},{5,6},{6,7},{7,4},{8,9},{9,10},{10,1... | collective-permute-start | bytes 884744 | tf_op jit(solution)/shard_map/ppermute | solution.py:490
  17.4 16.1 %collective-permute-start.3 = (f32[9,8,1024]{2,1,0:T(8,128)}, f32[9,8,1024]{2,1,0:T(8,128)S(1)}, u32[]{:S(2)}, u32[]{:S(2)}) collective-permute-start(f32[9,8,1024]{2,1,0:T(8,128)} %get-tuple-element.44), channel_id=1, source_target_pairs={{0,3},{1,0},{2,1},{3,2},{4,7},{5,4},{6,5},{7,6},{8,11},{9,8},{10,9... | collective-permute-start | bytes 884744 | tf_op jit(solution)/shard_map/ppermute | solution.py:490
  23.0 6.1 %copy-start.2 = (s32[16384]{0:T(1024)S(1)}, s32[16384]{0:T(1024)}, u32[]{:S(2)}) copy-start(s32[16384]{0:T(1024)} %param.21) | copy-start | bytes 196612
  23.0 6.2 %copy-start.3 = (s32[16384]{0:T(1024)S(1)}, s32[16384]{0:T(1024)}, u32[]{:S(2)}) copy-start(s32[16384]{0:T(1024)} %param.22) | copy-start | bytes 196612
  23.0 6.2 %copy-start.4 = (f32[128,128]{1,0:T(8,128)S(1)}, f32[128,128]{1,0:T(8,128)}, u32[]{:S(2)}) copy-start(f32[128,128]{1,0:T(8,128)} %get-tuple-element.48.act_ref) | copy-start | bytes 196612
  23.0 10.5 %copy-start.6 = (s32[4]{0:T(128)S(1)}, s32[4]{0:T(128)}, u32[]{:S(2)}) copy-start(s32[4]{0:T(128)} %pad_add_fusion.meta) | copy-start | bytes 52
  23.0 10.5 %copy-start.9 = (f32[1,128]{1,0:T(1,128)S(1)}, f32[1,128]{1,0:T(1,128)}, u32[]{:S(2)}) copy-start(f32[1,128]{1,0:T(1,128)} %get-tuple-element.45.cell_ref) | copy-start | bytes 1540
  29.2 7.5 %copy-start = (f32[4,64,1024]{2,1,0:T(8,128)S(1)}, f32[4,64,1024]{2,1,0:T(8,128)}, u32[]{:S(2)}) copy-start(f32[4,64,1024]{2,1,0:T(8,128)} %p_ref.5) | copy-start | bytes 3145732
  29.2 7.5 %copy-start.1 = (f32[4,64,1024]{2,1,0:T(8,128)S(1)}, f32[4,64,1024]{2,1,0:T(8,128)}, u32[]{:S(2)}) copy-start(f32[4,64,1024]{2,1,0:T(8,128)} %c_ref.3) | copy-start | bytes 3145732
  29.2 1.0 %copy-start.5 = (f32[128,128]{1,0:T(8,128)S(1)}, f32[128,128]{1,0:T(8,128)}, u32[]{:S(2)}) copy-start(f32[128,128]{1,0:T(8,128)} %get-tuple-element.47.ion_ref) | copy-start | bytes 196612
  34.1 5.6 %collective-permute-start.5 = (f32[3,8,1024]{2,1,0:T(8,128)S(1)}, f32[3,8,1024]{2,1,0:T(8,128)S(1)}, u32[]{:S(2)}, u32[]{:S(2)}) collective-permute-start(f32[3,8,1024]{2,1,0:T(8,128)S(1)} %get-tuple-element.51), channel_id=1, source_target_pairs={{0,4},{4,0},{8,12},{12,8},{16,20},{20,16},{24,28},{28,24},{32,36},... | collective-permute-start | bytes 294920 | tf_op jit(solution)/shard_map/ppermute | solution.py:555
  34.2 8.0 %collective-permute-start.6 = (f32[3,8,1024]{2,1,0:T(8,128)S(1)}, f32[3,8,1024]{2,1,0:T(8,128)S(1)}, u32[]{:S(2)}, u32[]{:S(2)}) collective-permute-start(f32[3,8,1024]{2,1,0:T(8,128)S(1)} %get-tuple-element.52), channel_id=1, source_target_pairs={{4,8},{8,4},{12,16},{16,12},{20,24},{24,20},{28,32},{32,28},{36,40... | collective-permute-start | bytes 294920 | tf_op jit(solution)/shard_map/ppermute | solution.py:555
  36.6 5.6 %copy-start.7 = (s32[8,128]{1,0:T(8,128)S(1)}, s32[8,128]{1,0:T(8,128)}, u32[]{:S(2)}) copy-start(s32[8,128]{1,0:T(8,128)} %get-tuple-element.54.part_ref) | copy-start | bytes 12292
  36.7 5.6 %copy-start.8 = (f32[8,128]{1,0:T(8,128)S(1)}, f32[8,128]{1,0:T(8,128)}, u32[]{:S(2)}) copy-start(f32[8,128]{1,0:T(8,128)} %get-tuple-element.55.cond_ref) | copy-start | bytes 12292
  43.9 15.9 %collective-permute-start.11 = (f32[3,64,1024]{2,1,0:T(8,128)S(1)}, f32[3,64,1024]{2,1,0:T(8,128)S(1)}, u32[]{:S(2)}, u32[]{:S(2)}) collective-permute-start(f32[3,64,1024]{2,1,0:T(8,128)S(1)} %get-tuple-element.71), channel_id=1, source_target_pairs={{0,4},{4,0},{8,12},{12,8},{16,20},{20,16},{24,28},{28,24},{32,36},... | collective-permute-start | bytes 2359304 | tf_op jit(solution)/shard_map/ppermute | solution.py:582
  43.9 19.4 %collective-permute-start.7 = (f32[3,64,1024]{2,1,0:T(8,128)S(1)}, f32[3,64,1024]{2,1,0:T(8,128)S(1)}, u32[]{:S(2)}, u32[]{:S(2)}) collective-permute-start(f32[3,64,1024]{2,1,0:T(8,128)S(1)} %get-tuple-element.67), channel_id=1, source_target_pairs={{4,8},{8,4},{12,16},{16,12},{20,24},{24,20},{28,32},{32,28},{36,40... | collective-permute-start | bytes 2359304 | tf_op jit(solution)/shard_map/ppermute | solution.py:579
  46.6 6.1 %collective-permute-start.8 = (f32[4,8,1024]{2,1,0:T(8,128)S(1)}, f32[4,8,1024]{2,1,0:T(8,128)S(1)}, u32[]{:S(2)}, u32[]{:S(2)}) collective-permute-start(f32[4,8,1024]{2,1,0:T(8,128)S(1)} %get-tuple-element.59.after), channel_id=1, source_target_pairs={{0,1},{1,2},{2,3},{4,5},{5,6},{6,7},{8,9},{9,10},{10,11},{12,13},{... | collective-permute-start | bytes 393224 | tf_op jit(solution)/shard_map/ppermute | solution.py:490
  48.0 6.9 %collective-permute-start.9 = (f32[4,8,1024]{2,1,0:T(8,128)S(1)}, f32[4,8,1024]{2,1,0:T(8,128)S(1)}, u32[]{:S(2)}, u32[]{:S(2)}) collective-permute-start(f32[4,8,1024]{2,1,0:T(8,128)S(1)} %get-tuple-element.68), channel_id=1, source_target_pairs={{1,0},{2,1},{3,2},{5,4},{6,5},{7,6},{9,8},{10,9},{11,10},{13,12},{... | collective-permute-start | bytes 393224 | tf_op jit(solution)/shard_map/ppermute | solution.py:490
  55.5 4.2 %collective-permute-start.12 = (f32[2,8,1024]{2,1,0:T(8,128)S(1)}, f32[2,8,1024]{2,1,0:T(8,128)S(1)}, u32[]{:S(2)}, u32[]{:S(2)}) collective-permute-start(f32[2,8,1024]{2,1,0:T(8,128)S(1)} %get-tuple-element.72), channel_id=1, source_target_pairs={{0,4},{4,0},{8,12},{12,8},{16,20},{20,16},{24,28},{28,24},{32,36},... | collective-permute-start | bytes 196616 | tf_op jit(solution)/shard_map/ppermute | solution.py:604
  55.6 7.7 %collective-permute-start.10 = (f32[2,8,1024]{2,1,0:T(8,128)S(1)}, f32[2,8,1024]{2,1,0:T(8,128)S(1)}, u32[]{:S(2)}, u32[]{:S(2)}) collective-permute-start(f32[2,8,1024]{2,1,0:T(8,128)S(1)} %get-tuple-element.70), channel_id=1, source_target_pairs={{4,8},{8,4},{12,16},{16,12},{20,24},{24,20},{28,32},{32,28},{36,40... | collective-permute-start | bytes 196616 | tf_op jit(solution)/shard_map/ppermute | solution.py:604

commit v5 on v4

--- a/solution.py
+++ b/solution.py
@@ -1,5 +1,4 @@
 import functools
-import math
 
 import jax
 import jax.numpy as jnp
@@ -8,7 +7,6 @@
 from jax.experimental.pallas import tpu as pltpu
 from jax.sharding import PartitionSpec as P
 
-LOG2E = math.log2(math.e)
 SWEEPS = 4
 F32 = jnp.float32
 BF16 = jnp.bfloat16
@@ -38,6 +36,11 @@
     return lax.broadcasted_iota(jnp.int32, shape, dim)
 
 
+def place():
+    v, mine = lax.axis_index("vol"), lax.axis_index("mem")
+    return v & 1, (v != 0) & (v != lax.axis_size("vol") - 1), mine, v
+
+
 def plane_of(parity, j):
     return j + parity * (3 - 2 * j)
 
@@ -47,15 +50,16 @@
     return row + jnp.where(even, pltpu.roll(row, 127, 1), pltpu.roll(row, 1, 1))
 
 
-def gather_kernel(meta, cnt, p_hbm, c_hbm, in_ref, ex_ref, part_ref, cond_ref,
-                  volt_ref, cell_ref, act_ref, part_out, cond_out, a_hbm, b_hbm, up_hbm, down_hbm,
-                  p_ref, c_ref, note, sem):
-    par = meta[0]
-    loads = begin([(p_hbm.at[x], p_ref.at[x]) for x in range(4)] + [(c_hbm.at[x], c_ref.at[x]) for x in range(4)], sem, 0)
+def gather_kernel(cnt, p_hbm, c_hbm, in_hbm, ex_hbm, part_hbm, cond_hbm, st_hbm,
+                  st_near, volt_hbm, cell_hbm, act_hbm, part_out, cond_out, a_hbm, b_hbm, up_hbm, down_hbm,
+                  p_ref, c_ref, in_ref, ex_ref, part_ref, cond_ref, volt_ref, cell_ref, act_ref, part_two, cond_two,
+                  note, sem):
+    par, has_b, mine, v = place()
+    loads = begin(
+        [(in_hbm, in_ref), (ex_hbm, ex_ref)] + [(p_hbm.at[x], p_ref.at[x]) for x in range(4)]
+        + [(c_hbm.at[x], c_ref.at[x]) for x in range(4)] + [(part_hbm, part_ref), (cond_hbm, cond_ref)], sem, 0)
+    states = begin([(st_hbm.at[:, 4096 * i : 4096 * i + 4096], st_near.at[:, 4096 * i : 4096 * i + 4096]) for i in range(4)], sem, 31)
     twice = iota((8, 128), 1) // 2
-    for src, dst in ((part_ref, part_out), (cond_ref, cond_out)):
-        wide = jnp.concatenate([src[...], src[...]], axis=1)
-        dst[...] = jnp.take_along_axis(wide, twice, axis=1, mode="promise_in_bounds")
     sub = iota((8, 128), 0)
     low = sub < 4
     lane_row = iota((1, 128), 1)
@@ -89,12 +93,14 @@
                     act_ref[at, :] = jnp.where(used, 1.0, 0.0)
         return carry
 
+    loads[0].wait()
+    loads[1].wait()
     for x in range(4):
         if x < 2:
-            loads[x].wait()
+            loads[2 + x].wait()
         lax.fori_loop(4 * x, 4 * x + 4, body, 0, unroll=4)
         if x == 1:
-            for load in loads[2:]:
+            for load in loads[4:]:
                 load.wait()
             copies = []
             for i in range(3):
@@ -105,7 +111,12 @@
             for k, src in enumerate((c_ref, p_ref)):
                 copies.append((src.at[:, 56:64], up_hbm.at[4 * k : 4 * k + 4]))
                 copies.append((src.at[:, 0:8], down_hbm.at[4 * k : 4 * k + 4]))
-            sends = begin(copies, sem, 8)
+            for src, dst in ((part_ref, part_two), (cond_ref, cond_two)):
+                wide = jnp.concatenate([src[...], src[...]], axis=1)
+                dst[...] = jnp.take_along_axis(wide, twice, axis=1, mode="promise_in_bounds")
+            copies += [(part_two, part_out), (cond_two, cond_out)]
+            sends = begin(copies, sem, 12)
+    sends += begin([(volt_ref, volt_hbm), (act_ref, act_hbm)], sem, 26)
     act = act_ref[...]
     total = jnp.sum(jnp.transpose(volt_ref[...] * act), axis=0, keepdims=True)
     count = jnp.sum(jnp.transpose(act), axis=0, keepdims=True)
@@ -113,8 +124,8 @@
     cell_ref[...] = cells
     note[...] = jnp.zeros((8, 1024), F32)
     note[0:1, 0:128] = cells
-    sends += begin([(note, up_hbm.at[8]), (note, down_hbm.at[8])], sem, 20)
-    for send in sends:
+    sends += begin([(note, up_hbm.at[8]), (note, down_hbm.at[8]), (cell_ref, cell_hbm)], sem, 28)
+    for send in sends + states:
         send.wait()
 
 
@@ -125,18 +136,39 @@
     return made
 
 
-def ionic_kernel(cnt, typ, volt_ref, st_ref, rate_ref, out_ref, ion_ref):
-    step = pl.program_id(0)
-    cells = volt_ref.shape[0] // 2
+CHUNKS = 16
+ROOM = 24000000
+
+
+def ionic_kernel(cnt, typ, volt_ref, act_ref, in_ref, ex_ref, scale_ref, slope_ref, cond_ref, rev_ref, st_ref,
+                 out_hbm, ion_ref, s_ref, n_ref, out_ref, flat, rate_ref, sem):
+    width = 16384 // CHUNKS
+    at = lambda i: pl.ds(pl.multiple_of(i * width, width), width)
+    store = lambda i: pltpu.make_async_copy(out_ref.at[:, at(i)], out_hbm.at[:, at(i)], sem.at[i])
+    flat[...] = jnp.zeros((128, 128), F32)
+    logs = jnp.log(scale_ref[...])
+    flat[0:1, 0:40] = slope_ref[0:1]
+    flat[1:2, 0:40] = logs[0:1]
+    flat[2:3, 0:40] = -slope_ref[1:2]
+    flat[3:4, 0:40] = logs[1:2]
+    flat[4:7, 0:40] = cond_ref[...]
+    flat[7:10, 0:40] = cond_ref[...] * rev_ref[...]
+    turned = jnp.transpose(flat[...])
+    for i in range(10):
+        rate_ref[i] = jnp.broadcast_to(turned[0:40, i : i + 1], (40, 128))
     lane = iota((8, 128), 1)
+    row_iota = iota((32, 512), 0)
+    lane_iota = iota((128, 512), 0)
+    low = iota((8, 128), 0) < 4
+    odd_row = (iota((8, 128), 0) & 2) // 2
 
     def body(group, carry):
         rows8 = pl.ds(pl.multiple_of(8 * group, 8), 8)
         volts = volt_ref[rows8, :]
         counts, types, v, active, cols = [], [], [], [], []
         for q in range(4):
-            counts.append(cnt[step * cells + 4 * group + q])
-            types.append(typ[step * cells + 4 * group + q])
+            counts.append(cnt[4 * group + q])
+            types.append(typ[4 * group + q])
         for r in range(8):
             v.append(jnp.broadcast_to(volts[r : r + 1], (8, 128)))
             active.append(lane + (r % 2) * 128 < counts[r // 2])
@@ -149,37 +181,21 @@
                 g, gr = rate_ref[4 + types[q], rows], rate_ref[7 + types[q], rows]
                 for r in (2 * q, 2 * q + 1):
                     st = st_ref[rows, cols[r]]
-                    opening = jnp.exp2(rate[0] * v[r] + rate[1])
-                    closing = jnp.exp2(rate[2] * v[r] + rate[3])
+                    opening = jnp.exp(rate[0] * v[r] + rate[1])
+                    closing = jnp.exp(rate[2] * v[r] + rate[3])
                     total = opening + closing
-                    rec = pl.reciprocal(total, approx=True)
-                    rec = rec * (2.0 - total * rec)
-                    steady = opening * rec
-                    fresh = steady + (st - steady) * jnp.exp2(total * (-0.5 * LOG2E))
+                    steady = opening * inverse(total)
+                    fresh = steady + (st - steady) * jnp.exp(total * -0.5)
                     out_ref[rows, cols[r]] = jnp.where(active[r], fresh, st)
                     w1[r] = g * fresh if k == 0 else w1[r] + g * fresh
                     w2[r] = gr * fresh if k == 0 else w2[r] + gr * fresh
-        act = jnp.concatenate([jnp.where(a, 1.0, 0.0)[0:1] for a in active], axis=0)
+        store(group).start()
+        act = act_ref[rows8, :]
         ion = [jnp.sum(w1[r] * v[r] - w2[r], axis=0, keepdims=True) for r in range(8)]
         val = jnp.concatenate(ion, axis=0) * act
         ion_ref[rows8, :] = val
 
-        return carry
-
-    lax.fori_loop(0, cells // 4, body, 0)
-
-
-def scatter_kernel(ion_ref, act_ref, in_ref, ex_ref, s_ref, n_ref):
-    row_iota = iota((32, 512), 0)
-    lane_iota = iota((128, 512), 0)
-    low = iota((8, 128), 0) < 4
-    odd_row = (iota((8, 128), 0) & 2) // 2
-
-    def body(kk, carry):
-        rows8 = pl.ds(pl.multiple_of(8 * kk, 8), 8)
-        x = kk // 4
-        val = ion_ref[rows8, :]
-        act = act_ref[rows8, :]
+        x = group // 4
         hi = val.astype(BF16).astype(F32)
         lo = val - hi
         mids, lanes = [], []
@@ -202,7 +218,7 @@
                 right = jnp.where(line(lanes[0], lanes[1], s) == lane_iota, 1.0, 0.0).astype(BF16)
                 out = lax.dot_general(left, right, (((1,), (1,)), ((), ())), preferred_element_type=F32)
                 results.append((out[0:32] + out[32:64], out[64:96]))
-            row = pl.ds(pl.multiple_of((2 * (kk % 4) + q) * 8, 8), 8)
+            row = pl.ds(pl.multiple_of((2 * (group % 4) + q) * 8, 8), 8)
             for dst, e, o in ((s_ref, results[0][0], results[1][0]), (n_ref, results[0][1], results[1][1])):
                 for j in range(4):
                     ej, oj = e[8 * j : 8 * j + 8], o[8 * j : 8 * j + 8]
@@ -210,20 +226,22 @@
                     dst[x, row, 256 * j + 128 : 256 * j + 256] = pltpu.roll(jnp.where(low, oj, ej), 4, 0)
         return carry
 
-    lax.fori_loop(0, 16, body, 0, unroll=4)
-
-
-def edge_rows(meta, below, above):
+    lax.fori_loop(0, CHUNKS, body, 0, unroll=2)
+    for i in range(CHUNKS):
+        store(i).wait()
+
+
+def edge_rows(mine, below, above):
     sub = iota((8, 1024), 0)
-    bottom = (sub < 3) & (meta[2] != 3)
-    top = (sub >= 5) & (meta[2] != 0)
+    bottom = (sub < 3) & (mine != 3)
+    top = (sub >= 5) & (mine != 0)
     return jnp.where(bottom, above, jnp.where(top, below, 0.0))
 
 
-def early_edge_kernel(meta, below_ref, above_ref, far_ref, cell_ref, after, y_ref, table_ref, a_ref, b_ref):
-    par = meta[0]
+def early_edge_kernel(below_ref, above_ref, far_ref, cell_ref, after, y_ref, table_ref, a_ref, b_ref):
+    par, has_b, mine, v = place()
     for x in range(8):
-        y_ref[x] = edge_rows(meta, below_ref[x], above_ref[x])
+        y_ref[x] = edge_rows(mine, below_ref[x], above_ref[x])
     table = jnp.concatenate(
         [cell_ref[...], below_ref[8, 0:1, 0:128], far_ref[...], above_ref[8, 0:1, 0:128],
          jnp.zeros((4, 128), F32)], axis=0)
@@ -236,10 +254,10 @@
         ref[2, :, 0:128] = table
 
 
-def late_edge_kernel(meta, below_ref, above_ref, after, y_ref, a_ref, b_ref):
-    par = meta[0]
+def late_edge_kernel(below_ref, above_ref, after, y_ref, a_ref, b_ref):
+    par, has_b, mine, v = place()
     for x in range(4):
-        y_ref[x] = edge_rows(meta, below_ref[x], above_ref[x])
+        y_ref[x] = edge_rows(mine, below_ref[x], above_ref[x])
     for i in range(2):
         a_ref[i] = y_ref[plane_of(par, 3 - i)]
         b_ref[i] = y_ref[plane_of(par, i)]
@@ -310,8 +328,8 @@
     return ((t[0] + t[1]) + (t[2] + t[3])) + (t[4] + t[5])
 
 
-def prepare_kernel(meta, p_ref, c_ref, a_ref, b_ref, y_ref, s_ref, n_ref, w_ref, k_ref):
-    par = meta[0]
+def prepare_kernel(p_ref, c_ref, a_ref, b_ref, y_ref, s_ref, n_ref, w_ref, k_ref):
+    par, has_b, mine, v = place()
     conduct = reader(par, c_ref, a_ref, b_ref, y_ref)
     own = reader(par, p_ref, a_ref.at[3:4], b_ref.at[3:4], y_ref, own_y=4)
     for e in range(3, 7):
@@ -325,9 +343,9 @@
             k_ref[x, rows, :] = (-0.5 * inv) * n_ref[x, rows, :]
 
 
-def gap_kernel(meta, table_ref, ta_ref, tb_ref, part_ref, cond_ref, ion_ref, act_ref, w_ref, k_ref,
+def gap_kernel(table_ref, ta_ref, tb_ref, part_ref, cond_ref, ion_ref, act_ref, w_ref, k_ref,
                u_ref, a_ref, b_ref, up_ref, down_ref, mem_ref, spread):
-    par, mine, v = meta[0], meta[2], meta[3]
+    par, has_b, mine, v = place()
     part = part_ref[...]
     brick = part >> 6
     bx, by = brick >> 2, brick & 3
@@ -367,14 +385,14 @@
                 a_ref[3 - j, rows, :] = u
 
 
-def operator_kernel(meta, c_ref, a_ref, b_ref, y_ref, ca_ref, cb_ref, after, fx, fym, fyp, fzm, fzp, inv_ref):
-    par, has_b, mine = meta[0], meta[1], meta[2]
+def operator_kernel(c_ref, a_ref, b_ref, y_ref, ca_ref, cb_ref, after, fx, fym, fyp, fzm, fzp, inv_ref):
+    par, has_b, mine, v = place()
     conduct = reader(par, c_ref, a_ref, b_ref, y_ref, ca_ref, cb_ref)
     sub = iota((8, 1024), 0)
     bottom = (sub < 3) & (mine != 3)
     top = (sub >= 5) & (mine != 0)
     keep = jnp.where(bottom | top, 1.0, 0.0)
-    inside = jnp.where(has_b == 1, 1.0, 0.0)
+    inside = jnp.where(has_b, 1.0, 0.0)
     for e in range(1, 9):
         plane = Plane(conduct, e)
         for t in range(8 if e in (1, 8) else 9):
@@ -435,9 +453,9 @@
         out_ref[at, rows, :] = before + (a * u + b * res)
 
 
-def near_kernel(meta, p_ref, fx, fym, fyp, fzm, fzp, inv, u_ref, a_ref, y_ref, ca_ref,
+def near_kernel(p_ref, fx, fym, fyp, fzm, fzp, inv, u_ref, a_ref, y_ref, ca_ref,
                 u1_out, r_out, u2_out, done_ref, u1_far, r_far, u2_far):
-    par = meta[0]
+    par, has_b, mine, v = place()
     coef = (fx, fym, fyp, fzm, fzp, inv)
     u0 = reader(par, u_ref, a_ref, None, y_ref, ca_ref)
     u1_held = ((u1_out, 4, 6), (u1_far, 6, 9))
@@ -451,9 +469,9 @@
     step_three(coef, p_ref, u0, stored(*u1_held), stored(*u2_held), stored(*r2_held), 6, plane_of(par, 3), done_ref, 0)
 
 
-def far_kernel(meta, p_ref, fx, fym, fyp, fzm, fzp, inv, u_ref, b_ref, y_ref, cb_ref, u1_in, r_in, u2_in, done_ref,
-               out_ref, u1_far, r_far, u2_far):
-    par = meta[0]
+def far_kernel(p_ref, fx, fym, fyp, fzm, fzp, inv, u_ref, b_ref, y_ref, cb_ref, u1_in, r_in, u2_in, done_ref,
+               out_hbm, u1_far, r_far, u2_far, out_ref, sem):
+    par, has_b, mine, v = place()
     coef = (fx, fym, fyp, fzm, fzp, inv)
     u0 = reader(par, u_ref, None, b_ref, y_ref, None, cb_ref)
     u1_new = ((u1_far, 1, 4),)
@@ -464,14 +482,21 @@
     r2 = stored(*r2_new, (r_in.at[1:2], 5, 6))
     u2_new = ((u2_far, 2, 5),)
     u2 = stored(*u2_new, (u2_in, 5, 7))
+    sends = begin([(done_ref.at[0], out_hbm.at[plane_of(par, 3)])], sem, 3)
     for e in (1, 2, 3):
         step_one(coef, u0, e, r1_new, u1_new)
     for e in (2, 3, 4):
         step_two(coef, u1, r1, e, r2_new, u2_new)
     for e in (3, 4, 5):
         x = plane_of(par, e - 3)
-        step_three(coef, p_ref, u0, u1, u2, r2, e, x, out_ref, x)
-    out_ref[plane_of(par, 3)] = done_ref[0]
+        step_three(coef, p_ref, u0, u1, u2, r2, e, x, out_ref, e - 3)
+        sends += begin([(out_ref.at[e - 3], out_hbm.at[x])], sem, e - 3)
+    for send in sends:
+        send.wait()
+
+
+def near(*dims, kind=F32):
+    return pltpu.VMEM(dims, kind)
 
 
 def shape(*dims, kind=F32):
@@ -480,11 +505,7 @@
 
 def per_device(potential, conductivity, ion_states, rate_scale, rate_slope, type_cond, reversal,
                facet_counts, intra_voxel, extra_voxel, cell_type, gap_partner, gap_cond):
-    v, m = lax.axis_index("vol"), lax.axis_index("mem")
-    par = v & 1
     nv = lax.axis_size("vol")
-    has_b = jnp.where((v == 0) | (v == nv - 1), 0, 1)
-    meta = jnp.stack([par, has_b, m, v]).astype(jnp.int32)
     swap_a = [pair for i in range(0, nv, 2) for pair in ((i, i + 1), (i + 1, i))]
     swap_b = [pair for i in range(1, nv - 1, 2) for pair in ((i, i + 1), (i + 1, i))]
     on_mem = lambda x, pairs: lax.ppermute(x, "mem", pairs)
@@ -495,86 +516,71 @@
     intra = intra_voxel.reshape(128, 128)
     extra = extra_voxel.reshape(128, 128)
 
-    volt, cells, act, part_lane, cond_lane, send_a, send_b, send_up, send_down = pl.pallas_call(
+    states_near, volt, cells, act, part_lane, cond_lane, send_a, send_b, send_up, send_down = pl.pallas_call(
         gather_kernel,
-        out_shape=(shape(128, 128), shape(1, 128), shape(128, 128), shape(8, 128, kind=jnp.int32), shape(8, 128),
-                   shape(4, 64, 1024), shape(4, 64, 1024), shape(9, 8, 1024), shape(9, 8, 1024)),
-        in_specs=[SM, SM, HBM, HBM] + [VM] * 4,
-        out_specs=(VM,) * 5 + (ANY,) * 4,
-        scratch_shapes=[pltpu.VMEM((4, 64, 1024), F32), pltpu.VMEM((4, 64, 1024), F32), pltpu.VMEM((8, 1024), F32),
-                        pltpu.SemaphoreType.DMA((22,))],
-        compiler_params=grant(60),
+        out_shape=(near(40, 16384), near(128, 128), near(1, 128), near(128, 128),
+                   near(8, 128, kind=jnp.int32), near(8, 128),
+                   near(4, 64, 1024), near(4, 64, 1024), near(9, 8, 1024), near(9, 8, 1024)),
+        in_specs=[SM] + [ANY] * 7,
+        out_specs=(ANY,) * 10,
+        scratch_shapes=[pltpu.VMEM((4, 64, 1024), F32), pltpu.VMEM((4, 64, 1024), F32),
+                        pltpu.VMEM((128, 128), jnp.int32), pltpu.VMEM((128, 128), jnp.int32),
+                        pltpu.VMEM((8, 64), jnp.int32), pltpu.VMEM((8, 64), F32), pltpu.VMEM((128, 128), F32),
+                        pltpu.VMEM((1, 128), F32), pltpu.VMEM((128, 128), F32), pltpu.VMEM((8, 128), jnp.int32),
+                        pltpu.VMEM((8, 128), F32), pltpu.VMEM((8, 1024), F32), pltpu.SemaphoreType.DMA((35,))],
+        compiler_params=grant(54),
         cost_estimate=pl.CostEstimate(flops=4000000, bytes_accessed=5000000, transcendentals=0),
         name="voltages",
-    )(meta, facet_counts, potential, conductivity, intra, extra, gap_partner.T, gap_cond.T)
+    )(facet_counts, potential, conductivity, intra, extra, gap_partner.T, gap_cond.T, ion_states)
 
     below, above, far = on_mem(send_up, ring(1)), on_mem(send_down, ring(3)), on_mem(cells, ring(2))
     early_b, early_a = to_b(send_b), to_a(send_a)
 
-    rates = jnp.concatenate([
-        jnp.stack([rate_slope[0] * LOG2E, jnp.log2(rate_scale[0]), rate_slope[1] * (-LOG2E), jnp.log2(rate_scale[1])]),
-        type_cond, type_cond * reversal[None, :]], axis=0)
-    rates = jnp.broadcast_to(rates[:, :, None], (10, 40, 128))
-    steps = 4
-    width = 16384 // steps
-    facet_rows = pl.BlockSpec((128 // steps, 128), lambda i, *_: (i, 0))
-    state_block = pl.BlockSpec((40, width), lambda i, *_: (0, i))
-    states_next, ion = pl.pallas_call(
+    states_next, ion, source, count = pl.pallas_call(
         ionic_kernel,
-        out_shape=(shape(40, 16384), shape(128, 128)),
-        grid_spec=pltpu.PrefetchScalarGridSpec(
-            num_scalar_prefetch=2,
-            grid=(steps,),
-            in_specs=[facet_rows, state_block, pl.BlockSpec((10, 40, 128), lambda i, *_: (0, 0, 0))],
-            out_specs=(state_block, facet_rows),
-        ),
-        compiler_params=grant(60),
-        cost_estimate=pl.CostEstimate(flops=16000000, bytes_accessed=7300000, transcendentals=2600000),
+        out_shape=(shape(40, 16384), shape(128, 128), shape(4, 64, 1024), shape(4, 64, 1024)),
+        in_specs=[SM, SM] + [VM] * 9,
+        out_specs=(ANY, VM, VM, VM),
+        scratch_shapes=[pltpu.VMEM((40, 16384), F32), pltpu.VMEM((128, 128), F32),
+                        pltpu.VMEM((10, 40, 128), F32), pltpu.SemaphoreType.DMA((CHUNKS,))],
+        compiler_params=pltpu.CompilerParams(vmem_limit_bytes=ROOM),
+        cost_estimate=pl.CostEstimate(flops=816000000, bytes_accessed=7300000, transcendentals=2600000),
         name="ionic",
-    )(facet_counts, cell_type, volt, ion_states, rates)
-
-    source, count = pl.pallas_call(
-        scatter_kernel,
-        out_shape=(shape(4, 64, 1024), shape(4, 64, 1024)),
-        in_specs=[VM] * 4,
-        out_specs=(VM, VM),
-        compiler_params=grant(8),
-        cost_estimate=pl.CostEstimate(flops=800000000, bytes_accessed=2300000, transcendentals=0),
-        name="scatter",
-    )(ion, act, intra, extra)
+    )(facet_counts, cell_type, volt, act, intra, extra, rate_scale, rate_slope, type_cond, reversal.reshape(1, 40),
+      states_near)
 
     y_early, table, more_a, more_b = pl.pallas_call(
         early_edge_kernel,
         out_shape=(shape(8, 8, 1024), shape(8, 128), shape(3, 8, 1024), shape(3, 8, 1024)),
-        in_specs=[SM] + [VM] * 4 + [ANY],
+        in_specs=[VM] * 4 + [ANY],
         out_specs=(VM,) * 4,
         compiler_params=grant(6),
         cost_estimate=pl.CostEstimate(flops=300000, bytes_accessed=1000000, transcendentals=0),
         name="early_edges",
-    )(meta, below, above, far, cells, source)
+    )(below, above, far, cells, source)
     more_b, more_a = to_b(more_b), to_a(more_a)
 
     w, k = pl.pallas_call(
         prepare_kernel,
         out_shape=(shape(4, 64, 1024), shape(4, 64, 1024)),
-        in_specs=[SM] + [VM] * 7,
+        in_specs=[VM] * 7,
         out_specs=(VM, VM),
         compiler_params=grant(20),
         cost_estimate=pl.CostEstimate(flops=16000000, bytes_accessed=8000000, transcendentals=0),
         name="prepare",
-    )(meta, potential, conductivity, early_a, early_b, y_early, source, count)
+    )(potential, conductivity, early_a, early_b, y_early, source, count)
 
     u, u_a, u_b, u_up, u_down, membrane = pl.pallas_call(
         gap_kernel,
         out_shape=(shape(4, 64, 1024), shape(3, 64, 1024), shape(3, 64, 1024), shape(4, 8, 1024),
                    shape(4, 8, 1024), shape(128, 128)),
-        in_specs=[SM] + [VM] * 9,
+        in_specs=[VM] * 9,
         out_specs=(VM,) * 6,
         scratch_shapes=[pltpu.VMEM((256, 128), F32)],
         compiler_params=grant(12),
         cost_estimate=pl.CostEstimate(flops=1000000, bytes_accessed=5000000, transcendentals=0),
         name="gap",
-    )(meta, table, more_a, more_b, part_lane, cond_lane, ion, act, w, k)
+    )(table, more_a, more_b, part_lane, cond_lane, ion, act, w, k)
 
     late_b = to_b(u_b)
     low_rows = on_mem(u_up, [(i, i + 1) for i in range(3)])
@@ -585,45 +591,45 @@
     operator = pl.pallas_call(
         operator_kernel,
         out_shape=(shape(9, 72, 1024),) + (shape(8, 72, 1024),) * 5,
-        in_specs=[SM] + [VM] * 6 + [ANY],
+        in_specs=[VM] * 6 + [ANY],
         out_specs=(VM,) * 6,
         compiler_params=grant(22),
         cost_estimate=pl.CostEstimate(flops=16000000, bytes_accessed=17000000, transcendentals=0),
         name="operator",
-    )(meta, conductivity, early_a, early_b, y_early, more_a, more_b, u_up)
+    )(conductivity, early_a, early_b, y_early, more_a, more_b, u_up)
 
     y_late, corner_a, corner_b = pl.pallas_call(
         late_edge_kernel,
         out_shape=(shape(4, 8, 1024), shape(2, 8, 1024), shape(2, 8, 1024)),
-        in_specs=[SM, VM, VM, ANY],
+        in_specs=[VM, VM, ANY],
         out_specs=(VM,) * 3,
         compiler_params=grant(4),
         cost_estimate=pl.CostEstimate(flops=100000, bytes_accessed=500000, transcendentals=0),
         name="late_edges",
-    )(meta, low_rows, high_rows, operator[-1])
+    )(low_rows, high_rows, operator[-1])
     corner_b, corner_a = to_b(corner_b), to_a(corner_a)
 
     u1, r, u2, done = pl.pallas_call(
         near_kernel,
         out_shape=(shape(2, 72, 1024), shape(2, 72, 1024), shape(2, 72, 1024), shape(1, 64, 1024)),
-        in_specs=[SM] + [VM] * 11,
+        in_specs=[VM] * 11,
         out_specs=(VM,) * 4,
         scratch_shapes=[big(3), big(3), big(1)],
         compiler_params=grant(30),
         cost_estimate=pl.CostEstimate(flops=25000000, bytes_accessed=10000000, transcendentals=0),
         name="near",
-    )(meta, potential, *operator, u, late_a, y_late, corner_a)
+    )(potential, *operator, u, late_a, y_late, corner_a)
 
     potential_next = pl.pallas_call(
         far_kernel,
         out_shape=shape(4, 64, 1024),
-        in_specs=[SM] + [VM] * 15,
-        out_specs=VM,
-        scratch_shapes=[big(3), big(4), big(3)],
+        in_specs=[VM] * 15,
+        out_specs=ANY,
+        scratch_shapes=[big(3), big(4), big(3), pltpu.VMEM((3, 64, 1024), F32), pltpu.SemaphoreType.DMA((4,))],
         compiler_params=grant(30),
         cost_estimate=pl.CostEstimate(flops=25000000, bytes_accessed=10000000, transcendentals=0),
         name="far",
-    )(meta, potential, *operator, u, late_b, y_late, corner_b, u1, r, u2, done)
+    )(potential, *operator, u, late_b, y_late, corner_b, u1, r, u2, done)
     return potential_next, states_next, membrane.reshape(16384)
 
 

time: 68.1 us -> 57.4 us (0.84)
  Pallas kernels: 32 us -> 23.8 us
  waiting for transfers between devices: 4.91 us -> 7.69 us
  local copies, waits for them, and re-layouts: 2.6 us -> 0.05 us
  other arithmetic: 2.07 us -> 0 us
    pallas_call x3 -> x2, Pallas kernels: 13.4 us -> 7.84 us  [the longest x1 4.83 us: per_device(): pl.pallas_call(gather_kernel, out_shape=(near(40, 16384), near(128, 128),...]
    another operation x2 -> x0, other arithmetic: 1.39 us -> none  [the longest x1 0.77 us: per_device(): jnp.log2(rate_scale[1])]
    pallas_call x1, Pallas kernels: 6.11 us -> 7.5 us  [per_device(): pl.pallas_call(ionic_kernel, out_shape=(shape(40, 16384), shape(128, 128)...]
    ppermute x2, waiting for transfers between devices: 0.16 us -> 1.41 us  [per_device(): corner_b, corner_a = (to_b(corner_b), to_a(corner_a))]
    pallas_call x1, Pallas kernels: 3.37 us -> 2.3 us  [per_device(): pl.pallas_call(near_kernel, out_shape=(shape(2, 72, 1024), shape(2, 72, 1...]
    unnamed x20, local copies, waits for them, and re-layouts: 1.01 us -> 0.05 us
    broadcast_in_dim x1 -> x0, local copies, waits for them, and re-layouts: 0.81 us -> none  [per_device(): rates = jnp.broadcast_to(rates[:, :, None], (10, 40, 128))]
    ppermute x2, waiting for transfers between devices: 2.56 us -> 3.36 us  [per_device(): more_b, more_a = (to_b(more_b), to_a(more_a))]
  transfers between devices with their start and end apart: 13 -> 13, of which waited for: 3 -> 3; matrix products, arithmetic and copies ran while one was open for 4% -> 0% of each run, Pallas kernels for 30% -> 26%
where the time goes in v5:
time: 57.4 us; the launch traced here: 57.2 us
  starting transfers between devices  24.5 us (43%)
  Pallas kernels  23.8 us (41%)
  waiting for transfers between devices  7.69 us (13%)
  between operations  1.11 us (2%)
    ppermute x5, starting transfers between devices, per_device(): on_mem = lambda x, pairs: lax.ppermute(x, 'mem', pairs)  9.17 us
    pallas_call x1, Pallas kernels, per_device(): pl.pallas_call(ionic_kernel, out_shape=(shape(40, 16384), shape(128, 128)...  7.5 us
    ppermute x2, starting transfers between devices, per_device(): early_b, early_a = (to_b(send_b), to_a(send_a))  6.39 us
    pallas_call x1, Pallas kernels, per_device(): pl.pallas_call(gather_kernel, out_shape=(near(40, 16384), near(128, 128),...  4.83 us
    ppermute x2, starting transfers between devices, per_device(): corner_b, corner_a = (to_b(corner_b), to_a(corner_a))  4.04 us
    ppermute x2, waiting for transfers between devices, per_device(): more_b, more_a = (to_b(more_b), to_a(more_a))  3.36 us
    pallas_call x1, Pallas kernels, per_device(): pl.pallas_call(far_kernel, out_shape=shape(4, 64, 1024), in_specs=[VM] *...  3.01 us
    ppermute x5, waiting for transfers between devices, per_device(): on_mem = lambda x, pairs: lax.ppermute(x, 'mem', pairs)  2.91 us
  transfers between devices with their start and end apart: 13, of which 3 were waited for; matrix products, arithmetic and copies ran while one was open for 0% of the time, Pallas kernels for 26%

profile of v5, /device:TPU:6, one launch (start us, length us, event | category | flops | bytes accessed | tf_op | source)
XLA Modules:
  0.0 57.2 jit_solution(7649541346002331213)
XLA Ops:
  0.7 4.8 %voltages.1 = (f32[40,16384]{1,0:T(8,128)S(1)}, f32[128,128]{1,0:T(8,128)S(1)}, f32[1,128]{1,0:T(1,128)S(1)}, f32[128,128]{1,0:T(8,128)S(1)}, s32[8,128]{1,0:T(8...) custom-call(s32[64]{0:T(128)} %cnt.3, ...), custom_call_target="tpu_custom_call" | custom-call | flops 4000000 | bytes 5000000 | tf_op jit(solution)/shard_map/voltages/pallas_call | solution.py:519
  5.6 0.1 collective-permute-start
  5.6 6.3 %collective-permute-start.1 = (f32[4,64,1024]{2,1,0:T(8,128)S(1)}, f32[4,64,1024]{2,1,0:T(8,128)S(1)}, u32[]{:S(2)}, u32[]{:S(2)}) collective-permute-start(f32[4,64,1024]{2,1,0:T(8,128)S(1)} %get-tuple-element.43), channel_id=1, source_target_pairs={{4,8},{8,4},{12,16},{16,12},{20,24},{24,20},{28,32},{32,28},{36,40... | collective-permute-start | bytes 3145736 | tf_op jit(solution)/shard_map/ppermute | solution.py:537
  12.0 1.6 %collective-permute-start.2 = (f32[9,8,1024]{2,1,0:T(8,128)S(1)}, f32[9,8,1024]{2,1,0:T(8,128)S(1)}, u32[]{:S(2)}, u32[]{:S(2)}) collective-permute-start(f32[9,8,1024]{2,1,0:T(8,128)S(1)} %get-tuple-element.44), channel_id=1, source_target_pairs={{0,1},{1,2},{2,3},{3,0},{4,5},{5,6},{6,7},{7,4},{8,9},{9,10},{10,1... | collective-permute-start | bytes 884744 | tf_op jit(solution)/shard_map/ppermute | solution.py:511
  13.6 1.7 %collective-permute-start.3 = (f32[9,8,1024]{2,1,0:T(8,128)S(1)}, f32[9,8,1024]{2,1,0:T(8,128)S(1)}, u32[]{:S(2)}, u32[]{:S(2)}) collective-permute-start(f32[9,8,1024]{2,1,0:T(8,128)S(1)} %get-tuple-element.45), channel_id=1, source_target_pairs={{0,3},{1,0},{2,1},{3,2},{4,7},{5,4},{6,5},{7,6},{8,11},{9,8},{10,9... | collective-permute-start | bytes 884744 | tf_op jit(solution)/shard_map/ppermute | solution.py:511
  15.3 2.0 %collective-permute-start.4 = (f32[1,128]{1,0:T(1,128)S(1)}, f32[1,128]{1,0:T(1,128)S(1)}, u32[]{:S(2)}, u32[]{:S(2)}) collective-permute-start(f32[1,128]{1,0:T(1,128)S(1)} %get-tuple-element.46.cell_ref), channel_id=1, source_target_pairs={{0,2},{1,3},{2,0},{3,1},{4,6},{5,7},{6,4},{7,5},{8,10},{9,11},{10,... | collective-permute-start | bytes 1544 | tf_op jit(solution)/shard_map/ppermute | solution.py:511
  17.3 0.0 copy-start
  17.3 7.5 %ionic.1 = (f32[40,16384]{1,0:T(8,128)}, f32[128,128]{1,0:T(8,128)S(1)}, f32[4,64,1024]{2,1,0:T(8,128)S(1)}, f32[4,64,1024]{2,1,0:T(8,128)S(1)}) custom-call(s32[64]{0:T(128)S(1)} %copy-done.4, s32[64]{0:T(128)S(1)} %copy-done.8, f32[128,128]{1,0:T(8,128)S(1)} %get-tuple-element.47.volt_ref, f32[128,128]{1,0:T(8,128)S(1)} %get-tuple-element.48.act_ref, ...), custom_call_target="tpu_custom_call" | custom-call | flops 816000000 | bytes 7300000 | tf_op jit(solution)/shard_map/ionic/pallas_call | solution.py:539
  24.9 0.1 early_edges.1
  24.9 0.1 collective-permute-start.5
  25.0 2.4 %collective-permute-start.6 = (f32[3,8,1024]{2,1,0:T(8,128)S(1)}, f32[3,8,1024]{2,1,0:T(8,128)S(1)}, u32[]{:S(2)}, u32[]{:S(2)}) collective-permute-start(f32[3,8,1024]{2,1,0:T(8,128)S(1)} %get-tuple-element.53), channel_id=1, source_target_pairs={{4,8},{8,4},{12,16},{16,12},{20,24},{24,20},{28,32},{32,28},{36,40... | collective-permute-start | bytes 294920 | tf_op jit(solution)/shard_map/ppermute | solution.py:561
  27.5 2.2 %prepare.1 = (f32[4,64,1024]{2,1,0:T(8,128)S(1)}, f32[4,64,1024]{2,1,0:T(8,128)S(1)}) custom-call(f32[4,64,1024]{2,1,0:T(8,128)S(1)} %copy-done, f32[4,64,1024]{2,1,0:T(8,128)S(1)} %copy-done.1, f32[4,64,1024]{2,1,0:T(8,128)S(1)} %collective-permute-done.a_ref, f32[4,64,1024]{2,1,0:T(8,128)S(1)} %collective-permute-done.1.b_ref, ...), custom_call_target="tpu_custom_call" | custom-call | flops 16000000 | bytes 8000000 | tf_op jit(solution)/shard_map/prepare/pallas_call | solution.py:563
  29.7 3.4 %collective-permute-done.6.tb_ref.cb_ref = f32[3,8,1024]{2,1,0:T(8,128)S(1)} collective-permute-done((f32[3,8,1024]{2,1,0:T(8,128)S(1)}, f32[3,8,1024]{2,1,0:T(8,128)S(1)}, u32[]{:S(2)}, u32[]{:S(2)}) %collective-permute-start.6) | collective-permute-done | bytes 98336 | tf_op jit(solution)/shard_map/ppermute | solution.py:561
  33.1 1.1 %gap.1 = (f32[4,64,1024]{2,1,0:T(8,128)S(1)}, f32[3,64,1024]{2,1,0:T(8,128)S(1)}, f32[3,64,1024]{2,1,0:T(8,128)S(1)}, f32[4,8,1024]{2,1,0:T(8,128)S(1)}, f32[4,8,1024]{2,1,0:T(8,128)S(1)}, /*index=5*/f32[128,128]{1,0:T(8,128)}) custom-call(f32[8,128]{1,0:T(8,128)S(1)} %get-tuple-element.54.table_ref, f32[3,8,1024]{2,1,0:T(8,128)S(1)} %collective-permute-done.5.ta_ref.ca_ref, ...), custom_call_target="tpu_custom_call" | custom-call | flops 1000000 | bytes 5000000 | tf_op jit(solution)/shard_map/gap/pallas_call | solution.py:573
  34.1 2.4 %collective-permute-start.7 = (f32[3,64,1024]{2,1,0:T(8,128)S(1)}, f32[3,64,1024]{2,1,0:T(8,128)S(1)}, u32[]{:S(2)}, u32[]{:S(2)}) collective-permute-start(f32[3,64,1024]{2,1,0:T(8,128)S(1)} %get-tuple-element.69), channel_id=1, source_target_pairs={{4,8},{8,4},{12,16},{16,12},{20,24},{24,20},{28,32},{32,28},{36,40... | collective-permute-start | bytes 2359304 | tf_op jit(solution)/shard_map/ppermute | solution.py:585
  36.5 2.6 %collective-permute-start.8 = (f32[4,8,1024]{2,1,0:T(8,128)S(1)}, f32[4,8,1024]{2,1,0:T(8,128)S(1)}, u32[]{:S(2)}, u32[]{:S(2)}) collective-permute-start(f32[4,8,1024]{2,1,0:T(8,128)S(1)} %get-tuple-element.61.after), channel_id=1, source_target_pairs={{0,1},{1,2},{2,3},{4,5},{5,6},{6,7},{8,9},{9,10},{10,11},{12,13},{... | collective-permute-start | bytes 393224 | tf_op jit(solution)/shard_map/ppermute | solution.py:511
  39.1 1.3 %collective-permute-start.9 = (f32[4,8,1024]{2,1,0:T(8,128)S(1)}, f32[4,8,1024]{2,1,0:T(8,128)S(1)}, u32[]{:S(2)}, u32[]{:S(2)}) collective-permute-start(f32[4,8,1024]{2,1,0:T(8,128)S(1)} %get-tuple-element.70), channel_id=1, source_target_pairs={{1,0},{2,1},{3,2},{5,4},{6,5},{7,6},{9,8},{10,9},{11,10},{13,12},{... | collective-permute-start | bytes 393224 | tf_op jit(solution)/shard_map/ppermute | solution.py:511
  40.4 2.8 %operator.1 = (f32[9,72,1024]{2,1,0:T(8,128)S(1)}, f32[8,72,1024]{2,1,0:T(8,128)S(1)}, f32[8,72,1024]{2,1,0:T(8,128)S(1)}, f32[8,72,1024]{2,1,0:T(8,128)S(1)}, f...) custom-call(f32[4,64,1024]{2,1,0:T(8,128)S(1)} %copy-done.1, f32[4,64,1024]{2,1,0:T(8,128)S(1)} %collective-permute-done.a_ref, ...), custom_call_target="tpu_custom_call" | custom-call | flops 16000000 | bytes 17000000 | tf_op jit(solution)/shard_map/operator/pallas_call | solution.py:591
  43.3 2.9 %collective-permute-done.9.above_ref = f32[4,8,1024]{2,1,0:T(8,128)S(1)} collective-permute-done((f32[4,8,1024]{2,1,0:T(8,128)S(1)}, f32[4,8,1024]{2,1,0:T(8,128)S(1)}, u32[]{:S(2)}, u32[]{:S(2)}) %collective-permute-start.9) | collective-permute-done | bytes 131104 | tf_op jit(solution)/shard_map/ppermute | solution.py:511
  46.2 0.1 collective-permute-start.12
  46.3 4.0 %collective-permute-start.10 = (f32[2,8,1024]{2,1,0:T(8,128)S(1)}, f32[2,8,1024]{2,1,0:T(8,128)S(1)}, u32[]{:S(2)}, u32[]{:S(2)}) collective-permute-start(f32[2,8,1024]{2,1,0:T(8,128)S(1)} %get-tuple-element.72), channel_id=1, source_target_pairs={{4,8},{8,4},{12,16},{16,12},{20,24},{24,20},{28,32},{32,28},{36,40... | collective-permute-start | bytes 196616 | tf_op jit(solution)/shard_map/ppermute | solution.py:610
  50.3 2.3 %near.1 = (f32[2,72,1024]{2,1,0:T(8,128)S(1)}, f32[2,72,1024]{2,1,0:T(8,128)S(1)}, f32[2,72,1024]{2,1,0:T(8,128)S(1)}, f32[1,64,1024]{2,1,0:T(8,128)S(1)}) custom-call(f32[4,64,1024]{2,1,0:T(8,128)S(1)} %copy-done, f32[9,72,1024]{2,1,0:T(8,128)S(1)} %get-tuple-element.62.fx, f32[8,72,1024]{2,1,0:T(8,128)S(1)} %get-tuple-element.63.fym, ...), custom_call_target="tpu_custom_call" | custom-call | flops 25000000 | bytes 10000000 | tf_op jit(solution)/shard_map/near/pallas_call | solution.py:612
  52.6 1.4 %collective-permute-done.10.cb_ref = f32[2,8,1024]{2,1,0:T(8,128)S(1)} collective-permute-done((f32[2,8,1024]{2,1,0:T(8,128)S(1)}, f32[2,8,1024]{2,1,0:T(8,128)S(1)}, u32[]{:S(2)}, u32[]{:S(2)}) %collective-permute-start.10) | collective-permute-done | bytes 65568 | tf_op jit(solution)/shard_map/ppermute | solution.py:610
  54.0 3.0 %far.1 = f32[4,64,1024]{2,1,0:T(8,128)} custom-call(f32[4,64,1024]{2,1,0:T(8,128)S(1)} %copy-done, f32[9,72,1024]{2,1,0:T(8,128)S(1)} %get-tuple-element.62.fx, f32[8,72,1024]{2,1,0:T(8,128)S(1)} %get-tuple-element.63.fym, f32[8,72,1024]{2,1,0:T(8,128)S(1)} %get-tuple-element.64.fyp, f32[8,72,1024]{2,1,0:T(8,128)S(1)} %get-tuple-element.65.fzm, ...), custom_call_target="tpu_custom_call" | custom-call | flops 25000000 | bytes 10000000 | tf_op jit(solution)/shard_map/far/pallas_call | solution.py:623
  (31 shorter events, 0.1 us)
Async XLA Ops:
  0.6 16.6 %copy-start.2 = (s32[16384]{0:T(1024)S(1)}, s32[16384]{0:T(1024)}, u32[]{:S(2)}) copy-start(s32[16384]{0:T(1024)} %param.21) | copy-start | bytes 196612
  0.6 16.6 %copy-start.3 = (s32[16384]{0:T(1024)S(1)}, s32[16384]{0:T(1024)}, u32[]{:S(2)}) copy-start(s32[16384]{0:T(1024)} %param.22) | copy-start | bytes 196612
  0.7 16.6 %copy-start.4 = (s32[64]{0:T(128)S(1)}, s32[64]{0:T(128)}, u32[]{:S(2)}) copy-start(s32[64]{0:T(128)} %cnt.3) | copy-start | bytes 772
  0.7 16.6 %copy-start.5 = (f32[3,40]{1,0:T(4,128)S(1)}, f32[3,40]{1,0:T(4,128)}, u32[]{:S(2)}) copy-start(f32[3,40]{1,0:T(4,128)} %cond_ref.1) | copy-start | bytes 1444
  0.7 16.6 %copy-start.6 = (f32[2,40]{1,0:T(2,128)S(1)}, f32[2,40]{1,0:T(2,128)}, u32[]{:S(2)}) copy-start(f32[2,40]{1,0:T(2,128)} %scale_ref.1) | copy-start | bytes 964
  0.7 16.6 %copy-start.7 = (f32[2,40]{1,0:T(2,128)S(1)}, f32[2,40]{1,0:T(2,128)}, u32[]{:S(2)}) copy-start(f32[2,40]{1,0:T(2,128)} %slope_ref.1) | copy-start | bytes 964
  0.7 16.6 %copy-start.8 = (s32[64]{0:T(128)S(1)}, s32[64]{0:T(128)}, u32[]{:S(2)}) copy-start(s32[64]{0:T(128)} %typ.1) | copy-start | bytes 772
  0.7 16.6 %copy-start.9 = (f32[40]{0:T(128)S(1)}, f32[40]{0:T(128)}, u32[]{:S(2)}) copy-start(f32[40]{0:T(128)} %param.19) | copy-start | bytes 484
  5.6 21.9 %collective-permute-start = (f32[4,64,1024]{2,1,0:T(8,128)S(1)}, f32[4,64,1024]{2,1,0:T(8,128)S(1)}, u32[]{:S(2)}, u32[]{:S(2)}) collective-permute-start(f32[4,64,1024]{2,1,0:T(8,128)S(1)} %get-tuple-element.42), channel_id=1, source_target_pairs={{0,4},{4,0},{8,12},{12,8},{16,20},{20,16},{24,28},{28,24},{32,36},... | collective-permute-start | bytes 3145736 | tf_op jit(solution)/shard_map/ppermute | solution.py:537
  5.6 21.8 %collective-permute-start.1 = (f32[4,64,1024]{2,1,0:T(8,128)S(1)}, f32[4,64,1024]{2,1,0:T(8,128)S(1)}, u32[]{:S(2)}, u32[]{:S(2)}) collective-permute-start(f32[4,64,1024]{2,1,0:T(8,128)S(1)} %get-tuple-element.43), channel_id=1, source_target_pairs={{4,8},{8,4},{12,16},{16,12},{20,24},{24,20},{28,32},{32,28},{36,40... | collective-permute-start | bytes 3145736 | tf_op jit(solution)/shard_map/ppermute | solution.py:537
  12.0 12.9 %collective-permute-start.2 = (f32[9,8,1024]{2,1,0:T(8,128)S(1)}, f32[9,8,1024]{2,1,0:T(8,128)S(1)}, u32[]{:S(2)}, u32[]{:S(2)}) collective-permute-start(f32[9,8,1024]{2,1,0:T(8,128)S(1)} %get-tuple-element.44), channel_id=1, source_target_pairs={{0,1},{1,2},{2,3},{3,0},{4,5},{5,6},{6,7},{7,4},{8,9},{9,10},{10,1... | collective-permute-start | bytes 884744 | tf_op jit(solution)/shard_map/ppermute | solution.py:511
  13.6 11.3 %collective-permute-start.3 = (f32[9,8,1024]{2,1,0:T(8,128)S(1)}, f32[9,8,1024]{2,1,0:T(8,128)S(1)}, u32[]{:S(2)}, u32[]{:S(2)}) collective-permute-start(f32[9,8,1024]{2,1,0:T(8,128)S(1)} %get-tuple-element.45), channel_id=1, source_target_pairs={{0,3},{1,0},{2,1},{3,2},{4,7},{5,4},{6,5},{7,6},{8,11},{9,8},{10,9... | collective-permute-start | bytes 884744 | tf_op jit(solution)/shard_map/ppermute | solution.py:511
  15.3 9.6 %collective-permute-start.4 = (f32[1,128]{1,0:T(1,128)S(1)}, f32[1,128]{1,0:T(1,128)S(1)}, u32[]{:S(2)}, u32[]{:S(2)}) collective-permute-start(f32[1,128]{1,0:T(1,128)S(1)} %get-tuple-element.46.cell_ref), channel_id=1, source_target_pairs={{0,2},{1,3},{2,0},{3,1},{4,6},{5,7},{6,4},{7,5},{8,10},{9,11},{10,... | collective-permute-start | bytes 1544 | tf_op jit(solution)/shard_map/ppermute | solution.py:511
  17.3 10.2 %copy-start = (f32[4,64,1024]{2,1,0:T(8,128)S(1)}, f32[4,64,1024]{2,1,0:T(8,128)}, u32[]{:S(2)}) copy-start(f32[4,64,1024]{2,1,0:T(8,128)} %p_ref.5) | copy-start | bytes 3145732
  17.3 10.2 %copy-start.1 = (f32[4,64,1024]{2,1,0:T(8,128)S(1)}, f32[4,64,1024]{2,1,0:T(8,128)}, u32[]{:S(2)}) copy-start(f32[4,64,1024]{2,1,0:T(8,128)} %c_ref.3) | copy-start | bytes 3145732
  24.9 4.8 %collective-permute-start.5 = (f32[3,8,1024]{2,1,0:T(8,128)S(1)}, f32[3,8,1024]{2,1,0:T(8,128)S(1)}, u32[]{:S(2)}, u32[]{:S(2)}) collective-permute-start(f32[3,8,1024]{2,1,0:T(8,128)S(1)} %get-tuple-element.52), channel_id=1, source_target_pairs={{0,4},{4,0},{8,12},{12,8},{16,20},{20,16},{24,28},{28,24},{32,36},... | collective-permute-start | bytes 294920 | tf_op jit(solution)/shard_map/ppermute | solution.py:561
  25.0 8.0 %collective-permute-start.6 = (f32[3,8,1024]{2,1,0:T(8,128)S(1)}, f32[3,8,1024]{2,1,0:T(8,128)S(1)}, u32[]{:S(2)}, u32[]{:S(2)}) collective-permute-start(f32[3,8,1024]{2,1,0:T(8,128)S(1)} %get-tuple-element.53), channel_id=1, source_target_pairs={{4,8},{8,4},{12,16},{16,12},{20,24},{24,20},{28,32},{32,28},{36,40... | collective-permute-start | bytes 294920 | tf_op jit(solution)/shard_map/ppermute | solution.py:561
  34.1 16.1 %collective-permute-start.11 = (f32[3,64,1024]{2,1,0:T(8,128)S(1)}, f32[3,64,1024]{2,1,0:T(8,128)S(1)}, u32[]{:S(2)}, u32[]{:S(2)}) collective-permute-start(f32[3,64,1024]{2,1,0:T(8,128)S(1)} %get-tuple-element.73), channel_id=1, source_target_pairs={{0,4},{4,0},{8,12},{12,8},{16,20},{20,16},{24,28},{28,24},{32,36},... | collective-permute-start | bytes 2359304 | tf_op jit(solution)/shard_map/ppermute | solution.py:588
  34.1 19.9 %collective-permute-start.7 = (f32[3,64,1024]{2,1,0:T(8,128)S(1)}, f32[3,64,1024]{2,1,0:T(8,128)S(1)}, u32[]{:S(2)}, u32[]{:S(2)}) collective-permute-start(f32[3,64,1024]{2,1,0:T(8,128)S(1)} %get-tuple-element.69), channel_id=1, source_target_pairs={{4,8},{8,4},{12,16},{16,12},{20,24},{24,20},{28,32},{32,28},{36,40... | collective-permute-start | bytes 2359304 | tf_op jit(solution)/shard_map/ppermute | solution.py:585
  36.5 6.7 %collective-permute-start.8 = (f32[4,8,1024]{2,1,0:T(8,128)S(1)}, f32[4,8,1024]{2,1,0:T(8,128)S(1)}, u32[]{:S(2)}, u32[]{:S(2)}) collective-permute-start(f32[4,8,1024]{2,1,0:T(8,128)S(1)} %get-tuple-element.61.after), channel_id=1, source_target_pairs={{0,1},{1,2},{2,3},{4,5},{5,6},{6,7},{8,9},{9,10},{10,11},{12,13},{... | collective-permute-start | bytes 393224 | tf_op jit(solution)/shard_map/ppermute | solution.py:511
  39.1 7.0 %collective-permute-start.9 = (f32[4,8,1024]{2,1,0:T(8,128)S(1)}, f32[4,8,1024]{2,1,0:T(8,128)S(1)}, u32[]{:S(2)}, u32[]{:S(2)}) collective-permute-start(f32[4,8,1024]{2,1,0:T(8,128)S(1)} %get-tuple-element.70), channel_id=1, source_target_pairs={{1,0},{2,1},{3,2},{5,4},{6,5},{7,6},{9,8},{10,9},{11,10},{13,12},{... | collective-permute-start | bytes 393224 | tf_op jit(solution)/shard_map/ppermute | solution.py:511
  46.2 4.1 %collective-permute-start.12 = (f32[2,8,1024]{2,1,0:T(8,128)S(1)}, f32[2,8,1024]{2,1,0:T(8,128)S(1)}, u32[]{:S(2)}, u32[]{:S(2)}) collective-permute-start(f32[2,8,1024]{2,1,0:T(8,128)S(1)} %get-tuple-element.74), channel_id=1, source_target_pairs={{0,4},{4,0},{8,12},{12,8},{16,20},{20,16},{24,28},{28,24},{32,36},... | collective-permute-start | bytes 196616 | tf_op jit(solution)/shard_map/ppermute | solution.py:610
  46.3 7.7 %collective-permute-start.10 = (f32[2,8,1024]{2,1,0:T(8,128)S(1)}, f32[2,8,1024]{2,1,0:T(8,128)S(1)}, u32[]{:S(2)}, u32[]{:S(2)}) collective-permute-start(f32[2,8,1024]{2,1,0:T(8,128)S(1)} %get-tuple-element.72), channel_id=1, source_target_pairs={{4,8},{8,4},{12,16},{16,12},{20,24},{24,20},{28,32},{32,28},{36,40... | collective-permute-start | bytes 196616 | tf_op jit(solution)/shard_map/ppermute | solution.py:610

commit v6 on v5

--- a/solution.py
+++ b/solution.py
@@ -157,8 +157,7 @@
     for i in range(10):
         rate_ref[i] = jnp.broadcast_to(turned[0:40, i : i + 1], (40, 128))
     lane = iota((8, 128), 1)
-    row_iota = iota((32, 512), 0)
-    lane_iota = iota((128, 512), 0)
+    numbers = [(iota((16, 512), 0) + 16 * k).astype(F32).astype(BF16) for k in range(8)]
     low = iota((8, 128), 0) < 4
     odd_row = (iota((8, 128), 0) & 2) // 2
 
@@ -201,8 +200,8 @@
         mids, lanes = [], []
         for ref in (in_ref, ex_ref):
             o = ref[rows8, :] & 4095
-            mids.append((((o >> 7) & 7) ^ odd_row) * 4 + (o >> 10))
-            lanes.append(o & 127)
+            mids.append(((((o >> 7) & 7) ^ odd_row) * 4 + (o >> 10)).astype(F32))
+            lanes.append((o & 127).astype(F32))
 
         def line(a, b, s):
             r = 2 * s
@@ -211,11 +210,13 @@
         for q in range(2):
             results = []
             for s in (2 * q, 2 * q + 1):
-                hit = line(mids[0], mids[1], s) == row_iota
-                left = jnp.concatenate(
-                    [jnp.where(hit, line(piece, -piece, s), 0.0).astype(BF16) for piece in (hi, lo, act)], axis=0
-                )
-                right = jnp.where(line(lanes[0], lanes[1], s) == lane_iota, 1.0, 0.0).astype(BF16)
+                packed = lambda row: jnp.broadcast_to(row, (16, 512)).astype(BF16)
+                mid, at = packed(line(mids[0], mids[1], s)), packed(line(lanes[0], lanes[1], s))
+                pieces = [packed(line(piece, -piece, s)) for piece in (hi, lo, act)]
+                hits = [mid == numbers[0], mid == numbers[1]]
+                none, one = jnp.zeros((16, 512), BF16), jnp.ones((16, 512), BF16)
+                left = jnp.concatenate([jnp.where(hit, piece, none) for piece in pieces for hit in hits], axis=0)
+                right = jnp.concatenate([jnp.where(at == number, one, none) for number in numbers], axis=0)
                 out = lax.dot_general(left, right, (((1,), (1,)), ((), ())), preferred_element_type=F32)
                 results.append((out[0:32] + out[32:64], out[64:96]))
             row = pl.ds(pl.multiple_of((2 * (group % 4) + q) * 8, 8), 8)
@@ -263,14 +264,15 @@
         b_ref[i] = y_ref[plane_of(par, i)]
 
 
-def reader(par, own, a, b, y, ca=None, cb=None, own_y=0):
+def reader(par, inside, own, a, b, y, ca=None, cb=None, own_y=0):
     def get(e, t):
         rows = slice(8 * t, 8 * t + 8)
         if 3 <= e <= 6:
             x = plane_of(par, e - 3)
             return own[x, rows, :] if t < 8 else y[own_y + x]
         halo, corner, i = (a, ca, e - 7) if e > 6 else (b, cb, 2 - e)
-        return halo[i, rows, :] if t < 8 else corner[i]
+        value = halo[i, rows, :] if t < 8 else corner[i]
+        return value if e > 6 else value * inside
 
     return get
 
@@ -330,8 +332,9 @@
 
 def prepare_kernel(p_ref, c_ref, a_ref, b_ref, y_ref, s_ref, n_ref, w_ref, k_ref):
     par, has_b, mine, v = place()
-    conduct = reader(par, c_ref, a_ref, b_ref, y_ref)
-    own = reader(par, p_ref, a_ref.at[3:4], b_ref.at[3:4], y_ref, own_y=4)
+    inside = jnp.where(has_b, 1.0, 0.0)
+    conduct = reader(par, inside, c_ref, a_ref, b_ref, y_ref)
+    own = reader(par, inside, p_ref, a_ref.at[3:4], b_ref.at[3:4], y_ref, own_y=4)
     for e in range(3, 7):
         x = plane_of(par, e - 3)
         pc, pp = Plane(conduct, e), Plane(own, e)
@@ -387,12 +390,12 @@
 
 def operator_kernel(c_ref, a_ref, b_ref, y_ref, ca_ref, cb_ref, after, fx, fym, fyp, fzm, fzp, inv_ref):
     par, has_b, mine, v = place()
-    conduct = reader(par, c_ref, a_ref, b_ref, y_ref, ca_ref, cb_ref)
+    inside = jnp.where(has_b, 1.0, 0.0)
+    conduct = reader(par, inside, c_ref, a_ref, b_ref, y_ref, ca_ref, cb_ref)
     sub = iota((8, 1024), 0)
     bottom = (sub < 3) & (mine != 3)
     top = (sub >= 5) & (mine != 0)
     keep = jnp.where(bottom | top, 1.0, 0.0)
-    inside = jnp.where(has_b, 1.0, 0.0)
     for e in range(1, 9):
         plane = Plane(conduct, e)
         for t in range(8 if e in (1, 8) else 9):
@@ -456,8 +459,9 @@
 def near_kernel(p_ref, fx, fym, fyp, fzm, fzp, inv, u_ref, a_ref, y_ref, ca_ref,
                 u1_out, r_out, u2_out, done_ref, u1_far, r_far, u2_far):
     par, has_b, mine, v = place()
+    inside = jnp.where(has_b, 1.0, 0.0)
     coef = (fx, fym, fyp, fzm, fzp, inv)
-    u0 = reader(par, u_ref, a_ref, None, y_ref, ca_ref)
+    u0 = reader(par, inside, u_ref, a_ref, None, y_ref, ca_ref)
     u1_held = ((u1_out, 4, 6), (u1_far, 6, 9))
     r1_held = ((r_out, 4, 5), (r_far, 5, 8))
     r2_held = ((r_out.at[1:2], 5, 6), (r_far.at[1:2], 6, 7))
@@ -472,8 +476,9 @@
 def far_kernel(p_ref, fx, fym, fyp, fzm, fzp, inv, u_ref, b_ref, y_ref, cb_ref, u1_in, r_in, u2_in, done_ref,
                out_hbm, u1_far, r_far, u2_far, out_ref, sem):
     par, has_b, mine, v = place()
+    inside = jnp.where(has_b, 1.0, 0.0)
     coef = (fx, fym, fyp, fzm, fzp, inv)
-    u0 = reader(par, u_ref, None, b_ref, y_ref, None, cb_ref)
+    u0 = reader(par, inside, u_ref, None, b_ref, y_ref, None, cb_ref)
     u1_new = ((u1_far, 1, 4),)
     u1 = stored(*u1_new, (u1_in, 4, 6))
     r1_new = ((r_far, 2, 4),)
@@ -507,7 +512,7 @@
                facet_counts, intra_voxel, extra_voxel, cell_type, gap_partner, gap_cond):
     nv = lax.axis_size("vol")
     swap_a = [pair for i in range(0, nv, 2) for pair in ((i, i + 1), (i + 1, i))]
-    swap_b = [pair for i in range(1, nv - 1, 2) for pair in ((i, i + 1), (i + 1, i))]
+    swap_b = [pair for i in range(1, nv - 1, 2) for pair in ((i, i + 1), (i + 1, i))] + [(0, 0), (nv - 1, nv - 1)]
     on_mem = lambda x, pairs: lax.ppermute(x, "mem", pairs)
     ring = lambda d: [(i, (i + d) % 4) for i in range(4)]
     to_a = functools.partial(lax.ppermute, axis_name="vol", perm=swap_a)
@@ -583,8 +588,7 @@
     )(table, more_a, more_b, part_lane, cond_lane, ion, act, w, k)
 
     late_b = to_b(u_b)
-    low_rows = on_mem(u_up, [(i, i + 1) for i in range(3)])
-    high_rows = on_mem(u_down, [(i + 1, i) for i in range(3)])
+    low_rows, high_rows = on_mem(u_up, ring(1)), on_mem(u_down, ring(3))
     late_a = to_a(u_a)
 
     big = lambda n: pltpu.VMEM((n, 72, 1024), F32)

time: 57.4 us -> 54.5 us (0.949)
  waiting for transfers between devices: 7.69 us -> 5.02 us
    ppermute x5, waiting for transfers between devices: 2.91 us -> 0.52 us  [per_device(): on_mem = lambda x, pairs: lax.ppermute(x, 'mem', pairs)]
    ppermute x5, starting transfers between devices: 9.17 us -> 8.59 us  [per_device(): on_mem = lambda x, pairs: lax.ppermute(x, 'mem', pairs)]
  transfers between devices with their start and end apart: 13 -> 13, of which waited for: 3 -> 3; matrix products, arithmetic and copies ran while one was open for 0% -> 0% of each run, Pallas kernels for 26% -> 27%
where the time goes in v6:
time: 54.5 us; the launch traced here: 54.2 us
  starting transfers between devices  24.3 us (45%)
  Pallas kernels  23.7 us (43%)
  waiting for transfers between devices  5.02 us (9%)
  between operations  1.09 us (2%)
    ppermute x5, starting transfers between devices, per_device(): on_mem = lambda x, pairs: lax.ppermute(x, 'mem', pairs)  8.59 us
    pallas_call x1, Pallas kernels, per_device(): pl.pallas_call(ionic_kernel, out_shape=(shape(40, 16384), shape(128, 128)...  7.29 us
    ppermute x2, starting transfers between devices, per_device(): early_b, early_a = (to_b(send_b), to_a(send_a))  6.39 us
    pallas_call x1, Pallas kernels, per_device(): pl.pallas_call(gather_kernel, out_shape=(near(40, 16384), near(128, 128),...  4.83 us
    ppermute x2, starting transfers between devices, per_device(): corner_b, corner_a = (to_b(corner_b), to_a(corner_a))  4.48 us
    ppermute x2, waiting for transfers between devices, per_device(): more_b, more_a = (to_b(more_b), to_a(more_a))  3.34 us
    pallas_call x1, Pallas kernels, per_device(): pl.pallas_call(far_kernel, out_shape=shape(4, 64, 1024), in_specs=[VM] *...  3.04 us
    pallas_call x1, Pallas kernels, per_device(): pl.pallas_call(operator_kernel, out_shape=(shape(9, 72, 1024),) + (shape(...  2.89 us
  transfers between devices with their start and end apart: 13, of which 3 were waited for; matrix products, arithmetic and copies ran while one was open for 0% of the time, Pallas kernels for 27%

profile of v6, /device:TPU:6, one launch (start us, length us, event | category | flops | bytes accessed | tf_op | source)
XLA Modules:
  0.0 54.2 jit_solution(1195082375518425877)
XLA Ops:
  0.7 4.8 %voltages.1 = (f32[40,16384]{1,0:T(8,128)S(1)}, f32[128,128]{1,0:T(8,128)S(1)}, f32[1,128]{1,0:T(1,128)S(1)}, f32[128,128]{1,0:T(8,128)S(1)}, s32[8,128]{1,0:T(8...) custom-call(s32[64]{0:T(128)} %cnt.3, ...), custom_call_target="tpu_custom_call" | custom-call | flops 4000000 | bytes 5000000 | tf_op jit(solution)/shard_map/voltages/pallas_call | solution.py:524
  5.6 0.1 collective-permute-start
  5.6 6.3 %collective-permute-start.1 = (f32[4,64,1024]{2,1,0:T(8,128)S(1)}, f32[4,64,1024]{2,1,0:T(8,128)S(1)}, u32[]{:S(2)}, u32[]{:S(2)}) collective-permute-start(f32[4,64,1024]{2,1,0:T(8,128)S(1)} %get-tuple-element.43), channel_id=1, source_target_pairs={{4,8},{8,4},{12,16},{16,12},{20,24},{24,20},{28,32},{32,28},{36,40... | collective-permute-start | bytes 3145736 | tf_op jit(solution)/shard_map/ppermute | solution.py:542
  12.0 1.6 %collective-permute-start.2 = (f32[9,8,1024]{2,1,0:T(8,128)S(1)}, f32[9,8,1024]{2,1,0:T(8,128)S(1)}, u32[]{:S(2)}, u32[]{:S(2)}) collective-permute-start(f32[9,8,1024]{2,1,0:T(8,128)S(1)} %get-tuple-element.44), channel_id=1, source_target_pairs={{0,1},{1,2},{2,3},{3,0},{4,5},{5,6},{6,7},{7,4},{8,9},{9,10},{10,1... | collective-permute-start | bytes 884744 | tf_op jit(solution)/shard_map/ppermute | solution.py:516
  13.6 1.7 %collective-permute-start.3 = (f32[9,8,1024]{2,1,0:T(8,128)S(1)}, f32[9,8,1024]{2,1,0:T(8,128)S(1)}, u32[]{:S(2)}, u32[]{:S(2)}) collective-permute-start(f32[9,8,1024]{2,1,0:T(8,128)S(1)} %get-tuple-element.45), channel_id=1, source_target_pairs={{0,3},{1,0},{2,1},{3,2},{4,7},{5,4},{6,5},{7,6},{8,11},{9,8},{10,9... | collective-permute-start | bytes 884744 | tf_op jit(solution)/shard_map/ppermute | solution.py:516
  15.3 2.0 %collective-permute-start.4 = (f32[1,128]{1,0:T(1,128)S(1)}, f32[1,128]{1,0:T(1,128)S(1)}, u32[]{:S(2)}, u32[]{:S(2)}) collective-permute-start(f32[1,128]{1,0:T(1,128)S(1)} %get-tuple-element.46.cell_ref), channel_id=1, source_target_pairs={{0,2},{1,3},{2,0},{3,1},{4,6},{5,7},{6,4},{7,5},{8,10},{9,11},{10,... | collective-permute-start | bytes 1544 | tf_op jit(solution)/shard_map/ppermute | solution.py:516
  17.3 0.0 copy-start
  17.3 7.3 %ionic.1 = (f32[40,16384]{1,0:T(8,128)}, f32[128,128]{1,0:T(8,128)S(1)}, f32[4,64,1024]{2,1,0:T(8,128)S(1)}, f32[4,64,1024]{2,1,0:T(8,128)S(1)}) custom-call(s32[64]{0:T(128)S(1)} %copy-done.4, s32[64]{0:T(128)S(1)} %copy-done.8, f32[128,128]{1,0:T(8,128)S(1)} %get-tuple-element.47.volt_ref, f32[128,128]{1,0:T(8,128)S(1)} %get-tuple-element.48.act_ref, ...), custom_call_target="tpu_custom_call" | custom-call | flops 816000000 | bytes 7300000 | tf_op jit(solution)/shard_map/ionic/pallas_call | solution.py:544
  24.7 0.1 early_edges.1
  24.7 0.1 collective-permute-start.5
  24.8 2.4 %collective-permute-start.6 = (f32[3,8,1024]{2,1,0:T(8,128)S(1)}, f32[3,8,1024]{2,1,0:T(8,128)S(1)}, u32[]{:S(2)}, u32[]{:S(2)}) collective-permute-start(f32[3,8,1024]{2,1,0:T(8,128)S(1)} %get-tuple-element.53), channel_id=1, source_target_pairs={{4,8},{8,4},{12,16},{16,12},{20,24},{24,20},{28,32},{32,28},{36,40... | collective-permute-start | bytes 294920 | tf_op jit(solution)/shard_map/ppermute | solution.py:566
  27.3 2.2 %prepare.1 = (f32[4,64,1024]{2,1,0:T(8,128)S(1)}, f32[4,64,1024]{2,1,0:T(8,128)S(1)}) custom-call(f32[4,64,1024]{2,1,0:T(8,128)S(1)} %copy-done, f32[4,64,1024]{2,1,0:T(8,128)S(1)} %copy-done.1, f32[4,64,1024]{2,1,0:T(8,128)S(1)} %collective-permute-done.a_ref, f32[4,64,1024]{2,1,0:T(8,128)S(1)} %collective-permute-done.1.b_ref, ...), custom_call_target="tpu_custom_call" | custom-call | flops 16000000 | bytes 8000000 | tf_op jit(solution)/shard_map/prepare/pallas_call | solution.py:568
  29.5 3.3 %collective-permute-done.6.tb_ref.cb_ref = f32[3,8,1024]{2,1,0:T(8,128)S(1)} collective-permute-done((f32[3,8,1024]{2,1,0:T(8,128)S(1)}, f32[3,8,1024]{2,1,0:T(8,128)S(1)}, u32[]{:S(2)}, u32[]{:S(2)}) %collective-permute-start.6) | collective-permute-done | bytes 98336 | tf_op jit(solution)/shard_map/ppermute | solution.py:566
  32.9 1.1 %gap.1 = (f32[4,64,1024]{2,1,0:T(8,128)S(1)}, f32[3,64,1024]{2,1,0:T(8,128)S(1)}, f32[3,64,1024]{2,1,0:T(8,128)S(1)}, f32[4,8,1024]{2,1,0:T(8,128)S(1)}, f32[4,8,1024]{2,1,0:T(8,128)S(1)}, /*index=5*/f32[128,128]{1,0:T(8,128)}) custom-call(f32[8,128]{1,0:T(8,128)S(1)} %get-tuple-element.54.table_ref, f32[3,8,1024]{2,1,0:T(8,128)S(1)} %collective-permute-done.5.ta_ref.ca_ref, ...), custom_call_target="tpu_custom_call" | custom-call | flops 1000000 | bytes 5000000 | tf_op jit(solution)/shard_map/gap/pallas_call | solution.py:578
  33.9 2.4 %collective-permute-start.7 = (f32[3,64,1024]{2,1,0:T(8,128)S(1)}, f32[3,64,1024]{2,1,0:T(8,128)S(1)}, u32[]{:S(2)}, u32[]{:S(2)}) collective-permute-start(f32[3,64,1024]{2,1,0:T(8,128)S(1)} %get-tuple-element.69), channel_id=1, source_target_pairs={{4,8},{8,4},{12,16},{16,12},{20,24},{24,20},{28,32},{32,28},{36,40... | collective-permute-start | bytes 2359304 | tf_op jit(solution)/shard_map/ppermute | solution.py:590
  36.3 0.7 %collective-permute-start.8 = (f32[4,8,1024]{2,1,0:T(8,128)S(1)}, f32[4,8,1024]{2,1,0:T(8,128)S(1)}, u32[]{:S(2)}, u32[]{:S(2)}) collective-permute-start(f32[4,8,1024]{2,1,0:T(8,128)S(1)} %get-tuple-element.61.after), channel_id=1, source_target_pairs={{0,1},{1,2},{2,3},{3,0},{4,5},{5,6},{6,7},{7,4},{8,9},{9,10},{10,1... | collective-permute-start | bytes 393224 | tf_op jit(solution)/shard_map/ppermute | solution.py:516
  37.1 2.6 %collective-permute-start.9 = (f32[4,8,1024]{2,1,0:T(8,128)S(1)}, f32[4,8,1024]{2,1,0:T(8,128)S(1)}, u32[]{:S(2)}, u32[]{:S(2)}) collective-permute-start(f32[4,8,1024]{2,1,0:T(8,128)S(1)} %get-tuple-element.70), channel_id=1, source_target_pairs={{0,3},{1,0},{2,1},{3,2},{4,7},{5,4},{6,5},{7,6},{8,11},{9,8},{10,9... | collective-permute-start | bytes 393224 | tf_op jit(solution)/shard_map/ppermute | solution.py:516
  39.6 2.9 %operator.1 = (f32[9,72,1024]{2,1,0:T(8,128)S(1)}, f32[8,72,1024]{2,1,0:T(8,128)S(1)}, f32[8,72,1024]{2,1,0:T(8,128)S(1)}, f32[8,72,1024]{2,1,0:T(8,128)S(1)}, f...) custom-call(f32[4,64,1024]{2,1,0:T(8,128)S(1)} %copy-done.1, f32[4,64,1024]{2,1,0:T(8,128)S(1)} %collective-permute-done.a_ref, ...), custom_call_target="tpu_custom_call" | custom-call | flops 16000000 | bytes 17000000 | tf_op jit(solution)/shard_map/operator/pallas_call | solution.py:595
  42.5 0.5 collective-permute-done.8.below_ref
  43.1 0.3 collective-permute-start.12
  43.3 4.2 %collective-permute-start.10 = (f32[2,8,1024]{2,1,0:T(8,128)S(1)}, f32[2,8,1024]{2,1,0:T(8,128)S(1)}, u32[]{:S(2)}, u32[]{:S(2)}) collective-permute-start(f32[2,8,1024]{2,1,0:T(8,128)S(1)} %get-tuple-element.72), channel_id=1, source_target_pairs={{4,8},{8,4},{12,16},{16,12},{20,24},{24,20},{28,32},{32,28},{36,40... | collective-permute-start | bytes 196616 | tf_op jit(solution)/shard_map/ppermute | solution.py:614
  47.6 2.3 %near.1 = (f32[2,72,1024]{2,1,0:T(8,128)S(1)}, f32[2,72,1024]{2,1,0:T(8,128)S(1)}, f32[2,72,1024]{2,1,0:T(8,128)S(1)}, f32[1,64,1024]{2,1,0:T(8,128)S(1)}) custom-call(f32[4,64,1024]{2,1,0:T(8,128)S(1)} %copy-done, f32[9,72,1024]{2,1,0:T(8,128)S(1)} %get-tuple-element.62.fx, f32[8,72,1024]{2,1,0:T(8,128)S(1)} %get-tuple-element.63.fym, ...), custom_call_target="tpu_custom_call" | custom-call | flops 25000000 | bytes 10000000 | tf_op jit(solution)/shard_map/near/pallas_call | solution.py:616
  49.9 1.1 %collective-permute-done.10.cb_ref = f32[2,8,1024]{2,1,0:T(8,128)S(1)} collective-permute-done((f32[2,8,1024]{2,1,0:T(8,128)S(1)}, f32[2,8,1024]{2,1,0:T(8,128)S(1)}, u32[]{:S(2)}, u32[]{:S(2)}) %collective-permute-start.10) | collective-permute-done | bytes 65568 | tf_op jit(solution)/shard_map/ppermute | solution.py:614
  51.0 3.0 %far.1 = f32[4,64,1024]{2,1,0:T(8,128)} custom-call(f32[4,64,1024]{2,1,0:T(8,128)S(1)} %copy-done, f32[9,72,1024]{2,1,0:T(8,128)S(1)} %get-tuple-element.62.fx, f32[8,72,1024]{2,1,0:T(8,128)S(1)} %get-tuple-element.63.fym, f32[8,72,1024]{2,1,0:T(8,128)S(1)} %get-tuple-element.64.fyp, f32[8,72,1024]{2,1,0:T(8,128)S(1)} %get-tuple-element.65.fzm, ...), custom_call_target="tpu_custom_call" | custom-call | flops 25000000 | bytes 10000000 | tf_op jit(solution)/shard_map/far/pallas_call | solution.py:627
  (31 shorter events, 0.1 us)
Async XLA Ops:
  0.6 16.6 %copy-start.2 = (s32[16384]{0:T(1024)S(1)}, s32[16384]{0:T(1024)}, u32[]{:S(2)}) copy-start(s32[16384]{0:T(1024)} %param.21) | copy-start | bytes 196612
  0.6 16.6 %copy-start.3 = (s32[16384]{0:T(1024)S(1)}, s32[16384]{0:T(1024)}, u32[]{:S(2)}) copy-start(s32[16384]{0:T(1024)} %param.22) | copy-start | bytes 196612
  0.7 16.6 %copy-start.4 = (s32[64]{0:T(128)S(1)}, s32[64]{0:T(128)}, u32[]{:S(2)}) copy-start(s32[64]{0:T(128)} %cnt.3) | copy-start | bytes 772
  0.7 16.6 %copy-start.5 = (f32[3,40]{1,0:T(4,128)S(1)}, f32[3,40]{1,0:T(4,128)}, u32[]{:S(2)}) copy-start(f32[3,40]{1,0:T(4,128)} %cond_ref.1) | copy-start | bytes 1444
  0.7 16.6 %copy-start.6 = (f32[2,40]{1,0:T(2,128)S(1)}, f32[2,40]{1,0:T(2,128)}, u32[]{:S(2)}) copy-start(f32[2,40]{1,0:T(2,128)} %scale_ref.1) | copy-start | bytes 964
  0.7 16.6 %copy-start.7 = (f32[2,40]{1,0:T(2,128)S(1)}, f32[2,40]{1,0:T(2,128)}, u32[]{:S(2)}) copy-start(f32[2,40]{1,0:T(2,128)} %slope_ref.1) | copy-start | bytes 964
  0.7 16.6 %copy-start.8 = (s32[64]{0:T(128)S(1)}, s32[64]{0:T(128)}, u32[]{:S(2)}) copy-start(s32[64]{0:T(128)} %typ.1) | copy-start | bytes 772
  0.7 16.6 %copy-start.9 = (f32[40]{0:T(128)S(1)}, f32[40]{0:T(128)}, u32[]{:S(2)}) copy-start(f32[40]{0:T(128)} %param.19) | copy-start | bytes 484
  5.6 21.7 %collective-permute-start = (f32[4,64,1024]{2,1,0:T(8,128)S(1)}, f32[4,64,1024]{2,1,0:T(8,128)S(1)}, u32[]{:S(2)}, u32[]{:S(2)}) collective-permute-start(f32[4,64,1024]{2,1,0:T(8,128)S(1)} %get-tuple-element.42), channel_id=1, source_target_pairs={{0,4},{4,0},{8,12},{12,8},{16,20},{20,16},{24,28},{28,24},{32,36},... | collective-permute-start | bytes 3145736 | tf_op jit(solution)/shard_map/ppermute | solution.py:542
  5.6 21.6 %collective-permute-start.1 = (f32[4,64,1024]{2,1,0:T(8,128)S(1)}, f32[4,64,1024]{2,1,0:T(8,128)S(1)}, u32[]{:S(2)}, u32[]{:S(2)}) collective-permute-start(f32[4,64,1024]{2,1,0:T(8,128)S(1)} %get-tuple-element.43), channel_id=1, source_target_pairs={{4,8},{8,4},{12,16},{16,12},{20,24},{24,20},{28,32},{32,28},{36,40... | collective-permute-start | bytes 3145736 | tf_op jit(solution)/shard_map/ppermute | solution.py:542
  12.0 12.7 %collective-permute-start.2 = (f32[9,8,1024]{2,1,0:T(8,128)S(1)}, f32[9,8,1024]{2,1,0:T(8,128)S(1)}, u32[]{:S(2)}, u32[]{:S(2)}) collective-permute-start(f32[9,8,1024]{2,1,0:T(8,128)S(1)} %get-tuple-element.44), channel_id=1, source_target_pairs={{0,1},{1,2},{2,3},{3,0},{4,5},{5,6},{6,7},{7,4},{8,9},{9,10},{10,1... | collective-permute-start | bytes 884744 | tf_op jit(solution)/shard_map/ppermute | solution.py:516
  13.6 11.0 %collective-permute-start.3 = (f32[9,8,1024]{2,1,0:T(8,128)S(1)}, f32[9,8,1024]{2,1,0:T(8,128)S(1)}, u32[]{:S(2)}, u32[]{:S(2)}) collective-permute-start(f32[9,8,1024]{2,1,0:T(8,128)S(1)} %get-tuple-element.45), channel_id=1, source_target_pairs={{0,3},{1,0},{2,1},{3,2},{4,7},{5,4},{6,5},{7,6},{8,11},{9,8},{10,9... | collective-permute-start | bytes 884744 | tf_op jit(solution)/shard_map/ppermute | solution.py:516
  15.3 9.4 %collective-permute-start.4 = (f32[1,128]{1,0:T(1,128)S(1)}, f32[1,128]{1,0:T(1,128)S(1)}, u32[]{:S(2)}, u32[]{:S(2)}) collective-permute-start(f32[1,128]{1,0:T(1,128)S(1)} %get-tuple-element.46.cell_ref), channel_id=1, source_target_pairs={{0,2},{1,3},{2,0},{3,1},{4,6},{5,7},{6,4},{7,5},{8,10},{9,11},{10,... | collective-permute-start | bytes 1544 | tf_op jit(solution)/shard_map/ppermute | solution.py:516
  17.3 9.9 %copy-start = (f32[4,64,1024]{2,1,0:T(8,128)S(1)}, f32[4,64,1024]{2,1,0:T(8,128)}, u32[]{:S(2)}) copy-start(f32[4,64,1024]{2,1,0:T(8,128)} %p_ref.5) | copy-start | bytes 3145732
  17.3 9.9 %copy-start.1 = (f32[4,64,1024]{2,1,0:T(8,128)S(1)}, f32[4,64,1024]{2,1,0:T(8,128)}, u32[]{:S(2)}) copy-start(f32[4,64,1024]{2,1,0:T(8,128)} %c_ref.3) | copy-start | bytes 3145732
  24.7 4.8 %collective-permute-start.5 = (f32[3,8,1024]{2,1,0:T(8,128)S(1)}, f32[3,8,1024]{2,1,0:T(8,128)S(1)}, u32[]{:S(2)}, u32[]{:S(2)}) collective-permute-start(f32[3,8,1024]{2,1,0:T(8,128)S(1)} %get-tuple-element.52), channel_id=1, source_target_pairs={{0,4},{4,0},{8,12},{12,8},{16,20},{20,16},{24,28},{28,24},{32,36},... | collective-permute-start | bytes 294920 | tf_op jit(solution)/shard_map/ppermute | solution.py:566
  24.8 8.0 %collective-permute-start.6 = (f32[3,8,1024]{2,1,0:T(8,128)S(1)}, f32[3,8,1024]{2,1,0:T(8,128)S(1)}, u32[]{:S(2)}, u32[]{:S(2)}) collective-permute-start(f32[3,8,1024]{2,1,0:T(8,128)S(1)} %get-tuple-element.53), channel_id=1, source_target_pairs={{4,8},{8,4},{12,16},{16,12},{20,24},{24,20},{28,32},{32,28},{36,40... | collective-permute-start | bytes 294920 | tf_op jit(solution)/shard_map/ppermute | solution.py:566
  33.9 13.7 %collective-permute-start.11 = (f32[3,64,1024]{2,1,0:T(8,128)S(1)}, f32[3,64,1024]{2,1,0:T(8,128)S(1)}, u32[]{:S(2)}, u32[]{:S(2)}) collective-permute-start(f32[3,64,1024]{2,1,0:T(8,128)S(1)} %get-tuple-element.73), channel_id=1, source_target_pairs={{0,4},{4,0},{8,12},{12,8},{16,20},{20,16},{24,28},{28,24},{32,36},... | collective-permute-start | bytes 2359304 | tf_op jit(solution)/shard_map/ppermute | solution.py:592
  33.9 17.1 %collective-permute-start.7 = (f32[3,64,1024]{2,1,0:T(8,128)S(1)}, f32[3,64,1024]{2,1,0:T(8,128)S(1)}, u32[]{:S(2)}, u32[]{:S(2)}) collective-permute-start(f32[3,64,1024]{2,1,0:T(8,128)S(1)} %get-tuple-element.69), channel_id=1, source_target_pairs={{4,8},{8,4},{12,16},{16,12},{20,24},{24,20},{28,32},{32,28},{36,40... | collective-permute-start | bytes 2359304 | tf_op jit(solution)/shard_map/ppermute | solution.py:590
  36.3 6.7 %collective-permute-start.8 = (f32[4,8,1024]{2,1,0:T(8,128)S(1)}, f32[4,8,1024]{2,1,0:T(8,128)S(1)}, u32[]{:S(2)}, u32[]{:S(2)}) collective-permute-start(f32[4,8,1024]{2,1,0:T(8,128)S(1)} %get-tuple-element.61.after), channel_id=1, source_target_pairs={{0,1},{1,2},{2,3},{3,0},{4,5},{5,6},{6,7},{7,4},{8,9},{9,10},{10,1... | collective-permute-start | bytes 393224 | tf_op jit(solution)/shard_map/ppermute | solution.py:516
  37.1 6.0 %collective-permute-start.9 = (f32[4,8,1024]{2,1,0:T(8,128)S(1)}, f32[4,8,1024]{2,1,0:T(8,128)S(1)}, u32[]{:S(2)}, u32[]{:S(2)}) collective-permute-start(f32[4,8,1024]{2,1,0:T(8,128)S(1)} %get-tuple-element.70), channel_id=1, source_target_pairs={{0,3},{1,0},{2,1},{3,2},{4,7},{5,4},{6,5},{7,6},{8,11},{9,8},{10,9... | collective-permute-start | bytes 393224 | tf_op jit(solution)/shard_map/ppermute | solution.py:516
  43.1 4.5 %collective-permute-start.12 = (f32[2,8,1024]{2,1,0:T(8,128)S(1)}, f32[2,8,1024]{2,1,0:T(8,128)S(1)}, u32[]{:S(2)}, u32[]{:S(2)}) collective-permute-start(f32[2,8,1024]{2,1,0:T(8,128)S(1)} %get-tuple-element.74), channel_id=1, source_target_pairs={{0,4},{4,0},{8,12},{12,8},{16,20},{20,16},{24,28},{28,24},{32,36},... | collective-permute-start | bytes 196616 | tf_op jit(solution)/shard_map/ppermute | solution.py:614
  43.3 7.7 %collective-permute-start.10 = (f32[2,8,1024]{2,1,0:T(8,128)S(1)}, f32[2,8,1024]{2,1,0:T(8,128)S(1)}, u32[]{:S(2)}, u32[]{:S(2)}) collective-permute-start(f32[2,8,1024]{2,1,0:T(8,128)S(1)} %get-tuple-element.72), channel_id=1, source_target_pairs={{4,8},{8,4},{12,16},{16,12},{20,24},{24,20},{28,32},{32,28},{36,40... | collective-permute-start | bytes 196616 | tf_op jit(solution)/shard_map/ppermute | solution.py:614

commit v7 on v6

--- a/solution.py
+++ b/solution.py
@@ -140,8 +140,8 @@
 ROOM = 24000000
 
 
-def ionic_kernel(cnt, typ, volt_ref, act_ref, in_ref, ex_ref, scale_ref, slope_ref, cond_ref, rev_ref, st_ref,
-                 out_hbm, ion_ref, s_ref, n_ref, out_ref, flat, rate_ref, sem):
+def ionic_kernel(cnt, typ, volt_ref, act_ref, scale_ref, slope_ref, cond_ref, rev_ref, st_ref,
+                 out_hbm, ion_ref, out_ref, flat, rate_ref, sem):
     width = 16384 // CHUNKS
     at = lambda i: pl.ds(pl.multiple_of(i * width, width), width)
     store = lambda i: pltpu.make_async_copy(out_ref.at[:, at(i)], out_hbm.at[:, at(i)], sem.at[i])
@@ -157,9 +157,6 @@
     for i in range(10):
         rate_ref[i] = jnp.broadcast_to(turned[0:40, i : i + 1], (40, 128))
     lane = iota((8, 128), 1)
-    numbers = [(iota((16, 512), 0) + 16 * k).astype(F32).astype(BF16) for k in range(8)]
-    low = iota((8, 128), 0) < 4
-    odd_row = (iota((8, 128), 0) & 2) // 2
 
     def body(group, carry):
         rows8 = pl.ds(pl.multiple_of(8 * group, 8), 8)
@@ -193,7 +190,21 @@
         ion = [jnp.sum(w1[r] * v[r] - w2[r], axis=0, keepdims=True) for r in range(8)]
         val = jnp.concatenate(ion, axis=0) * act
         ion_ref[rows8, :] = val
-
+        return carry
+
+    lax.fori_loop(0, CHUNKS, body, 0, unroll=2)
+    for i in range(CHUNKS):
+        store(i).wait()
+
+
+def scatter_kernel(ion_ref, act_ref, in_ref, ex_ref, after, s_ref, n_ref):
+    numbers = [(iota((16, 512), 0) + 16 * k).astype(F32).astype(BF16) for k in range(8)]
+    low = iota((8, 128), 0) < 4
+    odd_row = (iota((8, 128), 0) & 2) // 2
+
+    def body(group, carry):
+        rows8 = pl.ds(pl.multiple_of(8 * group, 8), 8)
+        val, act = ion_ref[rows8, :], act_ref[rows8, :]
         x = group // 4
         hi = val.astype(BF16).astype(F32)
         lo = val - hi
@@ -227,9 +238,7 @@
                     dst[x, row, 256 * j + 128 : 256 * j + 256] = pltpu.roll(jnp.where(low, oj, ej), 4, 0)
         return carry
 
-    lax.fori_loop(0, CHUNKS, body, 0, unroll=2)
-    for i in range(CHUNKS):
-        store(i).wait()
+    lax.fori_loop(0, 16, body, 0, unroll=4)
 
 
 def edge_rows(mine, below, above):
@@ -541,18 +550,17 @@
     below, above, far = on_mem(send_up, ring(1)), on_mem(send_down, ring(3)), on_mem(cells, ring(2))
     early_b, early_a = to_b(send_b), to_a(send_a)
 
-    states_next, ion, source, count = pl.pallas_call(
+    states_next, ion = pl.pallas_call(
         ionic_kernel,
-        out_shape=(shape(40, 16384), shape(128, 128), shape(4, 64, 1024), shape(4, 64, 1024)),
-        in_specs=[SM, SM] + [VM] * 9,
-        out_specs=(ANY, VM, VM, VM),
+        out_shape=(shape(40, 16384), near(128, 128)),
+        in_specs=[SM, SM] + [VM] * 7,
+        out_specs=(ANY, VM),
         scratch_shapes=[pltpu.VMEM((40, 16384), F32), pltpu.VMEM((128, 128), F32),
                         pltpu.VMEM((10, 40, 128), F32), pltpu.SemaphoreType.DMA((CHUNKS,))],
         compiler_params=pltpu.CompilerParams(vmem_limit_bytes=ROOM),
-        cost_estimate=pl.CostEstimate(flops=816000000, bytes_accessed=7300000, transcendentals=2600000),
+        cost_estimate=pl.CostEstimate(flops=16000000, bytes_accessed=5300000, transcendentals=2600000),
         name="ionic",
-    )(facet_counts, cell_type, volt, act, intra, extra, rate_scale, rate_slope, type_cond, reversal.reshape(1, 40),
-      states_near)
+    )(facet_counts, cell_type, volt, act, rate_scale, rate_slope, type_cond, reversal.reshape(1, 40), states_near)
 
     y_early, table, more_a, more_b = pl.pallas_call(
         early_edge_kernel,
@@ -562,8 +570,18 @@
         compiler_params=grant(6),
         cost_estimate=pl.CostEstimate(flops=300000, bytes_accessed=1000000, transcendentals=0),
         name="early_edges",
-    )(below, above, far, cells, source)
+    )(below, above, far, cells, ion)
     more_b, more_a = to_b(more_b), to_a(more_a)
+
+    source, count = pl.pallas_call(
+        scatter_kernel,
+        out_shape=(near(4, 64, 1024), near(4, 64, 1024)),
+        in_specs=[VM] * 4 + [ANY],
+        out_specs=(VM, VM),
+        compiler_params=grant(12),
+        cost_estimate=pl.CostEstimate(flops=800000000, bytes_accessed=2300000, transcendentals=0),
+        name="scatter",
+    )(ion, act, intra, extra, table)
 
     w, k = pl.pallas_call(
         prepare_kernel,

time: 54.5 us -> 54 us (level)
  waiting for transfers between devices: 5.02 us -> 1.95 us
  starting transfers between devices: 24.3 us -> 26.6 us
    ppermute x2, waiting for transfers between devices: 3.34 us -> 0.01 us  [per_device(): more_b, more_a = (to_b(more_b), to_a(more_a))]
    ppermute x2, starting transfers between devices: 2.49 us -> 4.3 us  [per_device(): more_b, more_a = (to_b(more_b), to_a(more_a))]
    ppermute x1, starting transfers between devices: 2.39 us -> 3.57 us  [per_device(): late_b = to_b(u_b)]
    ppermute x2, starting transfers between devices: 4.48 us -> 3.76 us  [per_device(): corner_b, corner_a = (to_b(corner_b), to_a(corner_a))]
    ppermute x2, waiting for transfers between devices: 1.15 us -> 1.87 us  [per_device(): corner_b, corner_a = (to_b(corner_b), to_a(corner_a))]
    pallas_call x1 -> x2, Pallas kernels: 7.29 us -> 7.44 us  [the longest x1 4.2 us: per_device(): pl.pallas_call(ionic_kernel, out_shape=(shape(40, 16384), near(128, 128))...]
  transfers between devices with their start and end apart: 13 -> 13, of which waited for: 3 -> 2; matrix products, arithmetic and copies ran while one was open for 0% -> 0% of each run, Pallas kernels for 27% -> 28%
where the time goes in v7:
time: 54 us; the launch traced here: 53.6 us
  starting transfers between devices  26.6 us (49%)
  Pallas kernels  23.9 us (44%)
  waiting for transfers between devices  1.95 us (4%)
  between operations  1.1 us (2%)
    ppermute x5, starting transfers between devices, per_device(): on_mem = lambda x, pairs: lax.ppermute(x, 'mem', pairs)  8.59 us
    ppermute x2, starting transfers between devices, per_device(): early_b, early_a = (to_b(send_b), to_a(send_a))  6.39 us
    pallas_call x1, Pallas kernels, per_device(): pl.pallas_call(gather_kernel, out_shape=(near(40, 16384), near(128, 128),...  4.83 us
    ppermute x2, starting transfers between devices, per_device(): more_b, more_a = (to_b(more_b), to_a(more_a))  4.3 us
    pallas_call x1, Pallas kernels, per_device(): pl.pallas_call(ionic_kernel, out_shape=(shape(40, 16384), near(128, 128))...  4.2 us
    ppermute x2, starting transfers between devices, per_device(): corner_b, corner_a = (to_b(corner_b), to_a(corner_a))  3.76 us
    ppermute x1, starting transfers between devices, per_device(): late_b = to_b(u_b)  3.57 us
    pallas_call x1, Pallas kernels, per_device(): pl.pallas_call(scatter_kernel, out_shape=(near(4, 64, 1024), near(4, 64,...  3.25 us
  transfers between devices with their start and end apart: 13, of which 2 were waited for; matrix products, arithmetic and copies ran while one was open for 0% of the time, Pallas kernels for 28%

profile of v7, /device:TPU:6, one launch (start us, length us, event | category | flops | bytes accessed | tf_op | source)
XLA Modules:
  0.0 53.6 jit_solution(599835763749639365)
XLA Ops:
  0.7 4.8 %voltages.1 = (f32[40,16384]{1,0:T(8,128)S(1)}, f32[128,128]{1,0:T(8,128)S(1)}, f32[1,128]{1,0:T(1,128)S(1)}, f32[128,128]{1,0:T(8,128)S(1)}, s32[8,128]{1,0:T(8...) custom-call(s32[64]{0:T(128)} %cnt.3, ...), custom_call_target="tpu_custom_call" | custom-call | flops 4000000 | bytes 5000000 | tf_op jit(solution)/shard_map/voltages/pallas_call | solution.py:533
  5.5 0.1 collective-permute-start
  5.6 6.3 %collective-permute-start.1 = (f32[4,64,1024]{2,1,0:T(8,128)S(1)}, f32[4,64,1024]{2,1,0:T(8,128)S(1)}, u32[]{:S(2)}, u32[]{:S(2)}) collective-permute-start(f32[4,64,1024]{2,1,0:T(8,128)S(1)} %get-tuple-element.43), channel_id=1, source_target_pairs={{4,8},{8,4},{12,16},{16,12},{20,24},{24,20},{28,32},{32,28},{36,40... | collective-permute-start | bytes 3145736 | tf_op jit(solution)/shard_map/ppermute | solution.py:551
  11.9 1.6 %collective-permute-start.2 = (f32[9,8,1024]{2,1,0:T(8,128)S(1)}, f32[9,8,1024]{2,1,0:T(8,128)S(1)}, u32[]{:S(2)}, u32[]{:S(2)}) collective-permute-start(f32[9,8,1024]{2,1,0:T(8,128)S(1)} %get-tuple-element.44), channel_id=1, source_target_pairs={{0,1},{1,2},{2,3},{3,0},{4,5},{5,6},{6,7},{7,4},{8,9},{9,10},{10,1... | collective-permute-start | bytes 884744 | tf_op jit(solution)/shard_map/ppermute | solution.py:525
  13.6 1.7 %collective-permute-start.3 = (f32[9,8,1024]{2,1,0:T(8,128)S(1)}, f32[9,8,1024]{2,1,0:T(8,128)S(1)}, u32[]{:S(2)}, u32[]{:S(2)}) collective-permute-start(f32[9,8,1024]{2,1,0:T(8,128)S(1)} %get-tuple-element.45), channel_id=1, source_target_pairs={{0,3},{1,0},{2,1},{3,2},{4,7},{5,4},{6,5},{7,6},{8,11},{9,8},{10,9... | collective-permute-start | bytes 884744 | tf_op jit(solution)/shard_map/ppermute | solution.py:525
  15.2 2.0 %collective-permute-start.4 = (f32[1,128]{1,0:T(1,128)S(1)}, f32[1,128]{1,0:T(1,128)S(1)}, u32[]{:S(2)}, u32[]{:S(2)}) collective-permute-start(f32[1,128]{1,0:T(1,128)S(1)} %get-tuple-element.46.cell_ref), channel_id=1, source_target_pairs={{0,2},{1,3},{2,0},{3,1},{4,6},{5,7},{6,4},{7,5},{8,10},{9,11},{10,... | collective-permute-start | bytes 1544 | tf_op jit(solution)/shard_map/ppermute | solution.py:525
  17.3 4.2 %ionic.1 = (f32[40,16384]{1,0:T(8,128)}, f32[128,128]{1,0:T(8,128)S(1)}) custom-call(s32[64]{0:T(128)S(1)} %copy-done.4, s32[64]{0:T(128)S(1)} %copy-done.8, f32[128,128]{1,0:T(8,128)S(1)} %get-tuple-element.47.volt_ref, f32[128,128]{1,0:T(8,128)S(1)} %get-tuple-element.48.act_ref, f32[2,40]{1,0:T(2,128)S(1)} %copy-done.6, f32[2,40]{1,0:T(2,128)S(1)} %copy-done.7, ...), custom_call_target="tpu_custom_call" | custom-call | flops 16000000 | bytes 5300000 | tf_op jit(solution)/shard_map/ionic/pallas_call | solution.py:553
  21.5 0.0 copy-start
  21.5 0.1 early_edges.1
  21.6 0.1 collective-permute-start.5
  21.7 4.2 %collective-permute-start.6 = (f32[3,8,1024]{2,1,0:T(8,128)S(1)}, f32[3,8,1024]{2,1,0:T(8,128)S(1)}, u32[]{:S(2)}, u32[]{:S(2)}) collective-permute-start(f32[3,8,1024]{2,1,0:T(8,128)S(1)} %get-tuple-element.53), channel_id=1, source_target_pairs={{4,8},{8,4},{12,16},{16,12},{20,24},{24,20},{28,32},{32,28},{36,40... | collective-permute-start | bytes 294920 | tf_op jit(solution)/shard_map/ppermute | solution.py:574
  25.9 3.2 %scatter.1 = (f32[4,64,1024]{2,1,0:T(8,128)S(1)}, f32[4,64,1024]{2,1,0:T(8,128)S(1)}) custom-call(f32[128,128]{1,0:T(8,128)S(1)} %get-tuple-element.50.after.ion_ref, f32[128,128]{1,0:T(8,128)S(1)} %get-tuple-element.48.act_ref, s32[128,128]{1,0:T(8,128)S(1)} %bitcast.7, s32[128,128]{1,0:T(8,128)S(1)} %bitcast.9, f32[8,128]{1,0:T(8,128)S(1)} %get-tuple-element.54.after.table_ref), custom_call_target="tpu_custom_call" | custom-call | flops 800000000 | bytes 2300000 | tf_op jit(solution)/shard_map/scatter/pallas_call | solution.py:576
  29.2 2.2 %prepare.1 = (f32[4,64,1024]{2,1,0:T(8,128)S(1)}, f32[4,64,1024]{2,1,0:T(8,128)S(1)}) custom-call(f32[4,64,1024]{2,1,0:T(8,128)S(1)} %copy-done, f32[4,64,1024]{2,1,0:T(8,128)S(1)} %copy-done.1, f32[4,64,1024]{2,1,0:T(8,128)S(1)} %collective-permute-done.a_ref, f32[4,64,1024]{2,1,0:T(8,128)S(1)} %collective-permute-done.1.b_ref, ...), custom_call_target="tpu_custom_call" | custom-call | flops 16000000 | bytes 8000000 | tf_op jit(solution)/shard_map/prepare/pallas_call | solution.py:586
  31.5 1.1 %gap.1 = (f32[4,64,1024]{2,1,0:T(8,128)S(1)}, f32[3,64,1024]{2,1,0:T(8,128)S(1)}, f32[3,64,1024]{2,1,0:T(8,128)S(1)}, f32[4,8,1024]{2,1,0:T(8,128)S(1)}, f32[4,8,1024]{2,1,0:T(8,128)S(1)}, /*index=5*/f32[128,128]{1,0:T(8,128)}) custom-call(f32[8,128]{1,0:T(8,128)S(1)} %get-tuple-element.54.after.table_ref, ...), custom_call_target="tpu_custom_call" | custom-call | flops 1000000 | bytes 5000000 | tf_op jit(solution)/shard_map/gap/pallas_call | solution.py:596
  32.6 3.6 %collective-permute-start.7 = (f32[3,64,1024]{2,1,0:T(8,128)S(1)}, f32[3,64,1024]{2,1,0:T(8,128)S(1)}, u32[]{:S(2)}, u32[]{:S(2)}) collective-permute-start(f32[3,64,1024]{2,1,0:T(8,128)S(1)} %get-tuple-element.69), channel_id=1, source_target_pairs={{4,8},{8,4},{12,16},{16,12},{20,24},{24,20},{28,32},{32,28},{36,40... | collective-permute-start | bytes 2359304 | tf_op jit(solution)/shard_map/ppermute | solution.py:608
  36.2 1.1 %collective-permute-start.8 = (f32[4,8,1024]{2,1,0:T(8,128)S(1)}, f32[4,8,1024]{2,1,0:T(8,128)S(1)}, u32[]{:S(2)}, u32[]{:S(2)}) collective-permute-start(f32[4,8,1024]{2,1,0:T(8,128)S(1)} %get-tuple-element.61.after), channel_id=1, source_target_pairs={{0,1},{1,2},{2,3},{3,0},{4,5},{5,6},{6,7},{7,4},{8,9},{9,10},{10,1... | collective-permute-start | bytes 393224 | tf_op jit(solution)/shard_map/ppermute | solution.py:525
  37.3 2.2 %collective-permute-start.9 = (f32[4,8,1024]{2,1,0:T(8,128)S(1)}, f32[4,8,1024]{2,1,0:T(8,128)S(1)}, u32[]{:S(2)}, u32[]{:S(2)}) collective-permute-start(f32[4,8,1024]{2,1,0:T(8,128)S(1)} %get-tuple-element.70), channel_id=1, source_target_pairs={{0,3},{1,0},{2,1},{3,2},{4,7},{5,4},{6,5},{7,6},{8,11},{9,8},{10,9... | collective-permute-start | bytes 393224 | tf_op jit(solution)/shard_map/ppermute | solution.py:525
  39.5 2.9 %operator.1 = (f32[9,72,1024]{2,1,0:T(8,128)S(1)}, f32[8,72,1024]{2,1,0:T(8,128)S(1)}, f32[8,72,1024]{2,1,0:T(8,128)S(1)}, f32[8,72,1024]{2,1,0:T(8,128)S(1)}, f...) custom-call(f32[4,64,1024]{2,1,0:T(8,128)S(1)} %copy-done.1, f32[4,64,1024]{2,1,0:T(8,128)S(1)} %collective-permute-done.a_ref, ...), custom_call_target="tpu_custom_call" | custom-call | flops 16000000 | bytes 17000000 | tf_op jit(solution)/shard_map/operator/pallas_call | solution.py:613
  42.4 0.1 collective-permute-done.8.below_ref
  42.4 0.3 collective-permute-start.12
  42.7 3.5 %collective-permute-start.10 = (f32[2,8,1024]{2,1,0:T(8,128)S(1)}, f32[2,8,1024]{2,1,0:T(8,128)S(1)}, u32[]{:S(2)}, u32[]{:S(2)}) collective-permute-start(f32[2,8,1024]{2,1,0:T(8,128)S(1)} %get-tuple-element.72), channel_id=1, source_target_pairs={{4,8},{8,4},{12,16},{16,12},{20,24},{24,20},{28,32},{32,28},{36,40... | collective-permute-start | bytes 196616 | tf_op jit(solution)/shard_map/ppermute | solution.py:632
  46.2 2.3 %near.1 = (f32[2,72,1024]{2,1,0:T(8,128)S(1)}, f32[2,72,1024]{2,1,0:T(8,128)S(1)}, f32[2,72,1024]{2,1,0:T(8,128)S(1)}, f32[1,64,1024]{2,1,0:T(8,128)S(1)}) custom-call(f32[4,64,1024]{2,1,0:T(8,128)S(1)} %copy-done, f32[9,72,1024]{2,1,0:T(8,128)S(1)} %get-tuple-element.62.fx, f32[8,72,1024]{2,1,0:T(8,128)S(1)} %get-tuple-element.63.fym, ...), custom_call_target="tpu_custom_call" | custom-call | flops 25000000 | bytes 10000000 | tf_op jit(solution)/shard_map/near/pallas_call | solution.py:634
  48.5 1.9 %collective-permute-done.10.cb_ref = f32[2,8,1024]{2,1,0:T(8,128)S(1)} collective-permute-done((f32[2,8,1024]{2,1,0:T(8,128)S(1)}, f32[2,8,1024]{2,1,0:T(8,128)S(1)}, u32[]{:S(2)}, u32[]{:S(2)}) %collective-permute-start.10) | collective-permute-done | bytes 65568 | tf_op jit(solution)/shard_map/ppermute | solution.py:632
  50.4 3.0 %far.1 = f32[4,64,1024]{2,1,0:T(8,128)} custom-call(f32[4,64,1024]{2,1,0:T(8,128)S(1)} %copy-done, f32[9,72,1024]{2,1,0:T(8,128)S(1)} %get-tuple-element.62.fx, f32[8,72,1024]{2,1,0:T(8,128)S(1)} %get-tuple-element.63.fym, f32[8,72,1024]{2,1,0:T(8,128)S(1)} %get-tuple-element.64.fyp, f32[8,72,1024]{2,1,0:T(8,128)S(1)} %get-tuple-element.65.fzm, ...), custom_call_target="tpu_custom_call" | custom-call | flops 25000000 | bytes 10000000 | tf_op jit(solution)/shard_map/far/pallas_call | solution.py:645
  (32 shorter events, 0.1 us)
Async XLA Ops:
  0.6 16.6 %copy-start.4 = (s32[64]{0:T(128)S(1)}, s32[64]{0:T(128)}, u32[]{:S(2)}) copy-start(s32[64]{0:T(128)} %cnt.3) | copy-start | bytes 772
  0.6 16.6 %copy-start.5 = (f32[3,40]{1,0:T(4,128)S(1)}, f32[3,40]{1,0:T(4,128)}, u32[]{:S(2)}) copy-start(f32[3,40]{1,0:T(4,128)} %cond_ref.1) | copy-start | bytes 1444
  0.7 16.6 %copy-start.6 = (f32[2,40]{1,0:T(2,128)S(1)}, f32[2,40]{1,0:T(2,128)}, u32[]{:S(2)}) copy-start(f32[2,40]{1,0:T(2,128)} %scale_ref.1) | copy-start | bytes 964
  0.7 16.6 %copy-start.7 = (f32[2,40]{1,0:T(2,128)S(1)}, f32[2,40]{1,0:T(2,128)}, u32[]{:S(2)}) copy-start(f32[2,40]{1,0:T(2,128)} %slope_ref.1) | copy-start | bytes 964
  0.7 16.6 %copy-start.8 = (s32[64]{0:T(128)S(1)}, s32[64]{0:T(128)}, u32[]{:S(2)}) copy-start(s32[64]{0:T(128)} %typ.1) | copy-start | bytes 772
  0.7 16.6 %copy-start.9 = (f32[40]{0:T(128)S(1)}, f32[40]{0:T(128)}, u32[]{:S(2)}) copy-start(f32[40]{0:T(128)} %param.19) | copy-start | bytes 484
  5.5 23.7 %collective-permute-start = (f32[4,64,1024]{2,1,0:T(8,128)S(1)}, f32[4,64,1024]{2,1,0:T(8,128)S(1)}, u32[]{:S(2)}, u32[]{:S(2)}) collective-permute-start(f32[4,64,1024]{2,1,0:T(8,128)S(1)} %get-tuple-element.42), channel_id=1, source_target_pairs={{0,4},{4,0},{8,12},{12,8},{16,20},{20,16},{24,28},{28,24},{32,36},... | collective-permute-start | bytes 3145736 | tf_op jit(solution)/shard_map/ppermute | solution.py:551
  5.6 23.6 %collective-permute-start.1 = (f32[4,64,1024]{2,1,0:T(8,128)S(1)}, f32[4,64,1024]{2,1,0:T(8,128)S(1)}, u32[]{:S(2)}, u32[]{:S(2)}) collective-permute-start(f32[4,64,1024]{2,1,0:T(8,128)S(1)} %get-tuple-element.43), channel_id=1, source_target_pairs={{4,8},{8,4},{12,16},{16,12},{20,24},{24,20},{28,32},{32,28},{36,40... | collective-permute-start | bytes 3145736 | tf_op jit(solution)/shard_map/ppermute | solution.py:551
  11.9 9.6 %collective-permute-start.2 = (f32[9,8,1024]{2,1,0:T(8,128)S(1)}, f32[9,8,1024]{2,1,0:T(8,128)S(1)}, u32[]{:S(2)}, u32[]{:S(2)}) collective-permute-start(f32[9,8,1024]{2,1,0:T(8,128)S(1)} %get-tuple-element.44), channel_id=1, source_target_pairs={{0,1},{1,2},{2,3},{3,0},{4,5},{5,6},{6,7},{7,4},{8,9},{9,10},{10,1... | collective-permute-start | bytes 884744 | tf_op jit(solution)/shard_map/ppermute | solution.py:525
  13.6 8.0 %collective-permute-start.3 = (f32[9,8,1024]{2,1,0:T(8,128)S(1)}, f32[9,8,1024]{2,1,0:T(8,128)S(1)}, u32[]{:S(2)}, u32[]{:S(2)}) collective-permute-start(f32[9,8,1024]{2,1,0:T(8,128)S(1)} %get-tuple-element.45), channel_id=1, source_target_pairs={{0,3},{1,0},{2,1},{3,2},{4,7},{5,4},{6,5},{7,6},{8,11},{9,8},{10,9... | collective-permute-start | bytes 884744 | tf_op jit(solution)/shard_map/ppermute | solution.py:525
  15.2 6.3 %collective-permute-start.4 = (f32[1,128]{1,0:T(1,128)S(1)}, f32[1,128]{1,0:T(1,128)S(1)}, u32[]{:S(2)}, u32[]{:S(2)}) collective-permute-start(f32[1,128]{1,0:T(1,128)S(1)} %get-tuple-element.46.cell_ref), channel_id=1, source_target_pairs={{0,2},{1,3},{2,0},{3,1},{4,6},{5,7},{6,4},{7,5},{8,10},{9,11},{10,... | collective-permute-start | bytes 1544 | tf_op jit(solution)/shard_map/ppermute | solution.py:525
  17.3 8.7 %copy-start.2 = (s32[16384]{0:T(1024)S(1)}, s32[16384]{0:T(1024)}, u32[]{:S(2)}) copy-start(s32[16384]{0:T(1024)} %param.21) | copy-start | bytes 196612
  17.3 8.7 %copy-start.3 = (s32[16384]{0:T(1024)S(1)}, s32[16384]{0:T(1024)}, u32[]{:S(2)}) copy-start(s32[16384]{0:T(1024)} %param.22) | copy-start | bytes 196612
  21.5 7.7 %copy-start = (f32[4,64,1024]{2,1,0:T(8,128)S(1)}, f32[4,64,1024]{2,1,0:T(8,128)}, u32[]{:S(2)}) copy-start(f32[4,64,1024]{2,1,0:T(8,128)} %p_ref.5) | copy-start | bytes 3145732
  21.5 7.7 %copy-start.1 = (f32[4,64,1024]{2,1,0:T(8,128)S(1)}, f32[4,64,1024]{2,1,0:T(8,128)}, u32[]{:S(2)}) copy-start(f32[4,64,1024]{2,1,0:T(8,128)} %c_ref.3) | copy-start | bytes 3145732
  21.6 9.9 %collective-permute-start.5 = (f32[3,8,1024]{2,1,0:T(8,128)S(1)}, f32[3,8,1024]{2,1,0:T(8,128)S(1)}, u32[]{:S(2)}, u32[]{:S(2)}) collective-permute-start(f32[3,8,1024]{2,1,0:T(8,128)S(1)} %get-tuple-element.52), channel_id=1, source_target_pairs={{0,4},{4,0},{8,12},{12,8},{16,20},{20,16},{24,28},{28,24},{32,36},... | collective-permute-start | bytes 294920 | tf_op jit(solution)/shard_map/ppermute | solution.py:574
  21.7 9.8 %collective-permute-start.6 = (f32[3,8,1024]{2,1,0:T(8,128)S(1)}, f32[3,8,1024]{2,1,0:T(8,128)S(1)}, u32[]{:S(2)}, u32[]{:S(2)}) collective-permute-start(f32[3,8,1024]{2,1,0:T(8,128)S(1)} %get-tuple-element.53), channel_id=1, source_target_pairs={{4,8},{8,4},{12,16},{16,12},{20,24},{24,20},{28,32},{32,28},{36,40... | collective-permute-start | bytes 294920 | tf_op jit(solution)/shard_map/ppermute | solution.py:574
  32.6 13.7 %collective-permute-start.11 = (f32[3,64,1024]{2,1,0:T(8,128)S(1)}, f32[3,64,1024]{2,1,0:T(8,128)S(1)}, u32[]{:S(2)}, u32[]{:S(2)}) collective-permute-start(f32[3,64,1024]{2,1,0:T(8,128)S(1)} %get-tuple-element.73), channel_id=1, source_target_pairs={{0,4},{4,0},{8,12},{12,8},{16,20},{20,16},{24,28},{28,24},{32,36},... | collective-permute-start | bytes 2359304 | tf_op jit(solution)/shard_map/ppermute | solution.py:610
  32.6 17.8 %collective-permute-start.7 = (f32[3,64,1024]{2,1,0:T(8,128)S(1)}, f32[3,64,1024]{2,1,0:T(8,128)S(1)}, u32[]{:S(2)}, u32[]{:S(2)}) collective-permute-start(f32[3,64,1024]{2,1,0:T(8,128)S(1)} %get-tuple-element.69), channel_id=1, source_target_pairs={{4,8},{8,4},{12,16},{16,12},{20,24},{24,20},{28,32},{32,28},{36,40... | collective-permute-start | bytes 2359304 | tf_op jit(solution)/shard_map/ppermute | solution.py:608
  36.2 6.2 %collective-permute-start.8 = (f32[4,8,1024]{2,1,0:T(8,128)S(1)}, f32[4,8,1024]{2,1,0:T(8,128)S(1)}, u32[]{:S(2)}, u32[]{:S(2)}) collective-permute-start(f32[4,8,1024]{2,1,0:T(8,128)S(1)} %get-tuple-element.61.after), channel_id=1, source_target_pairs={{0,1},{1,2},{2,3},{3,0},{4,5},{5,6},{6,7},{7,4},{8,9},{9,10},{10,1... | collective-permute-start | bytes 393224 | tf_op jit(solution)/shard_map/ppermute | solution.py:525
  37.3 5.1 %collective-permute-start.9 = (f32[4,8,1024]{2,1,0:T(8,128)S(1)}, f32[4,8,1024]{2,1,0:T(8,128)S(1)}, u32[]{:S(2)}, u32[]{:S(2)}) collective-permute-start(f32[4,8,1024]{2,1,0:T(8,128)S(1)} %get-tuple-element.70), channel_id=1, source_target_pairs={{0,3},{1,0},{2,1},{3,2},{4,7},{5,4},{6,5},{7,6},{8,11},{9,8},{10,9... | collective-permute-start | bytes 393224 | tf_op jit(solution)/shard_map/ppermute | solution.py:525
  42.4 3.8 %collective-permute-start.12 = (f32[2,8,1024]{2,1,0:T(8,128)S(1)}, f32[2,8,1024]{2,1,0:T(8,128)S(1)}, u32[]{:S(2)}, u32[]{:S(2)}) collective-permute-start(f32[2,8,1024]{2,1,0:T(8,128)S(1)} %get-tuple-element.74), channel_id=1, source_target_pairs={{0,4},{4,0},{8,12},{12,8},{16,20},{20,16},{24,28},{28,24},{32,36},... | collective-permute-start | bytes 196616 | tf_op jit(solution)/shard_map/ppermute | solution.py:632
  42.7 7.7 %collective-permute-start.10 = (f32[2,8,1024]{2,1,0:T(8,128)S(1)}, f32[2,8,1024]{2,1,0:T(8,128)S(1)}, u32[]{:S(2)}, u32[]{:S(2)}) collective-permute-start(f32[2,8,1024]{2,1,0:T(8,128)S(1)} %get-tuple-element.72), channel_id=1, source_target_pairs={{4,8},{8,4},{12,16},{16,12},{20,24},{24,20},{28,32},{32,28},{36,40... | collective-permute-start | bytes 196616 | tf_op jit(solution)/shard_map/ppermute | solution.py:632

commit v8 on v7

--- a/solution.py
+++ b/solution.py
@@ -197,15 +197,17 @@
         store(i).wait()
 
 
-def scatter_kernel(ion_ref, act_ref, in_ref, ex_ref, after, s_ref, n_ref):
+def scatter_kernel(first, ion_ref, act_ref, in_ref, ex_ref, after, s_ref, n_ref):
+    par, has_b, mine, v = place()
     numbers = [(iota((16, 512), 0) + 16 * k).astype(F32).astype(BF16) for k in range(8)]
     low = iota((8, 128), 0) < 4
     odd_row = (iota((8, 128), 0) & 2) // 2
 
-    def body(group, carry):
+    def body(turn, carry):
+        group = 4 * plane_of(par, first + turn // 4) + turn % 4
         rows8 = pl.ds(pl.multiple_of(8 * group, 8), 8)
         val, act = ion_ref[rows8, :], act_ref[rows8, :]
-        x = group // 4
+        x = turn // 4
         hi = val.astype(BF16).astype(F32)
         lo = val - hi
         mids, lanes = [], []
@@ -230,7 +232,7 @@
                 right = jnp.concatenate([jnp.where(at == number, one, none) for number in numbers], axis=0)
                 out = lax.dot_general(left, right, (((1,), (1,)), ((), ())), preferred_element_type=F32)
                 results.append((out[0:32] + out[32:64], out[64:96]))
-            row = pl.ds(pl.multiple_of((2 * (group % 4) + q) * 8, 8), 8)
+            row = pl.ds(pl.multiple_of((2 * (turn % 4) + q) * 8, 8), 8)
             for dst, e, o in ((s_ref, results[0][0], results[1][0]), (n_ref, results[0][1], results[1][1])):
                 for j in range(4):
                     ej, oj = e[8 * j : 8 * j + 8], o[8 * j : 8 * j + 8]
@@ -238,7 +240,7 @@
                     dst[x, row, 256 * j + 128 : 256 * j + 256] = pltpu.roll(jnp.where(low, oj, ej), 4, 0)
         return carry
 
-    lax.fori_loop(0, 16, body, 0, unroll=4)
+    lax.fori_loop(0, 8, body, 0, unroll=4)
 
 
 def edge_rows(mine, below, above):
@@ -339,20 +341,22 @@
     return ((t[0] + t[1]) + (t[2] + t[3])) + (t[4] + t[5])
 
 
-def prepare_kernel(p_ref, c_ref, a_ref, b_ref, y_ref, s_ref, n_ref, w_ref, k_ref):
+def prepare_kernel(p_ref, c_ref, a_ref, b_ref, y_ref, s_one, n_one, s_two, n_two, w_ref, k_ref):
     par, has_b, mine, v = place()
     inside = jnp.where(has_b, 1.0, 0.0)
     conduct = reader(par, inside, c_ref, a_ref, b_ref, y_ref)
     own = reader(par, inside, p_ref, a_ref.at[3:4], b_ref.at[3:4], y_ref, own_y=4)
     for e in range(3, 7):
         x = plane_of(par, e - 3)
+        s_ref, n_ref = (s_one, n_one) if e < 5 else (s_two, n_two)
+        at = (e - 3) % 2
         pc, pp = Plane(conduct, e), Plane(own, e)
         for t in range(8):
             rows = slice(8 * t, 8 * t + 8)
             fs, inv = couplings(pc, t)
             p, *views = pp.views(t)
-            w_ref[x, rows, :] = (p + weighted(fs, views) - 0.5 * s_ref[x, rows, :]) * inv - p
-            k_ref[x, rows, :] = (-0.5 * inv) * n_ref[x, rows, :]
+            w_ref[x, rows, :] = (p + weighted(fs, views) - 0.5 * s_ref[at, rows, :]) * inv - p
+            k_ref[x, rows, :] = (-0.5 * inv) * n_ref[at, rows, :]
 
 
 def gap_kernel(table_ref, ta_ref, tb_ref, part_ref, cond_ref, ion_ref, act_ref, w_ref, k_ref,
@@ -562,6 +566,19 @@
         name="ionic",
     )(facet_counts, cell_type, volt, act, rate_scale, rate_slope, type_cond, reversal.reshape(1, 40), states_near)
 
+    def scatter(first, after):
+        return pl.pallas_call(
+            functools.partial(scatter_kernel, first),
+            out_shape=(near(2, 64, 1024), near(2, 64, 1024)),
+            in_specs=[VM] * 4 + [ANY],
+            out_specs=(VM, VM),
+            compiler_params=grant(12),
+            cost_estimate=pl.CostEstimate(flops=400000000, bytes_accessed=1200000, transcendentals=0),
+            name="scatter",
+        )(ion, act, intra, extra, after)
+
+    half_one = scatter(0, volt)
+
     y_early, table, more_a, more_b = pl.pallas_call(
         early_edge_kernel,
         out_shape=(shape(8, 8, 1024), shape(8, 128), shape(3, 8, 1024), shape(3, 8, 1024)),
@@ -570,28 +587,20 @@
         compiler_params=grant(6),
         cost_estimate=pl.CostEstimate(flops=300000, bytes_accessed=1000000, transcendentals=0),
         name="early_edges",
-    )(below, above, far, cells, ion)
+    )(below, above, far, cells, half_one[0])
     more_b, more_a = to_b(more_b), to_a(more_a)
 
-    source, count = pl.pallas_call(
-        scatter_kernel,
-        out_shape=(near(4, 64, 1024), near(4, 64, 1024)),
-        in_specs=[VM] * 4 + [ANY],
-        out_specs=(VM, VM),
-        compiler_params=grant(12),
-        cost_estimate=pl.CostEstimate(flops=800000000, bytes_accessed=2300000, transcendentals=0),
-        name="scatter",
-    )(ion, act, intra, extra, table)
+    half_two = scatter(2, table)
 
     w, k = pl.pallas_call(
         prepare_kernel,
         out_shape=(shape(4, 64, 1024), shape(4, 64, 1024)),
-        in_specs=[VM] * 7,
+        in_specs=[VM] * 9,
         out_specs=(VM, VM),
         compiler_params=grant(20),
         cost_estimate=pl.CostEstimate(flops=16000000, bytes_accessed=8000000, transcendentals=0),
         name="prepare",
-    )(potential, conductivity, early_a, early_b, y_early, source, count)
+    )(potential, conductivity, early_a, early_b, y_early, *half_one, *half_two)
 
     u, u_a, u_b, u_up, u_down, membrane = pl.pallas_call(
         gap_kernel,

time: 54 us -> 53.8 us (level)
  starting transfers between devices: 26.6 us -> 24.8 us
  waiting for transfers between devices: 1.95 us -> 3.5 us
    ppermute x2, starting transfers between devices: 4.3 us -> 2.63 us  [per_device(): more_b, more_a = (to_b(more_b), to_a(more_a))]
    ppermute x2, waiting for transfers between devices: 0.01 us -> 1.55 us  [per_device(): more_b, more_a = (to_b(more_b), to_a(more_a))]
    pallas_call x1 -> x2, Pallas kernels: 3.25 us -> 3.28 us  [scatter(): pl.pallas_call(functools.partial(scatter_kernel, first), out_shape=(near(...]
  transfers between devices with their start and end apart: 13 -> 13, of which waited for: 2 -> 3; matrix products, arithmetic and copies ran while one was open for 0% -> 0% of each run, Pallas kernels for 28% -> 28%
where the time goes in v8:
time: 53.8 us; the launch traced here: 53.3 us
  starting transfers between devices  24.8 us (46%)
  Pallas kernels  23.9 us (44%)
  waiting for transfers between devices  3.5 us (7%)
  between operations  1.11 us (2%)
    ppermute x5, starting transfers between devices, per_device(): on_mem = lambda x, pairs: lax.ppermute(x, 'mem', pairs)  8.59 us
    ppermute x2, starting transfers between devices, per_device(): early_b, early_a = (to_b(send_b), to_a(send_a))  6.39 us
    pallas_call x1, Pallas kernels, per_device(): pl.pallas_call(gather_kernel, out_shape=(near(40, 16384), near(128, 128),...  4.83 us
    pallas_call x1, Pallas kernels, per_device(): pl.pallas_call(ionic_kernel, out_shape=(shape(40, 16384), near(128, 128))...  4.19 us
    ppermute x1, starting transfers between devices, per_device(): late_b = to_b(u_b)  3.58 us
    ppermute x2, starting transfers between devices, per_device(): corner_b, corner_a = (to_b(corner_b), to_a(corner_a))  3.57 us
    pallas_call x2, Pallas kernels, scatter(): pl.pallas_call(functools.partial(scatter_kernel, first), out_shape=(near(...  3.28 us
    pallas_call x1, Pallas kernels, per_device(): pl.pallas_call(far_kernel, out_shape=shape(4, 64, 1024), in_specs=[VM] *...  3.04 us
  transfers between devices with their start and end apart: 13, of which 3 were waited for; matrix products, arithmetic and copies ran while one was open for 0% of the time, Pallas kernels for 28%

profile of v8, /device:TPU:6, one launch (start us, length us, event | category | flops | bytes accessed | tf_op | source)
XLA Modules:
  0.0 53.3 jit_solution(7342586893233975380)
XLA Ops:
  0.7 4.8 %voltages.1 = (f32[40,16384]{1,0:T(8,128)S(1)}, f32[128,128]{1,0:T(8,128)S(1)}, f32[1,128]{1,0:T(1,128)S(1)}, f32[128,128]{1,0:T(8,128)S(1)}, s32[8,128]{1,0:T(8...) custom-call(s32[64]{0:T(128)} %cnt.3, ...), custom_call_target="tpu_custom_call" | custom-call | flops 4000000 | bytes 5000000 | tf_op jit(solution)/shard_map/voltages/pallas_call | solution.py:537
  5.5 0.1 collective-permute-start
  5.6 6.3 %collective-permute-start.1 = (f32[4,64,1024]{2,1,0:T(8,128)S(1)}, f32[4,64,1024]{2,1,0:T(8,128)S(1)}, u32[]{:S(2)}, u32[]{:S(2)}) collective-permute-start(f32[4,64,1024]{2,1,0:T(8,128)S(1)} %get-tuple-element.45), channel_id=1, source_target_pairs={{4,8},{8,4},{12,16},{16,12},{20,24},{24,20},{28,32},{32,28},{36,40... | collective-permute-start | bytes 3145736 | tf_op jit(solution)/shard_map/ppermute | solution.py:555
  11.9 1.6 %collective-permute-start.2 = (f32[9,8,1024]{2,1,0:T(8,128)S(1)}, f32[9,8,1024]{2,1,0:T(8,128)S(1)}, u32[]{:S(2)}, u32[]{:S(2)}) collective-permute-start(f32[9,8,1024]{2,1,0:T(8,128)S(1)} %get-tuple-element.46), channel_id=1, source_target_pairs={{0,1},{1,2},{2,3},{3,0},{4,5},{5,6},{6,7},{7,4},{8,9},{9,10},{10,1... | collective-permute-start | bytes 884744 | tf_op jit(solution)/shard_map/ppermute | solution.py:529
  13.6 1.7 %collective-permute-start.3 = (f32[9,8,1024]{2,1,0:T(8,128)S(1)}, f32[9,8,1024]{2,1,0:T(8,128)S(1)}, u32[]{:S(2)}, u32[]{:S(2)}) collective-permute-start(f32[9,8,1024]{2,1,0:T(8,128)S(1)} %get-tuple-element.47), channel_id=1, source_target_pairs={{0,3},{1,0},{2,1},{3,2},{4,7},{5,4},{6,5},{7,6},{8,11},{9,8},{10,9... | collective-permute-start | bytes 884744 | tf_op jit(solution)/shard_map/ppermute | solution.py:529
  15.2 2.0 %collective-permute-start.4 = (f32[1,128]{1,0:T(1,128)S(1)}, f32[1,128]{1,0:T(1,128)S(1)}, u32[]{:S(2)}, u32[]{:S(2)}) collective-permute-start(f32[1,128]{1,0:T(1,128)S(1)} %get-tuple-element.48.cell_ref), channel_id=1, source_target_pairs={{0,2},{1,3},{2,0},{3,1},{4,6},{5,7},{6,4},{7,5},{8,10},{9,11},{10,... | collective-permute-start | bytes 1544 | tf_op jit(solution)/shard_map/ppermute | solution.py:529
  17.3 4.2 %ionic.1 = (f32[40,16384]{1,0:T(8,128)}, f32[128,128]{1,0:T(8,128)S(1)}) custom-call(s32[64]{0:T(128)S(1)} %copy-done.4, s32[64]{0:T(128)S(1)} %copy-done.8, f32[128,128]{1,0:T(8,128)S(1)} %get-tuple-element.49.volt_ref.after, f32[128,128]{1,0:T(8,128)S(1)} %get-tuple-element.50.act_ref, f32[2,40]{1,0:T(2,128)S(1)} %copy-done.6, f32[2,40]{1,0:T(2,128)S(1)} %copy-done.7, ...), custom_call_target="tpu_custom_call" | custom-call | flops 16000000 | bytes 5300000 | tf_op jit(solution)/shard_map/ionic/pallas_call | solution.py:557
  21.5 1.6 %scatter.2 = (f32[2,64,1024]{2,1,0:T(8,128)S(1)}, f32[2,64,1024]{2,1,0:T(8,128)S(1)}) custom-call(f32[128,128]{1,0:T(8,128)S(1)} %get-tuple-element.52.ion_ref, f32[128,128]{1,0:T(8,128)S(1)} %get-tuple-element.50.act_ref, s32[128,128]{1,0:T(8,128)S(1)} %bitcast.7, s32[128,128]{1,0:T(8,128)S(1)} %bitcast.10, f32[128,128]{1,0:T(8,128)S(1)} %get-tuple-element.49.volt_ref.after), custom_call_target="tpu_custom_call" | custom-call | flops 400000000 | bytes 1200000 | tf_op jit(solution)/shard_map/scatter/pallas_call | solution.py:570
  23.2 0.1 early_edges.1
  23.3 0.1 collective-permute-start.5
  23.4 2.5 %collective-permute-start.6 = (f32[3,8,1024]{2,1,0:T(8,128)S(1)}, f32[3,8,1024]{2,1,0:T(8,128)S(1)}, u32[]{:S(2)}, u32[]{:S(2)}) collective-permute-start(f32[3,8,1024]{2,1,0:T(8,128)S(1)} %get-tuple-element.56), channel_id=1, source_target_pairs={{4,8},{8,4},{12,16},{16,12},{20,24},{24,20},{28,32},{32,28},{36,40... | collective-permute-start | bytes 294920 | tf_op jit(solution)/shard_map/ppermute | solution.py:591
  25.9 1.6 %scatter.3 = (f32[2,64,1024]{2,1,0:T(8,128)S(1)}, f32[2,64,1024]{2,1,0:T(8,128)S(1)}) custom-call(f32[128,128]{1,0:T(8,128)S(1)} %get-tuple-element.52.ion_ref, f32[128,128]{1,0:T(8,128)S(1)} %get-tuple-element.50.act_ref, s32[128,128]{1,0:T(8,128)S(1)} %bitcast.8, s32[128,128]{1,0:T(8,128)S(1)} %bitcast.11, f32[8,128]{1,0:T(8,128)S(1)} %get-tuple-element.57.after.table_ref), custom_call_target="tpu_custom_call" | custom-call | flops 400000000 | bytes 1200000 | tf_op jit(solution)/shard_map/scatter/pallas_call | solution.py:570
  27.6 2.2 %prepare.1 = (f32[4,64,1024]{2,1,0:T(8,128)S(1)}, f32[4,64,1024]{2,1,0:T(8,128)S(1)}) custom-call(f32[4,64,1024]{2,1,0:T(8,128)S(1)} %copy-done, f32[4,64,1024]{2,1,0:T(8,128)S(1)} %copy-done.1, f32[4,64,1024]{2,1,0:T(8,128)S(1)} %collective-permute-done.a_ref, f32[4,64,1024]{2,1,0:T(8,128)S(1)} %collective-permute-done.1.b_ref, ...), custom_call_target="tpu_custom_call" | custom-call | flops 16000000 | bytes 8000000 | tf_op jit(solution)/shard_map/prepare/pallas_call | solution.py:595
  29.9 1.5 %collective-permute-done.6.tb_ref.cb_ref = f32[3,8,1024]{2,1,0:T(8,128)S(1)} collective-permute-done((f32[3,8,1024]{2,1,0:T(8,128)S(1)}, f32[3,8,1024]{2,1,0:T(8,128)S(1)}, u32[]{:S(2)}, u32[]{:S(2)}) %collective-permute-start.6) | collective-permute-done | bytes 98336 | tf_op jit(solution)/shard_map/ppermute | solution.py:591
  31.4 1.1 %gap.1 = (f32[4,64,1024]{2,1,0:T(8,128)S(1)}, f32[3,64,1024]{2,1,0:T(8,128)S(1)}, f32[3,64,1024]{2,1,0:T(8,128)S(1)}, f32[4,8,1024]{2,1,0:T(8,128)S(1)}, f32[4,8,1024]{2,1,0:T(8,128)S(1)}, /*index=5*/f32[128,128]{1,0:T(8,128)}) custom-call(f32[8,128]{1,0:T(8,128)S(1)} %get-tuple-element.57.after.table_ref, ...), custom_call_target="tpu_custom_call" | custom-call | flops 1000000 | bytes 5000000 | tf_op jit(solution)/shard_map/gap/pallas_call | solution.py:605
  32.5 3.6 %collective-permute-start.7 = (f32[3,64,1024]{2,1,0:T(8,128)S(1)}, f32[3,64,1024]{2,1,0:T(8,128)S(1)}, u32[]{:S(2)}, u32[]{:S(2)}) collective-permute-start(f32[3,64,1024]{2,1,0:T(8,128)S(1)} %get-tuple-element.73), channel_id=1, source_target_pairs={{4,8},{8,4},{12,16},{16,12},{20,24},{24,20},{28,32},{32,28},{36,40... | collective-permute-start | bytes 2359304 | tf_op jit(solution)/shard_map/ppermute | solution.py:617
  36.1 0.7 %collective-permute-start.8 = (f32[4,8,1024]{2,1,0:T(8,128)S(1)}, f32[4,8,1024]{2,1,0:T(8,128)S(1)}, u32[]{:S(2)}, u32[]{:S(2)}) collective-permute-start(f32[4,8,1024]{2,1,0:T(8,128)S(1)} %get-tuple-element.65.after), channel_id=1, source_target_pairs={{0,1},{1,2},{2,3},{3,0},{4,5},{5,6},{6,7},{7,4},{8,9},{9,10},{10,1... | collective-permute-start | bytes 393224 | tf_op jit(solution)/shard_map/ppermute | solution.py:529
  36.8 2.6 %collective-permute-start.9 = (f32[4,8,1024]{2,1,0:T(8,128)S(1)}, f32[4,8,1024]{2,1,0:T(8,128)S(1)}, u32[]{:S(2)}, u32[]{:S(2)}) collective-permute-start(f32[4,8,1024]{2,1,0:T(8,128)S(1)} %get-tuple-element.74), channel_id=1, source_target_pairs={{0,3},{1,0},{2,1},{3,2},{4,7},{5,4},{6,5},{7,6},{8,11},{9,8},{10,9... | collective-permute-start | bytes 393224 | tf_op jit(solution)/shard_map/ppermute | solution.py:529
  39.4 2.9 %operator.1 = (f32[9,72,1024]{2,1,0:T(8,128)S(1)}, f32[8,72,1024]{2,1,0:T(8,128)S(1)}, f32[8,72,1024]{2,1,0:T(8,128)S(1)}, f32[8,72,1024]{2,1,0:T(8,128)S(1)}, f...) custom-call(f32[4,64,1024]{2,1,0:T(8,128)S(1)} %copy-done.1, f32[4,64,1024]{2,1,0:T(8,128)S(1)} %collective-permute-done.a_ref, ...), custom_call_target="tpu_custom_call" | custom-call | flops 16000000 | bytes 17000000 | tf_op jit(solution)/shard_map/operator/pallas_call | solution.py:622
  42.4 0.1 collective-permute-start.12
  42.5 3.5 %collective-permute-start.10 = (f32[2,8,1024]{2,1,0:T(8,128)S(1)}, f32[2,8,1024]{2,1,0:T(8,128)S(1)}, u32[]{:S(2)}, u32[]{:S(2)}) collective-permute-start(f32[2,8,1024]{2,1,0:T(8,128)S(1)} %get-tuple-element.76), channel_id=1, source_target_pairs={{4,8},{8,4},{12,16},{16,12},{20,24},{24,20},{28,32},{32,28},{36,40... | collective-permute-start | bytes 196616 | tf_op jit(solution)/shard_map/ppermute | solution.py:641
  46.0 2.3 %near.1 = (f32[2,72,1024]{2,1,0:T(8,128)S(1)}, f32[2,72,1024]{2,1,0:T(8,128)S(1)}, f32[2,72,1024]{2,1,0:T(8,128)S(1)}, f32[1,64,1024]{2,1,0:T(8,128)S(1)}) custom-call(f32[4,64,1024]{2,1,0:T(8,128)S(1)} %copy-done, f32[9,72,1024]{2,1,0:T(8,128)S(1)} %get-tuple-element.66.fx, f32[8,72,1024]{2,1,0:T(8,128)S(1)} %get-tuple-element.67.fym, ...), custom_call_target="tpu_custom_call" | custom-call | flops 25000000 | bytes 10000000 | tf_op jit(solution)/shard_map/near/pallas_call | solution.py:643
  48.3 1.9 %collective-permute-done.10.cb_ref = f32[2,8,1024]{2,1,0:T(8,128)S(1)} collective-permute-done((f32[2,8,1024]{2,1,0:T(8,128)S(1)}, f32[2,8,1024]{2,1,0:T(8,128)S(1)}, u32[]{:S(2)}, u32[]{:S(2)}) %collective-permute-start.10) | collective-permute-done | bytes 65568 | tf_op jit(solution)/shard_map/ppermute | solution.py:641
  50.1 3.0 %far.1 = f32[4,64,1024]{2,1,0:T(8,128)} custom-call(f32[4,64,1024]{2,1,0:T(8,128)S(1)} %copy-done, f32[9,72,1024]{2,1,0:T(8,128)S(1)} %get-tuple-element.66.fx, f32[8,72,1024]{2,1,0:T(8,128)S(1)} %get-tuple-element.67.fym, f32[8,72,1024]{2,1,0:T(8,128)S(1)} %get-tuple-element.68.fyp, f32[8,72,1024]{2,1,0:T(8,128)S(1)} %get-tuple-element.69.fzm, ...), custom_call_target="tpu_custom_call" | custom-call | flops 25000000 | bytes 10000000 | tf_op jit(solution)/shard_map/far/pallas_call | solution.py:654
  (33 shorter events, 0.2 us)
Async XLA Ops:
  0.6 16.6 %copy-start.4 = (s32[64]{0:T(128)S(1)}, s32[64]{0:T(128)}, u32[]{:S(2)}) copy-start(s32[64]{0:T(128)} %cnt.3) | copy-start | bytes 772
  0.6 16.6 %copy-start.5 = (f32[3,40]{1,0:T(4,128)S(1)}, f32[3,40]{1,0:T(4,128)}, u32[]{:S(2)}) copy-start(f32[3,40]{1,0:T(4,128)} %cond_ref.1) | copy-start | bytes 1444
  0.7 16.6 %copy-start.6 = (f32[2,40]{1,0:T(2,128)S(1)}, f32[2,40]{1,0:T(2,128)}, u32[]{:S(2)}) copy-start(f32[2,40]{1,0:T(2,128)} %scale_ref.1) | copy-start | bytes 964
  0.7 16.6 %copy-start.7 = (f32[2,40]{1,0:T(2,128)S(1)}, f32[2,40]{1,0:T(2,128)}, u32[]{:S(2)}) copy-start(f32[2,40]{1,0:T(2,128)} %slope_ref.1) | copy-start | bytes 964
  0.7 16.6 %copy-start.8 = (s32[64]{0:T(128)S(1)}, s32[64]{0:T(128)}, u32[]{:S(2)}) copy-start(s32[64]{0:T(128)} %typ.1) | copy-start | bytes 772
  0.7 16.6 %copy-start.9 = (f32[40]{0:T(128)S(1)}, f32[40]{0:T(128)}, u32[]{:S(2)}) copy-start(f32[40]{0:T(128)} %param.19) | copy-start | bytes 484
  5.5 22.0 %collective-permute-start = (f32[4,64,1024]{2,1,0:T(8,128)S(1)}, f32[4,64,1024]{2,1,0:T(8,128)S(1)}, u32[]{:S(2)}, u32[]{:S(2)}) collective-permute-start(f32[4,64,1024]{2,1,0:T(8,128)S(1)} %get-tuple-element.44), channel_id=1, source_target_pairs={{0,4},{4,0},{8,12},{12,8},{16,20},{20,16},{24,28},{28,24},{32,36},... | collective-permute-start | bytes 3145736 | tf_op jit(solution)/shard_map/ppermute | solution.py:555
  5.6 21.9 %collective-permute-start.1 = (f32[4,64,1024]{2,1,0:T(8,128)S(1)}, f32[4,64,1024]{2,1,0:T(8,128)S(1)}, u32[]{:S(2)}, u32[]{:S(2)}) collective-permute-start(f32[4,64,1024]{2,1,0:T(8,128)S(1)} %get-tuple-element.45), channel_id=1, source_target_pairs={{4,8},{8,4},{12,16},{16,12},{20,24},{24,20},{28,32},{32,28},{36,40... | collective-permute-start | bytes 3145736 | tf_op jit(solution)/shard_map/ppermute | solution.py:555
  11.9 11.3 %collective-permute-start.2 = (f32[9,8,1024]{2,1,0:T(8,128)S(1)}, f32[9,8,1024]{2,1,0:T(8,128)S(1)}, u32[]{:S(2)}, u32[]{:S(2)}) collective-permute-start(f32[9,8,1024]{2,1,0:T(8,128)S(1)} %get-tuple-element.46), channel_id=1, source_target_pairs={{0,1},{1,2},{2,3},{3,0},{4,5},{5,6},{6,7},{7,4},{8,9},{9,10},{10,1... | collective-permute-start | bytes 884744 | tf_op jit(solution)/shard_map/ppermute | solution.py:529
  13.6 9.6 %collective-permute-start.3 = (f32[9,8,1024]{2,1,0:T(8,128)S(1)}, f32[9,8,1024]{2,1,0:T(8,128)S(1)}, u32[]{:S(2)}, u32[]{:S(2)}) collective-permute-start(f32[9,8,1024]{2,1,0:T(8,128)S(1)} %get-tuple-element.47), channel_id=1, source_target_pairs={{0,3},{1,0},{2,1},{3,2},{4,7},{5,4},{6,5},{7,6},{8,11},{9,8},{10,9... | collective-permute-start | bytes 884744 | tf_op jit(solution)/shard_map/ppermute | solution.py:529
  15.2 7.9 %collective-permute-start.4 = (f32[1,128]{1,0:T(1,128)S(1)}, f32[1,128]{1,0:T(1,128)S(1)}, u32[]{:S(2)}, u32[]{:S(2)}) collective-permute-start(f32[1,128]{1,0:T(1,128)S(1)} %get-tuple-element.48.cell_ref), channel_id=1, source_target_pairs={{0,2},{1,3},{2,0},{3,1},{4,6},{5,7},{6,4},{7,5},{8,10},{9,11},{10,... | collective-permute-start | bytes 1544 | tf_op jit(solution)/shard_map/ppermute | solution.py:529
  17.3 4.2 %copy-start.2 = (s32[16384]{0:T(1024)S(1)}, s32[16384]{0:T(1024)}, u32[]{:S(2)}) copy-start(s32[16384]{0:T(1024)} %param.21) | copy-start | bytes 196612
  17.3 4.2 %copy-start.3 = (s32[16384]{0:T(1024)S(1)}, s32[16384]{0:T(1024)}, u32[]{:S(2)}) copy-start(s32[16384]{0:T(1024)} %param.22) | copy-start | bytes 196612
  21.5 6.1 %copy-start = (f32[4,64,1024]{2,1,0:T(8,128)S(1)}, f32[4,64,1024]{2,1,0:T(8,128)}, u32[]{:S(2)}) copy-start(f32[4,64,1024]{2,1,0:T(8,128)} %p_ref.5) | copy-start | bytes 3145732
  21.5 6.1 %copy-start.1 = (f32[4,64,1024]{2,1,0:T(8,128)S(1)}, f32[4,64,1024]{2,1,0:T(8,128)}, u32[]{:S(2)}) copy-start(f32[4,64,1024]{2,1,0:T(8,128)} %c_ref.3) | copy-start | bytes 3145732
  23.3 6.6 %collective-permute-start.5 = (f32[3,8,1024]{2,1,0:T(8,128)S(1)}, f32[3,8,1024]{2,1,0:T(8,128)S(1)}, u32[]{:S(2)}, u32[]{:S(2)}) collective-permute-start(f32[3,8,1024]{2,1,0:T(8,128)S(1)} %get-tuple-element.55), channel_id=1, source_target_pairs={{0,4},{4,0},{8,12},{12,8},{16,20},{20,16},{24,28},{28,24},{32,36},... | collective-permute-start | bytes 294920 | tf_op jit(solution)/shard_map/ppermute | solution.py:591
  23.4 8.0 %collective-permute-start.6 = (f32[3,8,1024]{2,1,0:T(8,128)S(1)}, f32[3,8,1024]{2,1,0:T(8,128)S(1)}, u32[]{:S(2)}, u32[]{:S(2)}) collective-permute-start(f32[3,8,1024]{2,1,0:T(8,128)S(1)} %get-tuple-element.56), channel_id=1, source_target_pairs={{4,8},{8,4},{12,16},{16,12},{20,24},{24,20},{28,32},{32,28},{36,40... | collective-permute-start | bytes 294920 | tf_op jit(solution)/shard_map/ppermute | solution.py:591
  32.5 13.5 %collective-permute-start.11 = (f32[3,64,1024]{2,1,0:T(8,128)S(1)}, f32[3,64,1024]{2,1,0:T(8,128)S(1)}, u32[]{:S(2)}, u32[]{:S(2)}) collective-permute-start(f32[3,64,1024]{2,1,0:T(8,128)S(1)} %get-tuple-element.77), channel_id=1, source_target_pairs={{0,4},{4,0},{8,12},{12,8},{16,20},{20,16},{24,28},{28,24},{32,36},... | collective-permute-start | bytes 2359304 | tf_op jit(solution)/shard_map/ppermute | solution.py:619
  32.5 17.7 %collective-permute-start.7 = (f32[3,64,1024]{2,1,0:T(8,128)S(1)}, f32[3,64,1024]{2,1,0:T(8,128)S(1)}, u32[]{:S(2)}, u32[]{:S(2)}) collective-permute-start(f32[3,64,1024]{2,1,0:T(8,128)S(1)} %get-tuple-element.73), channel_id=1, source_target_pairs={{4,8},{8,4},{12,16},{16,12},{20,24},{24,20},{28,32},{32,28},{36,40... | collective-permute-start | bytes 2359304 | tf_op jit(solution)/shard_map/ppermute | solution.py:617
  36.1 6.2 %collective-permute-start.8 = (f32[4,8,1024]{2,1,0:T(8,128)S(1)}, f32[4,8,1024]{2,1,0:T(8,128)S(1)}, u32[]{:S(2)}, u32[]{:S(2)}) collective-permute-start(f32[4,8,1024]{2,1,0:T(8,128)S(1)} %get-tuple-element.65.after), channel_id=1, source_target_pairs={{0,1},{1,2},{2,3},{3,0},{4,5},{5,6},{6,7},{7,4},{8,9},{9,10},{10,1... | collective-permute-start | bytes 393224 | tf_op jit(solution)/shard_map/ppermute | solution.py:529
  36.8 5.5 %collective-permute-start.9 = (f32[4,8,1024]{2,1,0:T(8,128)S(1)}, f32[4,8,1024]{2,1,0:T(8,128)S(1)}, u32[]{:S(2)}, u32[]{:S(2)}) collective-permute-start(f32[4,8,1024]{2,1,0:T(8,128)S(1)} %get-tuple-element.74), channel_id=1, source_target_pairs={{0,3},{1,0},{2,1},{3,2},{4,7},{5,4},{6,5},{7,6},{8,11},{9,8},{10,9... | collective-permute-start | bytes 393224 | tf_op jit(solution)/shard_map/ppermute | solution.py:529
  42.4 3.6 %collective-permute-start.12 = (f32[2,8,1024]{2,1,0:T(8,128)S(1)}, f32[2,8,1024]{2,1,0:T(8,128)S(1)}, u32[]{:S(2)}, u32[]{:S(2)}) collective-permute-start(f32[2,8,1024]{2,1,0:T(8,128)S(1)} %get-tuple-element.78), channel_id=1, source_target_pairs={{0,4},{4,0},{8,12},{12,8},{16,20},{20,16},{24,28},{28,24},{32,36},... | collective-permute-start | bytes 196616 | tf_op jit(solution)/shard_map/ppermute | solution.py:641
  42.5 7.7 %collective-permute-start.10 = (f32[2,8,1024]{2,1,0:T(8,128)S(1)}, f32[2,8,1024]{2,1,0:T(8,128)S(1)}, u32[]{:S(2)}, u32[]{:S(2)}) collective-permute-start(f32[2,8,1024]{2,1,0:T(8,128)S(1)} %get-tuple-element.76), channel_id=1, source_target_pairs={{4,8},{8,4},{12,16},{16,12},{20,24},{24,20},{28,32},{32,28},{36,40... | collective-permute-start | bytes 196616 | tf_op jit(solution)/shard_map/ppermute | solution.py:641

commit v9 on v8

--- a/solution.py
+++ b/solution.py
@@ -240,7 +240,7 @@
                     dst[x, row, 256 * j + 128 : 256 * j + 256] = pltpu.roll(jnp.where(low, oj, ej), 4, 0)
         return carry
 
-    lax.fori_loop(0, 8, body, 0, unroll=4)
+    lax.fori_loop(0, 8, body, 0, unroll=8)
 
 
 def edge_rows(mine, below, above):
@@ -439,10 +439,10 @@
             ref[e - start, 8 * t : 8 * t + 8, :] = value
 
 
-def step_one(coef, u0, e, r_held, u1_held):
+def step_one(coef, u0, e, r_held, u1_held, tiles=None):
     a, b = sweep_factors()[0]
     plane = Plane(u0, e)
-    for t in range(8 if e in (1, 8) else 9):
+    for t in tiles or range(8 if e in (1, 8) else 9):
         u, res = coupled(coef, u0, plane, t)
         put(r_held, e, t, res)
         put(u1_held, e, t, a * u + b * res)
@@ -486,23 +486,39 @@
     step_three(coef, p_ref, u0, stored(*u1_held), stored(*u2_held), stored(*r2_held), 6, plane_of(par, 3), done_ref, 0)
 
 
+def either(early, late):
+    return lambda e, t: early(e, t) if e < 4 and t in ahead(e) else late(e, t)
+
+
+def ahead(e):
+    return range(8) if e == 3 else range(1, 7)
+
+
+def middle_kernel(fx, fym, fyp, fzm, fzp, inv, u_ref, b_ref, y_ref, after, u1_out, r_out):
+    par, has_b, mine, v = place()
+    inside = jnp.where(has_b, 1.0, 0.0)
+    u0 = reader(par, inside, u_ref, None, b_ref, y_ref)
+    for e in (1, 2, 3):
+        step_one((fx, fym, fyp, fzm, fzp, inv), u0, e, ((r_out, 2, 4),), ((u1_out, 1, 4),), ahead(e))
+
+
 def far_kernel(p_ref, fx, fym, fyp, fzm, fzp, inv, u_ref, b_ref, y_ref, cb_ref, u1_in, r_in, u2_in, done_ref,
-               out_hbm, u1_far, r_far, u2_far, out_ref, sem):
+               u1_mid, r_mid, out_hbm, u1_far, r_far, u2_far, out_ref, sem):
     par, has_b, mine, v = place()
     inside = jnp.where(has_b, 1.0, 0.0)
     coef = (fx, fym, fyp, fzm, fzp, inv)
     u0 = reader(par, inside, u_ref, None, b_ref, y_ref, None, cb_ref)
     u1_new = ((u1_far, 1, 4),)
-    u1 = stored(*u1_new, (u1_in, 4, 6))
+    u1 = either(stored((u1_mid, 1, 4)), stored(*u1_new, (u1_in, 4, 6)))
     r1_new = ((r_far, 2, 4),)
-    r1 = stored(*r1_new, (r_in, 4, 5))
+    r1 = either(stored((r_mid, 2, 4)), stored(*r1_new, (r_in, 4, 5)))
     r2_new = ((r_far.at[2:4], 3, 5),)
     r2 = stored(*r2_new, (r_in.at[1:2], 5, 6))
     u2_new = ((u2_far, 2, 5),)
     u2 = stored(*u2_new, (u2_in, 5, 7))
     sends = begin([(done_ref.at[0], out_hbm.at[plane_of(par, 3)])], sem, 3)
     for e in (1, 2, 3):
-        step_one(coef, u0, e, r1_new, u1_new)
+        step_one(coef, u0, e, r1_new, u1_new, [t for t in range(8 if e == 1 else 9) if t not in ahead(e)])
     for e in (2, 3, 4):
         step_two(coef, u1, r1, e, r2_new, u2_new)
     for e in (3, 4, 5):
@@ -651,16 +667,26 @@
         name="near",
     )(potential, *operator, u, late_a, y_late, corner_a)
 
+    u1_mid, r_mid = pl.pallas_call(
+        middle_kernel,
+        out_shape=(shape(3, 72, 1024), shape(2, 72, 1024)),
+        in_specs=[VM] * 9 + [ANY],
+        out_specs=(VM,) * 2,
+        compiler_params=grant(30),
+        cost_estimate=pl.CostEstimate(flops=8000000, bytes_accessed=4000000, transcendentals=0),
+        name="middle",
+    )(*operator, u, late_b, y_late, done)
+
     potential_next = pl.pallas_call(
         far_kernel,
         out_shape=shape(4, 64, 1024),
-        in_specs=[VM] * 15,
+        in_specs=[VM] * 17,
         out_specs=ANY,
         scratch_shapes=[big(3), big(4), big(3), pltpu.VMEM((3, 64, 1024), F32), pltpu.SemaphoreType.DMA((4,))],
         compiler_params=grant(30),
         cost_estimate=pl.CostEstimate(flops=25000000, bytes_accessed=10000000, transcendentals=0),
         name="far",
-    )(potential, *operator, u, late_b, y_late, corner_b, u1, r, u2, done)
+    )(potential, *operator, u, late_b, y_late, corner_b, u1, r, u2, done, u1_mid, r_mid)
     return potential_next, states_next, membrane.reshape(16384)
 
 

time: 53.8 us -> 53.9 us (level)
  waiting for transfers between devices: 3.5 us -> 5.57 us
  starting transfers between devices: 24.8 us -> 23.2 us
    ppermute x5, waiting for transfers between devices: 0.06 us -> 2.4 us  [per_device(): on_mem = lambda x, pairs: lax.ppermute(x, 'mem', pairs)]
    ppermute x5, starting transfers between devices: 8.59 us -> 7.38 us  [per_device(): on_mem = lambda x, pairs: lax.ppermute(x, 'mem', pairs)]
    pallas_call x0 -> x1, Pallas kernels: none -> 0.59 us  [per_device(): pl.pallas_call(middle_kernel, out_shape=(shape(3, 72, 1024), shape(2, 72,...]
  transfers between devices with their start and end apart: 13 -> 13, of which waited for: 3 -> 4; matrix products, arithmetic and copies ran while one was open for 0% -> 0% of each run, Pallas kernels for 28% -> 28%
where the time goes in v9:
time: 53.9 us; the launch traced here: 53.7 us
  Pallas kernels  23.7 us (44%)
  starting transfers between devices  23.2 us (43%)
  waiting for transfers between devices  5.57 us (10%)
  between operations  1.12 us (2%)
    ppermute x5, starting transfers between devices, per_device(): on_mem = lambda x, pairs: lax.ppermute(x, 'mem', pairs)  7.38 us
    ppermute x2, starting transfers between devices, per_device(): early_b, early_a = (to_b(send_b), to_a(send_a))  6.39 us
    pallas_call x1, Pallas kernels, per_device(): pl.pallas_call(gather_kernel, out_shape=(near(40, 16384), near(128, 128),...  4.83 us
    pallas_call x1, Pallas kernels, per_device(): pl.pallas_call(ionic_kernel, out_shape=(shape(40, 16384), near(128, 128))...  4.2 us
    ppermute x1, starting transfers between devices, per_device(): late_b = to_b(u_b)  3.44 us
    ppermute x2, starting transfers between devices, per_device(): corner_b, corner_a = (to_b(corner_b), to_a(corner_a))  3.23 us
    pallas_call x2, Pallas kernels, scatter(): pl.pallas_call(functools.partial(scatter_kernel, first), out_shape=(near(...  2.97 us
    pallas_call x1, Pallas kernels, per_device(): pl.pallas_call(operator_kernel, out_shape=(shape(9, 72, 1024),) + (shape(...  2.89 us
  transfers between devices with their start and end apart: 13, of which 4 were waited for; matrix products, arithmetic and copies ran while one was open for 0% of the time, Pallas kernels for 28%

profile of v9, /device:TPU:6, one launch (start us, length us, event | category | flops | bytes accessed | tf_op | source)
XLA Modules:
  0.0 53.7 jit_solution(12928018683210973844)
XLA Ops:
  0.7 4.8 %voltages.1 = (f32[40,16384]{1,0:T(8,128)S(1)}, f32[128,128]{1,0:T(8,128)S(1)}, f32[1,128]{1,0:T(1,128)S(1)}, f32[128,128]{1,0:T(8,128)S(1)}, s32[8,128]{1,0:T(8...) custom-call(s32[64]{0:T(128)} %cnt.3, ...), custom_call_target="tpu_custom_call" | custom-call | flops 4000000 | bytes 5000000 | tf_op jit(solution)/shard_map/voltages/pallas_call | solution.py:553
  5.5 0.1 collective-permute-start
  5.6 6.3 %collective-permute-start.1 = (f32[4,64,1024]{2,1,0:T(8,128)S(1)}, f32[4,64,1024]{2,1,0:T(8,128)S(1)}, u32[]{:S(2)}, u32[]{:S(2)}) collective-permute-start(f32[4,64,1024]{2,1,0:T(8,128)S(1)} %get-tuple-element.47), channel_id=1, source_target_pairs={{4,8},{8,4},{12,16},{16,12},{20,24},{24,20},{28,32},{32,28},{36,40... | collective-permute-start | bytes 3145736 | tf_op jit(solution)/shard_map/ppermute | solution.py:571
  11.9 1.6 %collective-permute-start.2 = (f32[9,8,1024]{2,1,0:T(8,128)S(1)}, f32[9,8,1024]{2,1,0:T(8,128)S(1)}, u32[]{:S(2)}, u32[]{:S(2)}) collective-permute-start(f32[9,8,1024]{2,1,0:T(8,128)S(1)} %get-tuple-element.48), channel_id=1, source_target_pairs={{0,1},{1,2},{2,3},{3,0},{4,5},{5,6},{6,7},{7,4},{8,9},{9,10},{10,1... | collective-permute-start | bytes 884744 | tf_op jit(solution)/shard_map/ppermute | solution.py:545
  13.6 1.7 %collective-permute-start.3 = (f32[9,8,1024]{2,1,0:T(8,128)S(1)}, f32[9,8,1024]{2,1,0:T(8,128)S(1)}, u32[]{:S(2)}, u32[]{:S(2)}) collective-permute-start(f32[9,8,1024]{2,1,0:T(8,128)S(1)} %get-tuple-element.49), channel_id=1, source_target_pairs={{0,3},{1,0},{2,1},{3,2},{4,7},{5,4},{6,5},{7,6},{8,11},{9,8},{10,9... | collective-permute-start | bytes 884744 | tf_op jit(solution)/shard_map/ppermute | solution.py:545
  15.2 2.0 %collective-permute-start.4 = (f32[1,128]{1,0:T(1,128)S(1)}, f32[1,128]{1,0:T(1,128)S(1)}, u32[]{:S(2)}, u32[]{:S(2)}) collective-permute-start(f32[1,128]{1,0:T(1,128)S(1)} %get-tuple-element.50.cell_ref), channel_id=1, source_target_pairs={{0,2},{1,3},{2,0},{3,1},{4,6},{5,7},{6,4},{7,5},{8,10},{9,11},{10,... | collective-permute-start | bytes 1544 | tf_op jit(solution)/shard_map/ppermute | solution.py:545
  17.3 4.2 %ionic.1 = (f32[40,16384]{1,0:T(8,128)}, f32[128,128]{1,0:T(8,128)S(1)}) custom-call(s32[64]{0:T(128)S(1)} %copy-done.4, s32[64]{0:T(128)S(1)} %copy-done.8, f32[128,128]{1,0:T(8,128)S(1)} %get-tuple-element.51.volt_ref.after, f32[128,128]{1,0:T(8,128)S(1)} %get-tuple-element.52.act_ref, f32[2,40]{1,0:T(2,128)S(1)} %copy-done.6, f32[2,40]{1,0:T(2,128)S(1)} %copy-done.7, ...), custom_call_target="tpu_custom_call" | custom-call | flops 16000000 | bytes 5300000 | tf_op jit(solution)/shard_map/ionic/pallas_call | solution.py:573
  21.5 1.5 %scatter.2 = (f32[2,64,1024]{2,1,0:T(8,128)S(1)}, f32[2,64,1024]{2,1,0:T(8,128)S(1)}) custom-call(f32[128,128]{1,0:T(8,128)S(1)} %get-tuple-element.54.ion_ref, f32[128,128]{1,0:T(8,128)S(1)} %get-tuple-element.52.act_ref, s32[128,128]{1,0:T(8,128)S(1)} %bitcast.7, s32[128,128]{1,0:T(8,128)S(1)} %bitcast.10, f32[128,128]{1,0:T(8,128)S(1)} %get-tuple-element.51.volt_ref.after), custom_call_target="tpu_custom_call" | custom-call | flops 400000000 | bytes 1200000 | tf_op jit(solution)/shard_map/scatter/pallas_call | solution.py:586
  23.1 0.1 collective-permute-start.5
  23.2 2.7 %collective-permute-start.6 = (f32[3,8,1024]{2,1,0:T(8,128)S(1)}, f32[3,8,1024]{2,1,0:T(8,128)S(1)}, u32[]{:S(2)}, u32[]{:S(2)}) collective-permute-start(f32[3,8,1024]{2,1,0:T(8,128)S(1)} %get-tuple-element.58), channel_id=1, source_target_pairs={{4,8},{8,4},{12,16},{16,12},{20,24},{24,20},{28,32},{32,28},{36,40... | collective-permute-start | bytes 294920 | tf_op jit(solution)/shard_map/ppermute | solution.py:607
  25.9 1.5 %scatter.3 = (f32[2,64,1024]{2,1,0:T(8,128)S(1)}, f32[2,64,1024]{2,1,0:T(8,128)S(1)}) custom-call(f32[128,128]{1,0:T(8,128)S(1)} %get-tuple-element.54.ion_ref, f32[128,128]{1,0:T(8,128)S(1)} %get-tuple-element.52.act_ref, s32[128,128]{1,0:T(8,128)S(1)} %bitcast.8, s32[128,128]{1,0:T(8,128)S(1)} %bitcast.11, f32[8,128]{1,0:T(8,128)S(1)} %get-tuple-element.59.after.table_ref), custom_call_target="tpu_custom_call" | custom-call | flops 400000000 | bytes 1200000 | tf_op jit(solution)/shard_map/scatter/pallas_call | solution.py:586
  27.5 2.2 %prepare.1 = (f32[4,64,1024]{2,1,0:T(8,128)S(1)}, f32[4,64,1024]{2,1,0:T(8,128)S(1)}) custom-call(f32[4,64,1024]{2,1,0:T(8,128)S(1)} %copy-done, f32[4,64,1024]{2,1,0:T(8,128)S(1)} %copy-done.1, f32[4,64,1024]{2,1,0:T(8,128)S(1)} %collective-permute-done.a_ref, f32[4,64,1024]{2,1,0:T(8,128)S(1)} %collective-permute-done.1.b_ref, ...), custom_call_target="tpu_custom_call" | custom-call | flops 16000000 | bytes 8000000 | tf_op jit(solution)/shard_map/prepare/pallas_call | solution.py:611
  29.7 1.5 %collective-permute-done.6.tb_ref.cb_ref = f32[3,8,1024]{2,1,0:T(8,128)S(1)} collective-permute-done((f32[3,8,1024]{2,1,0:T(8,128)S(1)}, f32[3,8,1024]{2,1,0:T(8,128)S(1)}, u32[]{:S(2)}, u32[]{:S(2)}) %collective-permute-start.6) | collective-permute-done | bytes 98336 | tf_op jit(solution)/shard_map/ppermute | solution.py:607
  31.3 1.1 %gap.1 = (f32[4,64,1024]{2,1,0:T(8,128)S(1)}, f32[3,64,1024]{2,1,0:T(8,128)S(1)}, f32[3,64,1024]{2,1,0:T(8,128)S(1)}, f32[4,8,1024]{2,1,0:T(8,128)S(1)}, f32[4,8,1024]{2,1,0:T(8,128)S(1)}, /*index=5*/f32[128,128]{1,0:T(8,128)}) custom-call(f32[8,128]{1,0:T(8,128)S(1)} %get-tuple-element.59.after.table_ref, ...), custom_call_target="tpu_custom_call" | custom-call | flops 1000000 | bytes 5000000 | tf_op jit(solution)/shard_map/gap/pallas_call | solution.py:621
  32.3 3.4 %collective-permute-start.7 = (f32[3,64,1024]{2,1,0:T(8,128)S(1)}, f32[3,64,1024]{2,1,0:T(8,128)S(1)}, u32[]{:S(2)}, u32[]{:S(2)}) collective-permute-start(f32[3,64,1024]{2,1,0:T(8,128)S(1)} %get-tuple-element.75), channel_id=1, source_target_pairs={{4,8},{8,4},{12,16},{16,12},{20,24},{24,20},{28,32},{32,28},{36,40... | collective-permute-start | bytes 2359304 | tf_op jit(solution)/shard_map/ppermute | solution.py:633
  35.8 1.2 %collective-permute-start.9 = (f32[4,8,1024]{2,1,0:T(8,128)S(1)}, f32[4,8,1024]{2,1,0:T(8,128)S(1)}, u32[]{:S(2)}, u32[]{:S(2)}) collective-permute-start(f32[4,8,1024]{2,1,0:T(8,128)S(1)} %get-tuple-element.76), channel_id=1, source_target_pairs={{0,3},{1,0},{2,1},{3,2},{4,7},{5,4},{6,5},{7,6},{8,11},{9,8},{10,9... | collective-permute-start | bytes 393224 | tf_op jit(solution)/shard_map/ppermute | solution.py:545
  37.0 0.9 %collective-permute-start.8 = (f32[4,8,1024]{2,1,0:T(8,128)S(1)}, f32[4,8,1024]{2,1,0:T(8,128)S(1)}, u32[]{:S(2)}, u32[]{:S(2)}) collective-permute-start(f32[4,8,1024]{2,1,0:T(8,128)S(1)} %get-tuple-element.67.after), channel_id=1, source_target_pairs={{0,1},{1,2},{2,3},{3,0},{4,5},{5,6},{6,7},{7,4},{8,9},{9,10},{10,1... | collective-permute-start | bytes 393224 | tf_op jit(solution)/shard_map/ppermute | solution.py:545
  37.9 2.9 %operator.1 = (f32[9,72,1024]{2,1,0:T(8,128)S(1)}, f32[8,72,1024]{2,1,0:T(8,128)S(1)}, f32[8,72,1024]{2,1,0:T(8,128)S(1)}, f32[8,72,1024]{2,1,0:T(8,128)S(1)}, f...) custom-call(f32[4,64,1024]{2,1,0:T(8,128)S(1)} %copy-done.1, f32[4,64,1024]{2,1,0:T(8,128)S(1)} %collective-permute-done.a_ref, ...), custom_call_target="tpu_custom_call" | custom-call | flops 16000000 | bytes 17000000 | tf_op jit(solution)/shard_map/operator/pallas_call | solution.py:638
  40.8 2.3 %collective-permute-done.8.below_ref = f32[4,8,1024]{2,1,0:T(8,128)S(1)} collective-permute-done((f32[4,8,1024]{2,1,0:T(8,128)S(1)}, f32[4,8,1024]{2,1,0:T(8,128)S(1)}, u32[]{:S(2)}, u32[]{:S(2)}) %collective-permute-start.8) | collective-permute-done | bytes 131104 | tf_op jit(solution)/shard_map/ppermute | solution.py:545
  43.3 3.1 %collective-permute-start.10 = (f32[2,8,1024]{2,1,0:T(8,128)S(1)}, f32[2,8,1024]{2,1,0:T(8,128)S(1)}, u32[]{:S(2)}, u32[]{:S(2)}) collective-permute-start(f32[2,8,1024]{2,1,0:T(8,128)S(1)} %get-tuple-element.78), channel_id=1, source_target_pairs={{4,8},{8,4},{12,16},{16,12},{20,24},{24,20},{28,32},{32,28},{36,40... | collective-permute-start | bytes 196616 | tf_op jit(solution)/shard_map/ppermute | solution.py:657
  46.4 2.3 %near.1 = (f32[2,72,1024]{2,1,0:T(8,128)S(1)}, f32[2,72,1024]{2,1,0:T(8,128)S(1)}, f32[2,72,1024]{2,1,0:T(8,128)S(1)}, f32[1,64,1024]{2,1,0:T(8,128)S(1)}) custom-call(f32[4,64,1024]{2,1,0:T(8,128)S(1)} %copy-done, f32[9,72,1024]{2,1,0:T(8,128)S(1)} %get-tuple-element.68.fx, f32[8,72,1024]{2,1,0:T(8,128)S(1)} %get-tuple-element.69.fym, ...), custom_call_target="tpu_custom_call" | custom-call | flops 25000000 | bytes 10000000 | tf_op jit(solution)/shard_map/near/pallas_call | solution.py:659
  48.8 0.6 %middle.1 = (f32[3,72,1024]{2,1,0:T(8,128)S(1)}, f32[2,72,1024]{2,1,0:T(8,128)S(1)}) custom-call(f32[9,72,1024]{2,1,0:T(8,128)S(1)} %get-tuple-element.68.fx, f32[8,72,1024]{2,1,0:T(8,128)S(1)} %get-tuple-element.69.fym, f32[8,72,1024]{2,1,0:T(8,128)S(1)} %get-tuple-element.70.fyp, f32[8,72,1024]{2,1,0:T(8,128)S(1)} %get-tuple-element.71.fzm, ...), custom_call_target="tpu_custom_call" | custom-call | flops 8000000 | bytes 4000000 | tf_op jit(solution)/shard_map/middle/pallas_call | solution.py:670
  49.4 1.6 %collective-permute-done.10.cb_ref = f32[2,8,1024]{2,1,0:T(8,128)S(1)} collective-permute-done((f32[2,8,1024]{2,1,0:T(8,128)S(1)}, f32[2,8,1024]{2,1,0:T(8,128)S(1)}, u32[]{:S(2)}, u32[]{:S(2)}) %collective-permute-start.10) | collective-permute-done | bytes 65568 | tf_op jit(solution)/shard_map/ppermute | solution.py:657
  51.0 2.5 %far.1 = f32[4,64,1024]{2,1,0:T(8,128)} custom-call(f32[4,64,1024]{2,1,0:T(8,128)S(1)} %copy-done, f32[9,72,1024]{2,1,0:T(8,128)S(1)} %get-tuple-element.68.fx, f32[8,72,1024]{2,1,0:T(8,128)S(1)} %get-tuple-element.69.fym, f32[8,72,1024]{2,1,0:T(8,128)S(1)} %get-tuple-element.70.fyp, f32[8,72,1024]{2,1,0:T(8,128)S(1)} %get-tuple-element.71.fzm, ...), custom_call_target="tpu_custom_call" | custom-call | flops 25000000 | bytes 10000000 | tf_op jit(solution)/shard_map/far/pallas_call | solution.py:680
  (34 shorter events, 0.3 us)
Async XLA Ops:
  0.6 16.6 %copy-start.4 = (s32[64]{0:T(128)S(1)}, s32[64]{0:T(128)}, u32[]{:S(2)}) copy-start(s32[64]{0:T(128)} %cnt.3) | copy-start | bytes 772
  0.6 16.6 %copy-start.5 = (f32[3,40]{1,0:T(4,128)S(1)}, f32[3,40]{1,0:T(4,128)}, u32[]{:S(2)}) copy-start(f32[3,40]{1,0:T(4,128)} %cond_ref.1) | copy-start | bytes 1444
  0.7 16.6 %copy-start.6 = (f32[2,40]{1,0:T(2,128)S(1)}, f32[2,40]{1,0:T(2,128)}, u32[]{:S(2)}) copy-start(f32[2,40]{1,0:T(2,128)} %scale_ref.1) | copy-start | bytes 964
  0.7 16.6 %copy-start.7 = (f32[2,40]{1,0:T(2,128)S(1)}, f32[2,40]{1,0:T(2,128)}, u32[]{:S(2)}) copy-start(f32[2,40]{1,0:T(2,128)} %slope_ref.1) | copy-start | bytes 964
  0.7 16.6 %copy-start.8 = (s32[64]{0:T(128)S(1)}, s32[64]{0:T(128)}, u32[]{:S(2)}) copy-start(s32[64]{0:T(128)} %typ.1) | copy-start | bytes 772
  0.7 16.6 %copy-start.9 = (f32[40]{0:T(128)S(1)}, f32[40]{0:T(128)}, u32[]{:S(2)}) copy-start(f32[40]{0:T(128)} %param.19) | copy-start | bytes 484
  5.5 21.9 %collective-permute-start = (f32[4,64,1024]{2,1,0:T(8,128)S(1)}, f32[4,64,1024]{2,1,0:T(8,128)S(1)}, u32[]{:S(2)}, u32[]{:S(2)}) collective-permute-start(f32[4,64,1024]{2,1,0:T(8,128)S(1)} %get-tuple-element.46), channel_id=1, source_target_pairs={{0,4},{4,0},{8,12},{12,8},{16,20},{20,16},{24,28},{28,24},{32,36},... | collective-permute-start | bytes 3145736 | tf_op jit(solution)/shard_map/ppermute | solution.py:571
  5.6 21.8 %collective-permute-start.1 = (f32[4,64,1024]{2,1,0:T(8,128)S(1)}, f32[4,64,1024]{2,1,0:T(8,128)S(1)}, u32[]{:S(2)}, u32[]{:S(2)}) collective-permute-start(f32[4,64,1024]{2,1,0:T(8,128)S(1)} %get-tuple-element.47), channel_id=1, source_target_pairs={{4,8},{8,4},{12,16},{16,12},{20,24},{24,20},{28,32},{32,28},{36,40... | collective-permute-start | bytes 3145736 | tf_op jit(solution)/shard_map/ppermute | solution.py:571
  11.9 11.1 %collective-permute-start.2 = (f32[9,8,1024]{2,1,0:T(8,128)S(1)}, f32[9,8,1024]{2,1,0:T(8,128)S(1)}, u32[]{:S(2)}, u32[]{:S(2)}) collective-permute-start(f32[9,8,1024]{2,1,0:T(8,128)S(1)} %get-tuple-element.48), channel_id=1, source_target_pairs={{0,1},{1,2},{2,3},{3,0},{4,5},{5,6},{6,7},{7,4},{8,9},{9,10},{10,1... | collective-permute-start | bytes 884744 | tf_op jit(solution)/shard_map/ppermute | solution.py:545
  13.6 9.5 %collective-permute-start.3 = (f32[9,8,1024]{2,1,0:T(8,128)S(1)}, f32[9,8,1024]{2,1,0:T(8,128)S(1)}, u32[]{:S(2)}, u32[]{:S(2)}) collective-permute-start(f32[9,8,1024]{2,1,0:T(8,128)S(1)} %get-tuple-element.49), channel_id=1, source_target_pairs={{0,3},{1,0},{2,1},{3,2},{4,7},{5,4},{6,5},{7,6},{8,11},{9,8},{10,9... | collective-permute-start | bytes 884744 | tf_op jit(solution)/shard_map/ppermute | solution.py:545
  15.2 7.8 %collective-permute-start.4 = (f32[1,128]{1,0:T(1,128)S(1)}, f32[1,128]{1,0:T(1,128)S(1)}, u32[]{:S(2)}, u32[]{:S(2)}) collective-permute-start(f32[1,128]{1,0:T(1,128)S(1)} %get-tuple-element.50.cell_ref), channel_id=1, source_target_pairs={{0,2},{1,3},{2,0},{3,1},{4,6},{5,7},{6,4},{7,5},{8,10},{9,11},{10,... | collective-permute-start | bytes 1544 | tf_op jit(solution)/shard_map/ppermute | solution.py:545
  17.3 4.3 %copy-start.2 = (s32[16384]{0:T(1024)S(1)}, s32[16384]{0:T(1024)}, u32[]{:S(2)}) copy-start(s32[16384]{0:T(1024)} %param.21) | copy-start | bytes 196612
  17.3 4.3 %copy-start.3 = (s32[16384]{0:T(1024)S(1)}, s32[16384]{0:T(1024)}, u32[]{:S(2)}) copy-start(s32[16384]{0:T(1024)} %param.22) | copy-start | bytes 196612
  21.5 6.0 %copy-start = (f32[4,64,1024]{2,1,0:T(8,128)S(1)}, f32[4,64,1024]{2,1,0:T(8,128)}, u32[]{:S(2)}) copy-start(f32[4,64,1024]{2,1,0:T(8,128)} %p_ref.5) | copy-start | bytes 3145732
  21.5 6.0 %copy-start.1 = (f32[4,64,1024]{2,1,0:T(8,128)S(1)}, f32[4,64,1024]{2,1,0:T(8,128)}, u32[]{:S(2)}) copy-start(f32[4,64,1024]{2,1,0:T(8,128)} %c_ref.3) | copy-start | bytes 3145732
  23.1 6.6 %collective-permute-start.5 = (f32[3,8,1024]{2,1,0:T(8,128)S(1)}, f32[3,8,1024]{2,1,0:T(8,128)S(1)}, u32[]{:S(2)}, u32[]{:S(2)}) collective-permute-start(f32[3,8,1024]{2,1,0:T(8,128)S(1)} %get-tuple-element.57), channel_id=1, source_target_pairs={{0,4},{4,0},{8,12},{12,8},{16,20},{20,16},{24,28},{28,24},{32,36},... | collective-permute-start | bytes 294920 | tf_op jit(solution)/shard_map/ppermute | solution.py:607
  23.2 8.0 %collective-permute-start.6 = (f32[3,8,1024]{2,1,0:T(8,128)S(1)}, f32[3,8,1024]{2,1,0:T(8,128)S(1)}, u32[]{:S(2)}, u32[]{:S(2)}) collective-permute-start(f32[3,8,1024]{2,1,0:T(8,128)S(1)} %get-tuple-element.58), channel_id=1, source_target_pairs={{4,8},{8,4},{12,16},{16,12},{20,24},{24,20},{28,32},{32,28},{36,40... | collective-permute-start | bytes 294920 | tf_op jit(solution)/shard_map/ppermute | solution.py:607
  32.3 14.1 %collective-permute-start.11 = (f32[3,64,1024]{2,1,0:T(8,128)S(1)}, f32[3,64,1024]{2,1,0:T(8,128)S(1)}, u32[]{:S(2)}, u32[]{:S(2)}) collective-permute-start(f32[3,64,1024]{2,1,0:T(8,128)S(1)} %get-tuple-element.79), channel_id=1, source_target_pairs={{0,4},{4,0},{8,12},{12,8},{16,20},{20,16},{24,28},{28,24},{32,36},... | collective-permute-start | bytes 2359304 | tf_op jit(solution)/shard_map/ppermute | solution.py:635
  32.3 16.4 %collective-permute-start.7 = (f32[3,64,1024]{2,1,0:T(8,128)S(1)}, f32[3,64,1024]{2,1,0:T(8,128)S(1)}, u32[]{:S(2)}, u32[]{:S(2)}) collective-permute-start(f32[3,64,1024]{2,1,0:T(8,128)S(1)} %get-tuple-element.75), channel_id=1, source_target_pairs={{4,8},{8,4},{12,16},{16,12},{20,24},{24,20},{28,32},{32,28},{36,40... | collective-permute-start | bytes 2359304 | tf_op jit(solution)/shard_map/ppermute | solution.py:633
  35.8 5.0 %collective-permute-start.9 = (f32[4,8,1024]{2,1,0:T(8,128)S(1)}, f32[4,8,1024]{2,1,0:T(8,128)S(1)}, u32[]{:S(2)}, u32[]{:S(2)}) collective-permute-start(f32[4,8,1024]{2,1,0:T(8,128)S(1)} %get-tuple-element.76), channel_id=1, source_target_pairs={{0,3},{1,0},{2,1},{3,2},{4,7},{5,4},{6,5},{7,6},{8,11},{9,8},{10,9... | collective-permute-start | bytes 393224 | tf_op jit(solution)/shard_map/ppermute | solution.py:545
  37.0 6.2 %collective-permute-start.8 = (f32[4,8,1024]{2,1,0:T(8,128)S(1)}, f32[4,8,1024]{2,1,0:T(8,128)S(1)}, u32[]{:S(2)}, u32[]{:S(2)}) collective-permute-start(f32[4,8,1024]{2,1,0:T(8,128)S(1)} %get-tuple-element.67.after), channel_id=1, source_target_pairs={{0,1},{1,2},{2,3},{3,0},{4,5},{5,6},{6,7},{7,4},{8,9},{9,10},{10,1... | collective-permute-start | bytes 393224 | tf_op jit(solution)/shard_map/ppermute | solution.py:545
  43.2 3.2 %collective-permute-start.12 = (f32[2,8,1024]{2,1,0:T(8,128)S(1)}, f32[2,8,1024]{2,1,0:T(8,128)S(1)}, u32[]{:S(2)}, u32[]{:S(2)}) collective-permute-start(f32[2,8,1024]{2,1,0:T(8,128)S(1)} %get-tuple-element.80), channel_id=1, source_target_pairs={{0,4},{4,0},{8,12},{12,8},{16,20},{20,16},{24,28},{28,24},{32,36},... | collective-permute-start | bytes 196616 | tf_op jit(solution)/shard_map/ppermute | solution.py:657
  43.3 7.7 %collective-permute-start.10 = (f32[2,8,1024]{2,1,0:T(8,128)S(1)}, f32[2,8,1024]{2,1,0:T(8,128)S(1)}, u32[]{:S(2)}, u32[]{:S(2)}) collective-permute-start(f32[2,8,1024]{2,1,0:T(8,128)S(1)} %get-tuple-element.78), channel_id=1, source_target_pairs={{4,8},{8,4},{12,16},{16,12},{20,24},{24,20},{28,32},{32,28},{36,40... | collective-permute-start | bytes 196616 | tf_op jit(solution)/shard_map/ppermute | solution.py:657

commit v10 on v8

--- a/solution.py
+++ b/solution.py
@@ -240,7 +240,7 @@
                     dst[x, row, 256 * j + 128 : 256 * j + 256] = pltpu.roll(jnp.where(low, oj, ej), 4, 0)
         return carry
 
-    lax.fori_loop(0, 8, body, 0, unroll=4)
+    lax.fori_loop(0, 8, body, 0, unroll=8)
 
 
 def edge_rows(mine, below, above):

time: 53.8 us -> 53.5 us (level)
  no operation moved by 1% of the time
where the time goes in v10:
time: 53.5 us; the launch traced here: 53 us
  starting transfers between devices  24.9 us (47%)
  Pallas kernels  23.6 us (44%)
  waiting for transfers between devices  3.33 us (6%)
  between operations  1.11 us (2%)
    ppermute x5, starting transfers between devices, per_device(): on_mem = lambda x, pairs: lax.ppermute(x, 'mem', pairs)  8.59 us
    ppermute x2, starting transfers between devices, per_device(): early_b, early_a = (to_b(send_b), to_a(send_a))  6.39 us
    pallas_call x1, Pallas kernels, per_device(): pl.pallas_call(gather_kernel, out_shape=(near(40, 16384), near(128, 128),...  4.83 us
    pallas_call x1, Pallas kernels, per_device(): pl.pallas_call(ionic_kernel, out_shape=(shape(40, 16384), near(128, 128))...  4.19 us
    ppermute x2, starting transfers between devices, per_device(): corner_b, corner_a = (to_b(corner_b), to_a(corner_a))  3.71 us
    ppermute x1, starting transfers between devices, per_device(): late_b = to_b(u_b)  3.44 us
    pallas_call x1, Pallas kernels, per_device(): pl.pallas_call(far_kernel, out_shape=shape(4, 64, 1024), in_specs=[VM] *...  3.04 us
    pallas_call x2, Pallas kernels, scatter(): pl.pallas_call(functools.partial(scatter_kernel, first), out_shape=(near(...  2.96 us
  transfers between devices with their start and end apart: 13, of which 3 were waited for; matrix products, arithmetic and copies ran while one was open for 0% of the time, Pallas kernels for 28%

profile of v10, /device:TPU:6, one launch (start us, length us, event | category | flops | bytes accessed | tf_op | source)
XLA Modules:
  0.0 53.0 jit_solution(1816844384752124657)
XLA Ops:
  0.7 4.8 %voltages.1 = (f32[40,16384]{1,0:T(8,128)S(1)}, f32[128,128]{1,0:T(8,128)S(1)}, f32[1,128]{1,0:T(1,128)S(1)}, f32[128,128]{1,0:T(8,128)S(1)}, s32[8,128]{1,0:T(8...) custom-call(s32[64]{0:T(128)} %cnt.3, ...), custom_call_target="tpu_custom_call" | custom-call | flops 4000000 | bytes 5000000 | tf_op jit(solution)/shard_map/voltages/pallas_call | solution.py:537
  5.5 0.1 collective-permute-start
  5.6 6.3 %collective-permute-start.1 = (f32[4,64,1024]{2,1,0:T(8,128)S(1)}, f32[4,64,1024]{2,1,0:T(8,128)S(1)}, u32[]{:S(2)}, u32[]{:S(2)}) collective-permute-start(f32[4,64,1024]{2,1,0:T(8,128)S(1)} %get-tuple-element.45), channel_id=1, source_target_pairs={{4,8},{8,4},{12,16},{16,12},{20,24},{24,20},{28,32},{32,28},{36,40... | collective-permute-start | bytes 3145736 | tf_op jit(solution)/shard_map/ppermute | solution.py:555
  11.9 1.6 %collective-permute-start.2 = (f32[9,8,1024]{2,1,0:T(8,128)S(1)}, f32[9,8,1024]{2,1,0:T(8,128)S(1)}, u32[]{:S(2)}, u32[]{:S(2)}) collective-permute-start(f32[9,8,1024]{2,1,0:T(8,128)S(1)} %get-tuple-element.46), channel_id=1, source_target_pairs={{0,1},{1,2},{2,3},{3,0},{4,5},{5,6},{6,7},{7,4},{8,9},{9,10},{10,1... | collective-permute-start | bytes 884744 | tf_op jit(solution)/shard_map/ppermute | solution.py:529
  13.6 1.7 %collective-permute-start.3 = (f32[9,8,1024]{2,1,0:T(8,128)S(1)}, f32[9,8,1024]{2,1,0:T(8,128)S(1)}, u32[]{:S(2)}, u32[]{:S(2)}) collective-permute-start(f32[9,8,1024]{2,1,0:T(8,128)S(1)} %get-tuple-element.47), channel_id=1, source_target_pairs={{0,3},{1,0},{2,1},{3,2},{4,7},{5,4},{6,5},{7,6},{8,11},{9,8},{10,9... | collective-permute-start | bytes 884744 | tf_op jit(solution)/shard_map/ppermute | solution.py:529
  15.2 2.0 %collective-permute-start.4 = (f32[1,128]{1,0:T(1,128)S(1)}, f32[1,128]{1,0:T(1,128)S(1)}, u32[]{:S(2)}, u32[]{:S(2)}) collective-permute-start(f32[1,128]{1,0:T(1,128)S(1)} %get-tuple-element.48.cell_ref), channel_id=1, source_target_pairs={{0,2},{1,3},{2,0},{3,1},{4,6},{5,7},{6,4},{7,5},{8,10},{9,11},{10,... | collective-permute-start | bytes 1544 | tf_op jit(solution)/shard_map/ppermute | solution.py:529
  17.3 4.2 %ionic.1 = (f32[40,16384]{1,0:T(8,128)}, f32[128,128]{1,0:T(8,128)S(1)}) custom-call(s32[64]{0:T(128)S(1)} %copy-done.4, s32[64]{0:T(128)S(1)} %copy-done.8, f32[128,128]{1,0:T(8,128)S(1)} %get-tuple-element.49.volt_ref.after, f32[128,128]{1,0:T(8,128)S(1)} %get-tuple-element.50.act_ref, f32[2,40]{1,0:T(2,128)S(1)} %copy-done.6, f32[2,40]{1,0:T(2,128)S(1)} %copy-done.7, ...), custom_call_target="tpu_custom_call" | custom-call | flops 16000000 | bytes 5300000 | tf_op jit(solution)/shard_map/ionic/pallas_call | solution.py:557
  21.5 1.5 %scatter.2 = (f32[2,64,1024]{2,1,0:T(8,128)S(1)}, f32[2,64,1024]{2,1,0:T(8,128)S(1)}) custom-call(f32[128,128]{1,0:T(8,128)S(1)} %get-tuple-element.52.ion_ref, f32[128,128]{1,0:T(8,128)S(1)} %get-tuple-element.50.act_ref, s32[128,128]{1,0:T(8,128)S(1)} %bitcast.7, s32[128,128]{1,0:T(8,128)S(1)} %bitcast.10, f32[128,128]{1,0:T(8,128)S(1)} %get-tuple-element.49.volt_ref.after), custom_call_target="tpu_custom_call" | custom-call | flops 400000000 | bytes 1200000 | tf_op jit(solution)/shard_map/scatter/pallas_call | solution.py:570
  23.0 0.1 early_edges.1
  23.1 0.1 collective-permute-start.5
  23.2 2.7 %collective-permute-start.6 = (f32[3,8,1024]{2,1,0:T(8,128)S(1)}, f32[3,8,1024]{2,1,0:T(8,128)S(1)}, u32[]{:S(2)}, u32[]{:S(2)}) collective-permute-start(f32[3,8,1024]{2,1,0:T(8,128)S(1)} %get-tuple-element.56), channel_id=1, source_target_pairs={{4,8},{8,4},{12,16},{16,12},{20,24},{24,20},{28,32},{32,28},{36,40... | collective-permute-start | bytes 294920 | tf_op jit(solution)/shard_map/ppermute | solution.py:591
  25.9 1.5 %scatter.3 = (f32[2,64,1024]{2,1,0:T(8,128)S(1)}, f32[2,64,1024]{2,1,0:T(8,128)S(1)}) custom-call(f32[128,128]{1,0:T(8,128)S(1)} %get-tuple-element.52.ion_ref, f32[128,128]{1,0:T(8,128)S(1)} %get-tuple-element.50.act_ref, s32[128,128]{1,0:T(8,128)S(1)} %bitcast.8, s32[128,128]{1,0:T(8,128)S(1)} %bitcast.11, f32[8,128]{1,0:T(8,128)S(1)} %get-tuple-element.57.after.table_ref), custom_call_target="tpu_custom_call" | custom-call | flops 400000000 | bytes 1200000 | tf_op jit(solution)/shard_map/scatter/pallas_call | solution.py:570
  27.5 2.2 %prepare.1 = (f32[4,64,1024]{2,1,0:T(8,128)S(1)}, f32[4,64,1024]{2,1,0:T(8,128)S(1)}) custom-call(f32[4,64,1024]{2,1,0:T(8,128)S(1)} %copy-done, f32[4,64,1024]{2,1,0:T(8,128)S(1)} %copy-done.1, f32[4,64,1024]{2,1,0:T(8,128)S(1)} %collective-permute-done.a_ref, f32[4,64,1024]{2,1,0:T(8,128)S(1)} %collective-permute-done.1.b_ref, ...), custom_call_target="tpu_custom_call" | custom-call | flops 16000000 | bytes 8000000 | tf_op jit(solution)/shard_map/prepare/pallas_call | solution.py:595
  29.7 1.5 %collective-permute-done.6.tb_ref.cb_ref = f32[3,8,1024]{2,1,0:T(8,128)S(1)} collective-permute-done((f32[3,8,1024]{2,1,0:T(8,128)S(1)}, f32[3,8,1024]{2,1,0:T(8,128)S(1)}, u32[]{:S(2)}, u32[]{:S(2)}) %collective-permute-start.6) | collective-permute-done | bytes 98336 | tf_op jit(solution)/shard_map/ppermute | solution.py:591
  31.2 1.1 %gap.1 = (f32[4,64,1024]{2,1,0:T(8,128)S(1)}, f32[3,64,1024]{2,1,0:T(8,128)S(1)}, f32[3,64,1024]{2,1,0:T(8,128)S(1)}, f32[4,8,1024]{2,1,0:T(8,128)S(1)}, f32[4,8,1024]{2,1,0:T(8,128)S(1)}, /*index=5*/f32[128,128]{1,0:T(8,128)}) custom-call(f32[8,128]{1,0:T(8,128)S(1)} %get-tuple-element.57.after.table_ref, ...), custom_call_target="tpu_custom_call" | custom-call | flops 1000000 | bytes 5000000 | tf_op jit(solution)/shard_map/gap/pallas_call | solution.py:605
  32.3 3.4 %collective-permute-start.7 = (f32[3,64,1024]{2,1,0:T(8,128)S(1)}, f32[3,64,1024]{2,1,0:T(8,128)S(1)}, u32[]{:S(2)}, u32[]{:S(2)}) collective-permute-start(f32[3,64,1024]{2,1,0:T(8,128)S(1)} %get-tuple-element.73), channel_id=1, source_target_pairs={{4,8},{8,4},{12,16},{16,12},{20,24},{24,20},{28,32},{32,28},{36,40... | collective-permute-start | bytes 2359304 | tf_op jit(solution)/shard_map/ppermute | solution.py:617
  35.7 0.8 %collective-permute-start.8 = (f32[4,8,1024]{2,1,0:T(8,128)S(1)}, f32[4,8,1024]{2,1,0:T(8,128)S(1)}, u32[]{:S(2)}, u32[]{:S(2)}) collective-permute-start(f32[4,8,1024]{2,1,0:T(8,128)S(1)} %get-tuple-element.65.after), channel_id=1, source_target_pairs={{0,1},{1,2},{2,3},{3,0},{4,5},{5,6},{6,7},{7,4},{8,9},{9,10},{10,1... | collective-permute-start | bytes 393224 | tf_op jit(solution)/shard_map/ppermute | solution.py:529
  36.5 2.5 %collective-permute-start.9 = (f32[4,8,1024]{2,1,0:T(8,128)S(1)}, f32[4,8,1024]{2,1,0:T(8,128)S(1)}, u32[]{:S(2)}, u32[]{:S(2)}) collective-permute-start(f32[4,8,1024]{2,1,0:T(8,128)S(1)} %get-tuple-element.74), channel_id=1, source_target_pairs={{0,3},{1,0},{2,1},{3,2},{4,7},{5,4},{6,5},{7,6},{8,11},{9,8},{10,9... | collective-permute-start | bytes 393224 | tf_op jit(solution)/shard_map/ppermute | solution.py:529
  39.1 2.9 %operator.1 = (f32[9,72,1024]{2,1,0:T(8,128)S(1)}, f32[8,72,1024]{2,1,0:T(8,128)S(1)}, f32[8,72,1024]{2,1,0:T(8,128)S(1)}, f32[8,72,1024]{2,1,0:T(8,128)S(1)}, f...) custom-call(f32[4,64,1024]{2,1,0:T(8,128)S(1)} %copy-done.1, f32[4,64,1024]{2,1,0:T(8,128)S(1)} %collective-permute-done.a_ref, ...), custom_call_target="tpu_custom_call" | custom-call | flops 16000000 | bytes 17000000 | tf_op jit(solution)/shard_map/operator/pallas_call | solution.py:622
  42.0 0.1 collective-permute-start.12
  42.1 3.6 %collective-permute-start.10 = (f32[2,8,1024]{2,1,0:T(8,128)S(1)}, f32[2,8,1024]{2,1,0:T(8,128)S(1)}, u32[]{:S(2)}, u32[]{:S(2)}) collective-permute-start(f32[2,8,1024]{2,1,0:T(8,128)S(1)} %get-tuple-element.76), channel_id=1, source_target_pairs={{4,8},{8,4},{12,16},{16,12},{20,24},{24,20},{28,32},{32,28},{36,40... | collective-permute-start | bytes 196616 | tf_op jit(solution)/shard_map/ppermute | solution.py:641
  45.8 2.3 %near.1 = (f32[2,72,1024]{2,1,0:T(8,128)S(1)}, f32[2,72,1024]{2,1,0:T(8,128)S(1)}, f32[2,72,1024]{2,1,0:T(8,128)S(1)}, f32[1,64,1024]{2,1,0:T(8,128)S(1)}) custom-call(f32[4,64,1024]{2,1,0:T(8,128)S(1)} %copy-done, f32[9,72,1024]{2,1,0:T(8,128)S(1)} %get-tuple-element.66.fx, f32[8,72,1024]{2,1,0:T(8,128)S(1)} %get-tuple-element.67.fym, ...), custom_call_target="tpu_custom_call" | custom-call | flops 25000000 | bytes 10000000 | tf_op jit(solution)/shard_map/near/pallas_call | solution.py:643
  48.1 1.7 %collective-permute-done.10.cb_ref = f32[2,8,1024]{2,1,0:T(8,128)S(1)} collective-permute-done((f32[2,8,1024]{2,1,0:T(8,128)S(1)}, f32[2,8,1024]{2,1,0:T(8,128)S(1)}, u32[]{:S(2)}, u32[]{:S(2)}) %collective-permute-start.10) | collective-permute-done | bytes 65568 | tf_op jit(solution)/shard_map/ppermute | solution.py:641
  49.8 3.0 %far.1 = f32[4,64,1024]{2,1,0:T(8,128)} custom-call(f32[4,64,1024]{2,1,0:T(8,128)S(1)} %copy-done, f32[9,72,1024]{2,1,0:T(8,128)S(1)} %get-tuple-element.66.fx, f32[8,72,1024]{2,1,0:T(8,128)S(1)} %get-tuple-element.67.fym, f32[8,72,1024]{2,1,0:T(8,128)S(1)} %get-tuple-element.68.fyp, f32[8,72,1024]{2,1,0:T(8,128)S(1)} %get-tuple-element.69.fzm, ...), custom_call_target="tpu_custom_call" | custom-call | flops 25000000 | bytes 10000000 | tf_op jit(solution)/shard_map/far/pallas_call | solution.py:654
  (33 shorter events, 0.2 us)
Async XLA Ops:
  0.6 16.6 %copy-start.4 = (s32[64]{0:T(128)S(1)}, s32[64]{0:T(128)}, u32[]{:S(2)}) copy-start(s32[64]{0:T(128)} %cnt.3) | copy-start | bytes 772
  0.6 16.6 %copy-start.5 = (f32[3,40]{1,0:T(4,128)S(1)}, f32[3,40]{1,0:T(4,128)}, u32[]{:S(2)}) copy-start(f32[3,40]{1,0:T(4,128)} %cond_ref.1) | copy-start | bytes 1444
  0.7 16.6 %copy-start.6 = (f32[2,40]{1,0:T(2,128)S(1)}, f32[2,40]{1,0:T(2,128)}, u32[]{:S(2)}) copy-start(f32[2,40]{1,0:T(2,128)} %scale_ref.1) | copy-start | bytes 964
  0.7 16.6 %copy-start.7 = (f32[2,40]{1,0:T(2,128)S(1)}, f32[2,40]{1,0:T(2,128)}, u32[]{:S(2)}) copy-start(f32[2,40]{1,0:T(2,128)} %slope_ref.1) | copy-start | bytes 964
  0.7 16.6 %copy-start.8 = (s32[64]{0:T(128)S(1)}, s32[64]{0:T(128)}, u32[]{:S(2)}) copy-start(s32[64]{0:T(128)} %typ.1) | copy-start | bytes 772
  0.7 16.6 %copy-start.9 = (f32[40]{0:T(128)S(1)}, f32[40]{0:T(128)}, u32[]{:S(2)}) copy-start(f32[40]{0:T(128)} %param.19) | copy-start | bytes 484
  5.5 21.9 %collective-permute-start = (f32[4,64,1024]{2,1,0:T(8,128)S(1)}, f32[4,64,1024]{2,1,0:T(8,128)S(1)}, u32[]{:S(2)}, u32[]{:S(2)}) collective-permute-start(f32[4,64,1024]{2,1,0:T(8,128)S(1)} %get-tuple-element.44), channel_id=1, source_target_pairs={{0,4},{4,0},{8,12},{12,8},{16,20},{20,16},{24,28},{28,24},{32,36},... | collective-permute-start | bytes 3145736 | tf_op jit(solution)/shard_map/ppermute | solution.py:555
  5.6 21.8 %collective-permute-start.1 = (f32[4,64,1024]{2,1,0:T(8,128)S(1)}, f32[4,64,1024]{2,1,0:T(8,128)S(1)}, u32[]{:S(2)}, u32[]{:S(2)}) collective-permute-start(f32[4,64,1024]{2,1,0:T(8,128)S(1)} %get-tuple-element.45), channel_id=1, source_target_pairs={{4,8},{8,4},{12,16},{16,12},{20,24},{24,20},{28,32},{32,28},{36,40... | collective-permute-start | bytes 3145736 | tf_op jit(solution)/shard_map/ppermute | solution.py:555
  11.9 11.1 %collective-permute-start.2 = (f32[9,8,1024]{2,1,0:T(8,128)S(1)}, f32[9,8,1024]{2,1,0:T(8,128)S(1)}, u32[]{:S(2)}, u32[]{:S(2)}) collective-permute-start(f32[9,8,1024]{2,1,0:T(8,128)S(1)} %get-tuple-element.46), channel_id=1, source_target_pairs={{0,1},{1,2},{2,3},{3,0},{4,5},{5,6},{6,7},{7,4},{8,9},{9,10},{10,1... | collective-permute-start | bytes 884744 | tf_op jit(solution)/shard_map/ppermute | solution.py:529
  13.6 9.4 %collective-permute-start.3 = (f32[9,8,1024]{2,1,0:T(8,128)S(1)}, f32[9,8,1024]{2,1,0:T(8,128)S(1)}, u32[]{:S(2)}, u32[]{:S(2)}) collective-permute-start(f32[9,8,1024]{2,1,0:T(8,128)S(1)} %get-tuple-element.47), channel_id=1, source_target_pairs={{0,3},{1,0},{2,1},{3,2},{4,7},{5,4},{6,5},{7,6},{8,11},{9,8},{10,9... | collective-permute-start | bytes 884744 | tf_op jit(solution)/shard_map/ppermute | solution.py:529
  15.2 7.8 %collective-permute-start.4 = (f32[1,128]{1,0:T(1,128)S(1)}, f32[1,128]{1,0:T(1,128)S(1)}, u32[]{:S(2)}, u32[]{:S(2)}) collective-permute-start(f32[1,128]{1,0:T(1,128)S(1)} %get-tuple-element.48.cell_ref), channel_id=1, source_target_pairs={{0,2},{1,3},{2,0},{3,1},{4,6},{5,7},{6,4},{7,5},{8,10},{9,11},{10,... | collective-permute-start | bytes 1544 | tf_op jit(solution)/shard_map/ppermute | solution.py:529
  17.3 4.3 %copy-start.2 = (s32[16384]{0:T(1024)S(1)}, s32[16384]{0:T(1024)}, u32[]{:S(2)}) copy-start(s32[16384]{0:T(1024)} %param.21) | copy-start | bytes 196612
  17.3 4.2 %copy-start.3 = (s32[16384]{0:T(1024)S(1)}, s32[16384]{0:T(1024)}, u32[]{:S(2)}) copy-start(s32[16384]{0:T(1024)} %param.22) | copy-start | bytes 196612
  21.5 6.0 %copy-start = (f32[4,64,1024]{2,1,0:T(8,128)S(1)}, f32[4,64,1024]{2,1,0:T(8,128)}, u32[]{:S(2)}) copy-start(f32[4,64,1024]{2,1,0:T(8,128)} %p_ref.5) | copy-start | bytes 3145732
  21.5 6.0 %copy-start.1 = (f32[4,64,1024]{2,1,0:T(8,128)S(1)}, f32[4,64,1024]{2,1,0:T(8,128)}, u32[]{:S(2)}) copy-start(f32[4,64,1024]{2,1,0:T(8,128)} %c_ref.3) | copy-start | bytes 3145732
  23.1 6.6 %collective-permute-start.5 = (f32[3,8,1024]{2,1,0:T(8,128)S(1)}, f32[3,8,1024]{2,1,0:T(8,128)S(1)}, u32[]{:S(2)}, u32[]{:S(2)}) collective-permute-start(f32[3,8,1024]{2,1,0:T(8,128)S(1)} %get-tuple-element.55), channel_id=1, source_target_pairs={{0,4},{4,0},{8,12},{12,8},{16,20},{20,16},{24,28},{28,24},{32,36},... | collective-permute-start | bytes 294920 | tf_op jit(solution)/shard_map/ppermute | solution.py:591
  23.2 8.0 %collective-permute-start.6 = (f32[3,8,1024]{2,1,0:T(8,128)S(1)}, f32[3,8,1024]{2,1,0:T(8,128)S(1)}, u32[]{:S(2)}, u32[]{:S(2)}) collective-permute-start(f32[3,8,1024]{2,1,0:T(8,128)S(1)} %get-tuple-element.56), channel_id=1, source_target_pairs={{4,8},{8,4},{12,16},{16,12},{20,24},{24,20},{28,32},{32,28},{36,40... | collective-permute-start | bytes 294920 | tf_op jit(solution)/shard_map/ppermute | solution.py:591
  32.3 13.5 %collective-permute-start.11 = (f32[3,64,1024]{2,1,0:T(8,128)S(1)}, f32[3,64,1024]{2,1,0:T(8,128)S(1)}, u32[]{:S(2)}, u32[]{:S(2)}) collective-permute-start(f32[3,64,1024]{2,1,0:T(8,128)S(1)} %get-tuple-element.77), channel_id=1, source_target_pairs={{0,4},{4,0},{8,12},{12,8},{16,20},{20,16},{24,28},{28,24},{32,36},... | collective-permute-start | bytes 2359304 | tf_op jit(solution)/shard_map/ppermute | solution.py:619
  32.3 17.5 %collective-permute-start.7 = (f32[3,64,1024]{2,1,0:T(8,128)S(1)}, f32[3,64,1024]{2,1,0:T(8,128)S(1)}, u32[]{:S(2)}, u32[]{:S(2)}) collective-permute-start(f32[3,64,1024]{2,1,0:T(8,128)S(1)} %get-tuple-element.73), channel_id=1, source_target_pairs={{4,8},{8,4},{12,16},{16,12},{20,24},{24,20},{28,32},{32,28},{36,40... | collective-permute-start | bytes 2359304 | tf_op jit(solution)/shard_map/ppermute | solution.py:617
  35.7 6.2 %collective-permute-start.8 = (f32[4,8,1024]{2,1,0:T(8,128)S(1)}, f32[4,8,1024]{2,1,0:T(8,128)S(1)}, u32[]{:S(2)}, u32[]{:S(2)}) collective-permute-start(f32[4,8,1024]{2,1,0:T(8,128)S(1)} %get-tuple-element.65.after), channel_id=1, source_target_pairs={{0,1},{1,2},{2,3},{3,0},{4,5},{5,6},{6,7},{7,4},{8,9},{9,10},{10,1... | collective-permute-start | bytes 393224 | tf_op jit(solution)/shard_map/ppermute | solution.py:529
  36.5 5.5 %collective-permute-start.9 = (f32[4,8,1024]{2,1,0:T(8,128)S(1)}, f32[4,8,1024]{2,1,0:T(8,128)S(1)}, u32[]{:S(2)}, u32[]{:S(2)}) collective-permute-start(f32[4,8,1024]{2,1,0:T(8,128)S(1)} %get-tuple-element.74), channel_id=1, source_target_pairs={{0,3},{1,0},{2,1},{3,2},{4,7},{5,4},{6,5},{7,6},{8,11},{9,8},{10,9... | collective-permute-start | bytes 393224 | tf_op jit(solution)/shard_map/ppermute | solution.py:529
  42.0 3.7 %collective-permute-start.12 = (f32[2,8,1024]{2,1,0:T(8,128)S(1)}, f32[2,8,1024]{2,1,0:T(8,128)S(1)}, u32[]{:S(2)}, u32[]{:S(2)}) collective-permute-start(f32[2,8,1024]{2,1,0:T(8,128)S(1)} %get-tuple-element.78), channel_id=1, source_target_pairs={{0,4},{4,0},{8,12},{12,8},{16,20},{20,16},{24,28},{28,24},{32,36},... | collective-permute-start | bytes 196616 | tf_op jit(solution)/shard_map/ppermute | solution.py:641
  42.1 7.7 %collective-permute-start.10 = (f32[2,8,1024]{2,1,0:T(8,128)S(1)}, f32[2,8,1024]{2,1,0:T(8,128)S(1)}, u32[]{:S(2)}, u32[]{:S(2)}) collective-permute-start(f32[2,8,1024]{2,1,0:T(8,128)S(1)} %get-tuple-element.76), channel_id=1, source_target_pairs={{4,8},{8,4},{12,16},{16,12},{20,24},{24,20},{28,32},{32,28},{36,40... | collective-permute-start | bytes 196616 | tf_op jit(solution)/shard_map/ppermute | solution.py:641
